TPU v7x, 32 devices: a whole 2x2x4 slice. The times are simulated.
32 devices in a mesh: dp: 8 (over y, x, core), seq: 4 (over z).
Axes of the slice: x: 2, y: 2, z: 4, core: 2. Of those that a mesh axis runs over, the one named last changes fastest.
Arguments:
- inputs: bfloat16 [16, 2048, 1024], P('dp', 'seq'), may hold values from -6 to 6
- cotangent: bfloat16 [16, 2048, 1024], P('dp', 'seq'), may hold values from -6 to 6
- full_attention: int32 [16], P('dp'), may hold values from 0 to 1
- mix_gain: float32 [1024], replicated, may hold values from 0.5 to 1.5
- smooth_alpha: float32 [16, 1024], replicated, may hold values from 0.1 to 0.9
- smooth_damp: float32 [16, 1024], replicated, may hold values from 0.0001 to 0.3
- smooth_beta: float32 [16, 1024], replicated, may hold values from -0.75 to 0.75
- smooth_eta: float32 [16, 1024], replicated, may hold values from -1.5 to 1.5
- smooth_omega: float32 [1024], replicated, may hold values from -6 to 6
- value_proj: bfloat16 [1024, 2048], replicated, may hold values from -0.1875 to 0.1875
- mix_proj: bfloat16 [1024, 4224], replicated, may hold values from -0.1875 to 0.1875
- score_affine: float32 [4, 128], replicated, may hold values from -6 to 6
- relative_bias: float32 [4096], replicated, may hold values from -6 to 6
- out_proj: bfloat16 [2048, 1024], replicated, may hold values from -0.5 to 0.5
- feed_gain: float32 [1024], replicated, may hold values from 0.1 to 1.9
- feed_in: bfloat16 [1024, 4096], replicated, may hold values from -0.1875 to 0.1875
- feed_out: bfloat16 [4096, 1024], replicated, may hold values from -0.09375 to 0.09375
Outputs:
- block_out: bfloat16 [16, 2048, 1024], P('dp', 'seq')
- grad_input: float32 [16, 2048, 1024], P('dp', 'seq')
- mix_gain_grad: float32 [1024], replicated
- alpha_grad: float32 [16, 1024], replicated
- damp_grad: float32 [16, 1024], replicated
- beta_grad: float32 [16, 1024], replicated
- eta_grad: float32 [16, 1024], replicated
- omega_grad: float32 [1024], replicated
- value_grad: float32 [1024, 2048], P('dp', 'seq')
- mix_grad: float32 [1024, 4224], P('dp', 'seq')
- affine_grad: float32 [4, 128], replicated
- relative_grad: float32 [4096], replicated
- out_grad: float32 [2048, 1024], P('dp', 'seq')
- feed_gain_grad: float32 [1024], replicated
- feed_in_grad: float32 [1024, 4096], P('dp', 'seq')
- feed_out_grad: float32 [4096, 1024], P('dp', 'seq')
Inputs may be any that keep to these rules, and one draw needn't show every extreme that they name: `full_attention`: 1 marks a sequence whose tokens attend to all earlier tokens of it, 0 one whose tokens attend only within their block of 128 positions.
All inputs are finite; a program needn't handle non-finite values.
Results may differ from a plain program's by a relative error of at most 0.035.
Values may be sent and summed in bfloat16 or wider, within the bound.
No kernel may reach another device: no remote copies, remote signals or barrier semaphores. Data moves between devices by JAX's collectives and lax.ppermute only.
A program may use at most 512 MiB of HBM per device.

v0:
```python
import jax
import jax.numpy as jnp
from jax import lax
from jax.sharding import PartitionSpec as P

STRETCH = 128


EPSILON = 1e-05


def entering(x, axis, join, neutral, backward):
    count = lax.axis_size(axis)
    place = lax.axis_index(axis)
    ahead = count - 1 - place if backward else place
    gathered = jax.tree.map(
        lambda a, kind: lax.all_gather(a.astype(kind), axis), x, (jnp.bfloat16, jnp.bfloat16)
    )
    state = jax.tree.map(lambda a, e: jnp.zeros_like(a) + jnp.asarray(e, a.dtype), x, neutral)

    def one(hop, state):
        source = count - 1 - hop if backward else hop
        return join(
            state,
            jax.tree.map(
                lambda a, own: lax.dynamic_index_in_dim(a, source, 0, False).astype(own.dtype),
                gathered,
                x,
            ),
        )

    return lax.fori_loop(0, ahead, one, state)


def norm_forward(values, gain_vec):
    row_mean = jnp.mean(values, axis=-1, keepdims=True)
    centred = values - row_mean
    inv_std = lax.rsqrt(jnp.mean(centred * centred, axis=-1, keepdims=True) + EPSILON)
    unit_rows = centred * inv_std
    return (unit_rows * gain_vec, unit_rows, inv_std)


def norm_backward(grad_out, gain_vec, unit_rows, inv_std):
    scaled = grad_out * gain_vec
    centred = (
        scaled
        - jnp.mean(scaled, axis=-1, keepdims=True)
        - unit_rows * jnp.mean(scaled * unit_rows, axis=-1, keepdims=True)
    )
    return (centred * inv_std, jnp.sum(grad_out * unit_rows, axis=0))


def silu_slope(pre_act):
    sigmoid_val = jax.nn.sigmoid(pre_act)
    return sigmoid_val * (1.0 + pre_act * (1.0 - sigmoid_val))


def combine_linear(earlier, later):
    return (earlier[0] * later[0], later[0] * earlier[1] + later[1])


def block_states(inputs, coef, decay_rate):
    seq_count, row_count, model_width = inputs.shape
    block_rows = min(16, row_count)
    block_count = row_count // block_rows
    steps = inputs.reshape(seq_count, block_count, block_rows, model_width).transpose(2, 0, 1, 3)

    def advance(carried_state, row_slab):
        carried_state = decay_rate * carried_state + coef * row_slab[:, :, None, :]
        return (carried_state, carried_state)

    zero_state = jnp.zeros((seq_count, block_count) + decay_rate.shape, jnp.float32)
    block_ends, local_state = lax.scan(advance, zero_state, steps)
    return (local_state, block_ends)


def chain_blocks(block_ends, block_power, start_state):

    def link_block(carried_state, block_end):
        return (block_power * carried_state + block_end, carried_state)

    return lax.scan(link_block, start_state, jnp.transpose(block_ends, (1, 0, 2, 3)))


def assemble(local_state, before, decay_rate):
    block_rows = local_state.shape[0]
    seq_count = local_state.shape[1]
    block_count = local_state.shape[2]
    ramp_power = decay_rate[None] ** jnp.arange(1, block_rows + 1, dtype=jnp.float32)[:, None, None]
    whole_state = (
        local_state + ramp_power[:, None, None] * jnp.transpose(before, (1, 0, 2, 3))[None]
    )
    return jnp.transpose(whole_state, (1, 2, 0, 3, 4)).reshape(
        seq_count, block_count * block_rows, decay_rate.shape[0], decay_rate.shape[1]
    )


def skew(window, row_total, col_total):
    period = row_total + col_total
    repeated = jnp.tile(window, row_total + 1)
    flat_part = lax.slice_in_dim(repeated, row_total, row_total + row_total * (period - 1))
    return flat_part.reshape(row_total, period - 1)[:, :col_total]


def unskew(tile_vals, row_total, col_total):
    period = row_total + col_total
    padded = jnp.pad(tile_vals, ((0, 0), (0, period - 1 - col_total)))
    flat_part = padded.reshape(row_total * (period - 1))
    extended = jnp.pad(
        flat_part, (row_total, period * (row_total + 1) - row_total - row_total * (period - 1))
    )
    return jnp.sum(extended.reshape(row_total + 1, period), axis=0)


def attend(query_rows, key_rows, value_rows, bias_tile, allowed, score_scale):
    scores = (
        jnp.einsum("qz,kz->qk", query_rows, key_rows, preferred_element_type=jnp.float32)
        * score_scale
        + bias_tile
    )
    scores = jnp.where(allowed, scores, -1e30)
    row_max = jnp.max(scores, axis=1, keepdims=True)
    exp_terms = jnp.exp(scores - row_max)
    exp_total = jnp.sum(exp_terms, axis=1, keepdims=True)
    soft_probs = (exp_terms / exp_total).astype(jnp.bfloat16)
    attended = jnp.dot(soft_probs, value_rows, preferred_element_type=jnp.float32)
    return (attended, row_max[:, 0] + jnp.log(exp_total[:, 0]))


def score_grads(
    query_rows,
    key_rows,
    value_rows,
    grad_rows,
    log_total,
    delta_rows,
    bias_tile,
    allowed,
    score_scale,
):
    scores = (
        jnp.einsum("qz,kz->qk", query_rows, key_rows, preferred_element_type=jnp.float32)
        * score_scale
        + bias_tile
    )
    soft_probs = jnp.where(allowed, jnp.exp(scores - log_total[:, None]), 0.0)
    grad_probs = jnp.einsum("qv,kv->qk", grad_rows, value_rows, preferred_element_type=jnp.float32)
    grad_scores = (soft_probs * (grad_probs - delta_rows[:, None])).astype(jnp.bfloat16)
    return (soft_probs, grad_scores)


def attend_back(
    query_rows,
    key_rows,
    value_rows,
    grad_rows,
    log_total,
    delta_rows,
    bias_tile,
    allowed,
    score_scale,
):
    soft_probs, grad_scores = score_grads(
        query_rows,
        key_rows,
        value_rows,
        grad_rows,
        log_total,
        delta_rows,
        bias_tile,
        allowed,
        score_scale,
    )
    grad_query = jnp.dot(grad_scores, key_rows, preferred_element_type=jnp.float32) * score_scale
    grad_key = (
        jnp.einsum("qk,qz->kz", grad_scores, query_rows, preferred_element_type=jnp.float32)
        * score_scale
    )
    grad_value = jnp.einsum(
        "qk,qv->kv", soft_probs.astype(jnp.bfloat16), grad_rows, preferred_element_type=jnp.float32
    )
    return (grad_query, grad_key, grad_value, grad_scores)


def full_forward(query_rows, key_all, value_all, relative_bias, offset, score_scale):
    row_count = query_rows.shape[0]
    length = key_all.shape[0]
    window = lax.dynamic_slice_in_dim(
        relative_bias, length - offset - row_count, row_count + length
    )
    bias_tile = skew(window, row_count, length)
    allowed = jnp.arange(length)[None, :] <= offset + jnp.arange(row_count)[:, None]
    return attend(query_rows, key_all, value_all, bias_tile, allowed, score_scale)


def stretch_forward(query_rows, key_rows, value_rows, relative_bias, score_scale):
    row_count, key_width = query_rows.shape
    value_width = value_rows.shape[1]
    length = relative_bias.shape[0] // 2
    block_count = row_count // STRETCH
    window = lax.slice_in_dim(relative_bias, length - STRETCH, length + STRETCH)
    bias_tile = skew(window, STRETCH, STRETCH)
    allowed = jnp.arange(STRETCH)[None, :] <= jnp.arange(STRETCH)[:, None]

    def one_block(query_part, key_part, value_part):
        return attend(query_part, key_part, value_part, bias_tile, allowed, score_scale)

    attended, log_total = jax.vmap(one_block)(
        query_rows.reshape(block_count, STRETCH, key_width),
        key_rows.reshape(block_count, STRETCH, key_width),
        value_rows.reshape(block_count, STRETCH, value_width),
    )
    return (attended.reshape(row_count, value_width), log_total.reshape(row_count))


def full_backward(
    query_rows,
    key_all,
    value_all,
    grad_rows,
    log_total,
    delta_rows,
    relative_bias,
    offset,
    score_scale,
):
    row_count = query_rows.shape[0]
    length = key_all.shape[0]
    start_index = length - offset - row_count
    window = lax.dynamic_slice_in_dim(relative_bias, start_index, row_count + length)
    bias_tile = skew(window, row_count, length)
    allowed = jnp.arange(length)[None, :] <= offset + jnp.arange(row_count)[:, None]
    grad_query, grad_key, grad_value, grad_scores = attend_back(
        query_rows,
        key_all,
        value_all,
        grad_rows,
        log_total,
        delta_rows,
        bias_tile,
        allowed,
        score_scale,
    )
    rel_window = unskew(grad_scores.astype(jnp.float32), row_count, length)
    rel_term = lax.dynamic_update_slice_in_dim(
        jnp.zeros((2 * length,), jnp.float32), rel_window, start_index, 0
    )
    return (grad_query, grad_key, grad_value, rel_term)


def stretch_backward(
    query_rows, key_rows, value_rows, grad_rows, log_total, delta_rows, relative_bias, score_scale
):
    row_count, key_width = query_rows.shape
    value_width = value_rows.shape[1]
    length = relative_bias.shape[0] // 2
    block_count = row_count // STRETCH
    window = lax.slice_in_dim(relative_bias, length - STRETCH, length + STRETCH)
    bias_tile = skew(window, STRETCH, STRETCH)
    allowed = jnp.arange(STRETCH)[None, :] <= jnp.arange(STRETCH)[:, None]

    def one_block(query_part, key_part, value_part, grad_part, total_part, delta_part):
        return attend_back(
            query_part,
            key_part,
            value_part,
            grad_part,
            total_part,
            delta_part,
            bias_tile,
            allowed,
            score_scale,
        )

    grad_query, grad_key, grad_value, grad_scores = jax.vmap(one_block)(
        query_rows.reshape(block_count, STRETCH, key_width),
        key_rows.reshape(block_count, STRETCH, key_width),
        value_rows.reshape(block_count, STRETCH, value_width),
        grad_rows.reshape(block_count, STRETCH, value_width),
        log_total.reshape(block_count, STRETCH),
        delta_rows.reshape(block_count, STRETCH),
    )
    rel_window = unskew(jnp.sum(grad_scores.astype(jnp.float32), axis=0), STRETCH, STRETCH)
    rel_term = lax.dynamic_update_slice_in_dim(
        jnp.zeros((2 * length,), jnp.float32), rel_window, length - STRETCH, 0
    )
    return (
        grad_query.reshape(row_count, key_width),
        grad_key.reshape(row_count, key_width),
        grad_value.reshape(row_count, value_width),
        rel_term,
    )


def local(
    inputs,
    cotangent,
    full_attention,
    mix_gain,
    smooth_alpha,
    smooth_damp,
    smooth_beta,
    smooth_eta,
    smooth_omega,
    value_proj,
    mix_proj,
    score_affine,
    relative_bias,
    out_proj,
    feed_gain,
    feed_in,
    feed_out,
):
    seq_count, row_count, model_width = inputs.shape
    key_width = score_affine.shape[1]
    value_width = value_proj.shape[1]
    token_count = seq_count * row_count
    offset = lax.axis_index("seq") * row_count
    score_scale = float(key_width) ** (-0.5)
    length = relative_bias.shape[0] // 2
    flat_rows = inputs.reshape(token_count, model_width).astype(jnp.float32)
    normed, unit_one, inv_one = norm_forward(flat_rows, mix_gain)
    normed_seq = normed.reshape(seq_count, row_count, model_width)
    decay_rate = 1.0 - smooth_alpha * smooth_damp
    rate_in = smooth_alpha * smooth_beta
    span_power = decay_rate**row_count
    block_power = decay_rate ** min(16, row_count)
    empty_state = jnp.zeros((seq_count,) + decay_rate.shape, jnp.float32)
    unit_power = jnp.ones_like(decay_rate)
    local_state, block_ends = block_states(normed_seq, rate_in, decay_rate)
    zero_last, _ = chain_blocks(block_ends, block_power, empty_state)
    _, incoming = entering(
        (span_power, zero_last), "seq", combine_linear, (unit_power, empty_state), False
    )
    _, before_h = chain_blocks(block_ends, block_power, incoming)
    states = assemble(local_state, before_h, decay_rate)
    smoothed = (jnp.sum(smooth_eta * states, axis=2) + smooth_omega * normed_seq).reshape(
        token_count, model_width
    )
    mixed_low = jax.nn.silu(smoothed).astype(jnp.bfloat16)
    mix_base = jnp.dot(mixed_low, mix_proj, preferred_element_type=jnp.float32)
    shared_pre = mix_base[:, :key_width]
    reset_pre = mix_base[:, key_width : key_width + value_width]
    update_pre = mix_base[:, key_width + value_width : key_width + value_width + model_width]
    cand_pre = mix_base[:, key_width + value_width + model_width :]
    shared = jax.nn.silu(shared_pre)
    query_low = (shared * score_affine[0] + score_affine[1]).astype(jnp.bfloat16)
    key_low = (shared * score_affine[2] + score_affine[3]).astype(jnp.bfloat16)
    normed_low = normed.astype(jnp.bfloat16)
    value_pre = jnp.dot(normed_low, value_proj, preferred_element_type=jnp.float32)
    value_low = jax.nn.silu(value_pre).astype(jnp.bfloat16)
    query_seq = query_low.reshape(seq_count, row_count, key_width)
    key_seq = key_low.reshape(seq_count, row_count, key_width)
    value_seq = value_low.reshape(seq_count, row_count, value_width)
    keys_all, values_all = (
        lax.all_gather(key_seq, "seq", axis=1, tiled=True),
        lax.all_gather(value_seq, "seq", axis=1, tiled=True),
    )

    def forward_sequence(seq_item):
        query_rows, key_rows, value_rows, key_all, value_all, full_flag = seq_item
        return lax.cond(
            full_flag == 1,
            lambda: full_forward(
                query_rows, key_all, value_all, relative_bias, offset, score_scale
            ),
            lambda: stretch_forward(query_rows, key_rows, value_rows, relative_bias, score_scale),
        )

    attended_seq, log_total = lax.map(
        forward_sequence, (query_seq, key_seq, value_seq, keys_all, values_all, full_attention)
    )
    attended = attended_seq.reshape(token_count, value_width)
    reset_gate = jax.nn.silu(reset_pre)
    gated_low = (reset_gate * attended).astype(jnp.bfloat16)
    cand_in = cand_pre + jnp.dot(gated_low, out_proj, preferred_element_type=jnp.float32)
    candidate = jax.nn.silu(cand_in)
    update = jax.nn.sigmoid(update_pre)
    first_sum = flat_rows + update * (candidate - flat_rows)
    feed_normed, unit_two, inv_two = norm_forward(first_sum, feed_gain)
    feed_low = feed_normed.astype(jnp.bfloat16)
    hidden = jnp.dot(feed_low, feed_in, preferred_element_type=jnp.float32)
    act_low = jax.nn.silu(hidden).astype(jnp.bfloat16)
    result = first_sum + jnp.dot(act_low, feed_out, preferred_element_type=jnp.float32)
    block_out = result.astype(jnp.bfloat16).reshape(seq_count, row_count, model_width)
    cot_low = cotangent.reshape(token_count, model_width)
    feed_out_grad = jnp.einsum("nf,nd->fd", act_low, cot_low, preferred_element_type=jnp.float32)
    grad_act = jnp.einsum("nd,fd->nf", cot_low, feed_out, preferred_element_type=jnp.float32)
    grad_hidden = (grad_act * silu_slope(hidden)).astype(jnp.bfloat16)
    feed_in_grad = jnp.einsum(
        "nd,nf->df", feed_low, grad_hidden, preferred_element_type=jnp.float32
    )
    grad_feed_normed = jnp.einsum(
        "nf,df->nd", grad_hidden, feed_in, preferred_element_type=jnp.float32
    )
    grad_first_norm, feed_gain_grad = norm_backward(grad_feed_normed, feed_gain, unit_two, inv_two)
    grad_first = cot_low.astype(jnp.float32) + grad_first_norm
    grad_input = grad_first * (1.0 - update)
    grad_update_pre = grad_first * (candidate - flat_rows) * update * (1.0 - update)
    grad_cand = (grad_first * update * silu_slope(cand_in)).astype(jnp.bfloat16)
    out_grad = jnp.einsum("nv,nd->vd", gated_low, grad_cand, preferred_element_type=jnp.float32)
    grad_gated = jnp.einsum("nd,vd->nv", grad_cand, out_proj, preferred_element_type=jnp.float32)
    grad_reset_pre = grad_gated * attended * silu_slope(reset_pre)
    grad_att_low = (grad_gated * reset_gate).astype(jnp.bfloat16)
    delta_rows = jnp.sum(grad_att_low.astype(jnp.float32) * attended, axis=-1)
    grad_att_seq = grad_att_low.reshape(seq_count, row_count, value_width)
    delta_seq = delta_rows.reshape(seq_count, row_count)
    back_keys, back_values = (keys_all, values_all)

    def backward_sequence(seq_item):
        (
            query_rows,
            key_rows,
            value_rows,
            key_all,
            value_all,
            grad_rows,
            total_rows,
            delta_part,
            full_flag,
        ) = seq_item

        def stretch_padded():
            grad_query, grad_key, grad_value, rel_term = stretch_backward(
                query_rows,
                key_rows,
                value_rows,
                grad_rows,
                total_rows,
                delta_part,
                relative_bias,
                score_scale,
            )
            key_full = lax.dynamic_update_slice_in_dim(
                jnp.zeros((length, key_width), jnp.float32), grad_key, offset, 0
            )
            value_full = lax.dynamic_update_slice_in_dim(
                jnp.zeros((length, value_width), jnp.float32), grad_value, offset, 0
            )
            return (grad_query, key_full, value_full, rel_term)

        return lax.cond(
            full_flag == 1,
            lambda: full_backward(
                query_rows,
                key_all,
                value_all,
                grad_rows,
                total_rows,
                delta_part,
                relative_bias,
                offset,
                score_scale,
            ),
            stretch_padded,
        )

    grad_query, grad_key_all, grad_value_all, rel_terms = lax.map(
        backward_sequence,
        (
            query_seq,
            key_seq,
            value_seq,
            back_keys,
            back_values,
            grad_att_seq,
            log_total,
            delta_seq,
            full_attention,
        ),
    )
    grad_key, grad_value = (
        lax.psum_scatter(
            grad_key_all.astype(jnp.bfloat16), "seq", scatter_dimension=1, tiled=True
        ).astype(jnp.float32),
        lax.psum_scatter(
            grad_value_all.astype(jnp.bfloat16), "seq", scatter_dimension=1, tiled=True
        ).astype(jnp.float32),
    )
    relative_grad = jnp.sum(rel_terms, axis=0)
    grad_query = grad_query.reshape(token_count, key_width)
    grad_key = grad_key.reshape(token_count, key_width)
    affine_grad = jnp.stack(
        [
            jnp.sum(grad_query * shared, axis=0),
            jnp.sum(grad_query, axis=0),
            jnp.sum(grad_key * shared, axis=0),
            jnp.sum(grad_key, axis=0),
        ]
    )
    grad_shared_pre = (grad_query * score_affine[0] + grad_key * score_affine[2]) * silu_slope(
        shared_pre
    )
    grad_value_pre = (grad_value.reshape(token_count, value_width) * silu_slope(value_pre)).astype(
        jnp.bfloat16
    )
    value_grad = jnp.einsum(
        "nd,nv->dv", normed_low, grad_value_pre, preferred_element_type=jnp.float32
    )
    grad_normed = jnp.einsum(
        "nv,dv->nd", grad_value_pre, value_proj, preferred_element_type=jnp.float32
    )
    grad_base = jnp.concatenate(
        [grad_shared_pre, grad_reset_pre, grad_update_pre, grad_cand.astype(jnp.float32)], axis=1
    ).astype(jnp.bfloat16)
    mix_grad = jnp.einsum("nd,nm->dm", mixed_low, grad_base, preferred_element_type=jnp.float32)
    grad_mixed = jnp.einsum("nm,dm->nd", grad_base, mix_proj, preferred_element_type=jnp.float32)
    grad_smooth = (grad_mixed * silu_slope(smoothed)).reshape(seq_count, row_count, model_width)
    local_grad, grad_ends = block_states(grad_smooth[:, ::-1], smooth_eta, decay_rate)
    first_local, _ = chain_blocks(grad_ends, block_power, empty_state)
    _, arriving = entering(
        (span_power, first_local), "seq", combine_linear, (unit_power, empty_state), True
    )
    _, before_g = chain_blocks(grad_ends, block_power, arriving)
    adjoint = assemble(local_grad, before_g, decay_rate)[:, ::-1]
    with_state = jnp.sum(adjoint * states, axis=(0, 1))
    input_total = jnp.sum(adjoint * normed_seq[:, :, None, :], axis=(0, 1))
    eta_grad = jnp.sum(grad_smooth[:, :, None, :] * states, axis=(0, 1))
    omega_grad = jnp.sum(grad_smooth * normed_seq, axis=(0, 1))
    decay_total = (with_state - rate_in * input_total) / decay_rate
    alpha_grad = smooth_beta * input_total - smooth_damp * decay_total
    damp_grad = -smooth_alpha * decay_total
    beta_grad = smooth_alpha * input_total
    grad_through = jnp.sum(rate_in * adjoint, axis=2) + smooth_omega * grad_smooth
    grad_normed = grad_normed + grad_through.reshape(token_count, model_width)
    grad_from_norm, mix_gain_grad = norm_backward(grad_normed, mix_gain, unit_one, inv_one)
    grad_input = (grad_input + grad_from_norm).reshape(seq_count, row_count, model_width)
    (
        mix_gain_grad,
        alpha_grad,
        damp_grad,
        beta_grad,
        eta_grad,
        omega_grad,
        affine_grad,
        relative_grad,
        feed_gain_grad,
    ) = lax.psum(
        (
            mix_gain_grad,
            alpha_grad,
            damp_grad,
            beta_grad,
            eta_grad,
            omega_grad,
            affine_grad,
            relative_grad,
            feed_gain_grad,
        ),
        ("dp", "seq"),
    )
    value_grad, mix_grad, out_grad, feed_in_grad, feed_out_grad = (
        lax.psum_scatter(
            value_grad.astype(jnp.bfloat16), "dp", scatter_dimension=0, tiled=True
        ).astype(jnp.float32),
        lax.psum_scatter(
            mix_grad.astype(jnp.bfloat16), "dp", scatter_dimension=0, tiled=True
        ).astype(jnp.float32),
        lax.psum_scatter(
            out_grad.astype(jnp.bfloat16), "dp", scatter_dimension=0, tiled=True
        ).astype(jnp.float32),
        lax.psum_scatter(
            feed_in_grad.astype(jnp.bfloat16), "dp", scatter_dimension=0, tiled=True
        ).astype(jnp.float32),
        lax.psum_scatter(
            feed_out_grad.astype(jnp.bfloat16), "dp", scatter_dimension=0, tiled=True
        ).astype(jnp.float32),
    )
    value_grad, mix_grad, out_grad, feed_in_grad, feed_out_grad = (
        lax.psum_scatter(
            value_grad.astype(jnp.bfloat16), "seq", scatter_dimension=1, tiled=True
        ).astype(jnp.float32),
        lax.psum_scatter(
            mix_grad.astype(jnp.bfloat16), "seq", scatter_dimension=1, tiled=True
        ).astype(jnp.float32),
        lax.psum_scatter(
            out_grad.astype(jnp.bfloat16), "seq", scatter_dimension=1, tiled=True
        ).astype(jnp.float32),
        lax.psum_scatter(
            feed_in_grad.astype(jnp.bfloat16), "seq", scatter_dimension=1, tiled=True
        ).astype(jnp.float32),
        lax.psum_scatter(
            feed_out_grad.astype(jnp.bfloat16), "seq", scatter_dimension=1, tiled=True
        ).astype(jnp.float32),
    )
    return (
        block_out,
        grad_input,
        mix_gain_grad,
        alpha_grad,
        damp_grad,
        beta_grad,
        eta_grad,
        omega_grad,
        value_grad,
        mix_grad,
        affine_grad,
        relative_grad,
        out_grad,
        feed_gain_grad,
        feed_in_grad,
        feed_out_grad,
    )


def solution(mesh):
    return jax.shard_map(
        local,
        mesh=mesh,
        in_specs=(
            P("dp", "seq", None),
            P("dp", "seq", None),
            P("dp"),
            P(),
            P(),
            P(),
            P(),
            P(),
            P(),
            P(),
            P(),
            P(),
            P(),
            P(),
            P(),
            P(),
            P(),
        ),
        out_specs=(
            P("dp", "seq", None),
            P("dp", "seq", None),
            P(),
            P(),
            P(),
            P(),
            P(),
            P(),
            P("dp", "seq"),
            P("dp", "seq"),
            P(),
            P(),
            P("dp", "seq"),
            P(),
            P("dp", "seq"),
            P("dp", "seq"),
        ),
        check_vma=False,
    )
```

profile of v0, /device:TPU:0, one launch (start us, length us, event | category | flops | bytes accessed | tf_op | source)
XLA Modules:
  0.0 2035.4 jit_solution(15975441003094833082)
XLA Ops:
  13.7 15.8 all-gather
  34.5 21.3 %broadcast.271.clone2 = f32[16,2,32,16,1024]{4,3,0,2,1:T(8,128)} broadcast(f32[]{:T(128)} %constant.315.clone.1), dimensions={} | broadcast | bytes 67108864 | tf_op jit(solution)/shard_map/broadcast.45
  55.7 141.1 %while.132 = (s32[]{:T(128)}, f32[2,32,16,1024]{3,2,1,0:T(8,128)}, f32[16,2,32,16,1024]{4,3,0,2,1:T(8,128)}, f32[16,1024]{1,0:T(8,128)S(1)}, f32[16,1024]{1,0:T(...) while((s32[]{:T(128)}, f32[2,32,16,1024]{3,2,1,0:T(8,128)}, ...), condition=%wide.region_3.4_spmd.clone, body=%wide.region_2.3_spmd.clone.sunk | while | flops 4194307 | bytes 14024815 | solution.py:73
  201.6 31.7 %while.133 = (s32[]{:T(128)}, f32[2,16,1024]{2,1,0:T(8,128)S(1)}, f32[16,1024]{1,0:T(8,128)S(1)}, f32[32,2,16,1024]{3,2,1,0:T(8,128)}, s32[]{:T(128)}, /*index=5*/s32[]{:T(128)}) while((s32[]{:T(128)}, f32[2,16,1024]{2,1,0:T(8,128)S(1)}, f32[16,1024]{1,0:T(8,128)S(1)}, f32[32,2,16,1024]{3,2,1,0:T(8,128)}, s32[]{:T(128)}, ...), condition=%wide.region_5.6_spmd.clone, body=%wide.region_4.5_spmd.clone.sunk | while | flops 98307 | bytes 458843 | solution.py:82
  233.3 15.2 all-gather.1
  251.3 52.7 %while.127 = (s32[]{:T(128)}, f32[2,16,1024]{2,1,0:T(8,128)S(1)}, f32[32,2,16,1024]{3,2,1,0:T(8,128)}, f32[16,1024]{1,0:T(8,128)S(1)}, f32[32,2,16,1024]{3,2,1,0:T(8,128)}, /*index=5*/s32[]{:T(128)}) while((s32[]{:T(128)}, f32[2,16,1024]{2,1,0:T(8,128)S(1)}, f32[32,2,16,1024]{3,2,1,0:T(8,128)}, f32[16,1024]{1,0:T(8,128)S(1)}, ...), condition=%wide.region_9.10_spmd, body=%wide.region_8.9_spmd.sunk | while | flops 65538 | bytes 720981 | solution.py:82
  304.1 49.8 %fusion.52 = (f32[2,32,16,1024]{3,2,1,0:T(8,128)}, f32[16,2,32,16,1024]{4,3,0,2,1:T(8,128)}) fusion(f32[16,1024]{1,0:T(8,128)S(1)} %copy-done.34, f32[16,2,32,16,1024]{4,3,0,2,1:T(8,128)} %get-tuple-element.710, f32[16,16,1024]{2,1,0:T(8,128)S(1)} %broadcast_power_fusion, f32[32,2,16,1024]{3,2,1,0:T(8,128)} %get-tuple-element.714), kind=kLoop, calls=%fused_computation.108 | loop fusion | flops 66060288 | bytes 143720448 | tf_op jit(solution)/shard_map/reduce_sum | solution.py:337
  360.2 13.3 fusion.102
  391.5 22.7 %all-gather.6.cloned.1.call-done = bf16[2,2048,128]{2,1,0:T(8,128)(2,1)} async-done(((bf16[2,512,128]{2,1,0:T(8,128)(2,1)}), bf16[2,2048,128]{2,1,0:T(8,128)(2,1)}) %all-gather.6.cloned.1.call-update) | async-done | bytes 1048592 | tf_op jit(solution)/shard_map/all_gather | solution.py:356
  414.2 288.4 %all-gather.8.cloned.1.call-done = bf16[2,2048,2048]{2,1,0:T(8,128)(2,1)} async-done(((bf16[2,512,2048]{2,1,0:T(8,128)(2,1)}), bf16[2,2048,2048]{2,1,0:T(8,128)(2,1)}) %all-gather.8.cloned.1.call-update) | async-done | bytes 16777232 | tf_op jit(solution)/shard_map/all_gather | solution.py:357
  702.7 104.2 %while.128 = (s32[]{:T(128)}, f32[2,512,2048]{2,1,0:T(8,128)}, f32[2,512]{1,0:T(2,128)S(1)}, s32[2]{0:T(128)S(1)}, bf16[2,512,128]{2,1,0:T(8,128)(2,1)S(1)}, /*i...) while((s32[]{:T(128)}, f32[2,512,2048]{2,1,0:T(8,128)}, ...), condition=%wide.region_18.19_spmd, body=%wide.region_11.18_spmd.sunk | while | flops 4573888512 | bytes 96417128 | solution.py:370
  703.9 46.1 %conditional.4 = (f32[1,512,2048]{2,1,0:T(8,128)}, f32[1,512]{1,0:T(1,128)S(1)}) conditional(s32[]{:T(128)} %bitcast.362, (bf16[2,512,128]{2,1,0:T(8,128)(2,1)S(1)}, s32[]{:T(128)}, bf16[512,128]{1,0:T(8,128)(2,1)S(1)}, f32[4096]{0:T(1024)}, bf16[2,512,2048]{2,1,0:T(8,128)(2,1)}) %tuple.263, (s32[]{:T(128)}, bf16[2,2048,128]{2,1,0:T(8,128)(2,1)}, ...), branch_computations={%region_12.14_spmd, %region_15.17_spmd} | conditional | flops 4573888512 | bytes 87761504 | solution.py:362
  756.1 46.1 %conditional.4 = (f32[1,512,2048]{2,1,0:T(8,128)}, f32[1,512]{1,0:T(1,128)S(1)}) conditional(s32[]{:T(128)} %bitcast.362, (bf16[2,512,128]{2,1,0:T(8,128)(2,1)S(1)}, s32[]{:T(128)}, bf16[512,128]{1,0:T(8,128)(2,1)S(1)}, f32[4096]{0:T(1024)}, bf16[2,512,2048]{2,1,0:T(8,128)(2,1)}) %tuple.263, (s32[]{:T(128)}, bf16[2,2048,128]{2,1,0:T(8,128)(2,1)}, ...), branch_computations={%region_12.14_spmd, %region_15.17_spmd} | conditional | flops 4573888512 | bytes 87761504 | solution.py:362
  792.7 9.6 fusion.12
  814.7 11.5 fusion.99
  826.8 17.8 multiply_convert_fusion.1
  844.6 19.2 multiply_convert_fusion
  863.8 16.4 multiply_reduce_fusion.3
  889.3 14.7 fusion.56
  904.1 212.3 %while.129 = (s32[]{:T(128)}, f32[2,512,128]{2,1,0:T(8,128)}, bf16[2,2048,128]{2,1,0:T(8,128)(2,1)}, bf16[2,2048,2048]{2,1,0:T(8,128)(2,1)}, f32[2,4096]{1,0:T(2...) while((s32[]{:T(128)}, f32[2,512,128]{2,1,0:T(8,128)}, ...), condition=%wide.region_30.31_spmd, body=%wide.region_24.30_spmd.sunk | while | flops 9407891456 | bytes 196059760 | solution.py:458
  909.5 87.2 %conditional.5 = (f32[1,512,128]{2,1,0:T(8,128)}, bf16[1,2048,128]{2,1,0:T(8,128)(2,1)}, bf16[1,2048,2048]{2,1,0:T(8,128)(2,1)}, f32[1,4096]{1,0:T(1,128)}) conditional(s32[]{:T(128)} %bitcast.365, (bf16[2,512,128]{2,1,0:T(8,128)(2,1)}, s32[]{:T(128)}, bf16[512,128]{1,0:T(8,128)(2,1)S(1)}, f32[4096]{0:T(1024)}, f32[512]{0:T(512)S(1)}, ...), branch_computations={%region_25.27_spmd, %region_28.29_spmd} | conditional | flops 9407891456 | bytes 173177536 | solution.py:442
  945.7 10.0 fusion.34
  1015.3 87.2 %conditional.5 = (f32[1,512,128]{2,1,0:T(8,128)}, bf16[1,2048,128]{2,1,0:T(8,128)(2,1)}, bf16[1,2048,2048]{2,1,0:T(8,128)(2,1)}, f32[1,4096]{1,0:T(1,128)}) conditional(s32[]{:T(128)} %bitcast.365, (bf16[2,512,128]{2,1,0:T(8,128)(2,1)}, s32[]{:T(128)}, bf16[512,128]{1,0:T(8,128)(2,1)S(1)}, f32[4096]{0:T(1024)}, f32[512]{0:T(512)S(1)}, ...), branch_computations={%region_25.27_spmd, %region_28.29_spmd} | conditional | flops 9407891456 | bytes 173177536 | solution.py:442
  1051.5 10.0 fusion.34
  1128.0 14.7 convolution_convert_fusion.1
  1143.4 15.5 convolution_convert_fusion.2
  1163.3 14.8 convolution_convert_fusion
  1178.2 15.4 add_convert_fusion
  1193.7 17.9 multiply_reduce_fusion.4
  1211.6 32.7 %rev.6 = f32[2,512,1024]{2,1,0:T(8,128)} reverse(f32[2,512,1024]{2,1,0:T(8,128)} %bitcast.395), dimensions={1} | reverse | bytes 8388608 | tf_op jit(solution)/shard_map/rev | solution.py:509
  1244.3 21.4 %broadcast.271.clone = f32[16,2,32,16,1024]{4,3,0,2,1:T(8,128)} broadcast(f32[]{:T(128)} %constant.315.clone.1), dimensions={} | broadcast | bytes 67108864 | tf_op jit(solution)/shard_map/broadcast.45
  1265.7 141.2 %while.134 = (s32[]{:T(128)}, f32[2,32,16,1024]{3,2,1,0:T(8,128)}, f32[16,2,32,16,1024]{4,3,0,2,1:T(8,128)}, f32[16,1024]{1,0:T(8,128)S(1)}, f32[16,1024]{1,0:T(...) while((s32[]{:T(128)}, f32[2,32,16,1024]{3,2,1,0:T(8,128)}, ...), condition=%wide.region_34.35_spmd.clone, body=%wide.region_33.34_spmd.clone.sunk | while | flops 4194307 | bytes 14024815 | solution.py:73
  1411.7 11.6 reduce-scatter.15.cloned.1.call-done
  1439.3 31.9 %while.135 = (s32[]{:T(128)}, f32[2,16,1024]{2,1,0:T(8,128)S(1)}, f32[16,1024]{1,0:T(8,128)S(1)}, f32[32,2,16,1024]{3,2,1,0:T(8,128)}, s32[]{:T(128)}, /*index=5*/s32[]{:T(128)}) while((s32[]{:T(128)}, f32[2,16,1024]{2,1,0:T(8,128)S(1)}, f32[16,1024]{1,0:T(8,128)S(1)}, f32[32,2,16,1024]{3,2,1,0:T(8,128)}, s32[]{:T(128)}, ...), condition=%wide.region_36.37_spmd.clone, body=%wide.region_35.36_spmd.clone.sunk | while | flops 98307 | bytes 458843 | solution.py:82
  1471.1 14.6 all-gather.2
  1488.3 65.3 %reduce-scatter.33.cloned.1.call-done = bf16[512,1024]{1,0:T(8,128)(2,1)} async-done(((bf16[4096,1024]{1,0:T(8,128)(2,1)}), bf16[512,1024]{1,0:T(8,128)(2,1)}) %reduce-scatter.33.cloned.1.call-update) | async-done | bytes 1048592 | tf_op jit(solution)/shard_map/reduce_scatter | solution.py:565
  1556.2 53.0 %while.131 = (s32[]{:T(128)}, f32[2,16,1024]{2,1,0:T(8,128)S(1)}, f32[32,2,16,1024]{3,2,1,0:T(8,128)}, f32[16,1024]{1,0:T(8,128)S(1)}, f32[32,2,16,1024]{3,2,1,0:T(8,128)}, /*index=5*/s32[]{:T(128)}) while((s32[]{:T(128)}, f32[2,16,1024]{2,1,0:T(8,128)S(1)}, f32[32,2,16,1024]{3,2,1,0:T(8,128)}, f32[16,1024]{1,0:T(8,128)S(1)}, ...), condition=%wide.region_40.41_spmd, body=%wide.region_39.40_spmd.sunk | while | flops 65538 | bytes 720981 | solution.py:82
  1609.2 19.2 reduce-scatter.29.cloned.1.call-done
  1628.5 48.7 %multiply_add_fusion = f32[16,2,32,16,1024]{4,3,0,2,1:T(8,128)} fusion(f32[16,2,32,16,1024]{4,3,0,2,1:T(8,128)} %get-tuple-element.720, f32[16,16,1024]{2,1,0:T(8,128)S(1)} %copy-done.24, f32[32,2,16,1024]{3,2,1,0:T(8,128)} %get-tuple-element.724), kind=kLoop, calls=%fused_computation.113 | loop fusion | flops 33554432 | bytes 139460608 | tf_op jit(solution)/shard_map/add | solution.py:91
  1677.2 27.8 %reduce-scatter.23.cloned.1.call-done = bf16[128,4224]{1,0:T(8,128)(2,1)} async-done(((bf16[1024,4224]{1,0:T(8,128)(2,1)}), bf16[128,4224]{1,0:T(8,128)(2,1)}) %reduce-scatter.23.cloned.1.call-update) | async-done | bytes 1081360 | tf_op jit(solution)/shard_map/reduce_scatter | solution.py:556
  1707.5 50.4 %multiply_reduce_fusion.1 = (f32[16,1024]{1,0:T(8,128)S(1)}, f32[16,1024]{1,0:T(8,128)S(1)}, f32[2,512,1024]{2,1,0:T(8,128)}) fusion(f32[2,512,16,1024]{3,2,1,0:T(8,128)} %bitcast.76, f32[2,512,1024]{2,1,0:T(8,128)} %get-tuple-element.1109, f32[2,512,16,1024]{3,2,1,0:T(8,128)} %bitcast.79, f32[16,1024]{1,0:T(8,128)S(1)} %copy-done.30), kind=kLoop, calls=%fused_computation.111 | loop fusion | flops 99581952 | bytes 142802944 | tf_op jit(solution)/shard_map/reduce_sum | solution.py:517
  1759.9 23.5 %fusion.53 = f32[16,1024]{1,0:T(8,128)} fusion(f32[16,2,32,16,1024]{4,3,0,2,1:T(8,128)} %get-tuple-element.1091, f32[2,32,16,1024]{3,2,1,0:T(8,128)} %bitcast.396), kind=kLoop, calls=%fused_computation.109 | loop fusion | flops 33538048 | bytes 71368704 | tf_op jit(solution)/shard_map/reduce_sum | solution.py:518
  1786.6 24.9 %reduce-scatter.35.cloned.1.call-done = bf16[512,256]{1,0:T(8,128)(2,1)} async-done(((bf16[512,1024]{1,0:T(8,128)(2,1)}), bf16[512,256]{1,0:T(8,128)(2,1)}) %reduce-scatter.35.cloned.1.call-update) | async-done | bytes 262160 | tf_op jit(solution)/shard_map/reduce_scatter | solution.py:582
  1813.3 26.2 %reduce-scatter.31.cloned.1.call-done = bf16[128,1024]{1,0:T(8,128)(2,1)} async-done(((bf16[128,4096]{1,0:T(8,128)(2,1)}), bf16[128,1024]{1,0:T(8,128)(2,1)}) %reduce-scatter.31.cloned.1.call-update) | async-done | bytes 262160 | tf_op jit(solution)/shard_map/reduce_scatter | solution.py:579
  1841.3 27.0 %reduce-scatter.37.cloned.1.call-done = bf16[1056,128]{1,0:T(8,128)(2,1)} async-done(((bf16[4224,128]{1,0:T(8,128)(2,1)}), bf16[1056,128]{1,0:T(8,128)(2,1)}) %reduce-scatter.37.cloned.1.call-update) | async-done | bytes 270352
  1870.4 11.3 fusion.85
  1889.0 39.9 %all-reduce.5 = (f32[1024]{0:T(1024)}, f32[1024]{0:T(1024)}, f32[4,128]{1,0:T(4,128)}, f32[4096]{0:T(1024)}, f32[1024]{0:T(1024)}) all-reduce(f32[1024]{0:T(1024)S(1)} %get-tuple-element.933, f32[1024]{0:T(1024)S(1)} %copy-done.89, f32[4,128]{1,0:T(4,128)S(1)} %pad_maximum_fusion.3, ...), channel_id=1, replica_groups=mesh['dp'=8,'seq'=4] {'dp','seq'}, use_global_device_ids=true, to_apply=%region_45.46 | all-reduce | flops 7680 | bytes 61440 | tf_op jit(solution)/shard_map/psum | solution.py:538
  1930.5 92.1 %all-reduce.9.cloned.1.call-done = (f32[16,1024]{1,0:T(8,128)}, f32[16,1024]{1,0:T(8,128)}, f32[16,1024]{1,0:T(8,128)}, f32[16,1024]{1,0:T(8,128)}) async-done(((f32[16,1024]{1,0:T(8,128)}, f32[16,1024]{1,0:T(8,128)}, f32[16,1024]{1,0:T(8,128)}, f32[16,1024]{1,0:T(8,128)}), (f32[16,1024]{1,0:T(8,128)}, f32[16,1024]{1,0:T(8,128)}, f32[16,1024]{1,0:T(8,128)}, ...) | async-done | bytes 262160 | tf_op jit(solution)/shard_map/psum | solution.py:538
  (692 shorter events, 865.4 us)
Async XLA Ops:
  7.2 24.6 %copy-start.4 = (bf16[2,512,1024]{2,1,0:T(8,128)(2,1)S(1)}, bf16[2,512,1024]{2,1,0:T(8,128)(2,1)}, u32[]{:S(2)}) copy-start(bf16[2,512,1024]{2,1,0:T(8,128)(2,1)} %param.41) | copy-start | bytes 6291460
  7.2 24.6 %copy-start.54 = (f32[1024]{0:T(1024)S(1)}, f32[1024]{0:T(1024)}, u32[]{:S(2)}) copy-start(f32[1024]{0:T(1024)} %param.44) | copy-start | bytes 12292
  7.2 407.0 %all-gather.6.cloned.1.call-start = ((), (), s32[]{:S(2)}) async-start(), calls=%async_computation.12 | async-start | bytes 1310720 | tf_op jit(solution)/shard_map/all_gather | solution.py:356
  9.9 344.0 %copy-start.52 = (f32[2,512]{1,0:T(2,128)}, f32[2,512]{1,0:T(2,128)S(1)}, u32[]{:S(2)}) copy-start(f32[2,512]{1,0:T(2,128)S(1)} %get-tuple-element.1113) | copy-start | bytes 12292
  13.5 340.4 %copy-start.63 = (f32[2,512]{1,0:T(2,128)}, f32[2,512]{1,0:T(2,128)S(1)}, u32[]{:S(2)}) copy-start(f32[2,512]{1,0:T(2,128)S(1)} %get-tuple-element.1115) | copy-start | bytes 12292
  31.8 272.2 %copy-start.23 = (f32[16,16,1024]{2,1,0:T(8,128)}, f32[16,16,1024]{2,1,0:T(8,128)S(1)}, u32[]{:S(2)}) copy-start(f32[16,16,1024]{2,1,0:T(8,128)S(1)} %broadcast_power_fusion) | copy-start | bytes 3145732
  248.8 55.3 %copy-start.34 = (f32[16,1024]{1,0:T(8,128)S(1)}, f32[16,1024]{1,0:T(8,128)}, u32[]{:S(2)}) copy-start(f32[16,1024]{1,0:T(8,128)} %param.48) | copy-start | bytes 196612
  304.0 49.8 %copy-start.13 = (f32[16,1024]{1,0:T(8,128)}, f32[16,1024]{1,0:T(8,128)S(1)}, u32[]{:S(2)}) copy-start(f32[16,1024]{1,0:T(8,128)S(1)} %get-tuple-element.1894) | copy-start | bytes 196612
  304.0 49.8 %copy-start.86 = (f32[1024]{0:T(1024)S(1)}, f32[1024]{0:T(1024)}, u32[]{:S(2)}) copy-start(f32[1024]{0:T(1024)} %param.49) | copy-start | bytes 12292
  360.1 19.5 copy-start.82
  360.1 19.4 copy-start.84
  360.1 19.4 copy-start.92
  360.1 19.4 copy-start.93
  360.1 20.5 %copy-start.81 = (f32[1,4,2,128]{3,2,1,0:T(2,128)S(1)}, f32[1,4,2,128]{3,2,1,0:T(2,128)}, u32[]{:S(2)}) copy-start(f32[1,4,2,128]{3,2,1,0:T(2,128)} %get-tuple-element.1114) | copy-start | bytes 12292
  380.5 322.1 %all-gather.8.cloned.1.call-start = ((), (), s32[]{:S(2)}) async-start(), calls=%async_computation.13 | async-start | bytes 20971520 | tf_op jit(solution)/shard_map/all_gather | solution.py:357
  390.9 311.8 %copy-start.22 = (bf16[1024,128]{1,0:T(8,128)(2,1)S(1)}, bf16[1024,128]{1,0:T(8,128)(2,1)}, u32[]{:S(2)}) copy-start(bf16[1024,128]{1,0:T(8,128)(2,1)} %get-tuple-element.1106) | copy-start | bytes 786436
  390.9 311.8 %copy-start.98 = (s32[2]{0:T(128)S(1)}, s32[2]{0:T(128)}, u32[]{:S(2)}) copy-start(s32[2]{0:T(128)} %param.43) | copy-start | bytes 28
  391.0 770.3 %reduce-scatter.17.cloned.1.call-start = ((), (), s32[]{:S(2)}) async-start(), calls=%async_computation.15 | async-start | bytes 1310720 | tf_op jit(solution)/shard_map/reduce_scatter | solution.py:473
  826.2 54.1 %copy-start.58 = (f32[1024]{0:T(1024)}, f32[1024]{0:T(1024)S(1)}, u32[]{:S(2)}) copy-start(f32[1024]{0:T(1024)S(1)} %broadcast_multiply_fusion.4) | copy-start | bytes 12292
  826.8 53.5 %copy-start.69 = (f32[1024]{0:T(1024)}, f32[1024]{0:T(1024)S(1)}, u32[]{:S(2)}) copy-start(f32[1024]{0:T(1024)S(1)} %add_rsqrt_fusion) | copy-start | bytes 12292
  1116.4 307.0 %reduce-scatter.15.cloned.1.call-start = ((), (), s32[]{:S(2)}) async-start(), calls=%async_computation.14 | async-start | bytes 20971520 | tf_op jit(solution)/shard_map/reduce_scatter | solution.py:476
  1117.0 368.8 %reduce-scatter.25.cloned.1.call-start = ((), (), s32[]{:S(2)}) async-start(), calls=%async_computation.19 | async-start | bytes 4718592 | tf_op jit(solution)/shard_map/reduce_scatter | solution.py:559
  1126.4 427.3 %reduce-scatter.33.cloned.1.call-start = ((), (), s32[]{:S(2)}) async-start(), calls=%async_computation.23 | async-start | bytes 9437184 | tf_op jit(solution)/shard_map/reduce_scatter | solution.py:565
  1142.7 485.7 %reduce-scatter.29.cloned.1.call-start = ((), (), s32[]{:S(2)}) async-start(), calls=%async_computation.21 | async-start | bytes 9437184 | tf_op jit(solution)/shard_map/reduce_scatter | solution.py:562
  1158.9 546.1 %reduce-scatter.23.cloned.1.call-start = ((), (), s32[]{:S(2)}) async-start(), calls=%async_computation.18 | async-start | bytes 9732096 | tf_op jit(solution)/shard_map/reduce_scatter | solution.py:556
  1178.2 581.6 %reduce-scatter.19.cloned.1.call-start = ((), (), s32[]{:S(2)}) async-start(), calls=%async_computation.16 | async-start | bytes 4718592 | tf_op jit(solution)/shard_map/reduce_scatter | solution.py:553
  1244.3 21.4 %copy-start.21 = (f32[16,1024]{1,0:T(8,128)S(1)}, f32[16,1024]{1,0:T(8,128)}, u32[]{:S(2)}) copy-start(f32[16,1024]{1,0:T(8,128)} %copy-done.20) | copy-start | bytes 196612
  1244.3 21.4 %copy-start.35 = (f32[16,1024]{1,0:T(8,128)S(1)}, f32[16,1024]{1,0:T(8,128)}, u32[]{:S(2)}) copy-start(f32[16,1024]{1,0:T(8,128)} %param.48) | copy-start | bytes 196612
  1438.5 346.5 %reduce-scatter.27.cloned.1.call-start = ((), (), s32[]{:S(2)}) async-start(), calls=%async_computation.20 | async-start | bytes 655360 | tf_op jit(solution)/shard_map/reduce_scatter | solution.py:576
  1485.8 325.7 %reduce-scatter.35.cloned.1.call-start = ((), (), s32[]{:S(2)}) async-start(), calls=%async_computation.24 | async-start | bytes 1310720 | tf_op jit(solution)/shard_map/reduce_scatter | solution.py:582
  1553.7 285.8 %reduce-scatter.31.cloned.1.call-start = ((), (), s32[]{:S(2)}) async-start(), calls=%async_computation.22 | async-start | bytes 1310720 | tf_op jit(solution)/shard_map/reduce_scatter | solution.py:579
  1553.7 74.7 %copy-start.24 = (f32[16,16,1024]{2,1,0:T(8,128)S(1)}, f32[16,16,1024]{2,1,0:T(8,128)}, u32[]{:S(2)}) copy-start(f32[16,16,1024]{2,1,0:T(8,128)} %copy-done.23) | copy-start | bytes 3145732
  1628.4 239.8 %reduce-scatter.37.cloned.1.call-start = ((), (), s32[]{:S(2)}) async-start(), calls=%async_computation.25 | async-start | bytes 1351680
  1628.5 78.9 %copy-start.30 = (f32[16,1024]{1,0:T(8,128)S(1)}, f32[16,1024]{1,0:T(8,128)}, u32[]{:S(2)}) copy-start(f32[16,1024]{1,0:T(8,128)} %copy-done.29) | copy-start | bytes 196612
  1707.4 221.4 %reduce-scatter.21.cloned.1.call-start = ((), (), s32[]{:S(2)}) async-start(), calls=%async_computation.17 | async-start | bytes 655360 | tf_op jit(solution)/shard_map/reduce_scatter | solution.py:570
  1759.7 262.8 %all-reduce.9.cloned.1.call-start = ((), (), s32[]{:S(2)}) async-start(), calls=%async_computation.26 | async-start | bytes 524288 | tf_op jit(solution)/shard_map/psum | solution.py:538
  1759.8 23.6 %copy-start.43 = (bf16[2,512,128]{2,1,0:T(8,128)(2,1)S(1)}, bf16[2,512,128]{2,1,0:T(8,128)(2,1)}, u32[]{:S(2)}) copy-start(bf16[2,512,128]{2,1,0:T(8,128)(2,1)} %reduce-scatter.17.cloned.1.call-done) | copy-start | bytes 786436
  1759.8 23.8 %copy-start.90 = (f32[128]{0:T(128)S(1)}, f32[128]{0:T(128)}, u32[]{:S(2)}) copy-start(f32[128]{0:T(128)} %get-tuple-element.929) | copy-start | bytes 1540
  1759.8 23.8 %copy-start.91 = (f32[128]{0:T(128)S(1)}, f32[128]{0:T(128)}, u32[]{:S(2)}) copy-start(f32[128]{0:T(128)} %get-tuple-element.930) | copy-start | bytes 1540
  1759.8 23.8 %copy-start.95 = (f32[128]{0:T(128)S(1)}, f32[128]{0:T(128)}, u32[]{:S(2)}) copy-start(f32[128]{0:T(128)} %reduce_sum.276) | copy-start | bytes 1540
  1759.8 23.8 %copy-start.50 = (f32[16,1024]{1,0:T(8,128)S(1)}, f32[16,1024]{1,0:T(8,128)}, u32[]{:S(2)}) copy-start(f32[16,1024]{1,0:T(8,128)} %param.45) | copy-start | bytes 196612
  1759.8 24.4 %copy-start.46 = (f32[16,1024]{1,0:T(8,128)S(1)}, f32[16,1024]{1,0:T(8,128)}, u32[]{:S(2)}) copy-start(f32[16,1024]{1,0:T(8,128)} %param.46) | copy-start | bytes 196612
  1759.9 24.4 %copy-start.48 = (f32[16,1024]{1,0:T(8,128)S(1)}, f32[16,1024]{1,0:T(8,128)}, u32[]{:S(2)}) copy-start(f32[16,1024]{1,0:T(8,128)} %param.47) | copy-start | bytes 196612
  1783.4 87.0 %copy-start.7 = (bf16[2,512,1024]{2,1,0:T(8,128)(2,1)S(1)}, bf16[2,512,1024]{2,1,0:T(8,128)(2,1)}, u32[]{:S(2)}) copy-start(bf16[2,512,1024]{2,1,0:T(8,128)(2,1)} %param.41) | copy-start | bytes 6291460
  1783.4 87.0 %copy-start.56 = (f32[1024]{0:T(1024)S(1)}, f32[1024]{0:T(1024)}, u32[]{:S(2)}) copy-start(f32[1024]{0:T(1024)} %param.44) | copy-start | bytes 12292
  1783.4 87.0 %copy-start.66 = (f32[1,4,2,128]{3,1,2,0:T(4,128)S(1)}, f32[1,4,2,128]{3,1,2,0:T(4,128)}, u32[]{:S(2)}) copy-start(f32[1,4,2,128]{3,1,2,0:T(4,128)} %copy-done.65) | copy-start | bytes 12292
  1783.4 87.0 %copy-start.68 = (f32[1,4,2,128]{3,1,2,0:T(4,128)S(1)}, f32[1,4,2,128]{3,1,2,0:T(4,128)}, u32[]{:S(2)}) copy-start(f32[1,4,2,128]{3,1,2,0:T(4,128)} %copy-done.67) | copy-start | bytes 12292
  1783.4 87.0 %copy-start.87 = (f32[1024]{0:T(1024)S(1)}, f32[1024]{0:T(1024)}, u32[]{:S(2)}) copy-start(f32[1024]{0:T(1024)} %param.49) | copy-start | bytes 12292
  (69 other events, 545.7 us)
Sparse Core Ops, SparseCore 0:
  380.6 33.5 all-gather.5
  416.4 286.2 all-gather.7
  1116.5 25.4 reduce-scatter.16
  1144.3 278.9 reduce-scatter.14
  1426.6 52.0 reduce-scatter.24
  1482.3 71.3 reduce-scatter.32
  1557.1 71.2 reduce-scatter.28
  1632.4 72.6 reduce-scatter.22
  1708.4 51.2 reduce-scatter.18
  1761.9 21.6 reduce-scatter.26
  1786.0 25.4 reduce-scatter.34
  1813.6 25.7 reduce-scatter.30
  1841.9 26.3 reduce-scatter.36
  1870.5 20.3 reduce-scatter.20
  1898.1 124.3 all-reduce.8
where the time goes:
time: 2050 us; the launch traced here: 2040 us
  waiting for transfers between devices  608 us (30%)
  other arithmetic  590 us (29%)
  local copies, waits for them, and re-layouts  447 us (22%)
  matrix products  282 us (14%)
  blocking collectives  85.4 us (4%)
    all_gather x1, waiting for transfers between devices, local(): lax.all_gather(value_seq, 'seq', axis=1, tiled=True)  288 us
    dynamic_update_slice x32, other arithmetic, block_states(): block_ends, local_state = lax.scan(advance, zero_state, steps)  222 us
    add x128, other arithmetic, link_block(): return (block_power * carried_state + block_end, carried_state)  124 us
    psum x1, waiting for transfers between devices, local(): lax.psum((mix_gain_grad, alpha_grad, damp_grad, beta_grad, eta_grad, omeg...  92.1 us
    reduce_scatter x1, waiting for transfers between devices, local(): lax.psum_scatter(feed_out_grad.astype(jnp.bfloat16), 'dp', scatter_dimens...  65.3 us
    dynamic_slice x64, local copies, waits for them, and re-layouts, block_states(): block_ends, local_state = lax.scan(advance, zero_state, steps)  59.8 us
    reduce_sum x1, other arithmetic, local(): input_total = jnp.sum(adjoint * normed_seq[:, :, None, :], axis=(0, 1))  50.4 us
    reduce_sum x1, other arithmetic, local(): jnp.sum(smooth_eta * states, axis=2) + smooth_omega * normed_seq  49.8 us
  transfers between devices with their start and end apart: 15, of which 11 were waited for; matrix products, arithmetic and copies ran while one was open for 27% of the time, Pallas kernels for 0%

commit v1 on v0

v1 whole, which is shorter than its diff:
```python
import functools

import jax
import jax.numpy as jnp
from jax import lax
from jax.experimental import pallas as pl
from jax.experimental.pallas import tpu as pltpu
from jax.sharding import PartitionSpec as P

STRETCH = 128
EPSILON = 1e-05
TILE = 256
MASKED = -1e30
VMEM_LIMIT = 60 * 1024 * 1024
AXES = ("dp", "seq")

f32 = jnp.float32
bf16 = jnp.bfloat16


def unit_rows_of(values):
    centred = values - jnp.mean(values, axis=-1, keepdims=True)
    inv_std = lax.rsqrt(jnp.mean(centred * centred, axis=-1, keepdims=True) + EPSILON)
    return centred * inv_std, inv_std


def norm_back_rows(grad_out, gain_vec, unit_rows, inv_std):
    scaled = grad_out * gain_vec
    return inv_std * (
        scaled
        - jnp.mean(scaled, axis=-1, keepdims=True)
        - unit_rows * jnp.mean(scaled * unit_rows, axis=-1, keepdims=True)
    )


def silu_slope(pre_act):
    sigmoid_val = jax.nn.sigmoid(pre_act)
    return sigmoid_val * (1.0 + pre_act * (1.0 - sigmoid_val))


def params(semantics, limit=VMEM_LIMIT):
    return pltpu.CompilerParams(dimension_semantics=semantics, vmem_limit_bytes=limit)


def ignoring(body, first, count):
    def called(*refs):
        return body(*refs[:first], *refs[first + count :])

    return called


def to_slab(slab, rows):
    count, groups = rows.shape[0], rows.shape[1] // 128
    for c in range(groups):
        slab[pl.ds(c, count, stride=groups), :] = rows[:, c * 128 : (c + 1) * 128]


def from_slab(slab, count, groups):
    return jnp.concatenate(
        [slab[pl.ds(c, count, stride=groups), :] for c in range(groups)], axis=1
    )


def slab_row(slab, t, groups):
    return slab[pl.ds(pl.multiple_of(t * groups, groups), groups), :]


def front_ends_body(x_ref, gain_ref, decay_ref, low_ref, end_ref, slab):
    states, groups, _ = decay_ref.shape
    count = x_ref.shape[1]

    @pl.when(pl.program_id(1) == 0)
    def _():
        end_ref[...] = jnp.zeros_like(end_ref)

    unit, _ = unit_rows_of(x_ref[0].astype(f32))
    normed = unit * gain_ref[...]
    low_ref[0] = normed.astype(bf16)
    to_slab(slab, normed)
    decay = [decay_ref[n] for n in range(states)]

    def step(t, state):
        row = slab_row(slab, t, groups)
        return tuple(d * s + row for d, s in zip(decay, state))

    state = lax.fori_loop(
        0, count, step, tuple(end_ref[0, n] for n in range(states)), unroll=8
    )
    for n in range(states):
        end_ref[0, n] = state[n]


def front_ends(x, gain, decay, block=256, after=()):
    slots, length, width = x.shape
    states, groups, lanes = decay.shape
    block = min(block, length)
    return pl.pallas_call(
        ignoring(front_ends_body, 3, len(after)),
        grid=(slots, length // block),
        in_specs=[
            pl.BlockSpec((1, block, width), lambda k, b: (k, b, 0)),
            pl.BlockSpec((1, width), lambda k, b: (0, 0)),
            pl.BlockSpec((states, groups, lanes), lambda k, b: (0, 0, 0)),
        ]
        + [pl.BlockSpec(memory_space=pl.ANY)] * len(after),
        out_specs=[
            pl.BlockSpec((1, block, width), lambda k, b: (k, b, 0)),
            pl.BlockSpec((1, states, groups, lanes), lambda k, b: (k, 0, 0, 0)),
        ],
        out_shape=[
            jax.ShapeDtypeStruct((slots, length, width), bf16),
            jax.ShapeDtypeStruct((slots, states, groups, lanes), f32),
        ],
        scratch_shapes=[pltpu.VMEM((block * groups, lanes), f32)],
        compiler_params=params(("arbitrary", "arbitrary")),
        name="front_ends",
        cost_estimate=pl.CostEstimate(
            flops=slots * length * width * states * 4,
            bytes_accessed=4 * slots * length * width,
            transcendentals=0,
        ),
    )(x, gain, decay, *after)


def front_scan_body(
    table_ref,
    x_ref,
    gain_ref,
    decay_ref,
    coef_ref,
    span_ref,
    omega_ref,
    ends_ref,
    smooth_ref,
    mixed_ref,
    check_ref,
    slab,
    out_slab,
    carry,
):
    states, groups, _ = decay_ref.shape
    count = x_ref.shape[1]
    slot = pl.program_id(0)
    total = ends_ref.shape[0]

    @pl.when(pl.program_id(1) == 0)
    def _():
        carry[...] = jnp.zeros_like(carry)

        def link(i, _):
            carry[...] = span_ref[...] * carry[...] + ends_ref[table_ref[total + i]]
            return 0

        lax.fori_loop(0, table_ref[slot], link, 0)

    unit, _ = unit_rows_of(x_ref[0].astype(f32))
    normed = unit * gain_ref[...]
    to_slab(slab, normed)
    decay = [decay_ref[n] for n in range(states)]
    coef = [coef_ref[n] for n in range(states)]
    state = tuple(carry[n] for n in range(states))
    for n in range(states):
        check_ref[0, 0, n] = state[n]

    def step(t, state):
        row = slab_row(slab, t, groups)
        state = tuple(d * s + row for d, s in zip(decay, state))
        parts = [c * s for c, s in zip(coef, state)]
        while len(parts) > 1:
            parts = [a + b for a, b in zip(parts[::2], parts[1::2])]
        out_slab[pl.ds(pl.multiple_of(t * groups, groups), groups), :] = parts[0]
        return state

    state = lax.fori_loop(0, count, step, state, unroll=8)
    for n in range(states):
        carry[n] = state[n]
    smoothed = from_slab(out_slab, count, groups) + omega_ref[...] * normed
    smooth_ref[0] = smoothed
    mixed_ref[0] = (smoothed * jax.nn.sigmoid(smoothed)).astype(bf16)


def front_scan(table, x, gain, decay, coef, span, omega, ends, block):
    slots, length, width = x.shape
    states, groups, lanes = decay.shape
    whole3 = pl.BlockSpec((states, groups, lanes), lambda k, b, t: (0, 0, 0))
    row = pl.BlockSpec((1, width), lambda k, b, t: (0, 0))
    tokens = pl.BlockSpec((1, block, width), lambda k, b, t: (k, b, 0))
    return pl.pallas_call(
        front_scan_body,
        grid_spec=pltpu.PrefetchScalarGridSpec(
            num_scalar_prefetch=1,
            grid=(slots, length // block),
            in_specs=[
                tokens,
                row,
                whole3,
                whole3,
                whole3,
                row,
                pl.BlockSpec(ends.shape, lambda k, b, t: (0, 0, 0, 0)),
            ],
            out_specs=[
                tokens,
                tokens,
                pl.BlockSpec((1, 1, states, groups, lanes), lambda k, b, t: (k, b, 0, 0, 0)),
            ],
            scratch_shapes=[
                pltpu.VMEM((block * groups, lanes), f32),
                pltpu.VMEM((block * groups, lanes), f32),
                pltpu.VMEM((states, groups, lanes), f32),
            ],
        ),
        out_shape=[
            jax.ShapeDtypeStruct((slots, length, width), f32),
            jax.ShapeDtypeStruct((slots, length, width), bf16),
            jax.ShapeDtypeStruct((slots, length // block, states, groups, lanes), f32),
        ],
        compiler_params=params(("arbitrary", "arbitrary")),
        name="front_scan",
        cost_estimate=pl.CostEstimate(
            flops=slots * length * width * states * 8,
            bytes_accessed=8 * slots * length * width,
            transcendentals=slots * length * width,
        ),
    )(table, x, gain, decay, coef, span, omega, ends)


def back_ends_body(gs_ref, decay_ref, end_ref, slab):
    states, groups, _ = decay_ref.shape
    count = gs_ref.shape[1]

    @pl.when(pl.program_id(1) == 0)
    def _():
        end_ref[...] = jnp.zeros_like(end_ref)

    to_slab(slab, gs_ref[0])
    decay = [decay_ref[n] for n in range(states)]

    def step(t, state):
        row = slab_row(slab, count - 1 - t, groups)
        return tuple(d * s + row for d, s in zip(decay, state))

    state = lax.fori_loop(
        0, count, step, tuple(end_ref[0, n] for n in range(states)), unroll=8
    )
    for n in range(states):
        end_ref[0, n] = state[n]


def back_ends(gs, decay, block=256, after=()):
    slots, length, width = gs.shape
    states, groups, lanes = decay.shape
    block = min(block, length)
    blocks = length // block
    return pl.pallas_call(
        ignoring(back_ends_body, 2, len(after)),
        grid=(slots, blocks),
        in_specs=[
            pl.BlockSpec((1, block, width), lambda k, b: (k, blocks - 1 - b, 0)),
            pl.BlockSpec((states, groups, lanes), lambda k, b: (0, 0, 0)),
        ]
        + [pl.BlockSpec(memory_space=pl.ANY)] * len(after),
        out_specs=pl.BlockSpec((1, states, groups, lanes), lambda k, b: (k, 0, 0, 0)),
        out_shape=jax.ShapeDtypeStruct((slots, states, groups, lanes), f32),
        scratch_shapes=[pltpu.VMEM((block * groups, lanes), f32)],
        compiler_params=params(("arbitrary", "arbitrary")),
        name="back_ends",
        cost_estimate=pl.CostEstimate(
            flops=slots * length * width * states * 4,
            bytes_accessed=4 * slots * length * width,
            transcendentals=0,
        ),
    )(gs, decay, *after)


def back_scan_body(
    table_ref,
    x_ref,
    gs_ref,
    gv_ref,
    gi_ref,
    check_ref,
    gain_ref,
    decay_ref,
    coef_ref,
    span_ref,
    omega_ref,
    ends_ref,
    grad_ref,
    qx_ref,
    qs_ref,
    gain_grad_ref,
    omega_grad_ref,
    slab,
    gs_slab,
    out_slab,
    history,
    carry,
):
    states, groups, _ = decay_ref.shape
    count = x_ref.shape[1]
    slot = pl.program_id(0)
    total = ends_ref.shape[0]

    @pl.when((slot == 0) & (pl.program_id(1) == 0))
    def _():
        qx_ref[...] = jnp.zeros_like(qx_ref)
        qs_ref[...] = jnp.zeros_like(qs_ref)
        gain_grad_ref[...] = jnp.zeros_like(gain_grad_ref)
        omega_grad_ref[...] = jnp.zeros_like(omega_grad_ref)

    @pl.when(pl.program_id(1) == 0)
    def _():
        carry[...] = jnp.zeros_like(carry)

        def link(i, _):
            carry[...] = (
                span_ref[...] * carry[...] + ends_ref[table_ref[total + total - 1 - i]]
            )
            return 0

        lax.fori_loop(0, total - 1 - table_ref[slot], link, 0)

    unit, inv = unit_rows_of(x_ref[0].astype(f32))
    normed = unit * gain_ref[...]
    gs = gs_ref[0]
    to_slab(slab, normed)
    to_slab(gs_slab, gs)
    decay = [decay_ref[n] for n in range(states)]

    def recompute(t, state):
        for n in range(states):
            history[t, n] = state[n]
        row = slab_row(slab, t, groups)
        return tuple(d * s + row for d, s in zip(decay, state))

    lax.fori_loop(
        0, count, recompute, tuple(check_ref[0, 0, n] for n in range(states)), unroll=4
    )

    half = states // 2
    for part in range(2):
        chosen = range(part * half, (part + 1) * half)
        decay = [decay_ref[n] for n in chosen]
        coef = [coef_ref[n] for n in chosen]

        def step(i, held):
            q, qx, qs = held
            t = count - 1 - i
            row = slab_row(slab, t, groups)
            g = slab_row(gs_slab, t, groups)
            q = tuple(d * a + g for d, a in zip(decay, q))
            parts = [c * a for c, a in zip(coef, q)]
            while len(parts) > 1:
                parts = [a + b for a, b in zip(parts[::2], parts[1::2])]
            spot = pl.ds(pl.multiple_of(t * groups, groups), groups)
            if part == 0:
                out_slab[spot, :] = parts[0]
            else:
                out_slab[spot, :] = out_slab[spot, :] + parts[0]
            qx = tuple(a + b * row for a, b in zip(qx, q))
            qs = tuple(a + b * history[t, n] for a, b, n in zip(qs, q, chosen))
            return q, qx, qs

        q, qx, qs = lax.fori_loop(
            0,
            count,
            step,
            (
                tuple(carry[n] for n in chosen),
                tuple(qx_ref[n] for n in chosen),
                tuple(qs_ref[n] for n in chosen),
            ),
            unroll=4,
        )
        for i, n in enumerate(chosen):
            carry[n] = q[i]
            qx_ref[n] = qx[i]
            qs_ref[n] = qs[i]

    grad_normed = (
        gv_ref[0] + from_slab(out_slab, count, groups) + omega_ref[...] * gs
    )
    gain_grad_ref[...] += jnp.sum(grad_normed * unit, axis=0, keepdims=True)
    omega_grad_ref[...] += jnp.sum(gs * normed, axis=0, keepdims=True)
    grad_ref[0] = (
        gi_ref[0] + norm_back_rows(grad_normed, gain_ref[...], unit, inv)
    ).astype(bf16)


def back_scan(table, x, gs, gv, gi, check, gain, decay, coef, span, omega, ends, after=()):
    slots, length, width = x.shape
    states, groups, lanes = decay.shape
    blocks = check.shape[1]
    block = length // blocks
    whole3 = pl.BlockSpec((states, groups, lanes), lambda k, b, t: (0, 0, 0))
    row = pl.BlockSpec((1, width), lambda k, b, t: (0, 0))
    tokens = pl.BlockSpec((1, block, width), lambda k, b, t: (k, blocks - 1 - b, 0))
    return pl.pallas_call(
        ignoring(back_scan_body, 12, len(after)),
        grid_spec=pltpu.PrefetchScalarGridSpec(
            num_scalar_prefetch=1,
            grid=(slots, blocks),
            in_specs=[
                tokens,
                tokens,
                tokens,
                tokens,
                pl.BlockSpec(
                    (1, 1, states, groups, lanes),
                    lambda k, b, t: (k, blocks - 1 - b, 0, 0, 0),
                ),
                row,
                whole3,
                whole3,
                whole3,
                row,
                pl.BlockSpec(ends.shape, lambda k, b, t: (0, 0, 0, 0)),
            ]
            + [pl.BlockSpec(memory_space=pl.ANY)] * len(after),
            out_specs=[tokens, whole3, whole3, row, row],
            scratch_shapes=[
                pltpu.VMEM((block * groups, lanes), f32),
                pltpu.VMEM((block * groups, lanes), f32),
                pltpu.VMEM((block * groups, lanes), f32),
                pltpu.VMEM((block, states, groups, lanes), f32),
                pltpu.VMEM((states, groups, lanes), f32),
            ],
        ),
        out_shape=[
            jax.ShapeDtypeStruct((slots, length, width), bf16),
            jax.ShapeDtypeStruct((states, groups, lanes), f32),
            jax.ShapeDtypeStruct((states, groups, lanes), f32),
            jax.ShapeDtypeStruct((1, width), f32),
            jax.ShapeDtypeStruct((1, width), f32),
        ],
        compiler_params=params(("arbitrary", "arbitrary")),
        name="back_scan",
        cost_estimate=pl.CostEstimate(
            flops=slots * length * width * states * 20,
            bytes_accessed=16 * slots * length * width,
            transcendentals=0,
        ),
    )(table, x, gs, gv, gi, check, gain, decay, coef, span, omega, ends, *after)


def load_chunks(table_ref, sources, total, length, sem):
    copies = []
    for slot in range(total):
        place = pl.ds(pl.multiple_of(table_ref[slot] * length, length), length)
        for own, others, kept in sources:
            source = own.at[slot] if slot < 2 else others.at[slot - 2]
            copies.append(
                pltpu.make_async_copy(source, kept.at[place, :], sem.at[len(copies)])
            )
    for copy in copies:
        copy.start()
    for copy in copies:
        copy.wait()


def attend_body(
    table_ref,
    q_ref,
    bias_ref,
    reset_ref,
    k_own,
    k_oth,
    v_own,
    v_oth,
    out_ref,
    gated_ref,
    lse_ref,
    keys,
    values,
    scores,
    probs,
    sem,
    *,
    total,
):
    length, key_width = q_ref.shape[1:]
    value_width = values.shape[1]
    tiles = length // TILE
    scale = float(key_width) ** (-0.5)

    @pl.when(pl.program_id(0) == 0)
    def _():
        load_chunks(
            table_ref, ((k_own, k_oth, keys), (v_own, v_oth, values)), total, length, sem
        )

    chunk = table_ref[pl.program_id(0)]
    reach = jnp.where(table_ref[2 * total] == 1, chunk + 1, 1)
    base = (chunk + 1 - reach) * length
    queries = q_ref[0]

    def first(kt, peak):
        spot = pl.ds(pl.multiple_of(base + kt * TILE, TILE), TILE)
        tile = (
            lax.dot_general(
                queries, keys[spot, :], (((1,), (1,)), ((), ())), preferred_element_type=f32
            )
            * scale
        )
        for r in range(tiles):
            rows = slice(r * TILE, (r + 1) * TILE)
            gap = (reach - 1) * tiles + r - kt + tiles - 1
            scores[kt, rows, :] = tile[rows] + bias_ref[gap]
        return jnp.maximum(peak, jnp.max(scores[kt], axis=1, keepdims=True))

    peak = lax.fori_loop(
        0, reach * tiles, first, jnp.full((length, 1), 2 * MASKED, f32)
    )

    def second(kt, sums):
        terms = jnp.exp(scores[kt] - peak)
        probs[:, pl.ds(pl.multiple_of(kt * TILE, TILE), TILE)] = terms.astype(bf16)
        return sums + jnp.sum(terms, axis=1, keepdims=True)

    sums = lax.fori_loop(0, reach * tiles, second, jnp.zeros((length, 1), f32))
    lse_ref[0] = peak + jnp.log(sums)
    inverse = 1.0 / sums

    for count in range(1, total + 1):

        @pl.when(reach == count)
        def _(count=count):
            width = count * length
            span = pl.ds(pl.multiple_of(base, length), width)

            def column(ct, _):
                at = pl.ds(pl.multiple_of(ct * TILE, TILE), TILE)
                rows = (
                    jnp.dot(probs[:, :width], values[span, at], preferred_element_type=f32)
                    * inverse
                )
                out_ref[0, :, at] = rows.astype(bf16)
                gate = reset_ref[0, :, at].astype(f32)
                gated_ref[0, :, at] = (gate * jax.nn.sigmoid(gate) * rows).astype(bf16)
                return 0

            lax.fori_loop(0, value_width // TILE, column, 0)


def attend(table, q, bias, reset, k_own, k_oth, v_own, v_oth):
    slots, length, key_width = q.shape
    value_width = v_own.shape[2]
    total = slots + k_oth.shape[0]
    anywhere = pl.BlockSpec(memory_space=pl.ANY)
    tokens = pl.BlockSpec((1, length, value_width), lambda k, t: (k, 0, 0))
    return pl.pallas_call(
        functools.partial(attend_body, total=total),
        grid_spec=pltpu.PrefetchScalarGridSpec(
            num_scalar_prefetch=1,
            grid=(slots,),
            in_specs=[
                pl.BlockSpec((1, length, key_width), lambda k, t: (k, 0, 0)),
                pl.BlockSpec(bias.shape, lambda k, t: (0, 0, 0)),
                tokens,
                anywhere,
                anywhere,
                anywhere,
                anywhere,
            ],
            out_specs=[
                tokens,
                tokens,
                pl.BlockSpec((1, length, 1), lambda k, t: (k, 0, 0)),
            ],
            scratch_shapes=[
                pltpu.VMEM((total * length, key_width), bf16),
                pltpu.VMEM((total * length, value_width), bf16),
                pltpu.VMEM((total * length // TILE, length, TILE), f32),
                pltpu.VMEM((length, total * length), bf16),
                pltpu.SemaphoreType.DMA((2 * total,)),
            ],
        ),
        out_shape=[
            jax.ShapeDtypeStruct((slots, length, value_width), bf16),
            jax.ShapeDtypeStruct((slots, length, value_width), bf16),
            jax.ShapeDtypeStruct((slots, length, 1), f32),
        ],
        compiler_params=params(("arbitrary",)),
        name="attend",
        cost_estimate=pl.CostEstimate(
            flops=slots * length * total * length * (key_width + value_width),
            bytes_accessed=20 * slots * length * value_width,
            transcendentals=slots * length * total * length,
        ),
    )(table, q, bias, reset, k_own, k_oth, v_own, v_oth)


def attend_back_body(
    table_ref,
    q_ref,
    grad_ref,
    lse_ref,
    bias_ref,
    k_own,
    k_oth,
    v_own,
    v_oth,
    gq_ref,
    gk_own,
    gk_oth,
    gv_own,
    gv_oth,
    rel_out,
    keys,
    values,
    gk_sum,
    gv_sum,
    probs_kept,
    grads_kept,
    rel_ref,
    sem,
    *,
    total,
):
    length, key_width = q_ref.shape[1:]
    value_width = values.shape[1]
    tiles = length // TILE
    scale = float(key_width) ** (-0.5)
    step = pl.program_id(0)
    nt = (((1,), (1,)), ((), ()))
    tn = (((0,), (0,)), ((), ()))

    @pl.when(step == 0)
    def _():
        gk_sum[...] = jnp.zeros_like(gk_sum)
        gv_sum[...] = jnp.zeros_like(gv_sum)
        rel_ref[...] = jnp.zeros_like(rel_ref)
        load_chunks(
            table_ref, ((k_own, k_oth, keys), (v_own, v_oth, values)), total, length, sem
        )

    chunk = table_ref[step]
    reach = jnp.where(table_ref[2 * total] == 1, chunk + 1, 1)
    base = (chunk + 1 - reach) * length
    queries = q_ref[0]
    log_total = lse_ref[0]

    def gap_of(kc, a, r):
        return (reach - 1 - kc) * tiles + r - a + tiles - 1

    def first(kc, delta):
        spot = pl.ds(pl.multiple_of(base + kc * length, length), length)
        grads_kept[kc] = lax.dot_general(
            values[spot, :], grad_ref[0], nt, preferred_element_type=f32
        )
        tile = (
            lax.dot_general(keys[spot, :], queries, nt, preferred_element_type=f32) * scale
        )
        for a in range(tiles):
            for r in range(tiles):
                rows = slice(a * TILE, (a + 1) * TILE)
                cols = slice(r * TILE, (r + 1) * TILE)
                probs_kept[kc, rows, cols] = jnp.exp(
                    tile[rows, cols] + bias_ref[gap_of(kc, a, r)] - log_total[:, cols]
                )
        return delta + jnp.sum(probs_kept[kc] * grads_kept[kc], axis=0, keepdims=True)

    delta = lax.fori_loop(0, reach, first, jnp.zeros((1, length), f32))

    def second(kc, grad_query):
        spot = pl.ds(pl.multiple_of(base + kc * length, length), length)
        probs = probs_kept[kc]
        grad_scores = (probs * (grads_kept[kc] - delta)).astype(bf16)
        probs = probs.astype(bf16)
        for a in range(tiles):
            for r in range(tiles):
                rel_ref[gap_of(kc, a, r)] += grad_scores[
                    a * TILE : (a + 1) * TILE, r * TILE : (r + 1) * TILE
                ].astype(f32)
        gk_sum[spot, :] += jnp.dot(grad_scores, queries, preferred_element_type=f32)

        def column(ct, _):
            at = pl.ds(pl.multiple_of(ct * 512, 512), 512)
            gv_sum[spot, at] += jnp.dot(
                probs, grad_ref[0, :, at], preferred_element_type=f32
            )
            return 0

        lax.fori_loop(0, value_width // 512, column, 0)
        return grad_query + lax.dot_general(
            grad_scores, keys[spot, :], tn, preferred_element_type=f32
        )

    grad_query = lax.fori_loop(0, reach, second, jnp.zeros((length, key_width), f32))
    gq_ref[0] = grad_query * scale

    @pl.when(step == pl.num_programs(0) - 1)
    def _():
        for slot in range(total):
            place = pl.ds(pl.multiple_of(table_ref[slot] * length, length), length)
            key_out, value_out = (gk_own, gv_own) if slot < 2 else (gk_oth, gv_oth)
            at = slot if slot < 2 else slot - 2
            key_out[at] = (gk_sum[place, :] * scale).astype(bf16)
            value_out[at] = gv_sum[place, :].astype(bf16)
        down = lax.broadcasted_iota(jnp.int32, (TILE, TILE), 0)
        across = lax.broadcasted_iota(jnp.int32, (TILE, TILE), 1)
        mirror = jnp.where(down + across == TILE - 1, 1.0, 0.0)
        for d in range(rel_out.shape[0]):
            flipped = jnp.dot(
                rel_ref[d + tiles - 1],
                mirror,
                precision=lax.Precision.HIGHEST,
                preferred_element_type=f32,
            )
            wide = jnp.concatenate([flipped, jnp.zeros((TILE, TILE), f32)], axis=1)
            turned = pltpu.roll(wide, 0, 1, stride=1, stride_axis=0)
            rel_out[d] = jnp.sum(turned, axis=0, keepdims=True)


def attend_back(table, q, grads, lse, bias, k_own, k_oth, v_own, v_oth, after=()):
    slots, length, key_width = q.shape
    value_width = v_own.shape[2]
    total = slots + k_oth.shape[0]
    rel_shape = (total * length // TILE, 1, 2 * TILE)
    anywhere = pl.BlockSpec(memory_space=pl.ANY)

    def all_of(shape):
        return pl.BlockSpec(
            shape, lambda k, t: (0,) * len(shape), pipeline_mode=pl.Buffered(1)
        )

    return pl.pallas_call(
        ignoring(functools.partial(attend_back_body, total=total), 9, len(after)),
        grid_spec=pltpu.PrefetchScalarGridSpec(
            num_scalar_prefetch=1,
            grid=(slots,),
            in_specs=[
                pl.BlockSpec((1, length, key_width), lambda k, t: (k, 0, 0)),
                pl.BlockSpec((1, length, value_width), lambda k, t: (k, 0, 0)),
                pl.BlockSpec((1, 1, length), lambda k, t: (k, 0, 0)),
                all_of(bias.shape),
                anywhere,
                anywhere,
                anywhere,
                anywhere,
            ]
            + [anywhere] * len(after),
            out_specs=[
                pl.BlockSpec((1, length, key_width), lambda k, t: (k, 0, 0)),
                all_of(k_own.shape),
                all_of(k_oth.shape),
                all_of(v_own.shape),
                all_of(v_oth.shape),
                all_of(rel_shape),
            ],
            scratch_shapes=[
                pltpu.VMEM((total * length, key_width), bf16),
                pltpu.VMEM((total * length, value_width), bf16),
                pltpu.VMEM((total * length, key_width), f32),
                pltpu.VMEM((total * length, value_width), f32),
                pltpu.VMEM((total, length, length), f32),
                pltpu.VMEM((total, length, length), f32),
                pltpu.VMEM(bias.shape, f32),
                pltpu.SemaphoreType.DMA((2 * total,)),
            ],
        ),
        out_shape=[
            jax.ShapeDtypeStruct((slots, length, key_width), f32),
            jax.ShapeDtypeStruct(k_own.shape, bf16),
            jax.ShapeDtypeStruct(k_oth.shape, bf16),
            jax.ShapeDtypeStruct(v_own.shape, bf16),
            jax.ShapeDtypeStruct(v_oth.shape, bf16),
            jax.ShapeDtypeStruct(rel_shape, f32),
        ],
        compiler_params=params(("arbitrary",)),
        name="attend_back",
        cost_estimate=pl.CostEstimate(
            flops=2 * slots * length * total * length * (key_width + value_width),
            bytes_accessed=20 * slots * length * value_width,
            transcendentals=slots * length * total * length,
        ),
    )(table, q, grads, lse, bias, k_own, k_oth, v_own, v_oth, *after)


def bias_body(flag_ref, back_row, front_row, back_ref, front_ref, *, spare):
    tile = pl.program_id(0) - spare
    full = flag_ref[0] == 1

    @pl.when(tile < 0)
    def _():
        back_ref[...] = jnp.full_like(back_ref, MASKED)
        front_ref[...] = jnp.full_like(front_ref, MASKED)

    @pl.when(tile >= 0)
    def _():
        down = lax.broadcasted_iota(jnp.int32, (TILE, TILE), 0)
        across = lax.broadcasted_iota(jnp.int32, (TILE, TILE), 1)
        near = jnp.where(down // STRETCH == across // STRETCH, 1, 0)
        for row, out, ordered in (
            (back_row, back_ref, jnp.where(down <= across, 1, 0)),
            (front_row, front_ref, jnp.where(across <= down, 1, 0)),
        ):
            wide = jnp.broadcast_to(row[0], (TILE, 2 * TILE))
            turned = pltpu.roll(wide, 0, 1, stride=1, stride_axis=0)[:, :TILE]
            allowed = jnp.where(
                tile == 0, jnp.where(full, ordered, ordered * near), jnp.where(full, 1, 0)
            )
            out[0] = jnp.where(allowed == 1, turned, MASKED)


def bias_tiles(relative_bias, spare, full):
    length = relative_bias.shape[0] // 2
    count = length // TILE
    windows = jnp.stack(
        [
            lax.slice_in_dim(relative_bias, length - d * TILE - TILE, length - d * TILE + TILE)
            for d in range(count)
        ]
    )
    front = jnp.concatenate([windows[:, TILE:], windows[:, :TILE]], axis=1)
    back = jnp.concatenate([windows[:, TILE:TILE + 1], windows[:, ::-1][:, TILE:], windows[:, ::-1][:, : TILE - 1]], axis=1)
    row = pl.BlockSpec((1, 1, 2 * TILE), lambda d, t: (jnp.maximum(d - spare, 0), 0, 0))
    out = pl.BlockSpec((1, TILE, TILE), lambda d, t: (d, 0, 0))
    shape = jax.ShapeDtypeStruct((spare + count, TILE, TILE), f32)
    return pl.pallas_call(
        functools.partial(bias_body, spare=spare),
        grid_spec=pltpu.PrefetchScalarGridSpec(
            num_scalar_prefetch=1,
            grid=(spare + count,),
            in_specs=[row, row],
            out_specs=[out, out],
        ),
        out_shape=[shape, shape],
        compiler_params=params(("arbitrary",)),
        name="bias",
    )(full.astype(jnp.int32)[None], back[:, None], front[:, None])


def bias_grad(sums, length):
    count = sums.shape[0]
    shifted = jnp.concatenate([jnp.zeros((count, 1), f32), sums[:, :-1]], axis=1)
    none = jnp.zeros((1, TILE), f32)
    blocks = jnp.concatenate([none, shifted[:, :TILE]]) + jnp.concatenate(
        [shifted[:, TILE:], none]
    )
    return jnp.concatenate(
        [blocks[::-1].reshape(-1), jnp.zeros((2 * length - (count + 1) * TILE,), f32)]
    )


def gate_body(
    back_ref,
    cot_ref,
    x_ref,
    cand_ref,
    update_ref,
    reset_ref,
    attended_ref,
    gain_ref,
    proj_ref,
    input_ref,
    main_ref,
    grad_att_ref,
    gain_grad_ref,
):
    width = x_ref.shape[1]
    value_width = proj_ref.shape[0]

    @pl.when(pl.program_id(0) == 0)
    def _():
        gain_grad_ref[...] = jnp.zeros_like(gain_grad_ref)

    x = x_ref[...].astype(f32)
    cand_in = cand_ref[...]
    gate = jax.nn.sigmoid(cand_in)
    candidate = cand_in * gate
    update = jax.nn.sigmoid(update_ref[...].astype(f32))
    change = candidate - x
    unit, inv = unit_rows_of(x + update * change)
    grad_feed = back_ref[...]
    gain_grad_ref[...] += jnp.sum(grad_feed * unit, axis=0, keepdims=True)
    grad_first = cot_ref[...].astype(f32) + norm_back_rows(
        grad_feed, gain_ref[...], unit, inv
    )
    kept = grad_first * (1.0 - update)
    input_ref[...] = kept
    main_ref[:, value_width : value_width + width] = (kept * change * update).astype(bf16)
    grad_cand = (grad_first * update * (gate + candidate * (1.0 - gate))).astype(bf16)
    main_ref[:, value_width + width :] = grad_cand
    for c in range(value_width // 512):
        at = slice(c * 512, (c + 1) * 512)
        grad_gated = mm_nt(grad_cand, proj_ref[at, :])
        reset = reset_ref[:, at].astype(f32)
        open_gate = jax.nn.sigmoid(reset)
        passed = reset * open_gate
        grad_att_ref[:, at] = (grad_gated * passed).astype(bf16)
        main_ref[:, at] = (
            grad_gated
            * attended_ref[:, at].astype(f32)
            * (open_gate + passed * (1.0 - open_gate))
        ).astype(bf16)


def gate(back, cot, x, cand_in, base, attended, gain, proj, after=()):
    tokens, width = x.shape
    value_width = proj.shape[0]
    rows = min(128, tokens)
    wide = value_width // width

    def block(columns, at=0):
        return pl.BlockSpec((rows, columns), lambda i: (i, at))

    return pl.pallas_call(
        ignoring(gate_body, 9, len(after)),
        grid=(tokens // rows,),
        in_specs=[
            block(width),
            block(width),
            block(width),
            block(width),
            block(width, wide),
            block(value_width),
            block(value_width),
            pl.BlockSpec((1, width), lambda i: (0, 0)),
            pl.BlockSpec(proj.shape, lambda i: (0, 0), pipeline_mode=pl.Buffered(1)),
        ]
        + [pl.BlockSpec(memory_space=pl.ANY)] * len(after),
        out_specs=[
            block(width),
            block(value_width + 2 * width),
            block(value_width),
            pl.BlockSpec((1, width), lambda i: (0, 0)),
        ],
        out_shape=[
            jax.ShapeDtypeStruct((tokens, width), f32),
            jax.ShapeDtypeStruct((tokens, value_width + 2 * width), bf16),
            jax.ShapeDtypeStruct((tokens, value_width), bf16),
            jax.ShapeDtypeStruct((1, width), f32),
        ],
        compiler_params=params(("arbitrary",)),
        name="gate",
        cost_estimate=pl.CostEstimate(
            flops=2 * tokens * width * value_width,
            bytes_accessed=40 * tokens * width,
            transcendentals=4 * tokens * width,
        ),
    )(back, cot, x, cand_in, base, base, attended, gain, proj, *after)


def ordered_transpose(ids_ref, source, plain, ordered):
    plain[...] = source[...].T
    count = ids_ref.shape[0]
    rows = plain.shape[0] // count

    def place(p, _):
        ordered[pl.ds(pl.multiple_of(p * rows, rows), rows), :] = plain[
            pl.ds(pl.multiple_of(ids_ref[p] * rows, rows), rows), :
        ]
        return 0

    lax.fori_loop(0, count, place, 0)


def feed_body(
    ids_ref,
    places_ref,
    low_ref,
    cot_ref,
    first_ref,
    in_ref,
    out_ref,
    result_ref,
    back_ref,
    out_send,
    out_keep,
    in_send,
    in_keep,
    total,
    cot_turned,
    low_turned,
    plain,
):
    step = pl.program_id(0)
    half = pl.num_programs(0) // 2
    tokens = low_ref.shape[0]
    rows = min(256, tokens)
    nt = (((1,), (1,)), ((), ()))

    @pl.when(step == 0)
    def _():
        cot_turned[...] = cot_ref[...].T
        ordered_transpose(ids_ref, low_ref, plain, low_turned)
        total[...] = first_ref[...]
        back_ref[...] = jnp.zeros_like(back_ref)

    acts, grads = [], []
    for r in range(tokens // rows):
        at = slice(r * rows, (r + 1) * rows)
        hidden = jnp.dot(low_ref[at, :], in_ref[...], preferred_element_type=f32)
        grad_act = lax.dot_general(
            cot_ref[at, :], out_ref[...], nt, preferred_element_type=f32
        )
        gate = jax.nn.sigmoid(hidden)
        act = hidden * gate
        grad = (grad_act * (gate + act * (1.0 - gate))).astype(bf16)
        act = act.astype(bf16)
        total[at, :] += jnp.dot(act, out_ref[...], preferred_element_type=f32)
        back_ref[at, :] += lax.dot_general(
            grad, in_ref[...], nt, preferred_element_type=f32
        )
        acts.append(act)
        grads.append(grad)
    out_grad = jnp.dot(
        cot_turned[...], jnp.concatenate(acts), preferred_element_type=f32
    ).astype(bf16)
    in_grad = jnp.dot(
        low_turned[...], jnp.concatenate(grads), preferred_element_type=f32
    ).astype(bf16)
    middle = in_grad.shape[0] // 2
    in_send[...] = in_grad[:middle].reshape(in_send.shape)
    in_keep[...] = in_grad[middle:].reshape(in_keep.shape)

    @pl.when(step < half)
    def _():
        out_send[0] = out_grad

    @pl.when(step >= half)
    def _():
        out_keep[0] = out_grad

    @pl.when(step == pl.num_programs(0) - 1)
    def _():
        result_ref[...] = total[...].astype(bf16)


def feed(ids, places, low, cot, first_sum, feed_in, feed_out, seq, after=()):
    tokens, width = low.shape
    features = feed_in.shape[1]
    parts = ids.shape[0]
    half = parts // 2
    columns = features // parts
    rows = width // parts
    share = parts // seq
    anywhere = pl.BlockSpec(memory_space=pl.ANY)

    def all_of(shape):
        return pl.BlockSpec(
            shape, lambda i, t, u: (0,) * len(shape), pipeline_mode=pl.Buffered(1)
        )

    def at(i, t):
        return t[jnp.minimum(i, parts - 1)]

    split = pl.BlockSpec(
        (half, 1, rows, columns), lambda i, t, u: (0, u[at(i, t) // share], 0, at(i, t) % share)
    )
    return pl.pallas_call(
        ignoring(feed_body, 7, len(after)),
        grid_spec=pltpu.PrefetchScalarGridSpec(
            num_scalar_prefetch=2,
            grid=(parts,),
            in_specs=[
                all_of(low.shape),
                all_of(cot.shape),
                all_of(first_sum.shape),
                pl.BlockSpec((width, columns), lambda i, t, u: (0, at(i, t))),
                pl.BlockSpec((columns, width), lambda i, t, u: (at(i, t), 0)),
            ]
            + [anywhere] * len(after),
            out_specs=[
                all_of(low.shape),
                all_of(low.shape),
                pl.BlockSpec(
                    (1, width, columns), lambda i, t, u: (jnp.minimum(i, half - 1), 0, 0)
                ),
                pl.BlockSpec(
                    (1, width, columns), lambda i, t, u: (jnp.maximum(i - half, 0), 0, 0)
                ),
                split,
                split,
            ],
            scratch_shapes=[
                pltpu.VMEM((tokens, width), f32),
                pltpu.VMEM((width, tokens), bf16),
                pltpu.VMEM((width, tokens), bf16),
                pltpu.VMEM((width, tokens), bf16),
            ],
        ),
        out_shape=[
            jax.ShapeDtypeStruct((tokens, width), bf16),
            jax.ShapeDtypeStruct((tokens, width), f32),
            jax.ShapeDtypeStruct((half, width, columns), bf16),
            jax.ShapeDtypeStruct((half, width, columns), bf16),
            jax.ShapeDtypeStruct((half, seq, rows, features // seq), bf16),
            jax.ShapeDtypeStruct((half, seq, rows, features // seq), bf16),
        ],
        compiler_params=params(("arbitrary",)),
        name="feed",
        cost_estimate=pl.CostEstimate(
            flops=12 * tokens * width * features,
            bytes_accessed=8 * width * features + 16 * tokens * width,
            transcendentals=tokens * features,
        ),
    )(ids, places, low, cot, first_sum, feed_in, feed_out, *after)


def by_columns_body(ids_ref, left_ref, right_ref, send, keep, turned):
    step = pl.program_id(0)
    half = pl.num_programs(0) // 2

    @pl.when(step == 0)
    def _():
        turned[...] = left_ref[...].T

    grad = jnp.dot(turned[...], right_ref[...], preferred_element_type=f32).astype(bf16)

    @pl.when(step < half)
    def _():
        send[0] = grad

    @pl.when(step >= half)
    def _():
        keep[0] = grad


def by_columns(ids, left, right, after=(), rows=None, at=0):
    tokens = left.shape[0]
    rows = rows or left.shape[1]
    parts = ids.shape[0]
    half = parts // 2
    columns = right.shape[1] // parts
    shape = jax.ShapeDtypeStruct((half, rows, columns), bf16)
    if columns % 128:
        left = left[:, at * rows : (at + 1) * rows]
        grad = mm_tn(left, right).astype(bf16).reshape(rows, parts, columns)
        grad = jnp.take(grad, ids, axis=1).transpose(1, 0, 2)
        return grad[:half], grad[half:]
    return pl.pallas_call(
        ignoring(by_columns_body, 3, len(after)),
        grid_spec=pltpu.PrefetchScalarGridSpec(
            num_scalar_prefetch=1,
            grid=(parts,),
            in_specs=[
                pl.BlockSpec(
                    (tokens, rows), lambda i, t: (0, at), pipeline_mode=pl.Buffered(1)
                ),
                pl.BlockSpec((tokens, columns), lambda i, t: (0, t[jnp.minimum(i, parts - 1)])),
            ]
            + [pl.BlockSpec(memory_space=pl.ANY)] * len(after),
            out_specs=[
                pl.BlockSpec(
                    (1, rows, columns), lambda i, t: (jnp.minimum(i, half - 1), 0, 0)
                ),
                pl.BlockSpec(
                    (1, rows, columns), lambda i, t: (jnp.maximum(i - half, 0), 0, 0)
                ),
            ],
            scratch_shapes=[pltpu.VMEM((rows, tokens), bf16)],
        ),
        out_shape=[shape, shape],
        compiler_params=params(("arbitrary",)),
        name="by_columns",
        cost_estimate=pl.CostEstimate(
            flops=2 * tokens * rows * right.shape[1],
            bytes_accessed=2 * (tokens + rows) * right.shape[1],
            transcendentals=0,
        ),
    )(ids, left, right, *after)


def by_rows_body(ids_ref, places_ref, left_ref, right_ref, send, keep, plain, turned):
    @pl.when(pl.program_id(0) == 0)
    def _():
        ordered_transpose(ids_ref, left_ref, plain, turned)

    grad = jnp.dot(turned[...], right_ref[...], preferred_element_type=f32).astype(bf16)
    middle = grad.shape[0] // 2
    send[...] = grad[:middle].reshape(send.shape)
    keep[...] = grad[middle:].reshape(keep.shape)


def by_rows(ids, places, left, right, seq=1, after=()):
    tokens, rows = left.shape
    parts = ids.shape[0]
    half = parts // 2
    if places is None:
        seq, places = 1, jnp.zeros((1,), jnp.int32)
    columns = right.shape[1] // seq
    tile = min(512, columns)
    share = columns // tile
    shape = jax.ShapeDtypeStruct((half, seq, rows // parts, columns), bf16)
    split = pl.BlockSpec(
        (half, 1, rows // parts, tile), lambda i, t, u: (0, u[jnp.minimum(i // share, seq - 1)], 0, i % share)
    )
    return pl.pallas_call(
        ignoring(by_rows_body, 4, len(after)),
        grid_spec=pltpu.PrefetchScalarGridSpec(
            num_scalar_prefetch=2,
            grid=(seq * share,),
            in_specs=[
                pl.BlockSpec(
                    left.shape, lambda i, t, u: (0, 0), pipeline_mode=pl.Buffered(1)
                ),
                pl.BlockSpec((tokens, tile), lambda i, t, u: (0, i)),
            ]
            + [pl.BlockSpec(memory_space=pl.ANY)] * len(after),
            out_specs=[split, split],
            scratch_shapes=[
                pltpu.VMEM((rows, tokens), bf16),
                pltpu.VMEM((rows, tokens), bf16),
            ],
        ),
        out_shape=[shape, shape],
        compiler_params=params(("arbitrary",)),
        name="by_rows",
        cost_estimate=pl.CostEstimate(
            flops=2 * tokens * rows * right.shape[1],
            bytes_accessed=2 * (tokens + rows) * right.shape[1],
            transcendentals=0,
        ),
    )(ids, places, left, right, *after)


class Layout:
    def __init__(self, mesh):
        self.dp = mesh.shape["dp"]
        self.seq = mesh.shape["seq"]
        self.members = self.seq // 2
        self.chips = self.seq // 4

    def pairs(self, move):
        return [
            (d * self.seq + z, e * self.seq + w)
            for d in range(self.dp)
            for z in range(self.seq)
            for e, w in [move(d, z)]
        ]

    def send(self, value, move):
        return lax.ppermute(value, AXES, self.pairs(move))

    def place(self, sequence, member):
        return member % 2 ^ (1 - sequence % 2), sequence * self.chips + member // 2

    def member(self, core, z):
        sequence = z // self.chips
        return (z % self.chips) * 2 + (core ^ (1 - sequence % 2))

    def home_to_work(self, round_index):
        def move(d, z):
            part = (1 if z >= self.seq // 2 else 0) ^ round_index
            core, at = self.place(2 * (d % 2) + part, min(z, self.seq - 1 - z))
            return d - d % 2 + core, at

        return move

    def spread(self, value):
        late = lax.axis_index("seq") >= self.seq // 2
        out = []
        for round_index in range(2):
            sent = lax.dynamic_index_in_dim(
                value, jnp.where(late, 1 - round_index, round_index), 0, False
            )
            out.append(self.send(sent, self.home_to_work(round_index)))
        return out

    def collect(self, values):
        back = []
        for round_index in range(2):
            pairs = [(b, a) for a, b in self.pairs(self.home_to_work(round_index))]
            back.append(lax.ppermute(values[round_index], AXES, pairs))
        late = lax.axis_index("seq") >= self.seq // 2
        return jnp.stack([jnp.where(late, back[1], back[0]), jnp.where(late, back[0], back[1])])

    def rotate(self, value, by):
        def move(d, z):
            member = (self.member(d % 2, z) + by) % self.members
            core, at = self.place(z // self.chips, member)
            return d - d % 2 + core, at

        return self.send(value, move)

    def gather(self, value):
        return jnp.concatenate([self.rotate(value, by) for by in range(1, self.members)], axis=0)

    def scatter_sum(self, own, others):
        slots = own.shape[0]
        total = own.astype(f32)
        for by in range(1, self.members):
            total = total + self.rotate(
                others[(by - 1) * slots : by * slots], self.members - by
            ).astype(f32)
        return total

    def orders(self):
        dp, z = lax.axis_index("dp"), lax.axis_index("seq")
        bits = self.dp.bit_length() - 1
        ids = []
        for core in range(2):
            orders = [[0, *range(1, bits)], [0, *reversed(range(1, bits))]]
            flips = []
            for p in range(self.dp):
                order = orders[core if p >= self.dp // 2 else 1 - core]
                flips.append(
                    sum(
                        (0 if p >> (bits - 1 - i) & 1 else 1) << bit
                        for i, bit in enumerate(order)
                    )
                )
            ids.append(dp ^ jnp.array(flips, jnp.int32))
        ids = jnp.where(dp % 2 == 0, ids[0], ids[1])
        bits = self.seq.bit_length() - 1
        flips = [
            sum((0 if p >> (bits - 1 - i) & 1 else 1) << i for i in range(bits))
            for p in range(self.seq)
        ]
        blocks = z ^ jnp.array(flips, jnp.int32)
        return ids, jnp.argsort(blocks).astype(jnp.int32), blocks

    def partner(self, stage):
        bits = self.dp.bit_length() - 1
        if stage == 0:
            return lambda d, z: (d ^ 1, z)
        if stage < bits:
            return lambda d, z: (d ^ (1 << stage if d % 2 == 0 else 1 << (bits - stage)), z)
        return lambda d, z: (d, z ^ (1 << (stage - bits)))

    def halve(self, held, stage):
        sent, kept = held
        arrived = self.send(sent, self.partner(stage))
        middle = kept.shape[0] // 2
        if middle == 0:
            return None, kept[0] + arrived[0]
        return kept[:middle] + arrived[:middle], kept[middle:] + arrived[middle:]

    def reduce_all(self, flat):
        core = lax.axis_index("dp") % 2
        count = flat.shape[0]
        split = jnp.pad(flat, (0, -count % 2048)).reshape(2, -1, 128)
        held = lax.dynamic_index_in_dim(split, core, 0, False)
        sent = lax.dynamic_index_in_dim(split, 1 - core, 0, False)
        held = held + self.send(sent, lambda d, z: (d ^ 1, z))
        for bit in range(1, self.dp.bit_length() - 1):
            held = held + self.send(held, lambda d, z: (d ^ (1 << bit), z))
        for bit in range(self.seq.bit_length() - 1):
            held = held + self.send(held, lambda d, z: (d, z ^ (1 << bit)))
        other = self.send(held, lambda d, z: (d ^ 1, z))
        return jnp.where(
            core == 0, jnp.stack([held, other]), jnp.stack([other, held])
        ).reshape(-1)[:count]


def mm(a, b):
    return jnp.dot(a, b, preferred_element_type=f32)


def mm_nt(a, b):
    return lax.dot_general(a, b, (((1,), (1,)), ((), ())), preferred_element_type=f32)


def mm_tn(a, b):
    return lax.dot_general(a, b, (((0,), (0,)), ((), ())), preferred_element_type=f32)


def layer(
    layout,
    inputs,
    cotangent,
    full_attention,
    mix_gain,
    smooth_alpha,
    smooth_damp,
    smooth_beta,
    smooth_eta,
    smooth_omega,
    value_proj,
    mix_proj,
    score_affine,
    relative_bias,
    out_proj,
    feed_gain,
    feed_in,
    feed_out,
):
    slots, chunk_rows, width = inputs.shape
    key_width = score_affine.shape[1]
    value_width = value_proj.shape[1]
    tokens = slots * chunk_rows
    total = layout.seq
    seq_length = relative_bias.shape[0] // 2
    block = min(64, chunk_rows)
    core = lax.axis_index("dp") % 2
    z = lax.axis_index("seq")

    sequence = z // layout.chips
    member = layout.member(core, z)
    swap = sequence % 2
    chunks = []
    for by in range(layout.members):
        source = (member - by) % layout.members
        low, high = source, total - 1 - source
        chunks += [jnp.where(swap == 0, low, high), jnp.where(swap == 0, high, low)]
    chunks = jnp.stack(chunks).astype(jnp.int32)
    slot_of = jnp.sum(
        jnp.where(chunks[None, :] == jnp.arange(total)[:, None], jnp.arange(total)[None, :], 0),
        axis=1,
    ).astype(jnp.int32)
    flags = full_attention.astype(f32)
    flags_other = layout.send(flags, lambda d, z: (d ^ 1, z))
    flags = jnp.where(
        core == 0, jnp.concatenate([flags, flags_other]), jnp.concatenate([flags_other, flags])
    )
    full = lax.dynamic_index_in_dim(flags, sequence, 0, False) == 1.0
    table = jnp.concatenate([chunks, slot_of, full.astype(jnp.int32)[None]])
    ids, places, blocks = layout.orders()

    x = jnp.stack(layout.spread(inputs))
    cot = jnp.concatenate(layout.spread(cotangent))
    bias_back, bias_front = bias_tiles(relative_bias, chunk_rows // TILE - 1, full)

    states = smooth_alpha.shape[0]
    lanes = (states, width // 128, 128)
    decay = 1.0 - smooth_alpha * smooth_damp
    rate = smooth_alpha * smooth_beta
    span = (decay**chunk_rows).reshape(lanes)
    coef = (smooth_eta * rate).reshape(lanes)
    decay_slab = decay.reshape(lanes)
    gain_row = mix_gain[None]
    omega_row = smooth_omega[None]
    mix_shared, mix_main = mix_proj[:, :key_width], mix_proj[:, key_width:]

    normed_low, ends = front_ends(
        x, gain_row, decay_slab, after=(bias_back, bias_front, mix_main, mix_shared, span, coef)
    )
    ends_all = jnp.concatenate([ends, layout.gather(ends)])
    normed_low = normed_low.reshape(tokens, width)
    value_pre = mm(normed_low, value_proj)
    value_low = jax.nn.silu(value_pre).astype(bf16).reshape(slots, chunk_rows, value_width)
    value_slope = silu_slope(value_pre).astype(bf16)
    value_others = layout.gather(value_low)
    smoothed, mixed, check = front_scan(
        table, x, gain_row, decay_slab, coef, span, omega_row, ends_all, block
    )
    smoothed = smoothed.reshape(tokens, width)
    mixed = mixed.reshape(tokens, width)

    shared_pre = mm(mixed, mix_shared)
    shared = jax.nn.silu(shared_pre)
    query_low = (shared * score_affine[0] + score_affine[1]).astype(bf16)
    key_low = (shared * score_affine[2] + score_affine[3]).astype(bf16)
    query_low = query_low.reshape(slots, chunk_rows, key_width)
    key_low = key_low.reshape(slots, chunk_rows, key_width)
    key_others = layout.gather(key_low)
    base = mm(mixed, mix_main).astype(bf16)
    attended, gated, lse = attend(
        table,
        query_low,
        bias_front,
        base.reshape(slots, chunk_rows, -1),
        key_low,
        key_others,
        value_low,
        value_others,
    )
    attended = attended.reshape(tokens, value_width)
    gated = gated.reshape(tokens, value_width)

    flat_low = x.reshape(tokens, width)
    flat = flat_low.astype(f32)
    update_pre = base[:, value_width : value_width + width].astype(f32)
    cand_in = base[:, value_width + width :].astype(f32) + mm(gated, out_proj)
    first_sum = flat + jax.nn.sigmoid(update_pre) * (jax.nn.silu(cand_in) - flat)
    unit_two, _ = unit_rows_of(first_sum)
    feed_low = (unit_two * feed_gain).astype(bf16)

    result, grad_feed, out_send, out_keep, in_send, in_keep = feed(
        ids, places, feed_low, cot, first_sum, feed_in, feed_out, layout.seq
    )
    result = result.reshape(slots, chunk_rows, width)
    block_out = layout.collect([result[0], result[1]])
    feed_out_sum = layout.halve((out_send, out_keep), 0)
    feed_in_sum = layout.halve((in_send, in_keep), 0)

    grad_input, grad_main, grad_att, feed_gain_grad = gate(
        grad_feed, cot, flat_low, cand_in, base, attended, feed_gain[None], out_proj
    )
    proj_sum = layout.halve(
        by_columns(
            ids,
            grad_main,
            gated,
            rows=width,
            at=grad_main.shape[1] // width - 1,
            after=(*feed_out_sum, *feed_in_sum),
        ),
        0,
    )
    mix_sum = layout.halve(by_rows(ids, None, mixed, grad_main), 0)
    feed_out_sum = layout.halve(feed_out_sum, 1)
    grad_query, gk_own, gk_oth, gv_own, gv_oth, rel_sums = attend_back(
        table,
        query_low,
        grad_att.reshape(slots, chunk_rows, value_width),
        lse.reshape(slots, 1, chunk_rows),
        bias_back,
        key_low,
        key_others,
        value_low,
        value_others,
        after=(*proj_sum, *feed_out_sum),
    )
    feed_in_sum = layout.halve(feed_in_sum, 1)
    grad_key = layout.scatter_sum(gk_own, gk_oth).reshape(tokens, key_width)
    grad_query = grad_query.reshape(tokens, key_width)
    grad_shared = (
        (grad_query * score_affine[0] + grad_key * score_affine[2]) * silu_slope(shared_pre)
    ).astype(bf16)
    grad_smooth = (mm_nt(grad_main, mix_main) + mm_nt(grad_shared, mix_shared)) * silu_slope(
        smoothed
    )
    grad_smooth = grad_smooth.reshape(slots, chunk_rows, width)
    back = back_ends(grad_smooth, decay_slab, after=(*feed_in_sum, *mix_sum))
    back_all = jnp.concatenate([back, layout.gather(back)])
    grad_value = layout.scatter_sum(gv_own, gv_oth).reshape(tokens, value_width)
    grad_value_pre = (grad_value * value_slope.astype(f32)).astype(bf16)
    value_sum = layout.halve(
        by_rows(ids, places, normed_low, grad_value_pre, layout.seq), 0
    )
    shared_sum = layout.halve(
        by_rows(ids, None, mixed, grad_shared), 0
    )
    grad_normed = mm_nt(grad_value_pre, value_proj)

    feed_out_sum = layout.halve(feed_out_sum, 2)
    proj_sum = layout.halve(proj_sum, 1)
    mix_sum = layout.halve(mix_sum, 1)
    grad_in, qx, qs, mix_gain_grad, omega_grad = back_scan(
        table,
        x,
        grad_smooth,
        grad_normed.reshape(slots, chunk_rows, width),
        grad_input.reshape(slots, chunk_rows, width),
        check,
        gain_row,
        decay_slab,
        coef,
        span,
        omega_row,
        back_all,
        after=(*value_sum, *shared_sum, *[v for v in feed_out_sum if v is not None], *proj_sum),
    )
    grad_in = layout.collect([grad_in[0], grad_in[1]]).astype(f32)

    affine_grad = jnp.stack(
        [
            jnp.sum(grad_query * shared_pre * jax.nn.sigmoid(shared_pre), axis=0),
            jnp.sum(grad_query, axis=0),
            jnp.sum(grad_key * shared_pre * jax.nn.sigmoid(shared_pre), axis=0),
            jnp.sum(grad_key, axis=0),
        ]
    )
    relative_grad = bias_grad(rel_sums[:, 0], seq_length)
    small = [
        qx.reshape(-1),
        qs.reshape(-1),
        mix_gain_grad.reshape(-1),
        omega_grad.reshape(-1),
        feed_gain_grad.reshape(-1),
        affine_grad.reshape(-1),
        relative_grad,
    ]
    sums = layout.reduce_all(jnp.concatenate(small))
    parts, start = [], 0
    for item in small:
        parts.append(lax.slice_in_dim(sums, start, start + item.shape[0]))
        start += item.shape[0]
    input_sum = parts[0].reshape(states, width)
    decay_sum = parts[1].reshape(states, width)
    input_total = smooth_eta * input_sum
    decay_total = smooth_eta * rate * decay_sum
    eta_grad = rate * input_sum
    alpha_grad = smooth_beta * input_total - smooth_damp * decay_total
    damp_grad = -smooth_alpha * decay_total
    beta_grad = smooth_alpha * input_total

    stages = layout.dp.bit_length() - 1

    def rest(held, stage):
        while stage < stages:
            held = layout.halve(held, stage)
            stage += 1
        return held[1]

    def over_seq(held):
        middle = layout.seq // 2
        held = (held[:middle], held[middle:])
        for stage in range(stages, stages + layout.seq.bit_length() - 1):
            held = layout.halve(held, stage)
        return held[1].astype(f32)

    feed_out_grad = over_seq(
        rest(feed_out_sum, 3).reshape(layout.seq, width // layout.seq, -1)[blocks]
    ).T
    feed_in_grad = over_seq(rest(feed_in_sum, 2))
    out_grad = over_seq(rest(proj_sum, 2).reshape(layout.seq, width // layout.seq, -1)[blocks]).T
    value_grad = over_seq(rest(value_sum, 1))
    mix_rows = jnp.concatenate([rest(shared_sum, 1)[0], rest(mix_sum, 2)[0]], axis=1)
    mix_rows = mix_rows.reshape(mix_rows.shape[0], layout.seq, -1).transpose(1, 0, 2)
    mix_grad = over_seq(mix_rows[blocks])
    return (
        block_out,
        grad_in,
        parts[2],
        alpha_grad,
        damp_grad,
        beta_grad,
        eta_grad,
        parts[3],
        value_grad,
        mix_grad,
        parts[5].reshape(4, key_width),
        parts[6],
        out_grad,
        parts[4],
        feed_in_grad,
        feed_out_grad,
    )


def solution(mesh):
    tokens = P("dp", "seq", None)
    split = P("dp", "seq")
    return jax.shard_map(
        functools.partial(layer, Layout(mesh)),
        mesh=mesh,
        in_specs=(tokens, tokens, P("dp")) + (P(),) * 14,
        out_specs=(tokens, tokens)
        + (P(),) * 6
        + (split, split, P(), P(), split, P(), split, split),
        check_vma=False,
    )
```

time: 2050 us -> 728 us (0.36)
  other arithmetic: 590 us -> 87 us
  waiting for transfers between devices: 608 us -> 163 us
  local copies, waits for them, and re-layouts: 447 us -> 44.9 us
  Pallas kernels: 0 us -> 253 us
  matrix products: 282 us -> 70.6 us
  starting transfers between devices: 1.18 us -> 96 us
  blocking collectives: 85.4 us -> 0 us
    all_gather x2 -> x0, waiting for transfers between devices: 311 us -> none  [the longest x1 288 us: local(): lax.all_gather(value_seq, 'seq', axis=1, tiled=True)]
    pallas_call x0 -> x13, Pallas kernels: none -> 253 us  [the longest x1 68.8 us: feed(): pl.pallas_call(ignoring(feed_body, 7, len(after)), grid_spec=pltpu.Prefet...]
    dynamic_update_slice x32 -> x0, other arithmetic: 222 us -> none  [block_states(): block_ends, local_state = lax.scan(advance, zero_state, steps)]
    dot_general x29 -> x7, matrix products: 282 us -> 70.6 us  [the longest x4 42.5 us: mm(): return jnp.dot(a, b, preferred_element_type=f32)]
    reduce_scatter x11 -> x0, waiting for transfers between devices: 177 us -> none  [the longest x1 65.3 us: local(): lax.psum_scatter(feed_out_grad.astype(jnp.bfloat16), 'dp', scatter_dimens...]
    ppermute x0 -> x49, waiting for transfers between devices: none -> 163 us  [the longest x45 163 us: send(): return lax.ppermute(value, AXES, self.pairs(move))]
    reduce_sum x14 -> x5, other arithmetic: 139 us -> 4 us  [the longest x1 2.08 us: layer(): jnp.sum(grad_query * shared_pre * jax.nn.sigmoid(shared_pre), axis=0)]
    add x141 -> x30, other arithmetic: 184 us -> 51.4 us  [the longest x17 33.5 us: halve(): return (kept[:middle] + arrived[:middle], kept[middle:] + arrived[middle:])]
  transfers between devices with their start and end apart: 15 -> 49, of which waited for: 11 -> 16; matrix products, arithmetic and copies ran while one was open for 27% -> 23% of each run, Pallas kernels for 0% -> 22%
where the time goes in v1:
time: 728 us; the launch traced here: 717 us
  Pallas kernels  253 us (35%)
  waiting for transfers between devices  163 us (22%)
  starting transfers between devices  96 us (13%)
  other arithmetic  87 us (12%)
  matrix products  70.6 us (10%)
  local copies, waits for them, and re-layouts  44.9 us (6%)
    ppermute x45, waiting for transfers between devices, send(): return lax.ppermute(value, AXES, self.pairs(move))  163 us
    ppermute x45, starting transfers between devices, send(): return lax.ppermute(value, AXES, self.pairs(move))  91.9 us
    pallas_call x1, Pallas kernels, feed(): pl.pallas_call(ignoring(feed_body, 7, len(after)), grid_spec=pltpu.Prefet...  68.8 us
    dot_general x4, matrix products, mm(): return jnp.dot(a, b, preferred_element_type=f32)  42.5 us
    pallas_call x1, Pallas kernels, back_scan(): pl.pallas_call(ignoring(back_scan_body, 12, len(after)), grid_spec=pltpu....  38.5 us
    add x17, other arithmetic, halve(): return (kept[:middle] + arrived[:middle], kept[middle:] + arrived[middle:])  33.5 us
    pallas_call x3, Pallas kernels, by_rows(): pl.pallas_call(ignoring(by_rows_body, 4, len(after)), grid_spec=pltpu.Pre...  29.9 us
    dot_general x3, matrix products, mm_nt(): lax.dot_general(a, b, (((1,), (1,)), ((), ())), preferred_element_type=f32)  28.1 us
  transfers between devices with their start and end apart: 49, of which 16 were waited for; matrix products, arithmetic and copies ran while one was open for 23% of the time, Pallas kernels for 22%

profile of v1, /device:TPU:0, one launch (start us, length us, event | category | flops | bytes accessed | tf_op | source)
XLA Modules:
  0.0 716.6 jit_solution(15960187251875750031)
XLA Ops:
  8.1 7.9 %slice.391.refs_5_ = bf16[1024,4096]{1,0:T(8,128)(2,1)} slice(bf16[1024,4224]{1,0:T(8,128)(2,1)} %param.30), slice={[0:1024], [128:4224]} | slice | bytes 16777216 | tf_op jit(solution)/shard_map/slice | solution.py:1426
  23.3 6.1 bias.1
  29.4 23.7 %collective-permute-done.1 = bf16[512,1024]{1,0:T(8,128)(2,1)} collective-permute-done((bf16[512,1024]{1,0:T(8,128)(2,1)S(1)}, bf16[512,1024]{1,0:T(8,128)(2,1)}, u32[]{:S(2)}, u32[]{:S(2)}) %collective-permute-start.1) | collective-permute-done | bytes 1048608 | tf_op jit(solution)/shard_map/ppermute | solution.py:1236
  53.1 2.8 pad_maximum_fusion.refs_0_.x_ref.refs_1_
  55.8 8.6 %front_ends.1 = (bf16[2,512,1024]{2,1,0:T(8,128)(2,1)}, f32[2,16,8,128]{3,2,1,0:T(8,128)}) custom-call(bf16[2,512,1024]{2,1,0:T(8,128)(2,1)} %pad_maximum_fusion.refs_0_.x_ref.refs_1_, f32[1,1024]{1,0:T(1,128)} %bitcast.254, f32[16,8,128]{2,1,0:T(8,128)} %bitcast.228, f32[9,256,256]{2,1,0:T(8,128)} %get-tuple-element.57.refs_3_.refs_4_, ...), custom_call_target="tpu_custom_call" | custom-call | flops 67108864 | bytes 4194304 | tf_op jit(solution)/shard_map/front_ends/pallas_call | solution.py:97
  64.5 12.6 %multiply_convert_fusion.1 = (bf16[1024,2048]{1,0:T(8,128)(2,1)}, f32[1024,2048]{1,0:T(8,128)}) fusion(bf16[1024,1024]{1,0:T(8,128)(2,1)} %bitcast.277, bf16[1024,2048]{1,0:T(8,128)(2,1)} %param.29), kind=kOutput, calls=%fused_computation.7 | convolution fusion | flops 4305453056 | bytes 18874368 | tf_op jit(solution)/shard_map/dot_general | solution.py:1350
  81.9 10.5 %collective-permute-done.6 = bf16[512,1024]{1,0:T(8,128)(2,1)} collective-permute-done((bf16[512,1024]{1,0:T(8,128)(2,1)S(1)}, bf16[512,1024]{1,0:T(8,128)(2,1)}, u32[]{:S(2)}, u32[]{:S(2)}) %collective-permute-start.6) | collective-permute-done | bytes 1048608 | tf_op jit(solution)/shard_map/ppermute | solution.py:1236
  94.7 29.8 %collective-permute-done.7 = bf16[512,1024]{1,0:T(8,128)(2,1)S(1)} collective-permute-done((bf16[512,1024]{1,0:T(8,128)(2,1)S(1)}, bf16[512,1024]{1,0:T(8,128)(2,1)S(1)}, u32[]{:S(2)}, u32[]{:S(2)}) %collective-permute-start.7) | collective-permute-done | bytes 1048608 | tf_op jit(solution)/shard_map/ppermute | solution.py:1236
  126.3 18.6 %front_scan.1 = (f32[2,512,1024]{2,1,0:T(8,128)}, bf16[2,512,1024]{2,1,0:T(8,128)(2,1)}, f32[2,8,16,8,128]{4,3,2,1,0:T(8,128)}) custom-call(s32[9]{0:T(128)} %concatenate.42.table_ref.refs_0_, bf16[2,512,1024]{2,1,0:T(8,128)(2,1)} %pad_maximum_fusion.refs_0_.x_ref.refs_1_, f32[1,1024]{1,0:T(1,128)} %bitcast.255, f32[16,8,128]{2,1,0:T(8,128)} %bitcast.229, ...), custom_call_target="tpu_custom_call" | custom-call | flops 134217728 | bytes 8388608 | tf_op jit(solution)/shard_map/front_scan/pallas_call | solution.py:188
  144.9 3.3 add_convert_fusion
  148.3 14.3 %convolution_convert_fusion.refs_4_.refs_5_ = bf16[1024,4096]{1,0:T(8,128)(2,1)} fusion(bf16[1024,1024]{1,0:T(8,128)(2,1)S(1)} %bitcast.227, bf16[1024,4224]{1,0:T(8,128)(2,1)} %param.30), kind=kOutput, calls=%fused_computation.9 | convolution fusion | flops 8594128896 | bytes 18874368 | tf_op jit(solution)/shard_map/dot_general | solution.py:1350
  163.3 16.4 %attend.1 = (bf16[2,512,2048]{2,1,0:T(8,128)(2,1)}, bf16[2,512,2048]{2,1,0:T(8,128)(2,1)}, f32[2,512,1]{2,1,0:T(8,128)}) custom-call(s32[9]{0:T(128)} %concatenate.42.table_ref.refs_0_, bf16[2,512,128]{2,1,0:T(8,128)(2,1)} %bitcast.249, f32[9,256,256]{2,1,0:T(8,128)} %get-tuple-element.58.refs_4_.bias_ref, bf16[2,512,4096]{2,1,0:T(8,128)(2,1)} %bitcast.211, ...), custom_call_target="tpu_custom_call" | custom-call | flops 4563402752 | bytes 41943040 | tf_op jit(solution)/shard_map/attend/pallas_call | solution.py:552
  179.7 12.3 %fusion.46 = (f32[1024]{0:T(1024)S(1)}, f32[1024,1024]{1,0:T(8,128)S(1)}, f32[1024,1024]{1,0:T(8,128)}) fusion(bf16[1024,4096]{1,0:T(8,128)(2,1)} %convolution_convert_fusion.refs_4_.refs_5_, bf16[2,512,1024]{2,1,0:T(8,128)(2,1)S(1)} %copy-done, bf16[1024,2048]{1,0:T(8,128)(2,1)} %bitcast.220, bf16[2048,1024]{1,0:T(8,128)(2,1)} %refs_8_.1), kind=kOutput, calls=%fused_computation.168 | convolution fusion | flops 4310694912 | bytes 23072768 | tf_op jit(solution)/shard_map/dot_general | solution.py:1350
  194.6 68.8 %feed.1 = (bf16[1024,1024]{1,0:T(8,128)(2,1)}, f32[1024,1024]{1,0:T(8,128)}, bf16[4,1024,512]{2,1,0:T(8,128)(2,1)}, bf16[4,1024,512]{2,1,0:T(8,128)(2,1)}, bf16[...) custom-call(s32[8]{0:T(128)} %broadcast_select_fusion.1.refs_0_, s32[4]{0:T(128)} %get-tuple-element.56.refs_1_, ...), custom_call_target="tpu_custom_call" | custom-call | flops 51539607552 | bytes 50331648 | tf_op jit(solution)/shard_map/feed/pallas_call | solution.py:1053
  264.0 23.9 %gate.1 = (f32[1024,1024]{1,0:T(8,128)}, bf16[1024,4096]{1,0:T(8,128)(2,1)}, bf16[1024,2048]{1,0:T(8,128)(2,1)}, f32[1,1024]{1,0:T(1,128)}) custom-call(f32[1024,1024]{1,0:T(8,128)} %get-tuple-element.64.refs_0_, bf16[1024,1024]{1,0:T(8,128)(2,1)} %constant_dynamic-update-slice_fusion.refs_3_.refs_1_, bf16[1024,1024]{1,0:T(8,128)(2,1)} %bitcast.212, ...), custom_call_target="tpu_custom_call" | custom-call | flops 4294967296 | bytes 41943040 | tf_op jit(solution)/shard_map/gate/pallas_call | solution.py:909
  287.8 15.3 %by_rows.3 = (bf16[4,1,128,4096]{3,2,1,0:T(8,128)(2,1)}, bf16[4,1,128,4096]{3,2,1,0:T(8,128)(2,1)}) custom-call(s32[8]{0:T(128)} %broadcast_select_fusion.1.refs_0_, s32[1]{0:T(128)} %constant.124.clone.1.refs_1_, bf16[1024,1024]{1,0:T(8,128)(2,1)} %bitcast.225, bf16[1024,4096]{1,0:T(8,128)(2,1)} %get-tuple-element.66.refs_1_.refs_3_), custom_call_target="tpu_custom_call" | custom-call | flops 8589934592 | bytes 16777216 | tf_op jit(solution)/shard_map/by_rows/pallas_call | solution.py:1191
  306.8 4.1 slice_add_fusion.4
  310.9 7.8 %collective-permute-start.13 = (bf16[2,1024,512]{2,1,0:T(8,128)(2,1)}, bf16[2,1024,512]{2,1,0:T(8,128)(2,1)}, u32[]{:S(2)}, u32[]{:S(2)}) collective-permute-start(bf16[2,1024,512]{2,1,0:T(8,128)(2,1)} %get-tuple-element.145.refs_3_), channel_id=1, source_target_pairs={{0,8},{1,9},{2,10},{3,11},{4,20},{5,21},{6,22},{7,23},{8,0},{9,1},... | collective-permute-start | bytes 6291464 | tf_op jit(solution)/shard_map/ppermute | solution.py:1236
  318.6 3.8 slice_add_fusion.2
  322.7 11.8 %by_columns.1 = (bf16[4,1024,256]{2,1,0:T(8,128)(2,1)}, bf16[4,1024,256]{2,1,0:T(8,128)(2,1)}) custom-call(s32[8]{0:T(128)} %broadcast_select_fusion.1.refs_0_, bf16[1024,4096]{1,0:T(8,128)(2,1)} %get-tuple-element.66.refs_1_.refs_3_, bf16[1024,2048]{1,0:T(8,128)(2,1)} %bitcast.221, bf16[2,1024,512]{2,1,0:T(8,128)(2,1)} %get-tuple-element.145.refs_3_, ...), custom_call_target="tpu_custom_call" | custom-call | flops 4294967296 | bytes 8388608 | tf_op jit(solution)/shard_map/by_columns/pallas_call | solution.py:1134
  334.5 5.2 slice_add_fusion
  347.3 3.1 collective-permute-start.21
  350.4 17.7 %collective-permute-done.16 = bf16[2,4,128,1024]{3,2,1,0:T(8,128)(2,1)} collective-permute-done((bf16[2,4,128,1024]{3,2,1,0:T(8,128)(2,1)}, bf16[2,4,128,1024]{3,2,1,0:T(8,128)(2,1)}, u32[]{:S(2)}, u32[]{:S(2)}) %collective-permute-start.16) | collective-permute-done | bytes 2097184 | tf_op jit(solution)/shard_map/ppermute | solution.py:1236
  370.4 3.1 slice_add_fusion.14
  375.8 34.5 %collective-permute-done.37 = bf16[2,1,128,4096]{3,2,1,0:T(8,128)(2,1)} collective-permute-done((bf16[2,1,128,4096]{3,2,1,0:T(8,128)(2,1)}, bf16[2,1,128,4096]{3,2,1,0:T(8,128)(2,1)}, u32[]{:S(2)}, u32[]{:S(2)}) %collective-permute-start.37) | collective-permute-done | bytes 2097184 | tf_op jit(solution)/shard_map/ppermute | solution.py:1236
  424.4 4.3 collective-permute-done.22
  430.7 22.3 %attend_back.1 = (f32[2,512,128]{2,1,0:T(8,128)}, bf16[2,512,128]{2,1,0:T(8,128)(2,1)}, bf16[2,512,128]{2,1,0:T(8,128)(2,1)}, bf16[2,512,2048]{2,1,0:T(8,128)(2,...) custom-call(s32[9]{0:T(128)} %concatenate.42.table_ref.refs_0_, bf16[2,512,128]{2,1,0:T(8,128)(2,1)} %bitcast.250, ...), custom_call_target="tpu_custom_call" | custom-call | flops 9126805504 | bytes 41943040 | tf_op jit(solution)/shard_map/attend_back/pallas_call | solution.py:728
  459.1 4.4 by_rows.5
  465.6 14.5 %collective-permute-start.35 = (bf16[2,1,128,128]{3,2,1,0:T(8,128)(2,1)S(1)}, bf16[2,1,128,128]{3,2,1,0:T(8,128)(2,1)S(1)}, u32[]{:S(2)}, u32[]{:S(2)}) collective-permute-start(bf16[2,1,128,128]{3,2,1,0:T(8,128)(2,1)S(1)} %get-tuple-element.168.refs_14_), channel_id=1, source_target_pairs={{0,8},{1,9},{2,10},{3,11},{4,20},{5,21},{6,22},{7,23},{8,0},{9,1},... | collective-permute-start | bytes 196616 | tf_op jit(solution)/shard_map/ppermute | solution.py:1236
  480.1 16.1 %fusion.7 = f32[1024,1024]{1,0:T(8,128)} fusion(f32[2,512,1024]{2,1,0:T(8,128)S(1)} %copy-done.51, f32[1024,1024]{1,0:T(8,128)S(1)} %fusion.37, bf16[1024,4096]{1,0:T(8,128)(2,1)} %get-tuple-element.66.refs_1_.refs_3_, bf16[1024,4224]{1,0:T(8,128)(2,1)} %param.30), kind=kOutput, calls=%fused_computation.20 | convolution fusion | flops 8599371776 | bytes 29360128 | tf_op jit(solution)/shard_map/dot_general | solution.py:1354
  496.2 8.0 %back_ends.1 = f32[2,16,8,128]{3,2,1,0:T(8,128)} custom-call(f32[2,512,1024]{2,1,0:T(8,128)} %bitcast.213, f32[16,8,128]{2,1,0:T(8,128)} %bitcast.230, bf16[1,4,128,1024]{3,2,1,0:T(8,128)(2,1)} %slice_add_fusion.11.refs_2_, bf16[1,4,128,1024]{3,2,1,0:T(8,128)(2,1)} %get-tuple-element.131.refs_3_, bf16[2,1,128,4096]{3,2,1,0:T(8,128)(2,1)} %get-tuple-element.141.refs_4_, ...), custom_call_target="tpu_custom_call" | custom-call | flops 67108864 | bytes 4194304 | tf_op jit(solution)/shard_map/back_ends/pallas_call | solution.py:255
  512.3 5.4 collective-permute-start.39
  517.7 5.4 convert_add_fusion
  523.1 6.8 fusion.refs_3_
  529.8 10.1 %by_rows.4 = (bf16[4,4,128,512]{3,2,1,0:T(8,128)(2,1)}, bf16[4,4,128,512]{3,2,1,0:T(8,128)(2,1)}) custom-call(s32[8]{0:T(128)} %broadcast_select_fusion.1.refs_0_, s32[4]{0:T(128)} %get-tuple-element.56.refs_1_, bf16[1024,1024]{1,0:T(8,128)(2,1)} %bitcast.278, bf16[1024,2048]{1,0:T(8,128)(2,1)} %fusion.refs_3_), custom_call_target="tpu_custom_call" | custom-call | flops 4294967296 | bytes 8388608 | tf_op jit(solution)/shard_map/by_rows/pallas_call | solution.py:1191
  548.1 3.0 collective-permute-start.46
  551.1 4.7 collective-permute-done.42
  556.9 14.3 %collective-permute-done.48 = bf16[1,256,512]{2,1,0:T(8,128)(2,1)S(1)} collective-permute-done((bf16[1,256,512]{2,1,0:T(8,128)(2,1)S(1)}, bf16[1,256,512]{2,1,0:T(8,128)(2,1)S(1)}, u32[]{:S(2)}, u32[]{:S(2)}) %collective-permute-start.48) | collective-permute-done | bytes 262176 | tf_op jit(solution)/shard_map/ppermute | solution.py:1236
  573.1 10.1 %fusion.52 = f32[1024,1024]{1,0:T(8,128)} fusion(bf16[1024,2048]{1,0:T(8,128)(2,1)} %fusion.refs_3_, bf16[1024,2048]{1,0:T(8,128)(2,1)} %param.29), kind=kOutput, calls=%fused_computation.174 | convolution fusion | flops 4294967296 | bytes 12582912 | tf_op jit(solution)/shard_map/dot_general | solution.py:1354
  583.2 3.3 slice_add_fusion.8
  586.6 38.5 %back_scan.1 = (bf16[2,512,1024]{2,1,0:T(8,128)(2,1)}, f32[16,8,128]{2,1,0:T(8,128)}, f32[16,8,128]{2,1,0:T(8,128)}, f32[1,1024]{1,0:T(1,128)}, f32[1,1024]{1,0:T(1,128)}) custom-call(s32[9]{0:T(128)} %concatenate.42.table_ref.refs_0_, bf16[2,512,1024]{2,1,0:T(8,128)(2,1)} %pad_maximum_fusion.refs_0_.x_ref.refs_1_, f32[2,512,1024]{2,1,0:T(8,128)} %bitcast.214, ...), custom_call_target="tpu_custom_call" | custom-call | flops 335544320 | bytes 16777216 | tf_op jit(solution)/shard_map/back_scan/pallas_call | solution.py:399
  648.1 3.0 collective-permute-start.29
  651.1 3.0 slice_bitcast_fusion.1
  656.1 5.8 collective-permute-start.30
  667.1 5.2 collective-permute-done.32
  673.7 17.1 %collective-permute-start.33 = (bf16[2,128,512]{2,1,0:T(8,128)(2,1)S(1)}, bf16[2,128,512]{2,1,0:T(8,128)(2,1)S(1)}, u32[]{:S(2)}, u32[]{:S(2)}) collective-permute-start(bf16[2,128,512]{2,1,0:T(8,128)(2,1)S(1)} %slice_bitcast_fusion.5), channel_id=1, source_target_pairs={{0,1},{1,0},{2,3},{3,2},{4,5},{5,4},{6,7},{7,6},{8,9},{9,8},{10,11... | collective-permute-start | bytes 786440 | tf_op jit(solution)/shard_map/ppermute | solution.py:1236
  692.2 9.9 %collective-permute-done.33 = bf16[2,128,512]{2,1,0:T(8,128)(2,1)S(1)} collective-permute-done((bf16[2,128,512]{2,1,0:T(8,128)(2,1)S(1)}, bf16[2,128,512]{2,1,0:T(8,128)(2,1)S(1)}, u32[]{:S(2)}, u32[]{:S(2)}) %collective-permute-start.33) | collective-permute-done | bytes 262176 | tf_op jit(solution)/shard_map/ppermute | solution.py:1236
  702.1 9.4 %collective-permute-start.34 = (bf16[1,128,512]{2,1,0:T(8,128)(2,1)S(1)}, bf16[1,128,512]{2,1,0:T(8,128)(2,1)S(1)}, u32[]{:S(2)}, u32[]{:S(2)}) collective-permute-start(bf16[1,128,512]{2,1,0:T(8,128)(2,1)S(1)} %slice_add_fusion.28), channel_id=1, source_target_pairs={{0,2},{1,3},{2,0},{3,1},{4,6},{5,7},{6,4},{7,5},{8,10},{9,11},{10,... | collective-permute-start | bytes 393224 | tf_op jit(solution)/shard_map/ppermute | solution.py:1236
  (296 shorter events, 123.5 us)
Async XLA Ops:
  2.4 27.0 %collective-permute-start = (bf16[512,1024]{1,0:T(8,128)(2,1)S(1)}, bf16[512,1024]{1,0:T(8,128)(2,1)S(1)}, u32[]{:S(2)}, u32[]{:S(2)}) collective-permute-start(bf16[512,1024]{1,0:T(8,128)(2,1)S(1)} %get-tuple-element.160), channel_id=1, source_target_pairs={{0,4},{1,0},{2,5},{3,1},{4,6},{5,2},{6,7},{7,3},{8,12},{9,8},{10,1... | collective-permute-start | bytes 3145736 | tf_op jit(solution)/shard_map/ppermute | solution.py:1236
  2.9 50.2 %collective-permute-start.1 = (bf16[512,1024]{1,0:T(8,128)(2,1)S(1)}, bf16[512,1024]{1,0:T(8,128)(2,1)}, u32[]{:S(2)}, u32[]{:S(2)}) collective-permute-start(bf16[512,1024]{1,0:T(8,128)(2,1)S(1)} %get-tuple-element.161), channel_id=1, source_target_pairs={{0,1},{1,5},{2,0},{3,4},{4,3},{5,7},{6,2},{7,6},{8,9},{9,13},{10,8... | collective-permute-start | bytes 3145736 | tf_op jit(solution)/shard_map/ppermute | solution.py:1236
  5.6 16.4 %collective-permute-start.2 = (f32[2]{0:T(128)S(1)}, f32[2]{0:T(128)S(1)}, u32[]{:S(2)}, u32[]{:S(2)}) collective-permute-start(f32[2]{0:T(128)S(1)} %convert_element_type.88), channel_id=1, source_target_pairs={{0,4},{1,5},{2,6},{3,7},{4,0},{5,1},{6,2},{7,3},{8,12},{9,13},{10,... | collective-permute-start | bytes 32 | tf_op jit(solution)/shard_map/ppermute | solution.py:1236
  77.1 85.5 %collective-permute-start.5 = (bf16[2,512,2048]{2,1,0:T(8,128)(2,1)}, bf16[2,512,2048]{2,1,0:T(8,128)(2,1)}, u32[]{:S(2)}, u32[]{:S(2)}) collective-permute-start(bf16[2,512,2048]{2,1,0:T(8,128)(2,1)} %bitcast.29.v_own.refs_7_), channel_id=1, source_target_pairs={{0,4},{1,5},{2,6},{3,7},{4,0},{5,1},{6,2},{7,3},{8,12},{9,13},{10,... | collective-permute-start | bytes 12582920 | tf_op jit(solution)/shard_map/ppermute | solution.py:1236
  77.4 15.0 %collective-permute-start.6 = (bf16[512,1024]{1,0:T(8,128)(2,1)S(1)}, bf16[512,1024]{1,0:T(8,128)(2,1)}, u32[]{:S(2)}, u32[]{:S(2)}) collective-permute-start(bf16[512,1024]{1,0:T(8,128)(2,1)S(1)} %get-tuple-element.159), channel_id=1, source_target_pairs={{0,4},{1,0},{2,5},{3,1},{4,6},{5,2},{6,7},{7,3},{8,12},{9,8},{10,1... | collective-permute-start | bytes 3145736 | tf_op jit(solution)/shard_map/ppermute | solution.py:1236
  77.9 46.6 %collective-permute-start.7 = (bf16[512,1024]{1,0:T(8,128)(2,1)S(1)}, bf16[512,1024]{1,0:T(8,128)(2,1)S(1)}, u32[]{:S(2)}, u32[]{:S(2)}) collective-permute-start(bf16[512,1024]{1,0:T(8,128)(2,1)S(1)} %get-tuple-element.158), channel_id=1, source_target_pairs={{0,1},{1,5},{2,0},{3,4},{4,3},{5,7},{6,2},{7,6},{8,9},{9,13},{10,8... | collective-permute-start | bytes 3145736 | tf_op jit(solution)/shard_map/ppermute | solution.py:1236
  81.6 44.0 %collective-permute-start.3 = (f32[2,16,8,128]{3,2,1,0:T(8,128)S(1)}, f32[2,16,8,128]{3,2,1,0:T(8,128)S(1)}, u32[]{:S(2)}, u32[]{:S(2)}) collective-permute-start(f32[2,16,8,128]{3,2,1,0:T(8,128)S(1)} %copy-done.38), channel_id=1, source_target_pairs={{0,4},{1,5},{2,6},{3,7},{4,0},{5,1},{6,2},{7,3},{8,12},{9,13},{10,... | collective-permute-start | bytes 393224 | tf_op jit(solution)/shard_map/ppermute | solution.py:1236
  148.2 14.4 %collective-permute-start.4 = (bf16[2,512,128]{2,1,0:T(8,128)(2,1)S(1)}, bf16[2,512,128]{2,1,0:T(8,128)(2,1)S(1)}, u32[]{:S(2)}, u32[]{:S(2)}) collective-permute-start(bf16[2,512,128]{2,1,0:T(8,128)(2,1)S(1)} %bitcast.246), channel_id=1, source_target_pairs={{0,4},{1,5},{2,6},{3,7},{4,0},{5,1},{6,2},{7,3},{8,12},{9,13},{10,... | collective-permute-start | bytes 786440 | tf_op jit(solution)/shard_map/ppermute | solution.py:1236
  263.5 43.3 %collective-permute-start.10 = (bf16[4,1024,512]{2,1,0:T(8,128)(2,1)}, bf16[4,1024,512]{2,1,0:T(8,128)(2,1)}, u32[]{:S(2)}, u32[]{:S(2)}) collective-permute-start(bf16[4,1024,512]{2,1,0:T(8,128)(2,1)} %get-tuple-element.70), channel_id=1, source_target_pairs={{0,4},{1,5},{2,6},{3,7},{4,0},{5,1},{6,2},{7,3},{8,12},{9,13},{10,... | collective-permute-start | bytes 12582920 | tf_op jit(solution)/shard_map/ppermute | solution.py:1236
  263.9 54.7 %collective-permute-start.11 = (bf16[4,4,128,1024]{3,2,1,0:T(8,128)(2,1)}, bf16[4,4,128,1024]{3,2,1,0:T(8,128)(2,1)}, u32[]{:S(2)}, u32[]{:S(2)}) collective-permute-start(bf16[4,4,128,1024]{3,2,1,0:T(8,128)(2,1)} %get-tuple-element.72), channel_id=1, source_target_pairs={{0,4},{1,5},{2,6},{3,7},{4,0},{5,1},{6,2},{7,3},{8,12},{9,13},{10,... | collective-permute-start | bytes 12582920 | tf_op jit(solution)/shard_map/ppermute | solution.py:1236
  303.2 31.3 %collective-permute-start.17 = (bf16[4,1,128,4096]{3,2,1,0:T(8,128)(2,1)}, bf16[4,1,128,4096]{3,2,1,0:T(8,128)(2,1)}, u32[]{:S(2)}, u32[]{:S(2)}) collective-permute-start(bf16[4,1,128,4096]{3,2,1,0:T(8,128)(2,1)} %get-tuple-element.84), channel_id=1, source_target_pairs={{0,4},{1,5},{2,6},{3,7},{4,0},{5,1},{6,2},{7,3},{8,12},{9,13},{10,... | collective-permute-start | bytes 12582920 | tf_op jit(solution)/shard_map/ppermute | solution.py:1236
  304.7 34.9 %collective-permute-start.8 = (bf16[512,1024]{1,0:T(8,128)(2,1)}, bf16[512,1024]{1,0:T(8,128)(2,1)S(1)}, u32[]{:S(2)}, u32[]{:S(2)}) collective-permute-start(bf16[512,1024]{1,0:T(8,128)(2,1)} %get-tuple-element.156), channel_id=1, source_target_pairs={{1,0},{5,1},{0,2},{4,3},{3,4},{7,5},{2,6},{6,7},{9,8},{13,9},{8,10... | collective-permute-start | bytes 3145736 | tf_op jit(solution)/shard_map/ppermute | solution.py:1267
  304.7 38.6 %collective-permute-start.9 = (bf16[512,1024]{1,0:T(8,128)(2,1)S(1)}, bf16[512,1024]{1,0:T(8,128)(2,1)S(1)}, u32[]{:S(2)}, u32[]{:S(2)}) collective-permute-start(bf16[512,1024]{1,0:T(8,128)(2,1)S(1)} %get-tuple-element.157), channel_id=1, source_target_pairs={{4,0},{0,1},{5,2},{1,3},{6,4},{2,5},{7,6},{3,7},{12,8},{8,9},{13,1... | collective-permute-start | bytes 3145736 | tf_op jit(solution)/shard_map/ppermute | solution.py:1267
  310.9 34.1 %collective-permute-start.13 = (bf16[2,1024,512]{2,1,0:T(8,128)(2,1)}, bf16[2,1024,512]{2,1,0:T(8,128)(2,1)}, u32[]{:S(2)}, u32[]{:S(2)}) collective-permute-start(bf16[2,1024,512]{2,1,0:T(8,128)(2,1)} %get-tuple-element.145.refs_3_), channel_id=1, source_target_pairs={{0,8},{1,9},{2,10},{3,11},{4,20},{5,21},{6,22},{7,23},{8,0},{9,1},... | collective-permute-start | bytes 6291464 | tf_op jit(solution)/shard_map/ppermute | solution.py:1236
  322.4 45.7 %collective-permute-start.16 = (bf16[2,4,128,1024]{3,2,1,0:T(8,128)(2,1)}, bf16[2,4,128,1024]{3,2,1,0:T(8,128)(2,1)}, u32[]{:S(2)}, u32[]{:S(2)}) collective-permute-start(bf16[2,4,128,1024]{3,2,1,0:T(8,128)(2,1)} %get-tuple-element.143.refs_5_), channel_id=1, source_target_pairs={{0,8},{1,9},{2,10},{3,11},{4,20},{5,21},{6,22},{7,23},{8,0},{9,1},... | collective-permute-start | bytes 6291464 | tf_op jit(solution)/shard_map/ppermute | solution.py:1236
  334.5 36.0 %collective-permute-start.12 = (bf16[4,1024,256]{2,1,0:T(8,128)(2,1)}, bf16[4,1024,256]{2,1,0:T(8,128)(2,1)}, u32[]{:S(2)}, u32[]{:S(2)}) collective-permute-start(bf16[4,1024,256]{2,1,0:T(8,128)(2,1)} %get-tuple-element.74), channel_id=1, source_target_pairs={{0,4},{1,5},{2,6},{3,7},{4,0},{5,1},{6,2},{7,3},{8,12},{9,13},{10,... | collective-permute-start | bytes 6291464 | tf_op jit(solution)/shard_map/ppermute | solution.py:1236
  339.7 70.7 %collective-permute-start.37 = (bf16[2,1,128,4096]{3,2,1,0:T(8,128)(2,1)}, bf16[2,1,128,4096]{3,2,1,0:T(8,128)(2,1)}, u32[]{:S(2)}, u32[]{:S(2)}) collective-permute-start(bf16[2,1,128,4096]{3,2,1,0:T(8,128)(2,1)} %get-tuple-element.141.refs_4_), channel_id=1, source_target_pairs={{0,8},{1,9},{2,10},{3,11},{4,20},{5,21},{6,22},{7,23},{8,0},{9,1},... | collective-permute-start | bytes 6291464 | tf_op jit(solution)/shard_map/ppermute | solution.py:1236
  347.3 65.4 %collective-permute-start.21 = (bf16[1,1024,512]{2,1,0:T(8,128)(2,1)S(1)}, bf16[1,1024,512]{2,1,0:T(8,128)(2,1)S(1)}, u32[]{:S(2)}, u32[]{:S(2)}) collective-permute-start(bf16[1,1024,512]{2,1,0:T(8,128)(2,1)S(1)} %slice_add_fusion.13.refs_11_), channel_id=1, source_target_pairs={{0,16},{1,17},{2,18},{3,19},{4,12},{5,13},{6,14},{7,15},{8,24},{9,... | collective-permute-start | bytes 3145736 | tf_op jit(solution)/shard_map/ppermute | solution.py:1236
  370.4 50.4 %collective-permute-start.44 = (bf16[1,4,128,1024]{3,2,1,0:T(8,128)(2,1)}, bf16[1,4,128,1024]{3,2,1,0:T(8,128)(2,1)}, u32[]{:S(2)}, u32[]{:S(2)}) collective-permute-start(bf16[1,4,128,1024]{3,2,1,0:T(8,128)(2,1)} %slice_add_fusion.11.refs_2_), channel_id=1, source_target_pairs={{0,16},{1,17},{2,18},{3,19},{4,12},{5,13},{6,14},{7,15},{8,24},{9,... | collective-permute-start | bytes 3145736 | tf_op jit(solution)/shard_map/ppermute | solution.py:1236
  373.5 55.2 %collective-permute-start.22 = (bf16[2,1024,256]{2,1,0:T(8,128)(2,1)}, bf16[2,1024,256]{2,1,0:T(8,128)(2,1)}, u32[]{:S(2)}, u32[]{:S(2)}) collective-permute-start(bf16[2,1024,256]{2,1,0:T(8,128)(2,1)} %get-tuple-element.149.refs_9_), channel_id=1, source_target_pairs={{0,8},{1,9},{2,10},{3,11},{4,20},{5,21},{6,22},{7,23},{8,0},{9,1},... | collective-permute-start | bytes 3145736 | tf_op jit(solution)/shard_map/ppermute | solution.py:1236
  412.7 40.4 %collective-permute-start.38 = (bf16[1,1,128,4096]{3,2,1,0:T(8,128)(2,1)}, bf16[1,1,128,4096]{3,2,1,0:T(8,128)(2,1)}, u32[]{:S(2)}, u32[]{:S(2)}) collective-permute-start(bf16[1,1,128,4096]{3,2,1,0:T(8,128)(2,1)} %slice_add_fusion.6), channel_id=1, source_target_pairs={{0,16},{1,17},{2,18},{3,19},{4,12},{5,13},{6,14},{7,15},{8,24},{9,... | collective-permute-start | bytes 3145736 | tf_op jit(solution)/shard_map/ppermute | solution.py:1236
  418.7 127.3 %collective-permute-start.47 = (bf16[2,256,512]{2,1,0:T(8,128)(2,1)}, bf16[2,256,512]{2,1,0:T(8,128)(2,1)}, u32[]{:S(2)}, u32[]{:S(2)}) collective-permute-start(bf16[2,256,512]{2,1,0:T(8,128)(2,1)} %slice.570), channel_id=1, source_target_pairs={{0,1},{1,0},{2,3},{3,2},{4,5},{5,4},{6,7},{7,6},{8,9},{9,8},{10,11... | collective-permute-start | bytes 1572872 | tf_op jit(solution)/shard_map/ppermute | solution.py:1236
  424.4 122.7 %collective-permute-start.45 = (bf16[2,128,1024]{2,1,0:T(8,128)(2,1)}, bf16[2,128,1024]{2,1,0:T(8,128)(2,1)}, u32[]{:S(2)}, u32[]{:S(2)}) collective-permute-start(bf16[2,128,1024]{2,1,0:T(8,128)(2,1)} %slice_bitcast_fusion.2), channel_id=1, source_target_pairs={{0,1},{1,0},{2,3},{3,2},{4,5},{5,4},{6,7},{7,6},{8,9},{9,8},{10,11... | collective-permute-start | bytes 1572872 | tf_op jit(solution)/shard_map/ppermute | solution.py:1236
  430.7 109.4 %collective-permute-start.41 = (bf16[1,1024,256]{2,1,0:T(8,128)(2,1)}, bf16[1,1024,256]{2,1,0:T(8,128)(2,1)}, u32[]{:S(2)}, u32[]{:S(2)}) collective-permute-start(bf16[1,1024,256]{2,1,0:T(8,128)(2,1)} %slice_add_fusion.19.refs_17_), channel_id=1, source_target_pairs={{0,16},{1,17},{2,18},{3,19},{4,12},{5,13},{6,14},{7,15},{8,24},{9,... | collective-permute-start | bytes 1572872 | tf_op jit(solution)/shard_map/ppermute | solution.py:1236
  453.0 2.9 collective-permute-start.14
  453.1 64.6 %collective-permute-start.15 = (bf16[2,512,2048]{2,1,0:T(8,128)(2,1)}, bf16[2,512,2048]{2,1,0:T(8,128)(2,1)}, u32[]{:S(2)}, u32[]{:S(2)}) collective-permute-start(bf16[2,512,2048]{2,1,0:T(8,128)(2,1)} %get-tuple-element.80), channel_id=1, source_target_pairs={{0,4},{1,5},{2,6},{3,7},{4,0},{5,1},{6,2},{7,3},{8,12},{9,13},{10,... | collective-permute-start | bytes 12582920 | tf_op jit(solution)/shard_map/ppermute | solution.py:1236
  463.6 2.0 collective-permute-start.20
  465.6 38.5 %collective-permute-start.35 = (bf16[2,1,128,128]{3,2,1,0:T(8,128)(2,1)S(1)}, bf16[2,1,128,128]{3,2,1,0:T(8,128)(2,1)S(1)}, u32[]{:S(2)}, u32[]{:S(2)}) collective-permute-start(bf16[2,1,128,128]{3,2,1,0:T(8,128)(2,1)S(1)} %get-tuple-element.168.refs_14_), channel_id=1, source_target_pairs={{0,8},{1,9},{2,10},{3,11},{4,20},{5,21},{6,22},{7,23},{8,0},{9,1},... | collective-permute-start | bytes 196616 | tf_op jit(solution)/shard_map/ppermute | solution.py:1236
  505.7 3.9 collective-permute-start.36
  512.3 116.1 %collective-permute-start.39 = (bf16[2,128,1056]{1,2,0:T(8,128)(2,1)}, bf16[2,128,1056]{1,2,0:T(8,128)(2,1)}, u32[]{:S(2)}, u32[]{:S(2)}) collective-permute-start(bf16[2,128,1056]{1,2,0:T(8,128)(2,1)} %slice.552), channel_id=1, source_target_pairs={{0,1},{1,0},{2,3},{3,2},{4,5},{5,4},{6,7},{7,6},{8,9},{9,8},{10,11... | collective-permute-start | bytes 1622024 | tf_op jit(solution)/shard_map/ppermute | solution.py:1236
  540.0 43.2 %collective-permute-start.19 = (bf16[4,4,128,512]{3,2,1,0:T(8,128)(2,1)}, bf16[4,4,128,512]{3,2,1,0:T(8,128)(2,1)}, u32[]{:S(2)}, u32[]{:S(2)}) collective-permute-start(bf16[4,4,128,512]{3,2,1,0:T(8,128)(2,1)} %get-tuple-element.86), channel_id=1, source_target_pairs={{0,4},{1,5},{2,6},{3,7},{4,0},{5,1},{6,2},{7,3},{8,12},{9,13},{10,... | collective-permute-start | bytes 6291464 | tf_op jit(solution)/shard_map/ppermute | solution.py:1236
  546.0 9.8 %collective-permute-start.42 = (bf16[2,256,256]{2,1,0:T(8,128)(2,1)S(1)}, bf16[2,256,256]{2,1,0:T(8,128)(2,1)S(1)}, u32[]{:S(2)}, u32[]{:S(2)}) collective-permute-start(bf16[2,256,256]{2,1,0:T(8,128)(2,1)S(1)} %slice.559), channel_id=1, source_target_pairs={{0,1},{1,0},{2,3},{3,2},{4,5},{5,4},{6,7},{7,6},{8,9},{9,8},{10,11... | collective-permute-start | bytes 786440 | tf_op jit(solution)/shard_map/ppermute | solution.py:1236
  547.1 24.2 %collective-permute-start.48 = (bf16[1,256,512]{2,1,0:T(8,128)(2,1)S(1)}, bf16[1,256,512]{2,1,0:T(8,128)(2,1)S(1)}, u32[]{:S(2)}, u32[]{:S(2)}) collective-permute-start(bf16[1,256,512]{2,1,0:T(8,128)(2,1)S(1)} %slice_add_fusion.22), channel_id=1, source_target_pairs={{0,2},{1,3},{2,0},{3,1},{4,6},{5,7},{6,4},{7,5},{8,10},{9,11},{10,... | collective-permute-start | bytes 786440 | tf_op jit(solution)/shard_map/ppermute | solution.py:1236
  548.1 83.9 %collective-permute-start.46 = (bf16[1,128,1024]{2,1,0:T(8,128)(2,1)S(1)}, bf16[1,128,1024]{2,1,0:T(8,128)(2,1)S(1)}, u32[]{:S(2)}, u32[]{:S(2)}) collective-permute-start(bf16[1,128,1024]{2,1,0:T(8,128)(2,1)S(1)} %slice_add_fusion.24), channel_id=1, source_target_pairs={{0,2},{1,3},{2,0},{3,1},{4,6},{5,7},{6,4},{7,5},{8,10},{9,11},{10,... | collective-permute-start | bytes 786440 | tf_op jit(solution)/shard_map/ppermute | solution.py:1236
  556.8 82.3 %collective-permute-start.43 = (bf16[1,256,256]{2,1,0:T(8,128)(2,1)S(1)}, bf16[1,256,256]{2,1,0:T(8,128)(2,1)}, u32[]{:S(2)}, u32[]{:S(2)}) collective-permute-start(bf16[1,256,256]{2,1,0:T(8,128)(2,1)S(1)} %slice_add_fusion.26), channel_id=1, source_target_pairs={{0,2},{1,3},{2,0},{3,1},{4,6},{5,7},{6,4},{7,5},{8,10},{9,11},{10,... | collective-permute-start | bytes 393224 | tf_op jit(solution)/shard_map/ppermute | solution.py:1236
  628.3 1.8 collective-permute-start.25
  630.1 15.5 %collective-permute-start.40 = (bf16[1,128,1056]{1,2,0:T(8,128)(2,1)}, bf16[1,128,1056]{1,2,0:T(8,128)(2,1)}, u32[]{:S(2)}, u32[]{:S(2)}) collective-permute-start(bf16[1,128,1056]{1,2,0:T(8,128)(2,1)} %slice_add_fusion.20), channel_id=1, source_target_pairs={{0,2},{1,3},{2,0},{3,1},{4,6},{5,7},{6,4},{7,5},{8,10},{9,11},{10,... | collective-permute-start | bytes 811016 | tf_op jit(solution)/shard_map/ppermute | solution.py:1236
  630.1 6.0 collective-permute-start.26
  636.0 25.9 %collective-permute-start.31 = (bf16[2,4,128,512]{3,2,1,0:T(8,128)(2,1)S(1)}, bf16[2,4,128,512]{3,2,1,0:T(8,128)(2,1)}, u32[]{:S(2)}, u32[]{:S(2)}) collective-permute-start(bf16[2,4,128,512]{3,2,1,0:T(8,128)(2,1)S(1)} %copy-done.14), channel_id=1, source_target_pairs={{0,8},{1,9},{2,10},{3,11},{4,20},{5,21},{6,22},{7,23},{8,0},{9,1},... | collective-permute-start | bytes 3145736 | tf_op jit(solution)/shard_map/ppermute | solution.py:1236
  637.0 5.6 collective-permute-start.27
  643.5 4.5 collective-permute-start.28
  648.1 8.1 %collective-permute-start.29 = (f32[160,128]{1,0:T(8,128)S(1)}, f32[160,128]{1,0:T(8,128)S(1)}, u32[]{:S(2)}, u32[]{:S(2)}) collective-permute-start(f32[160,128]{1,0:T(8,128)S(1)} %add.363), channel_id=1, source_target_pairs={{0,2},{1,3},{2,0},{3,1},{4,6},{5,7},{6,4},{7,5},{8,10},{9,11},{10,... | collective-permute-start | bytes 245768 | tf_op jit(solution)/shard_map/ppermute | solution.py:1236
  654.1 36.7 %collective-permute-start.23 = (bf16[512,1024]{1,0:T(8,128)(2,1)}, bf16[512,1024]{1,0:T(8,128)(2,1)S(1)}, u32[]{:S(2)}, u32[]{:S(2)}) collective-permute-start(bf16[512,1024]{1,0:T(8,128)(2,1)} %get-tuple-element.152), channel_id=1, source_target_pairs={{1,0},{5,1},{0,2},{4,3},{3,4},{7,5},{2,6},{6,7},{9,8},{13,9},{8,10... | collective-permute-start | bytes 3145736 | tf_op jit(solution)/shard_map/ppermute | solution.py:1267
  654.1 36.7 %collective-permute-start.24 = (bf16[512,1024]{1,0:T(8,128)(2,1)}, bf16[512,1024]{1,0:T(8,128)(2,1)}, u32[]{:S(2)}, u32[]{:S(2)}) collective-permute-start(bf16[512,1024]{1,0:T(8,128)(2,1)} %get-tuple-element.153), channel_id=1, source_target_pairs={{4,0},{0,1},{5,2},{1,3},{6,4},{2,5},{7,6},{3,7},{12,8},{8,9},{13,1... | collective-permute-start | bytes 3145736 | tf_op jit(solution)/shard_map/ppermute | solution.py:1267
  656.1 7.5 %collective-permute-start.30 = (f32[160,128]{1,0:T(8,128)S(1)}, f32[160,128]{1,0:T(8,128)S(1)}, u32[]{:S(2)}, u32[]{:S(2)}) collective-permute-start(f32[160,128]{1,0:T(8,128)S(1)} %add.364), channel_id=1, source_target_pairs={{0,4},{1,5},{2,6},{3,7},{4,0},{5,1},{6,2},{7,3},{8,12},{9,13},{10,... | collective-permute-start | bytes 245768 | tf_op jit(solution)/shard_map/ppermute | solution.py:1236
  663.0 9.4 %collective-permute-start.32 = (bf16[1,4,128,512]{3,2,1,0:T(8,128)(2,1)S(1)}, bf16[1,4,128,512]{3,2,1,0:T(8,128)(2,1)}, u32[]{:S(2)}, u32[]{:S(2)}) collective-permute-start(bf16[1,4,128,512]{3,2,1,0:T(8,128)(2,1)S(1)} %slice_add_fusion.16), channel_id=1, source_target_pairs={{0,16},{1,17},{2,18},{3,19},{4,12},{5,13},{6,14},{7,15},{8,24},{9,... | collective-permute-start | bytes 1572872 | tf_op jit(solution)/shard_map/ppermute | solution.py:1236
  673.7 28.5 %collective-permute-start.33 = (bf16[2,128,512]{2,1,0:T(8,128)(2,1)S(1)}, bf16[2,128,512]{2,1,0:T(8,128)(2,1)S(1)}, u32[]{:S(2)}, u32[]{:S(2)}) collective-permute-start(bf16[2,128,512]{2,1,0:T(8,128)(2,1)S(1)} %slice_bitcast_fusion.5), channel_id=1, source_target_pairs={{0,1},{1,0},{2,3},{3,2},{4,5},{5,4},{6,7},{7,6},{8,9},{9,8},{10,11... | collective-permute-start | bytes 786440 | tf_op jit(solution)/shard_map/ppermute | solution.py:1236
  702.1 13.3 %collective-permute-start.34 = (bf16[1,128,512]{2,1,0:T(8,128)(2,1)S(1)}, bf16[1,128,512]{2,1,0:T(8,128)(2,1)S(1)}, u32[]{:S(2)}, u32[]{:S(2)}) collective-permute-start(bf16[1,128,512]{2,1,0:T(8,128)(2,1)S(1)} %slice_add_fusion.28), channel_id=1, source_target_pairs={{0,2},{1,3},{2,0},{3,1},{4,6},{5,7},{6,4},{7,5},{8,10},{9,11},{10,... | collective-permute-start | bytes 393224 | tf_op jit(solution)/shard_map/ppermute | solution.py:1236
  (54 other events, 802.2 us)

commit v2 on v1

--- a/solution.py
+++ b/solution.py
@@ -275,6 +275,7 @@
 
 def back_scan_body(
     table_ref,
+    slot_ref,
     x_ref,
     gs_ref,
     gv_ref,
@@ -299,17 +300,17 @@
 ):
     states, groups, _ = decay_ref.shape
     count = x_ref.shape[1]
-    slot = pl.program_id(0)
+    slot = slot_ref[0]
     total = ends_ref.shape[0]
 
-    @pl.when((slot == 0) & (pl.program_id(1) == 0))
+    @pl.when(pl.program_id(0) == 0)
     def _():
         qx_ref[...] = jnp.zeros_like(qx_ref)
         qs_ref[...] = jnp.zeros_like(qs_ref)
         gain_grad_ref[...] = jnp.zeros_like(gain_grad_ref)
         omega_grad_ref[...] = jnp.zeros_like(omega_grad_ref)
 
-    @pl.when(pl.program_id(1) == 0)
+    @pl.when(pl.program_id(0) == 0)
     def _():
         carry[...] = jnp.zeros_like(carry)
 
@@ -383,24 +384,24 @@
     )
     gain_grad_ref[...] += jnp.sum(grad_normed * unit, axis=0, keepdims=True)
     omega_grad_ref[...] += jnp.sum(gs * normed, axis=0, keepdims=True)
-    grad_ref[0] = (
+    grad_ref[...] = (
         gi_ref[0] + norm_back_rows(grad_normed, gain_ref[...], unit, inv)
     ).astype(bf16)
 
 
-def back_scan(table, x, gs, gv, gi, check, gain, decay, coef, span, omega, ends, after=()):
-    slots, length, width = x.shape
+def back_scan(table, slot, x, gs, gv, gi, check, gain, decay, coef, span, omega, ends, after=()):
+    _, length, width = x.shape
     states, groups, lanes = decay.shape
     blocks = check.shape[1]
     block = length // blocks
-    whole3 = pl.BlockSpec((states, groups, lanes), lambda k, b, t: (0, 0, 0))
-    row = pl.BlockSpec((1, width), lambda k, b, t: (0, 0))
-    tokens = pl.BlockSpec((1, block, width), lambda k, b, t: (k, blocks - 1 - b, 0))
+    whole3 = pl.BlockSpec((states, groups, lanes), lambda b, t, u: (0, 0, 0))
+    row = pl.BlockSpec((1, width), lambda b, t, u: (0, 0))
+    tokens = pl.BlockSpec((1, block, width), lambda b, t, u: (slot, blocks - 1 - b, 0))
     return pl.pallas_call(
-        ignoring(back_scan_body, 12, len(after)),
+        ignoring(back_scan_body, 13, len(after)),
         grid_spec=pltpu.PrefetchScalarGridSpec(
-            num_scalar_prefetch=1,
-            grid=(slots, blocks),
+            num_scalar_prefetch=2,
+            grid=(blocks,),
             in_specs=[
                 tokens,
                 tokens,
@@ -408,17 +409,23 @@
                 tokens,
                 pl.BlockSpec(
                     (1, 1, states, groups, lanes),
-                    lambda k, b, t: (k, blocks - 1 - b, 0, 0, 0),
+                    lambda b, t, u: (slot, blocks - 1 - b, 0, 0, 0),
                 ),
                 row,
                 whole3,
                 whole3,
                 whole3,
                 row,
-                pl.BlockSpec(ends.shape, lambda k, b, t: (0, 0, 0, 0)),
+                pl.BlockSpec(ends.shape, lambda b, t, u: (0, 0, 0, 0)),
             ]
             + [pl.BlockSpec(memory_space=pl.ANY)] * len(after),
-            out_specs=[tokens, whole3, whole3, row, row],
+            out_specs=[
+                pl.BlockSpec((block, width), lambda b, t, u: (blocks - 1 - b, 0)),
+                whole3,
+                whole3,
+                row,
+                row,
+            ],
             scratch_shapes=[
                 pltpu.VMEM((block * groups, lanes), f32),
                 pltpu.VMEM((block * groups, lanes), f32),
@@ -428,20 +435,20 @@
             ],
         ),
         out_shape=[
-            jax.ShapeDtypeStruct((slots, length, width), bf16),
+            jax.ShapeDtypeStruct((length, width), bf16),
             jax.ShapeDtypeStruct((states, groups, lanes), f32),
             jax.ShapeDtypeStruct((states, groups, lanes), f32),
             jax.ShapeDtypeStruct((1, width), f32),
             jax.ShapeDtypeStruct((1, width), f32),
         ],
-        compiler_params=params(("arbitrary", "arbitrary")),
+        compiler_params=params(("arbitrary",)),
         name="back_scan",
         cost_estimate=pl.CostEstimate(
-            flops=slots * length * width * states * 20,
-            bytes_accessed=16 * slots * length * width,
+            flops=length * width * states * 20,
+            bytes_accessed=16 * length * width,
             transcendentals=0,
         ),
-    )(table, x, gs, gv, gi, check, gain, decay, coef, span, omega, ends, *after)
+    )(table, jnp.full((1,), slot, jnp.int32), x, gs, gv, gi, check, gain, decay, coef, span, omega, ends, *after)
 
 
 def load_chunks(table_ref, sources, total, length, sem):
@@ -846,7 +853,8 @@
 
 def gate_body(
     back_ref,
-    cot_ref,
+    cot_a,
+    cot_b,
     x_ref,
     cand_ref,
     update_ref,
@@ -875,7 +883,9 @@
     unit, inv = unit_rows_of(x + update * change)
     grad_feed = back_ref[...]
     gain_grad_ref[...] += jnp.sum(grad_feed * unit, axis=0, keepdims=True)
-    grad_first = cot_ref[...].astype(f32) + norm_back_rows(
+    early = pl.program_id(0) < pl.num_programs(0) // 2
+    cot = jnp.where(early, cot_a[...].astype(f32), cot_b[...].astype(f32))
+    grad_first = cot + norm_back_rows(
         grad_feed, gain_ref[...], unit, inv
     )
     kept = grad_first * (1.0 - update)
@@ -897,21 +907,23 @@
         ).astype(bf16)
 
 
-def gate(back, cot, x, cand_in, base, attended, gain, proj, after=()):
+def gate(back, cots, x, cand_in, base, attended, gain, proj, after=()):
     tokens, width = x.shape
     value_width = proj.shape[0]
     rows = min(128, tokens)
+    half = tokens // rows // 2
     wide = value_width // width
 
     def block(columns, at=0):
         return pl.BlockSpec((rows, columns), lambda i: (i, at))
 
     return pl.pallas_call(
-        ignoring(gate_body, 9, len(after)),
+        ignoring(gate_body, 10, len(after)),
         grid=(tokens // rows,),
         in_specs=[
             block(width),
-            block(width),
+            pl.BlockSpec((rows, width), lambda i: (jnp.minimum(i, half - 1), 0)),
+            pl.BlockSpec((rows, width), lambda i: (jnp.maximum(i - half, 0), 0)),
             block(width),
             block(width),
             block(width, wide),
@@ -940,7 +952,7 @@
             bytes_accessed=40 * tokens * width,
             transcendentals=4 * tokens * width,
         ),
-    )(back, cot, x, cand_in, base, base, attended, gain, proj, *after)
+    )(back, *cots, x, cand_in, base, base, attended, gain, proj, *after)
 
 
 def ordered_transpose(ids_ref, source, plain, ordered):
@@ -957,15 +969,34 @@
     lax.fori_loop(0, count, place, 0)
 
 
+def placed_transpose(places_ref, sources, plain, ordered):
+    start = 0
+    for source in sources:
+        plain[:, start : start + source.shape[0]] = source[...].T
+        start += source.shape[0]
+    count = places_ref.shape[0]
+    rows = plain.shape[0] // count
+
+    def place(q, _):
+        ordered[pl.ds(pl.multiple_of(places_ref[q] * rows, rows), rows), :] = plain[
+            pl.ds(pl.multiple_of(q * rows, rows), rows), :
+        ]
+        return 0
+
+    lax.fori_loop(0, count, place, 0)
+
+
 def feed_body(
     ids_ref,
     places_ref,
     low_ref,
-    cot_ref,
+    cot_a,
+    cot_b,
     first_ref,
     in_ref,
     out_ref,
-    result_ref,
+    result_a,
+    result_b,
     back_ref,
     out_send,
     out_keep,
@@ -979,22 +1010,22 @@
     step = pl.program_id(0)
     half = pl.num_programs(0) // 2
     tokens = low_ref.shape[0]
-    rows = min(256, tokens)
+    middle = tokens // 2
     nt = (((1,), (1,)), ((), ()))
 
     @pl.when(step == 0)
     def _():
-        cot_turned[...] = cot_ref[...].T
+        placed_transpose(places_ref, (cot_a, cot_b), plain, cot_turned)
         ordered_transpose(ids_ref, low_ref, plain, low_turned)
         total[...] = first_ref[...]
         back_ref[...] = jnp.zeros_like(back_ref)
 
     acts, grads = [], []
-    for r in range(tokens // rows):
-        at = slice(r * rows, (r + 1) * rows)
+    for r, cot_ref in enumerate((cot_a, cot_b)):
+        at = slice(r * middle, (r + 1) * middle)
         hidden = jnp.dot(low_ref[at, :], in_ref[...], preferred_element_type=f32)
         grad_act = lax.dot_general(
-            cot_ref[at, :], out_ref[...], nt, preferred_element_type=f32
+            cot_ref[...], out_ref[...], nt, preferred_element_type=f32
         )
         gate = jax.nn.sigmoid(hidden)
         act = hidden * gate
@@ -1012,9 +1043,9 @@
     in_grad = jnp.dot(
         low_turned[...], jnp.concatenate(grads), preferred_element_type=f32
     ).astype(bf16)
-    middle = in_grad.shape[0] // 2
-    in_send[...] = in_grad[:middle].reshape(in_send.shape)
-    in_keep[...] = in_grad[middle:].reshape(in_keep.shape)
+    split = in_grad.shape[0] // 2
+    in_send[...] = in_grad[:split].reshape(in_send.shape)
+    in_keep[...] = in_grad[split:].reshape(in_keep.shape)
 
     @pl.when(step < half)
     def _():
@@ -1026,10 +1057,11 @@
 
     @pl.when(step == pl.num_programs(0) - 1)
     def _():
-        result_ref[...] = total[...].astype(bf16)
-
-
-def feed(ids, places, low, cot, first_sum, feed_in, feed_out, seq, after=()):
+        result_a[...] = total[:middle, :].astype(bf16)
+        result_b[...] = total[middle:, :].astype(bf16)
+
+
+def feed(ids, places, low, cots, first_sum, feed_in, feed_out, seq, after=()):
     tokens, width = low.shape
     features = feed_in.shape[1]
     parts = ids.shape[0]
@@ -1051,20 +1083,22 @@
         (half, 1, rows, columns), lambda i, t, u: (0, u[at(i, t) // share], 0, at(i, t) % share)
     )
     return pl.pallas_call(
-        ignoring(feed_body, 7, len(after)),
+        ignoring(feed_body, 8, len(after)),
         grid_spec=pltpu.PrefetchScalarGridSpec(
             num_scalar_prefetch=2,
             grid=(parts,),
             in_specs=[
                 all_of(low.shape),
-                all_of(cot.shape),
+                all_of(cots[0].shape),
+                all_of(cots[1].shape),
                 all_of(first_sum.shape),
                 pl.BlockSpec((width, columns), lambda i, t, u: (0, at(i, t))),
                 pl.BlockSpec((columns, width), lambda i, t, u: (at(i, t), 0)),
             ]
             + [anywhere] * len(after),
             out_specs=[
-                all_of(low.shape),
+                all_of(cots[0].shape),
+                all_of(cots[1].shape),
                 all_of(low.shape),
                 pl.BlockSpec(
                     (1, width, columns), lambda i, t, u: (jnp.minimum(i, half - 1), 0, 0)
@@ -1083,7 +1117,8 @@
             ],
         ),
         out_shape=[
-            jax.ShapeDtypeStruct((tokens, width), bf16),
+            jax.ShapeDtypeStruct(cots[0].shape, bf16),
+            jax.ShapeDtypeStruct(cots[1].shape, bf16),
             jax.ShapeDtypeStruct((tokens, width), f32),
             jax.ShapeDtypeStruct((half, width, columns), bf16),
             jax.ShapeDtypeStruct((half, width, columns), bf16),
@@ -1097,16 +1132,16 @@
             bytes_accessed=8 * width * features + 16 * tokens * width,
             transcendentals=tokens * features,
         ),
-    )(ids, places, low, cot, first_sum, feed_in, feed_out, *after)
-
-
-def by_columns_body(ids_ref, left_ref, right_ref, send, keep, turned):
+    )(ids, places, low, *cots, first_sum, feed_in, feed_out, *after)
+
+
+def by_columns_body(ids_ref, places_ref, left_ref, right_ref, send, keep, plain, turned):
     step = pl.program_id(0)
     half = pl.num_programs(0) // 2
 
     @pl.when(step == 0)
     def _():
-        turned[...] = left_ref[...].T
+        placed_transpose(places_ref, (left_ref,), plain, turned)
 
     grad = jnp.dot(turned[...], right_ref[...], preferred_element_type=f32).astype(bf16)
 
@@ -1119,7 +1154,7 @@
         keep[0] = grad
 
 
-def by_columns(ids, left, right, after=(), rows=None, at=0):
+def by_columns(ids, places, left, right, after=(), rows=None, at=0):
     tokens = left.shape[0]
     rows = rows or left.shape[1]
     parts = ids.shape[0]
@@ -1130,28 +1165,33 @@
         left = left[:, at * rows : (at + 1) * rows]
         grad = mm_tn(left, right).astype(bf16).reshape(rows, parts, columns)
         grad = jnp.take(grad, ids, axis=1).transpose(1, 0, 2)
+        grad = grad.reshape(parts, places.shape[0], -1, columns)
+        grad = jnp.take(grad, jnp.argsort(places), axis=1).reshape(parts, rows, columns)
         return grad[:half], grad[half:]
     return pl.pallas_call(
-        ignoring(by_columns_body, 3, len(after)),
+        ignoring(by_columns_body, 4, len(after)),
         grid_spec=pltpu.PrefetchScalarGridSpec(
-            num_scalar_prefetch=1,
+            num_scalar_prefetch=2,
             grid=(parts,),
             in_specs=[
                 pl.BlockSpec(
-                    (tokens, rows), lambda i, t: (0, at), pipeline_mode=pl.Buffered(1)
+                    (tokens, rows), lambda i, t, u: (0, at), pipeline_mode=pl.Buffered(1)
                 ),
-                pl.BlockSpec((tokens, columns), lambda i, t: (0, t[jnp.minimum(i, parts - 1)])),
+                pl.BlockSpec((tokens, columns), lambda i, t, u: (0, t[jnp.minimum(i, parts - 1)])),
             ]
             + [pl.BlockSpec(memory_space=pl.ANY)] * len(after),
             out_specs=[
                 pl.BlockSpec(
-                    (1, rows, columns), lambda i, t: (jnp.minimum(i, half - 1), 0, 0)
+                    (1, rows, columns), lambda i, t, u: (jnp.minimum(i, half - 1), 0, 0)
                 ),
                 pl.BlockSpec(
-                    (1, rows, columns), lambda i, t: (jnp.maximum(i - half, 0), 0, 0)
+                    (1, rows, columns), lambda i, t, u: (jnp.maximum(i - half, 0), 0, 0)
                 ),
             ],
-            scratch_shapes=[pltpu.VMEM((rows, tokens), bf16)],
+            scratch_shapes=[
+                pltpu.VMEM((rows, tokens), bf16),
+                pltpu.VMEM((rows, tokens), bf16),
+            ],
         ),
         out_shape=[shape, shape],
         compiler_params=params(("arbitrary",)),
@@ -1161,7 +1201,7 @@
             bytes_accessed=2 * (tokens + rows) * right.shape[1],
             transcendentals=0,
         ),
-    )(ids, left, right, *after)
+    )(ids, places, left, right, *after)
 
 
 def by_rows_body(ids_ref, places_ref, left_ref, right_ref, send, keep, plain, turned):
@@ -1217,6 +1257,135 @@
     )(ids, places, left, right, *after)
 
 
+def value_back_body(
+    ids_ref,
+    places_ref,
+    left_ref,
+    own_ref,
+    other_ref,
+    slope_ref,
+    proj_ref,
+    total_ref,
+    send,
+    keep,
+    plain,
+    turned,
+):
+    @pl.when(pl.program_id(0) == 0)
+    def _():
+        total_ref[...] = jnp.zeros_like(total_ref)
+        ordered_transpose(ids_ref, left_ref, plain, turned)
+
+    grad = own_ref[...].astype(f32)
+    for k in range(other_ref.shape[0]):
+        grad = grad + other_ref[k].astype(f32)
+    grad = (grad * slope_ref[...].astype(f32)).astype(bf16)
+    total_ref[...] += mm_nt(grad, proj_ref[...])
+    weights = jnp.dot(turned[...], grad, preferred_element_type=f32).astype(bf16)
+    middle = weights.shape[0] // 2
+    send[...] = weights[:middle].reshape(send.shape)
+    keep[...] = weights[middle:].reshape(keep.shape)
+
+
+def value_back(ids, places, left, own, others, slope, proj, seq, after=()):
+    tokens, rows = left.shape
+    parts = ids.shape[0]
+    half = parts // 2
+    columns = proj.shape[1] // seq
+    tile = min(512, columns)
+    share = columns // tile
+    shape = jax.ShapeDtypeStruct((half, seq, rows // parts, columns), bf16)
+    split = pl.BlockSpec(
+        (half, 1, rows // parts, tile),
+        lambda i, t, u: (0, u[jnp.minimum(i // share, seq - 1)], 0, i % share),
+    )
+    stripe = pl.BlockSpec((tokens, tile), lambda i, t, u: (0, i))
+    fixed = pl.BlockSpec(
+        (tokens, rows), lambda i, t, u: (0, 0), pipeline_mode=pl.Buffered(1)
+    )
+    return pl.pallas_call(
+        ignoring(value_back_body, 7, len(after)),
+        grid_spec=pltpu.PrefetchScalarGridSpec(
+            num_scalar_prefetch=2,
+            grid=(seq * share,),
+            in_specs=[
+                fixed,
+                stripe,
+                pl.BlockSpec((others.shape[0], tokens, tile), lambda i, t, u: (0, 0, i)),
+                stripe,
+                pl.BlockSpec((rows, tile), lambda i, t, u: (0, i)),
+            ]
+            + [pl.BlockSpec(memory_space=pl.ANY)] * len(after),
+            out_specs=[fixed, split, split],
+            scratch_shapes=[
+                pltpu.VMEM((rows, tokens), bf16),
+                pltpu.VMEM((rows, tokens), bf16),
+            ],
+        ),
+        out_shape=[jax.ShapeDtypeStruct((tokens, rows), f32), shape, shape],
+        compiler_params=params(("arbitrary",)),
+        name="value_back",
+        cost_estimate=pl.CostEstimate(
+            flops=4 * tokens * rows * proj.shape[1],
+            bytes_accessed=20 * tokens * rows,
+            transcendentals=0,
+        ),
+    )(ids, places, left, own, others, slope, proj, *after)
+
+
+def stage_body(*refs, shapes):
+    count = len(shapes)
+    ins, outs = refs[: 2 * count], list(refs[2 * count :])
+    for k in range(count):
+        kept, arrived = ins[2 * k], ins[2 * k + 1]
+        for part in range(shapes[k][0]):
+            out = outs.pop(0)
+            out[...] = (kept[part].astype(f32) + arrived[part].astype(f32)).astype(out.dtype)
+
+
+def stage_sums(pairs, after=(), steps=4, wide=()):
+    shapes, ins, in_specs, out_specs, out_shapes, whole = [], [], [], [], [], []
+    for kept, _ in pairs:
+        rows = kept.size // kept.shape[-1] // min(2, kept.shape[0])
+        while rows % (16 * steps):
+            steps //= 2
+    for number, (kept, arrived) in enumerate(pairs):
+        halves = 1 if kept.shape[0] == 1 else 2
+        columns = kept.shape[-1]
+        rows = kept.size // columns // halves
+        rows_each = rows // steps
+        shapes.append((halves, rows, columns))
+        for v in (kept, arrived):
+            ins.append(v.reshape(halves, rows, columns))
+            in_specs.append(pl.BlockSpec((halves, rows_each, columns), lambda i: (0, i, 0)))
+        for _ in range(halves):
+            out_specs.append(pl.BlockSpec((rows_each, columns), lambda i: (i, 0)))
+            out_shapes.append(
+                jax.ShapeDtypeStruct((rows, columns), f32 if number in wide else bf16)
+            )
+        whole.append((halves, (kept.shape[0] // halves, *kept.shape[1:])))
+    sums = list(
+        pl.pallas_call(
+            ignoring(functools.partial(stage_body, shapes=shapes), len(ins), len(after)),
+            grid=(steps,),
+            in_specs=in_specs + [pl.BlockSpec(memory_space=pl.ANY)] * len(after),
+            out_specs=out_specs,
+            out_shape=out_shapes,
+            compiler_params=params(("arbitrary",)),
+            name="stage_sums",
+            cost_estimate=pl.CostEstimate(
+                flops=sum(v.size for v in ins),
+                bytes_accessed=sum(3 * v.size for v in ins),
+                transcendentals=0,
+            ),
+        )(*ins, *after)
+    )
+    out = []
+    for halves, shape in whole:
+        out.append(tuple(sums.pop(0).reshape(shape) for _ in range(halves)))
+    return out
+
+
 class Layout:
     def __init__(self, mesh):
         self.dp = mesh.shape["dp"]
@@ -1278,6 +1447,17 @@
 
     def gather(self, value):
         return jnp.concatenate([self.rotate(value, by) for by in range(1, self.members)], axis=0)
+
+    def returns(self, others):
+        slots = others.shape[0] // (self.members - 1)
+        return jnp.stack(
+            [
+                self.rotate(others[(by - 1) * slots : by * slots], self.members - by).reshape(
+                    -1, others.shape[-1]
+                )
+                for by in range(1, self.members)
+            ]
+        )
 
     def scatter_sum(self, own, others):
         slots = own.shape[0]
@@ -1321,13 +1501,26 @@
             return lambda d, z: (d ^ (1 << stage if d % 2 == 0 else 1 << (bits - stage)), z)
         return lambda d, z: (d, z ^ (1 << (stage - bits)))
 
-    def halve(self, held, stage):
-        sent, kept = held
-        arrived = self.send(sent, self.partner(stage))
-        middle = kept.shape[0] // 2
-        if middle == 0:
-            return None, kept[0] + arrived[0]
-        return kept[:middle] + arrived[:middle], kept[middle:] + arrived[middle:]
+    def turn(self, sums, after):
+        sums = [s for s in sums if s.arrived is not None]
+        if not sums:
+            return after
+        dp_stages = self.dp.bit_length() - 1
+        last = dp_stages + self.seq.bit_length() - 1
+        wide = [k for k, s in enumerate(sums) if s.stage + 1 == last]
+        out = stage_sums([(s.kept, s.arrived) for s in sums], after, wide=wide)
+        for s, held in zip(sums, out):
+            s.stage += 1
+            s.arrived = None
+            if s.stage == last:
+                s.total = held[0][0]
+            elif s.stage == dp_stages:
+                s.block = held[0]
+                if s.over_seq:
+                    s.begin_seq(held[0])
+            else:
+                s.send(*held)
+        return [part for held in out for part in held]
 
     def reduce_all(self, flat):
         core = lax.axis_index("dp") % 2
@@ -1344,6 +1537,22 @@
         return jnp.where(
             core == 0, jnp.stack([held, other]), jnp.stack([other, held])
         ).reshape(-1)[:count]
+
+
+class Sum:
+    def __init__(self, layout, sent, kept, over_seq=True):
+        self.layout, self.over_seq, self.stage = layout, over_seq, 0
+        self.block = self.total = None
+        self.send(sent, kept)
+
+    def send(self, sent, kept):
+        self.kept = kept
+        self.arrived = self.layout.send(sent, self.layout.partner(self.stage))
+
+    def begin_seq(self, block):
+        block = block.reshape(self.layout.seq, -1, block.shape[-1])
+        middle = self.layout.seq // 2
+        self.send(block[:middle], block[middle:])
 
 
 def mm(a, b):
@@ -1411,7 +1620,7 @@
     ids, places, blocks = layout.orders()
 
     x = jnp.stack(layout.spread(inputs))
-    cot = jnp.concatenate(layout.spread(cotangent))
+    cots = layout.spread(cotangent)
     bias_back, bias_front = bias_tiles(relative_bias, chunk_rows // TILE - 1, full)
 
     states = smooth_alpha.shape[0]
@@ -1469,30 +1678,30 @@
     unit_two, _ = unit_rows_of(first_sum)
     feed_low = (unit_two * feed_gain).astype(bf16)
 
-    result, grad_feed, out_send, out_keep, in_send, in_keep = feed(
-        ids, places, feed_low, cot, first_sum, feed_in, feed_out, layout.seq
-    )
-    result = result.reshape(slots, chunk_rows, width)
-    block_out = layout.collect([result[0], result[1]])
-    feed_out_sum = layout.halve((out_send, out_keep), 0)
-    feed_in_sum = layout.halve((in_send, in_keep), 0)
+    result_a, result_b, grad_feed, out_send, out_keep, in_send, in_keep = feed(
+        ids, places, feed_low, cots, first_sum, feed_in, feed_out, layout.seq
+    )
+    block_out = layout.collect([result_a, result_b])
+    feed_out_sum = Sum(layout, out_send, out_keep)
+    feed_in_sum = Sum(layout, in_send, in_keep)
 
     grad_input, grad_main, grad_att, feed_gain_grad = gate(
-        grad_feed, cot, flat_low, cand_in, base, attended, feed_gain[None], out_proj
-    )
-    proj_sum = layout.halve(
-        by_columns(
-            ids,
-            grad_main,
-            gated,
-            rows=width,
-            at=grad_main.shape[1] // width - 1,
-            after=(*feed_out_sum, *feed_in_sum),
-        ),
-        0,
-    )
-    mix_sum = layout.halve(by_rows(ids, None, mixed, grad_main), 0)
-    feed_out_sum = layout.halve(feed_out_sum, 1)
+        grad_feed, cots, flat_low, cand_in, base, attended, feed_gain[None], out_proj
+    )
+    after = layout.turn((feed_out_sum, feed_in_sum), (grad_att,))
+    proj_parts = by_columns(
+        ids,
+        places,
+        grad_main,
+        gated,
+        rows=width,
+        at=grad_main.shape[1] // width - 1,
+        after=after,
+    )
+    proj_sum = Sum(layout, *proj_parts)
+    mix_parts = by_rows(ids, None, mixed, grad_main, after=proj_parts)
+    mix_sum = Sum(layout, *mix_parts, over_seq=False)
+    after = layout.turn((proj_sum,), mix_parts)
     grad_query, gk_own, gk_oth, gv_own, gv_oth, rel_sums = attend_back(
         table,
         query_low,
@@ -1503,9 +1712,9 @@
         key_others,
         value_low,
         value_others,
-        after=(*proj_sum, *feed_out_sum),
-    )
-    feed_in_sum = layout.halve(feed_in_sum, 1)
+        after=after,
+    )
+    after = layout.turn((feed_out_sum, feed_in_sum, mix_sum), (grad_query,))
     grad_key = layout.scatter_sum(gk_own, gk_oth).reshape(tokens, key_width)
     grad_query = grad_query.reshape(tokens, key_width)
     grad_shared = (
@@ -1515,37 +1724,61 @@
         smoothed
     )
     grad_smooth = grad_smooth.reshape(slots, chunk_rows, width)
-    back = back_ends(grad_smooth, decay_slab, after=(*feed_in_sum, *mix_sum))
+    back = back_ends(grad_smooth, decay_slab, after=after)
     back_all = jnp.concatenate([back, layout.gather(back)])
-    grad_value = layout.scatter_sum(gv_own, gv_oth).reshape(tokens, value_width)
-    grad_value_pre = (grad_value * value_slope.astype(f32)).astype(bf16)
-    value_sum = layout.halve(
-        by_rows(ids, places, normed_low, grad_value_pre, layout.seq), 0
-    )
-    shared_sum = layout.halve(
-        by_rows(ids, None, mixed, grad_shared), 0
-    )
-    grad_normed = mm_nt(grad_value_pre, value_proj)
-
-    feed_out_sum = layout.halve(feed_out_sum, 2)
-    proj_sum = layout.halve(proj_sum, 1)
-    mix_sum = layout.halve(mix_sum, 1)
-    grad_in, qx, qs, mix_gain_grad, omega_grad = back_scan(
-        table,
-        x,
-        grad_smooth,
-        grad_normed.reshape(slots, chunk_rows, width),
-        grad_input.reshape(slots, chunk_rows, width),
-        check,
-        gain_row,
-        decay_slab,
-        coef,
-        span,
-        omega_row,
-        back_all,
-        after=(*value_sum, *shared_sum, *[v for v in feed_out_sum if v is not None], *proj_sum),
-    )
-    grad_in = layout.collect([grad_in[0], grad_in[1]]).astype(f32)
+    after = layout.turn((proj_sum, feed_out_sum, feed_in_sum), (back,))
+    grad_normed, value_send, value_keep = value_back(
+        ids,
+        places,
+        normed_low,
+        gv_own.reshape(tokens, value_width),
+        layout.returns(gv_oth),
+        value_slope,
+        value_proj,
+        layout.seq,
+        after=after,
+    )
+    value_sum = Sum(layout, value_send, value_keep)
+    shared_parts = by_rows(ids, None, mixed, grad_shared, after=(grad_normed,))
+    shared_sum = Sum(layout, *shared_parts, over_seq=False)
+    after = layout.turn((mix_sum, value_sum, shared_sum), shared_parts)
+
+    def scan_back(slot, after):
+        return back_scan(
+            table,
+            slot,
+            x,
+            grad_smooth,
+            grad_normed.reshape(slots, chunk_rows, width),
+            grad_input.reshape(slots, chunk_rows, width),
+            check,
+            gain_row,
+            decay_slab,
+            coef,
+            span,
+            omega_row,
+            back_all,
+            after=after,
+        )
+
+    first = scan_back(0, after)
+    after = layout.turn(
+        (feed_out_sum, feed_in_sum, proj_sum, mix_sum, value_sum, shared_sum), (first[0],)
+    )
+    second = scan_back(1, after)
+    grad_in = layout.collect([first[0], second[0]]).astype(f32)
+    after = layout.turn((proj_sum, value_sum, shared_sum), (second[0],))
+    while mix_sum.block is None or shared_sum.block is None:
+        after = layout.turn((mix_sum, shared_sum), after)
+    mix_rows = jnp.concatenate([shared_sum.block[0, 0], mix_sum.block[0, 0]], axis=1)
+    mix_rows = mix_rows.reshape(mix_rows.shape[0], layout.seq, -1).transpose(1, 0, 2)
+    mix_sum.begin_seq(mix_rows[blocks])
+    sums = (feed_out_sum, feed_in_sum, proj_sum, value_sum, mix_sum)
+    while any(v.total is None for v in sums):
+        after = layout.turn(sums, after)
+    feed_out_grad, feed_in_grad, out_grad, value_grad, mix_grad = (v.total for v in sums)
+    feed_out_grad, out_grad = feed_out_grad.T, out_grad.T
+    qx, qs, mix_gain_grad, omega_grad = (a + b for a, b in zip(first[1:], second[1:]))
 
     affine_grad = jnp.stack(
         [
@@ -1579,30 +1812,6 @@
     damp_grad = -smooth_alpha * decay_total
     beta_grad = smooth_alpha * input_total
 
-    stages = layout.dp.bit_length() - 1
-
-    def rest(held, stage):
-        while stage < stages:
-            held = layout.halve(held, stage)
-            stage += 1
-        return held[1]
-
-    def over_seq(held):
-        middle = layout.seq // 2
-        held = (held[:middle], held[middle:])
-        for stage in range(stages, stages + layout.seq.bit_length() - 1):
-            held = layout.halve(held, stage)
-        return held[1].astype(f32)
-
-    feed_out_grad = over_seq(
-        rest(feed_out_sum, 3).reshape(layout.seq, width // layout.seq, -1)[blocks]
-    ).T
-    feed_in_grad = over_seq(rest(feed_in_sum, 2))
-    out_grad = over_seq(rest(proj_sum, 2).reshape(layout.seq, width // layout.seq, -1)[blocks]).T
-    value_grad = over_seq(rest(value_sum, 1))
-    mix_rows = jnp.concatenate([rest(shared_sum, 1)[0], rest(mix_sum, 2)[0]], axis=1)
-    mix_rows = mix_rows.reshape(mix_rows.shape[0], layout.seq, -1).transpose(1, 0, 2)
-    mix_grad = over_seq(mix_rows[blocks])
     return (
         block_out,
         grad_in,

time: 728 us -> 631 us (0.87)
  other arithmetic: 87 us -> 24.5 us
  Pallas kernels: 253 us -> 311 us
  waiting for transfers between devices: 163 us -> 116 us
  starting transfers between devices: 96 us -> 63.2 us
    pallas_call x4 -> x15, Pallas kernels: 143 us -> 212 us  [the longest x1 68.6 us: feed(): pl.pallas_call(ignoring(feed_body, 8, len(after)), grid_spec=pltpu.Prefet...]
    add x24 -> x2, other arithmetic: 49.5 us -> 1.39 us  [layer(): a + b]
    ppermute x45, waiting for transfers between devices: 163 us -> 116 us  [send(): return lax.ppermute(value, AXES, self.pairs(move))]
    ppermute x45, starting transfers between devices: 91.9 us -> 57.4 us  [send(): return lax.ppermute(value, AXES, self.pairs(move))]
    convert_element_type x5 -> x1, other arithmetic: 13.5 us -> 2.28 us  [layer(): grad_in = layout.collect([first[0], second[0]]).astype(f32)]
    pallas_call x3 -> x2, Pallas kernels: 29.9 us -> 19.8 us  [by_rows(): pl.pallas_call(ignoring(by_rows_body, 4, len(after)), grid_spec=pltpu.Pre...]
    dot_general x3 -> x2, matrix products: 28.1 us -> 21.8 us  [mm_nt(): lax.dot_general(a, b, (((1,), (1,)), ((), ())), preferred_element_type=f32)]
  transfers between devices with their start and end apart: 49 -> 49, of which waited for: 16 -> 14; matrix products, arithmetic and copies ran while one was open for 23% -> 16% of each run, Pallas kernels for 22% -> 34%
where the time goes in v2:
time: 631 us; the launch traced here: 622 us
  Pallas kernels  311 us (49%)
  waiting for transfers between devices  116 us (18%)
  matrix products  64.2 us (10%)
  starting transfers between devices  63.2 us (10%)
  local copies, waits for them, and re-layouts  40.1 us (6%)
  other arithmetic  24.5 us (4%)
    ppermute x45, waiting for transfers between devices, send(): return lax.ppermute(value, AXES, self.pairs(move))  116 us
    pallas_call x1, Pallas kernels, feed(): pl.pallas_call(ignoring(feed_body, 8, len(after)), grid_spec=pltpu.Prefet...  68.6 us
    ppermute x45, starting transfers between devices, send(): return lax.ppermute(value, AXES, self.pairs(move))  57.4 us
    pallas_call x9, Pallas kernels, stage_sums(): pl.pallas_call(ignoring(functools.partial(stage_body, shapes=shapes), len...  50.4 us
    dot_general x4, matrix products, mm(): return jnp.dot(a, b, preferred_element_type=f32)  42.4 us
    pallas_call x2, Pallas kernels, back_scan(): pl.pallas_call(ignoring(back_scan_body, 13, len(after)), grid_spec=pltpu....  41 us
    pallas_call x1, Pallas kernels, gate(): pl.pallas_call(ignoring(gate_body, 10, len(after)), grid=(tokens // rows,...  23.6 us
    pallas_call x1, Pallas kernels, attend_back(): pl.pallas_call(ignoring(functools.partial(attend_back_body, total=total),...  22.2 us
  transfers between devices with their start and end apart: 49, of which 14 were waited for; matrix products, arithmetic and copies ran while one was open for 16% of the time, Pallas kernels for 34%

profile of v2, /device:TPU:0, one launch (start us, length us, event | category | flops | bytes accessed | tf_op | source)
XLA Modules:
  0.0 621.6 jit_solution(14715202196570049046)
XLA Ops:
  2.9 2.6 collective-permute-start.1
  5.6 2.4 collective-permute-start.2
  9.8 7.9 %slice.179.refs_5_ = bf16[1024,4096]{1,0:T(8,128)(2,1)} slice(bf16[1024,4224]{1,0:T(8,128)(2,1)} %param.30), slice={[0:1024], [128:4224]} | slice | bytes 16777216 | tf_op jit(solution)/shard_map/slice | solution.py:1635
  23.3 6.0 bias.1
  29.3 23.8 %collective-permute-done.1 = bf16[512,1024]{1,0:T(8,128)(2,1)} collective-permute-done((bf16[512,1024]{1,0:T(8,128)(2,1)S(1)}, bf16[512,1024]{1,0:T(8,128)(2,1)}, u32[]{:S(2)}, u32[]{:S(2)}) %collective-permute-start.1) | collective-permute-done | bytes 1048608 | tf_op jit(solution)/shard_map/ppermute | solution.py:1405
  53.1 2.7 pad_maximum_fusion.refs_0_.x_ref.refs_2_
  55.8 8.6 %front_ends.1 = (bf16[2,512,1024]{2,1,0:T(8,128)(2,1)}, f32[2,16,8,128]{3,2,1,0:T(8,128)}) custom-call(bf16[2,512,1024]{2,1,0:T(8,128)(2,1)} %pad_maximum_fusion.refs_0_.x_ref.refs_2_, f32[1,1024]{1,0:T(1,128)} %bitcast.362, f32[16,8,128]{2,1,0:T(8,128)} %bitcast.264, f32[9,256,256]{2,1,0:T(8,128)} %get-tuple-element.109.refs_3_.refs_4_, ...), custom_call_target="tpu_custom_call" | custom-call | flops 67108864 | bytes 4194304 | tf_op jit(solution)/shard_map/front_ends/pallas_call | solution.py:97
  64.5 12.9 %multiply_convert_fusion = (bf16[1024,2048]{1,0:T(8,128)(2,1)}, bf16[1024,2048]{1,0:T(8,128)(2,1)}) fusion(bf16[1024,1024]{1,0:T(8,128)(2,1)} %bitcast.389, bf16[1024,2048]{1,0:T(8,128)(2,1)} %refs_6_.3), kind=kOutput, calls=%fused_computation.1 | convolution fusion | flops 4315938816 | bytes 14680064 | tf_op jit(solution)/shard_map/dot_general | solution.py:1559
  85.5 18.6 %front_scan.1 = (f32[2,512,1024]{2,1,0:T(8,128)}, bf16[2,512,1024]{2,1,0:T(8,128)(2,1)}, f32[2,8,16,8,128]{4,3,2,1,0:T(8,128)}) custom-call(s32[9]{0:T(128)} %concatenate.39.table_ref.refs_0_, bf16[2,512,1024]{2,1,0:T(8,128)(2,1)} %pad_maximum_fusion.refs_0_.x_ref.refs_2_, f32[1,1024]{1,0:T(1,128)} %bitcast.363, f32[16,8,128]{2,1,0:T(8,128)} %bitcast.265, ...), custom_call_target="tpu_custom_call" | custom-call | flops 134217728 | bytes 8388608 | tf_op jit(solution)/shard_map/front_scan/pallas_call | solution.py:188
  104.1 3.2 add_convert_fusion
  107.5 14.2 %convolution_convert_fusion.refs_5_.refs_6_ = bf16[1024,4096]{1,0:T(8,128)(2,1)} fusion(bf16[1024,1024]{1,0:T(8,128)(2,1)S(1)} %bitcast.276, bf16[1024,4224]{1,0:T(8,128)(2,1)} %param.30), kind=kOutput, calls=%fused_computation.4 | convolution fusion | flops 8594128896 | bytes 18874368 | tf_op jit(solution)/shard_map/dot_general | solution.py:1559
  122.4 16.3 %attend.1 = (bf16[2,512,2048]{2,1,0:T(8,128)(2,1)}, bf16[2,512,2048]{2,1,0:T(8,128)(2,1)}, f32[2,512,1]{2,1,0:T(8,128)}) custom-call(s32[9]{0:T(128)} %concatenate.39.table_ref.refs_0_, bf16[2,512,128]{2,1,0:T(8,128)(2,1)} %bitcast.343, f32[9,256,256]{2,1,0:T(8,128)} %get-tuple-element.110.refs_4_.bias_ref, bf16[2,512,4096]{2,1,0:T(8,128)(2,1)} %bitcast.232, ...), custom_call_target="tpu_custom_call" | custom-call | flops 4563402752 | bytes 41943040 | tf_op jit(solution)/shard_map/attend/pallas_call | solution.py:559
  138.7 12.1 %fusion.24 = (f32[1024]{0:T(1024)S(1)}, f32[1024,1024]{1,0:T(8,128)S(1)}, f32[1024,1024]{1,0:T(8,128)}) fusion(bf16[1024,4096]{1,0:T(8,128)(2,1)} %convolution_convert_fusion.refs_5_.refs_6_, bf16[2,512,1024]{2,1,0:T(8,128)(2,1)S(1)} %copy-done, bf16[1024,2048]{1,0:T(8,128)(2,1)} %bitcast.258, bf16[2048,1024]{1,0:T(8,128)(2,1)} %refs_9_.1), kind=kOutput, calls=%fused_computation.96 | convolution fusion | flops 4310694912 | bytes 23072768 | tf_op jit(solution)/shard_map/dot_general | solution.py:1559
  154.4 68.6 %feed.1 = (bf16[512,1024]{1,0:T(8,128)(2,1)}, bf16[512,1024]{1,0:T(8,128)(2,1)}, f32[1024,1024]{1,0:T(8,128)}, bf16[4,1024,512]{2,1,0:T(8,128)(2,1)}, bf16[4,102...) custom-call(s32[8]{0:T(128)} %broadcast_select_fusion.1.refs_0_, ...), custom_call_target="tpu_custom_call" | custom-call | flops 51539607552 | bytes 50331648 | tf_op jit(solution)/shard_map/feed/pallas_call | solution.py:1085
  223.5 23.6 %gate.1 = (f32[1024,1024]{1,0:T(8,128)}, bf16[1024,4096]{1,0:T(8,128)(2,1)}, bf16[1024,2048]{1,0:T(8,128)(2,1)}, f32[1,1024]{1,0:T(1,128)}) custom-call(f32[1024,1024]{1,0:T(8,128)} %get-tuple-element.117.refs_0_, bf16[512,1024]{1,0:T(8,128)(2,1)} %collective-permute-done.6.refs_3_.refs_1_, bf16[512,1024]{1,0:T(8,128)(2,1)} %copy-done.13, ...), custom_call_target="tpu_custom_call" | custom-call | flops 4294967296 | bytes 41943040 | tf_op jit(solution)/shard_map/gate/pallas_call | solution.py:920
  247.1 9.3 %stage_sums.9 = (bf16[2048,512]{1,0:T(8,128)(2,1)}, bf16[2048,512]{1,0:T(8,128)(2,1)}, bf16[1024,1024]{1,0:T(8,128)(2,1)}, bf16[1024,1024]{1,0:T(8,128)(2,1)}) custom-call(bf16[2,2048,512]{2,1,0:T(8,128)(2,1)} %bitcast.251, bf16[2,2048,512]{2,1,0:T(8,128)(2,1)} %bitcast.39.refs_1_, bf16[2,1024,1024]{2,1,0:T(8,128)(2,1)} %bitcast.252, ...), custom_call_target="tpu_custom_call" | custom-call | flops 8388608 | bytes 25165824 | tf_op jit(solution)/shard_map/stage_sums/pallas_call | solution.py:1368
  256.4 11.9 %by_columns.1 = (bf16[4,1024,256]{2,1,0:T(8,128)(2,1)}, bf16[4,1024,256]{2,1,0:T(8,128)(2,1)}) custom-call(s32[8]{0:T(128)} %broadcast_select_fusion.1.refs_0_, s32[4]{0:T(128)} %get-tuple-element.108.refs_1_, bf16[1024,4096]{1,0:T(8,128)(2,1)} %get-tuple-element.119.refs_2_.refs_3_, bf16[1024,2048]{1,0:T(8,128)(2,1)} %bitcast.259, ...), custom_call_target="tpu_custom_call" | custom-call | flops 4294967296 | bytes 8388608 | tf_op jit(solution)/shard_map/by_columns/pallas_call | solution.py:1171
  268.7 15.4 %by_rows.2 = (bf16[4,1,128,4096]{3,2,1,0:T(8,128)(2,1)}, bf16[4,1,128,4096]{3,2,1,0:T(8,128)(2,1)}) custom-call(s32[8]{0:T(128)} %broadcast_select_fusion.1.refs_0_, s32[1]{0:T(128)} %constant.126.clone.1.refs_1_, bf16[1024,1024]{1,0:T(8,128)(2,1)} %bitcast.274, bf16[1024,4096]{1,0:T(8,128)(2,1)} %get-tuple-element.119.refs_2_.refs_3_, ...), custom_call_target="tpu_custom_call" | custom-call | flops 8589934592 | bytes 16777216 | tf_op jit(solution)/shard_map/by_rows/pallas_call | solution.py:1231
  287.1 4.2 stage_sums.10
  291.3 22.2 %attend_back.1 = (f32[2,512,128]{2,1,0:T(8,128)}, bf16[2,512,128]{2,1,0:T(8,128)(2,1)}, bf16[2,512,128]{2,1,0:T(8,128)(2,1)}, bf16[2,512,2048]{2,1,0:T(8,128)(2,...) custom-call(s32[9]{0:T(128)} %concatenate.39.table_ref.refs_0_, bf16[2,512,128]{2,1,0:T(8,128)(2,1)} %bitcast.344, ...), custom_call_target="tpu_custom_call" | custom-call | flops 9126805504 | bytes 41943040 | tf_op jit(solution)/shard_map/attend_back/pallas_call | solution.py:735
  314.1 6.3 %collective-permute-done.13 = bf16[2,512,128]{2,1,0:T(8,128)(2,1)S(1)} collective-permute-done((bf16[2,512,128]{2,1,0:T(8,128)(2,1)}, bf16[2,512,128]{2,1,0:T(8,128)(2,1)S(1)}, u32[]{:S(2)}, u32[]{:S(2)}) %collective-permute-start.13) | collective-permute-done | bytes 262176 | tf_op jit(solution)/shard_map/ppermute | solution.py:1405
  324.4 3.7 fusion.18
  328.1 5.8 collective-permute-done.17
  333.9 9.4 %stage_sums.11 = (bf16[1024,512]{1,0:T(8,128)(2,1)}, bf16[1024,512]{1,0:T(8,128)(2,1)}, bf16[512,1024]{1,0:T(8,128)(2,1)}, bf16[512,1024]{1,0:T(8,128)(2,1)}, bf...) custom-call(bf16[2,1024,512]{2,1,0:T(8,128)(2,1)} %bitcast.245, bf16[2,1024,512]{2,1,0:T(8,128)(2,1)} %copy-done.6, ...), custom_call_target="tpu_custom_call" | custom-call | flops 8388608 | bytes 25165824 | tf_op jit(solution)/shard_map/stage_sums/pallas_call | solution.py:1368
  345.4 18.1 %fusion.6 = f32[1024,1024]{1,0:T(8,128)} fusion(f32[2,512,1024]{2,1,0:T(8,128)} %get-tuple-element.139, f32[1024,1024]{1,0:T(8,128)} %fusion.18, bf16[1024,4096]{1,0:T(8,128)(2,1)} %get-tuple-element.119.refs_2_.refs_3_, bf16[1024,4224]{1,0:T(8,128)(2,1)} %param.30), kind=kOutput, calls=%fused_computation.15 | convolution fusion | flops 8599371776 | bytes 29360128 | tf_op jit(solution)/shard_map/dot_general | solution.py:1563
  365.0 8.0 %back_ends.1.refs_6_ = f32[2,16,8,128]{3,2,1,0:T(8,128)} custom-call(f32[2,512,1024]{2,1,0:T(8,128)} %bitcast.234, f32[16,8,128]{2,1,0:T(8,128)} %bitcast.266, bf16[1,1024,512]{2,1,0:T(8,128)(2,1)} %bitcast.312, bf16[1,1024,512]{2,1,0:T(8,128)(2,1)} %bitcast.253, bf16[1,4,128,1024]{3,2,1,0:T(8,128)(2,1)} %bitcast.310, bf16[1,4,128,1024]{3,2,1,0:T(8,128)(2,1)} %bitcast.255, ...), custom_call_target="tpu_custom_call" | custom-call | flops 67108864 | bytes 4194304 | tf_op jit(solution)/shard_map/back_ends/pallas_call | solution.py:255
  374.2 4.9 stage_sums.12
  379.1 16.1 %value_back.1 = (f32[1024,1024]{1,0:T(8,128)}, bf16[4,4,128,512]{3,2,1,0:T(8,128)(2,1)}, bf16[4,4,128,512]{3,2,1,0:T(8,128)(2,1)}) custom-call(s32[8]{0:T(128)} %broadcast_select_fusion.1.refs_0_, s32[4]{0:T(128)} %get-tuple-element.108.refs_1_, bf16[1024,1024]{1,0:T(8,128)(2,1)} %bitcast.390, bf16[1024,2048]{1,0:T(8,128)(2,1)} %bitcast.393, ...), custom_call_target="tpu_custom_call" | custom-call | flops 8589934592 | bytes 20971520 | tf_op jit(solution)/shard_map/value_back/pallas_call | solution.py:1306
  395.2 4.4 by_rows.3
  402.6 6.0 stage_sums.13
  414.5 13.9 %collective-permute-start.22 = (bf16[2,256,512]{2,1,0:T(8,128)(2,1)}, bf16[2,256,512]{2,1,0:T(8,128)(2,1)S(1)}, u32[]{:S(2)}, u32[]{:S(2)}) collective-permute-start(bf16[2,256,512]{2,1,0:T(8,128)(2,1)} %bitcast.76), channel_id=1, source_target_pairs={{0,1},{1,0},{2,3},{3,2},{4,5},{5,4},{6,7},{7,6},{8,9},{9,8},{10,11... | collective-permute-start | bytes 1572872 | tf_op jit(solution)/shard_map/ppermute | solution.py:1405
  431.7 20.4 %back_scan.2 = (bf16[512,1024]{1,0:T(8,128)(2,1)}, f32[16,8,128]{2,1,0:T(8,128)}, f32[16,8,128]{2,1,0:T(8,128)}, f32[1,1024]{1,0:T(1,128)}, f32[1,1024]{1,0:T(1,128)}) custom-call(s32[9]{0:T(128)} %concatenate.39.table_ref.refs_0_, s32[1]{0:T(128)} %constant.126.clone.1.refs_1_, bf16[2,512,1024]{2,1,0:T(8,128)(2,1)} %pad_maximum_fusion.refs_0_.x_ref.refs_2_, ...), custom_call_target="tpu_custom_call" | custom-call | flops 167772160 | bytes 8388608 | tf_op jit(solution)/shard_map/back_scan/pallas_call | solution.py:400
  452.9 2.3 collective-permute-start.8
  456.6 5.8 stage_sums.14
  462.5 20.6 %back_scan.3 = (bf16[512,1024]{1,0:T(8,128)(2,1)}, f32[16,8,128]{2,1,0:T(8,128)}, f32[16,8,128]{2,1,0:T(8,128)}, f32[1,1024]{1,0:T(1,128)}, f32[1,1024]{1,0:T(1,128)}) custom-call(s32[9]{0:T(128)} %concatenate.39.table_ref.refs_0_, s32[1]{0:T(128)} %constant.125.clone.1.refs_1_, bf16[2,512,1024]{2,1,0:T(8,128)(2,1)} %pad_maximum_fusion.refs_0_.x_ref.refs_2_, ...), custom_call_target="tpu_custom_call" | custom-call | flops 167772160 | bytes 8388608 | tf_op jit(solution)/shard_map/back_scan/pallas_call | solution.py:400
  489.1 4.2 collective-permute-done.34
  495.9 3.3 collective-permute-done.35
  502.1 4.0 collective-permute-done.36
  509.3 2.5 collective-permute-start.32
  517.0 2.5 collective-permute-start.38
  519.5 3.5 stage_sums.15
  527.6 47.8 %collective-permute-done.39.refs_1_ = bf16[1,256,512]{2,1,0:T(8,128)(2,1)} collective-permute-done((bf16[1,256,512]{2,1,0:T(8,128)(2,1)}, bf16[1,256,512]{2,1,0:T(8,128)(2,1)}, u32[]{:S(2)}, u32[]{:S(2)}) %collective-permute-start.39) | collective-permute-done | bytes 262176 | tf_op jit(solution)/shard_map/ppermute | solution.py:1405
  578.2 2.9 collective-permute-start.44
  583.8 2.5 collective-permute-done.44.refs_5_
  588.9 4.0 stage_sums.16
  597.7 2.3 maximum_convert_fusion
  601.9 13.2 %collective-permute-done.47.refs_1_ = bf16[1,128,512]{2,1,0:T(8,128)(2,1)S(1)} collective-permute-done((bf16[1,128,512]{2,1,0:T(8,128)(2,1)S(1)}, bf16[1,128,512]{2,1,0:T(8,128)(2,1)S(1)}, u32[]{:S(2)}, u32[]{:S(2)}) %collective-permute-start.47) | collective-permute-done | bytes 131104 | tf_op jit(solution)/shard_map/ppermute | solution.py:1405
  615.8 3.3 stage_sums.17
  (286 shorter events, 91.0 us)
Async XLA Ops:
  2.4 26.9 %collective-permute-start = (bf16[512,1024]{1,0:T(8,128)(2,1)S(1)}, bf16[512,1024]{1,0:T(8,128)(2,1)S(1)}, u32[]{:S(2)}, u32[]{:S(2)}) collective-permute-start(bf16[512,1024]{1,0:T(8,128)(2,1)S(1)} %get-tuple-element.278), channel_id=1, source_target_pairs={{0,4},{1,0},{2,5},{3,1},{4,6},{5,2},{6,7},{7,3},{8,12},{9,8},{10,1... | collective-permute-start | bytes 3145736 | tf_op jit(solution)/shard_map/ppermute | solution.py:1405
  2.9 50.2 %collective-permute-start.1 = (bf16[512,1024]{1,0:T(8,128)(2,1)S(1)}, bf16[512,1024]{1,0:T(8,128)(2,1)}, u32[]{:S(2)}, u32[]{:S(2)}) collective-permute-start(bf16[512,1024]{1,0:T(8,128)(2,1)S(1)} %get-tuple-element.279), channel_id=1, source_target_pairs={{0,1},{1,5},{2,0},{3,4},{4,3},{5,7},{6,2},{7,6},{8,9},{9,13},{10,8... | collective-permute-start | bytes 3145736 | tf_op jit(solution)/shard_map/ppermute | solution.py:1405
  5.6 16.4 %collective-permute-start.2 = (f32[2]{0:T(128)S(1)}, f32[2]{0:T(128)S(1)}, u32[]{:S(2)}, u32[]{:S(2)}) collective-permute-start(f32[2]{0:T(128)S(1)} %convert_element_type.50), channel_id=1, source_target_pairs={{0,4},{1,5},{2,6},{3,7},{4,0},{5,1},{6,2},{7,3},{8,12},{9,13},{10,... | collective-permute-start | bytes 32 | tf_op jit(solution)/shard_map/ppermute | solution.py:1405
  77.4 44.3 %collective-permute-start.5 = (bf16[2,512,2048]{2,1,0:T(8,128)(2,1)}, bf16[2,512,2048]{2,1,0:T(8,128)(2,1)}, u32[]{:S(2)}, u32[]{:S(2)}) collective-permute-start(bf16[2,512,2048]{2,1,0:T(8,128)(2,1)} %bitcast.29.v_own.refs_7_), channel_id=1, source_target_pairs={{0,4},{1,5},{2,6},{3,7},{4,0},{5,1},{6,2},{7,3},{8,12},{9,13},{10,... | collective-permute-start | bytes 12582920 | tf_op jit(solution)/shard_map/ppermute | solution.py:1405
  79.0 74.3 %collective-permute-start.7 = (bf16[512,1024]{1,0:T(8,128)(2,1)}, bf16[512,1024]{1,0:T(8,128)(2,1)S(1)}, u32[]{:S(2)}, u32[]{:S(2)}) collective-permute-start(bf16[512,1024]{1,0:T(8,128)(2,1)} %get-tuple-element.276), channel_id=1, source_target_pairs={{0,1},{1,5},{2,0},{3,4},{4,3},{5,7},{6,2},{7,6},{8,9},{9,13},{10,8... | collective-permute-start | bytes 3145736 | tf_op jit(solution)/shard_map/ppermute | solution.py:1405
  79.0 74.3 %collective-permute-start.6 = (bf16[512,1024]{1,0:T(8,128)(2,1)}, bf16[512,1024]{1,0:T(8,128)(2,1)}, u32[]{:S(2)}, u32[]{:S(2)}) collective-permute-start(bf16[512,1024]{1,0:T(8,128)(2,1)} %get-tuple-element.277), channel_id=1, source_target_pairs={{0,4},{1,0},{2,5},{3,1},{4,6},{5,2},{6,7},{7,3},{8,12},{9,8},{10,1... | collective-permute-start | bytes 3145736 | tf_op jit(solution)/shard_map/ppermute | solution.py:1405
  81.9 2.9 collective-permute-start.3
  107.3 14.4 %collective-permute-start.4 = (bf16[2,512,128]{2,1,0:T(8,128)(2,1)S(1)}, bf16[2,512,128]{2,1,0:T(8,128)(2,1)S(1)}, u32[]{:S(2)}, u32[]{:S(2)}) collective-permute-start(bf16[2,512,128]{2,1,0:T(8,128)(2,1)S(1)} %bitcast.340), channel_id=1, source_target_pairs={{0,4},{1,5},{2,6},{3,7},{4,0},{5,1},{6,2},{7,3},{8,12},{9,13},{10,... | collective-permute-start | bytes 786440 | tf_op jit(solution)/shard_map/ppermute | solution.py:1405
  223.0 24.1 %collective-permute-start.10 = (bf16[4,1024,512]{2,1,0:T(8,128)(2,1)}, bf16[4,1024,512]{2,1,0:T(8,128)(2,1)}, u32[]{:S(2)}, u32[]{:S(2)}) collective-permute-start(bf16[4,1024,512]{2,1,0:T(8,128)(2,1)} %get-tuple-element.123), channel_id=1, source_target_pairs={{0,4},{1,5},{2,6},{3,7},{4,0},{5,1},{6,2},{7,3},{8,12},{9,13},{10,... | collective-permute-start | bytes 12582920 | tf_op jit(solution)/shard_map/ppermute | solution.py:1405
  223.4 23.7 %collective-permute-start.11 = (bf16[4,4,128,1024]{3,2,1,0:T(8,128)(2,1)}, bf16[4,4,128,1024]{3,2,1,0:T(8,128)(2,1)}, u32[]{:S(2)}, u32[]{:S(2)}) collective-permute-start(bf16[4,4,128,1024]{3,2,1,0:T(8,128)(2,1)} %get-tuple-element.125), channel_id=1, source_target_pairs={{0,4},{1,5},{2,6},{3,7},{4,0},{5,1},{6,2},{7,3},{8,12},{9,13},{10,... | collective-permute-start | bytes 12582920 | tf_op jit(solution)/shard_map/ppermute | solution.py:1405
  268.3 18.8 %collective-permute-start.12 = (bf16[4,1024,256]{2,1,0:T(8,128)(2,1)}, bf16[4,1024,256]{2,1,0:T(8,128)(2,1)}, u32[]{:S(2)}, u32[]{:S(2)}) collective-permute-start(bf16[4,1024,256]{2,1,0:T(8,128)(2,1)} %get-tuple-element.131.refs_4_), channel_id=1, source_target_pairs={{0,4},{1,5},{2,6},{3,7},{4,0},{5,1},{6,2},{7,3},{8,12},{9,13},{10,... | collective-permute-start | bytes 6291464 | tf_op jit(solution)/shard_map/ppermute | solution.py:1405
  284.2 49.7 %collective-permute-start.18 = (bf16[4,1,128,4096]{3,2,1,0:T(8,128)(2,1)}, bf16[4,1,128,4096]{3,2,1,0:T(8,128)(2,1)}, u32[]{:S(2)}, u32[]{:S(2)}) collective-permute-start(bf16[4,1,128,4096]{3,2,1,0:T(8,128)(2,1)} %get-tuple-element.132.refs_2_), channel_id=1, source_target_pairs={{0,4},{1,5},{2,6},{3,7},{4,0},{5,1},{6,2},{7,3},{8,12},{9,13},{10,... | collective-permute-start | bytes 12582920 | tf_op jit(solution)/shard_map/ppermute | solution.py:1405
  285.1 43.1 %collective-permute-start.16 = (bf16[2,1024,512]{2,1,0:T(8,128)(2,1)}, bf16[2,1024,512]{2,1,0:T(8,128)(2,1)S(1)}, u32[]{:S(2)}, u32[]{:S(2)}) collective-permute-start(bf16[2,1024,512]{2,1,0:T(8,128)(2,1)} %bitcast.288), channel_id=1, source_target_pairs={{0,8},{1,9},{2,10},{3,11},{4,20},{5,21},{6,22},{7,23},{8,0},{9,1},... | collective-permute-start | bytes 6291464 | tf_op jit(solution)/shard_map/ppermute | solution.py:1405
  286.6 47.3 %collective-permute-start.17 = (bf16[2,4,128,1024]{3,2,1,0:T(8,128)(2,1)}, bf16[2,4,128,1024]{3,2,1,0:T(8,128)(2,1)}, u32[]{:S(2)}, u32[]{:S(2)}) collective-permute-start(bf16[2,4,128,1024]{3,2,1,0:T(8,128)(2,1)} %bitcast.286), channel_id=1, source_target_pairs={{0,8},{1,9},{2,10},{3,11},{4,20},{5,21},{6,22},{7,23},{8,0},{9,1},... | collective-permute-start | bytes 6291464 | tf_op jit(solution)/shard_map/ppermute | solution.py:1405
  313.5 65.6 %collective-permute-start.14 = (bf16[2,512,2048]{2,1,0:T(8,128)(2,1)}, bf16[2,512,2048]{2,1,0:T(8,128)(2,1)}, u32[]{:S(2)}, u32[]{:S(2)}) collective-permute-start(bf16[2,512,2048]{2,1,0:T(8,128)(2,1)} %get-tuple-element.141), channel_id=1, source_target_pairs={{0,4},{1,5},{2,6},{3,7},{4,0},{5,1},{6,2},{7,3},{8,12},{9,13},{10,... | collective-permute-start | bytes 12582920 | tf_op jit(solution)/shard_map/ppermute | solution.py:1405
  313.6 6.8 %collective-permute-start.13 = (bf16[2,512,128]{2,1,0:T(8,128)(2,1)}, bf16[2,512,128]{2,1,0:T(8,128)(2,1)S(1)}, u32[]{:S(2)}, u32[]{:S(2)}) collective-permute-start(bf16[2,512,128]{2,1,0:T(8,128)(2,1)} %get-tuple-element.138), channel_id=1, source_target_pairs={{0,4},{1,5},{2,6},{3,7},{4,0},{5,1},{6,2},{7,3},{8,12},{9,13},{10,... | collective-permute-start | bytes 786440 | tf_op jit(solution)/shard_map/ppermute | solution.py:1405
  320.4 52.6 %collective-permute-start.15 = (bf16[2,1024,256]{2,1,0:T(8,128)(2,1)}, bf16[2,1024,256]{2,1,0:T(8,128)(2,1)S(1)}, u32[]{:S(2)}, u32[]{:S(2)}) collective-permute-start(bf16[2,1024,256]{2,1,0:T(8,128)(2,1)} %bitcast.392), channel_id=1, source_target_pairs={{0,8},{1,9},{2,10},{3,11},{4,20},{5,21},{6,22},{7,23},{8,0},{9,1},... | collective-permute-start | bytes 3145736 | tf_op jit(solution)/shard_map/ppermute | solution.py:1405
  343.3 29.6 %collective-permute-start.19 = (bf16[1,1024,512]{2,1,0:T(8,128)(2,1)}, bf16[1,1024,512]{2,1,0:T(8,128)(2,1)}, u32[]{:S(2)}, u32[]{:S(2)}) collective-permute-start(bf16[1,1024,512]{2,1,0:T(8,128)(2,1)} %bitcast.311), channel_id=1, source_target_pairs={{0,16},{1,17},{2,18},{3,19},{4,12},{5,13},{6,14},{7,15},{8,24},{9,... | collective-permute-start | bytes 3145736 | tf_op jit(solution)/shard_map/ppermute | solution.py:1405
  344.9 29.2 %collective-permute-start.20 = (bf16[1,4,128,1024]{3,2,1,0:T(8,128)(2,1)}, bf16[1,4,128,1024]{3,2,1,0:T(8,128)(2,1)}, u32[]{:S(2)}, u32[]{:S(2)}) collective-permute-start(bf16[1,4,128,1024]{3,2,1,0:T(8,128)(2,1)} %bitcast.309), channel_id=1, source_target_pairs={{0,16},{1,17},{2,18},{3,19},{4,12},{5,13},{6,14},{7,15},{8,24},{9,... | collective-permute-start | bytes 3145736 | tf_op jit(solution)/shard_map/ppermute | solution.py:1405
  363.5 38.5 %collective-permute-start.25 = (bf16[2,1,128,4096]{3,2,0,1:T(8,128)(2,1)S(1)}, bf16[2,1,128,4096]{3,2,0,1:T(8,128)(2,1)}, u32[]{:S(2)}, u32[]{:S(2)}) collective-permute-start(bf16[2,1,128,4096]{3,2,0,1:T(8,128)(2,1)S(1)} %bitcast.270), channel_id=1, source_target_pairs={{0,8},{1,9},{2,10},{3,11},{4,20},{5,21},{6,22},{7,23},{8,0},{9,1},... | collective-permute-start | bytes 6291464 | tf_op jit(solution)/shard_map/ppermute | solution.py:1405
  395.2 6.7 %collective-permute-start.26 = (bf16[4,4,128,512]{3,2,1,0:T(8,128)(2,1)}, bf16[4,4,128,512]{3,2,1,0:T(8,128)(2,1)}, u32[]{:S(2)}, u32[]{:S(2)}) collective-permute-start(bf16[4,4,128,512]{3,2,1,0:T(8,128)(2,1)} %get-tuple-element.156), channel_id=1, source_target_pairs={{0,4},{1,5},{2,6},{3,7},{4,0},{5,1},{6,2},{7,3},{8,12},{9,13},{10,... | collective-permute-start | bytes 6291464 | tf_op jit(solution)/shard_map/ppermute | solution.py:1405
  399.7 2.2 collective-permute-start.27
  400.2 28.3 %collective-permute-start.21 = (f32[2,16,8,128]{3,2,1,0:T(8,128)S(1)}, f32[2,16,8,128]{3,2,1,0:T(8,128)S(1)}, u32[]{:S(2)}, u32[]{:S(2)}) collective-permute-start(f32[2,16,8,128]{3,2,1,0:T(8,128)S(1)} %copy-done.12), channel_id=1, source_target_pairs={{0,4},{1,5},{2,6},{3,7},{4,0},{5,1},{6,2},{7,3},{8,12},{9,13},{10,... | collective-permute-start | bytes 393224 | tf_op jit(solution)/shard_map/ppermute | solution.py:1405
  400.2 28.7 %collective-permute-start.24 = (bf16[1,1024,256]{2,1,0:T(8,128)(2,1)}, bf16[1,1024,256]{2,1,0:T(8,128)(2,1)S(1)}, u32[]{:S(2)}, u32[]{:S(2)}) collective-permute-start(bf16[1,1024,256]{2,1,0:T(8,128)(2,1)} %bitcast.69.refs_7_), channel_id=1, source_target_pairs={{0,16},{1,17},{2,18},{3,19},{4,12},{5,13},{6,14},{7,15},{8,24},{9,... | collective-permute-start | bytes 1572872 | tf_op jit(solution)/shard_map/ppermute | solution.py:1405
  408.6 47.4 %collective-permute-start.29 = (bf16[2,4,128,512]{3,2,1,0:T(8,128)(2,1)}, bf16[2,4,128,512]{3,2,1,0:T(8,128)(2,1)}, u32[]{:S(2)}, u32[]{:S(2)}) collective-permute-start(bf16[2,4,128,512]{3,2,1,0:T(8,128)(2,1)} %bitcast.307), channel_id=1, source_target_pairs={{0,8},{1,9},{2,10},{3,11},{4,20},{5,21},{6,22},{7,23},{8,0},{9,1},... | collective-permute-start | bytes 3145736 | tf_op jit(solution)/shard_map/ppermute | solution.py:1405
  410.1 45.9 %collective-permute-start.28 = (bf16[1,1,128,4096]{3,2,1,0:T(8,128)(2,1)}, bf16[1,1,128,4096]{3,2,1,0:T(8,128)(2,1)}, u32[]{:S(2)}, u32[]{:S(2)}) collective-permute-start(bf16[1,1,128,4096]{3,2,1,0:T(8,128)(2,1)} %bitcast.305), channel_id=1, source_target_pairs={{0,16},{1,17},{2,18},{3,19},{4,12},{5,13},{6,14},{7,15},{8,24},{9,... | collective-permute-start | bytes 3145736 | tf_op jit(solution)/shard_map/ppermute | solution.py:1405
  414.5 37.6 %collective-permute-start.22 = (bf16[2,256,512]{2,1,0:T(8,128)(2,1)}, bf16[2,256,512]{2,1,0:T(8,128)(2,1)S(1)}, u32[]{:S(2)}, u32[]{:S(2)}) collective-permute-start(bf16[2,256,512]{2,1,0:T(8,128)(2,1)} %bitcast.76), channel_id=1, source_target_pairs={{0,1},{1,0},{2,3},{3,2},{4,5},{5,4},{6,7},{7,6},{8,9},{9,8},{10,11... | collective-permute-start | bytes 1572872 | tf_op jit(solution)/shard_map/ppermute | solution.py:1405
  428.5 26.7 %collective-permute-start.23 = (bf16[2,128,1024]{2,1,0:T(8,128)(2,1)}, bf16[2,128,1024]{2,1,0:T(8,128)(2,1)S(1)}, u32[]{:S(2)}, u32[]{:S(2)}) collective-permute-start(bf16[2,128,1024]{2,1,0:T(8,128)(2,1)} %bitcast.78), channel_id=1, source_target_pairs={{0,1},{1,0},{2,3},{3,2},{4,5},{5,4},{6,7},{7,6},{8,9},{9,8},{10,11... | collective-permute-start | bytes 1572872 | tf_op jit(solution)/shard_map/ppermute | solution.py:1405
  428.9 27.1 %collective-permute-start.30 = (bf16[2,1,128,128]{3,2,0,1:T(8,128)(2,1)S(1)}, bf16[2,1,128,128]{3,2,0,1:T(8,128)(2,1)S(1)}, u32[]{:S(2)}, u32[]{:S(2)}) collective-permute-start(bf16[2,1,128,128]{3,2,0,1:T(8,128)(2,1)S(1)} %bitcast.360), channel_id=1, source_target_pairs={{0,8},{1,9},{2,10},{3,11},{4,20},{5,21},{6,22},{7,23},{8,0},{9,1},... | collective-permute-start | bytes 196616 | tf_op jit(solution)/shard_map/ppermute | solution.py:1405
  452.9 47.7 %collective-permute-start.8 = (bf16[512,1024]{1,0:T(8,128)(2,1)}, bf16[512,1024]{1,0:T(8,128)(2,1)S(1)}, u32[]{:S(2)}, u32[]{:S(2)}) collective-permute-start(bf16[512,1024]{1,0:T(8,128)(2,1)} %get-tuple-element.115), channel_id=1, source_target_pairs={{1,0},{5,1},{0,2},{4,3},{3,4},{7,5},{2,6},{6,7},{9,8},{13,9},{8,10... | collective-permute-start | bytes 3145736 | tf_op jit(solution)/shard_map/ppermute | solution.py:1436
  456.0 44.6 %collective-permute-start.9 = (bf16[512,1024]{1,0:T(8,128)(2,1)}, bf16[512,1024]{1,0:T(8,128)(2,1)S(1)}, u32[]{:S(2)}, u32[]{:S(2)}) collective-permute-start(bf16[512,1024]{1,0:T(8,128)(2,1)} %get-tuple-element.116), channel_id=1, source_target_pairs={{4,0},{0,1},{5,2},{1,3},{6,4},{2,5},{7,6},{3,7},{12,8},{8,9},{13,1... | collective-permute-start | bytes 3145736 | tf_op jit(solution)/shard_map/ppermute | solution.py:1436
  488.0 5.3 collective-permute-start.34
  488.2 28.0 %collective-permute-start.42 = (bf16[1,4,128,512]{3,2,1,0:T(8,128)(2,1)S(1)}, bf16[1,4,128,512]{3,2,1,0:T(8,128)(2,1)S(1)}, u32[]{:S(2)}, u32[]{:S(2)}) collective-permute-start(bf16[1,4,128,512]{3,2,1,0:T(8,128)(2,1)S(1)} %bitcast.328), channel_id=1, source_target_pairs={{0,16},{1,17},{2,18},{3,19},{4,12},{5,13},{6,14},{7,15},{8,24},{9,... | collective-permute-start | bytes 1572872 | tf_op jit(solution)/shard_map/ppermute | solution.py:1405
  493.4 5.8 collective-permute-start.35
  495.0 20.1 %collective-permute-start.41 = (bf16[2,256,256]{2,1,0:T(8,128)(2,1)S(1)}, bf16[2,256,256]{2,1,0:T(8,128)(2,1)S(1)}, u32[]{:S(2)}, u32[]{:S(2)}) collective-permute-start(bf16[2,256,256]{2,1,0:T(8,128)(2,1)S(1)} %bitcast.347), channel_id=1, source_target_pairs={{0,1},{1,0},{2,3},{3,2},{4,5},{5,4},{6,7},{7,6},{8,9},{9,8},{10,11... | collective-permute-start | bytes 786440 | tf_op jit(solution)/shard_map/ppermute | solution.py:1405
  499.2 6.9 %collective-permute-start.36 = (f32[160,128]{1,0:T(8,128)S(1)}, f32[160,128]{1,0:T(8,128)S(1)}, u32[]{:S(2)}, u32[]{:S(2)}) collective-permute-start(f32[160,128]{1,0:T(8,128)S(1)} %add.190), channel_id=1, source_target_pairs={{0,1},{1,0},{2,3},{3,2},{4,5},{5,4},{6,7},{7,6},{8,9},{9,8},{10,11... | collective-permute-start | bytes 245768 | tf_op jit(solution)/shard_map/ppermute | solution.py:1405
  500.8 12.4 %collective-permute-start.43 = (bf16[1,1,128,128]{3,2,1,0:T(8,128)(2,1)S(1)}, bf16[1,1,128,128]{3,2,1,0:T(8,128)(2,1)S(1)}, u32[]{:S(2)}, u32[]{:S(2)}) collective-permute-start(bf16[1,1,128,128]{3,2,1,0:T(8,128)(2,1)S(1)} %bitcast.370), channel_id=1, source_target_pairs={{0,16},{1,17},{2,18},{3,19},{4,12},{5,13},{6,14},{7,15},{8,24},{9,... | collective-permute-start | bytes 98312 | tf_op jit(solution)/shard_map/ppermute | solution.py:1405
  506.1 6.0 collective-permute-start.37
  509.3 84.5 %collective-permute-start.32 = (bf16[512,1024]{1,0:T(8,128)(2,1)}, bf16[512,1024]{1,0:T(8,128)(2,1)}, u32[]{:S(2)}, u32[]{:S(2)}) collective-permute-start(bf16[512,1024]{1,0:T(8,128)(2,1)} %get-tuple-element.165.refs_12_), channel_id=1, source_target_pairs={{4,0},{0,1},{5,2},{1,3},{6,4},{2,5},{7,6},{3,7},{12,8},{8,9},{13,1... | collective-permute-start | bytes 3145736 | tf_op jit(solution)/shard_map/ppermute | solution.py:1436
  512.1 63.3 %collective-permute-start.39 = (bf16[1,256,512]{2,1,0:T(8,128)(2,1)}, bf16[1,256,512]{2,1,0:T(8,128)(2,1)}, u32[]{:S(2)}, u32[]{:S(2)}) collective-permute-start(bf16[1,256,512]{2,1,0:T(8,128)(2,1)} %bitcast.98.refs_13_), channel_id=1, source_target_pairs={{0,2},{1,3},{2,0},{3,1},{4,6},{5,7},{6,4},{7,5},{8,10},{9,11},{10,... | collective-permute-start | bytes 786440 | tf_op jit(solution)/shard_map/ppermute | solution.py:1405
  513.2 70.6 %collective-permute-start.40 = (bf16[1,128,1024]{2,1,0:T(8,128)(2,1)}, bf16[1,128,1024]{2,1,0:T(8,128)(2,1)}, u32[]{:S(2)}, u32[]{:S(2)}) collective-permute-start(bf16[1,128,1024]{2,1,0:T(8,128)(2,1)} %bitcast.100.refs_15_), channel_id=1, source_target_pairs={{0,2},{1,3},{2,0},{3,1},{4,6},{5,7},{6,4},{7,5},{8,10},{9,11},{10,... | collective-permute-start | bytes 786440 | tf_op jit(solution)/shard_map/ppermute | solution.py:1405
  515.1 78.7 %collective-permute-start.31 = (bf16[512,1024]{1,0:T(8,128)(2,1)}, bf16[512,1024]{1,0:T(8,128)(2,1)}, u32[]{:S(2)}, u32[]{:S(2)}) collective-permute-start(bf16[512,1024]{1,0:T(8,128)(2,1)} %get-tuple-element.176.refs_6_), channel_id=1, source_target_pairs={{1,0},{5,1},{0,2},{4,3},{3,4},{7,5},{2,6},{6,7},{9,8},{13,9},{8,10... | collective-permute-start | bytes 3145736 | tf_op jit(solution)/shard_map/ppermute | solution.py:1436
  517.0 8.7 %collective-permute-start.38 = (f32[160,128]{1,0:T(8,128)S(1)}, f32[160,128]{1,0:T(8,128)}, u32[]{:S(2)}, u32[]{:S(2)}) collective-permute-start(f32[160,128]{1,0:T(8,128)S(1)} %add.192), channel_id=1, source_target_pairs={{0,4},{1,5},{2,6},{3,7},{4,0},{5,1},{6,2},{7,3},{8,12},{9,13},{10,... | collective-permute-start | bytes 245768 | tf_op jit(solution)/shard_map/ppermute | solution.py:1405
  525.7 52.5 %collective-permute-start.46 = (bf16[2,128,1056]{1,2,0:T(8,128)(2,1)S(1)}, bf16[2,128,1056]{1,2,0:T(8,128)(2,1)S(1)}, u32[]{:S(2)}, u32[]{:S(2)}) collective-permute-start(bf16[2,128,1056]{1,2,0:T(8,128)(2,1)S(1)} %get-tuple-element.281), channel_id=1, source_target_pairs={{0,1},{1,0},{2,3},{3,2},{4,5},{5,4},{6,7},{7,6},{8,9},{9,8},{10,11... | collective-permute-start | bytes 1622024 | tf_op jit(solution)/shard_map/ppermute | solution.py:1405
  575.3 12.9 %collective-permute-start.45 = (bf16[2,128,512]{2,1,0:T(8,128)(2,1)S(1)}, bf16[2,128,512]{2,1,0:T(8,128)(2,1)S(1)}, u32[]{:S(2)}, u32[]{:S(2)}) collective-permute-start(bf16[2,128,512]{2,1,0:T(8,128)(2,1)S(1)} %bitcast.348), channel_id=1, source_target_pairs={{0,1},{1,0},{2,3},{3,2},{4,5},{5,4},{6,7},{7,6},{8,9},{9,8},{10,11... | collective-permute-start | bytes 786440 | tf_op jit(solution)/shard_map/ppermute | solution.py:1405
  578.2 8.1 %collective-permute-start.44 = (bf16[1,256,256]{2,1,0:T(8,128)(2,1)}, bf16[1,256,256]{2,1,0:T(8,128)(2,1)S(1)}, u32[]{:S(2)}, u32[]{:S(2)}) collective-permute-start(bf16[1,256,256]{2,1,0:T(8,128)(2,1)} %bitcast.355), channel_id=1, source_target_pairs={{0,2},{1,3},{2,0},{3,1},{4,6},{5,7},{6,4},{7,5},{8,10},{9,11},{10,... | collective-permute-start | bytes 393224 | tf_op jit(solution)/shard_map/ppermute | solution.py:1405
  593.0 22.1 %collective-permute-start.48 = (bf16[1,128,1056]{2,1,0:T(8,128)(2,1)}, bf16[1,128,1056]{2,1,0:T(8,128)(2,1)S(1)}, u32[]{:S(2)}, u32[]{:S(2)}) collective-permute-start(bf16[1,128,1056]{2,1,0:T(8,128)(2,1)} %bitcast.338), channel_id=1, source_target_pairs={{0,2},{1,3},{2,0},{3,1},{4,6},{5,7},{6,4},{7,5},{8,10},{9,11},{10,... | collective-permute-start | bytes 811016 | tf_op jit(solution)/shard_map/ppermute | solution.py:1405
  595.5 19.5 %collective-permute-start.47 = (bf16[1,128,512]{2,1,0:T(8,128)(2,1)S(1)}, bf16[1,128,512]{2,1,0:T(8,128)(2,1)S(1)}, u32[]{:S(2)}, u32[]{:S(2)}) collective-permute-start(bf16[1,128,512]{2,1,0:T(8,128)(2,1)S(1)} %bitcast.354), channel_id=1, source_target_pairs={{0,2},{1,3},{2,0},{3,1},{4,6},{5,7},{6,4},{7,5},{8,10},{9,11},{10,... | collective-permute-start | bytes 393224 | tf_op jit(solution)/shard_map/ppermute | solution.py:1405
  (60 other events, 709.0 us)

commit v3 on v2

--- a/solution.py
+++ b/solution.py
@@ -13,6 +13,8 @@
 MASKED = -1e30
 VMEM_LIMIT = 60 * 1024 * 1024
 AXES = ("dp", "seq")
+BRIEF = pl.CostEstimate(flops=1, bytes_accessed=1, transcendentals=0)
+LONG = pl.CostEstimate(flops=10**11, bytes_accessed=1, transcendentals=0)
 
 f32 = jnp.float32
 bf16 = jnp.bfloat16
@@ -114,11 +116,7 @@
         scratch_shapes=[pltpu.VMEM((block * groups, lanes), f32)],
         compiler_params=params(("arbitrary", "arbitrary")),
         name="front_ends",
-        cost_estimate=pl.CostEstimate(
-            flops=slots * length * width * states * 4,
-            bytes_accessed=4 * slots * length * width,
-            transcendentals=0,
-        ),
+        cost_estimate=BRIEF,
     )(x, gain, decay, *after)
 
 
@@ -217,11 +215,7 @@
         ],
         compiler_params=params(("arbitrary", "arbitrary")),
         name="front_scan",
-        cost_estimate=pl.CostEstimate(
-            flops=slots * length * width * states * 8,
-            bytes_accessed=8 * slots * length * width,
-            transcendentals=slots * length * width,
-        ),
+        cost_estimate=LONG,
     )(table, x, gain, decay, coef, span, omega, ends)
 
 
@@ -265,11 +259,7 @@
         scratch_shapes=[pltpu.VMEM((block * groups, lanes), f32)],
         compiler_params=params(("arbitrary", "arbitrary")),
         name="back_ends",
-        cost_estimate=pl.CostEstimate(
-            flops=slots * length * width * states * 4,
-            bytes_accessed=4 * slots * length * width,
-            transcendentals=0,
-        ),
+        cost_estimate=BRIEF,
     )(gs, decay, *after)
 
 
@@ -443,11 +433,7 @@
         ],
         compiler_params=params(("arbitrary",)),
         name="back_scan",
-        cost_estimate=pl.CostEstimate(
-            flops=length * width * states * 20,
-            bytes_accessed=16 * length * width,
-            transcendentals=0,
-        ),
+        cost_estimate=LONG,
     )(table, jnp.full((1,), slot, jnp.int32), x, gs, gv, gi, check, gain, decay, coef, span, omega, ends, *after)
 
 
@@ -590,11 +576,7 @@
         ],
         compiler_params=params(("arbitrary",)),
         name="attend",
-        cost_estimate=pl.CostEstimate(
-            flops=slots * length * total * length * (key_width + value_width),
-            bytes_accessed=20 * slots * length * value_width,
-            transcendentals=slots * length * total * length,
-        ),
+        cost_estimate=BRIEF,
     )(table, q, bias, reset, k_own, k_oth, v_own, v_oth)
 
 
@@ -610,9 +592,8 @@
     v_oth,
     gq_ref,
     gk_own,
-    gk_oth,
     gv_own,
-    gv_oth,
+    both_oth,
     rel_out,
     keys,
     values,
@@ -701,10 +682,14 @@
     def _():
         for slot in range(total):
             place = pl.ds(pl.multiple_of(table_ref[slot] * length, length), length)
-            key_out, value_out = (gk_own, gv_own) if slot < 2 else (gk_oth, gv_oth)
-            at = slot if slot < 2 else slot - 2
-            key_out[at] = (gk_sum[place, :] * scale).astype(bf16)
-            value_out[at] = gv_sum[place, :].astype(bf16)
+            key_grad = (gk_sum[place, :] * scale).astype(bf16)
+            value_grad = gv_sum[place, :].astype(bf16)
+            if slot < 2:
+                gk_own[slot] = key_grad
+                gv_own[slot] = value_grad
+            else:
+                both_oth[slot - 2, :, :value_width] = value_grad
+                both_oth[slot - 2, :, value_width:] = key_grad
         down = lax.broadcasted_iota(jnp.int32, (TILE, TILE), 0)
         across = lax.broadcasted_iota(jnp.int32, (TILE, TILE), 1)
         mirror = jnp.where(down + across == TILE - 1, 1.0, 0.0)
@@ -725,6 +710,7 @@
     value_width = v_own.shape[2]
     total = slots + k_oth.shape[0]
     rel_shape = (total * length // TILE, 1, 2 * TILE)
+    both_shape = (k_oth.shape[0], length, key_width + value_width)
     anywhere = pl.BlockSpec(memory_space=pl.ANY)
 
     def all_of(shape):
@@ -751,9 +737,8 @@
             out_specs=[
                 pl.BlockSpec((1, length, key_width), lambda k, t: (k, 0, 0)),
                 all_of(k_own.shape),
-                all_of(k_oth.shape),
                 all_of(v_own.shape),
-                all_of(v_oth.shape),
+                all_of(both_shape),
                 all_of(rel_shape),
             ],
             scratch_shapes=[
@@ -770,18 +755,13 @@
         out_shape=[
             jax.ShapeDtypeStruct((slots, length, key_width), f32),
             jax.ShapeDtypeStruct(k_own.shape, bf16),
-            jax.ShapeDtypeStruct(k_oth.shape, bf16),
             jax.ShapeDtypeStruct(v_own.shape, bf16),
-            jax.ShapeDtypeStruct(v_oth.shape, bf16),
+            jax.ShapeDtypeStruct(both_shape, bf16),
             jax.ShapeDtypeStruct(rel_shape, f32),
         ],
         compiler_params=params(("arbitrary",)),
         name="attend_back",
-        cost_estimate=pl.CostEstimate(
-            flops=2 * slots * length * total * length * (key_width + value_width),
-            bytes_accessed=20 * slots * length * value_width,
-            transcendentals=slots * length * total * length,
-        ),
+        cost_estimate=LONG,
     )(table, q, grads, lse, bias, k_own, k_oth, v_own, v_oth, *after)
 
 
@@ -910,7 +890,7 @@
 def gate(back, cots, x, cand_in, base, attended, gain, proj, after=()):
     tokens, width = x.shape
     value_width = proj.shape[0]
-    rows = min(128, tokens)
+    rows = min(256, tokens // 2)
     half = tokens // rows // 2
     wide = value_width // width
 
@@ -947,11 +927,7 @@
         ],
         compiler_params=params(("arbitrary",)),
         name="gate",
-        cost_estimate=pl.CostEstimate(
-            flops=2 * tokens * width * value_width,
-            bytes_accessed=40 * tokens * width,
-            transcendentals=4 * tokens * width,
-        ),
+        cost_estimate=LONG,
     )(back, *cots, x, cand_in, base, base, attended, gain, proj, *after)
 
 
@@ -1080,7 +1056,8 @@
         return t[jnp.minimum(i, parts - 1)]
 
     split = pl.BlockSpec(
-        (half, 1, rows, columns), lambda i, t, u: (0, u[at(i, t) // share], 0, at(i, t) % share)
+        (half, 1, 1, rows, columns),
+        lambda i, t, u: (0, u[at(i, t) // share], at(i, t) % share, 0, 0),
     )
     return pl.pallas_call(
         ignoring(feed_body, 8, len(after)),
@@ -1122,16 +1099,12 @@
             jax.ShapeDtypeStruct((tokens, width), f32),
             jax.ShapeDtypeStruct((half, width, columns), bf16),
             jax.ShapeDtypeStruct((half, width, columns), bf16),
-            jax.ShapeDtypeStruct((half, seq, rows, features // seq), bf16),
-            jax.ShapeDtypeStruct((half, seq, rows, features // seq), bf16),
+            jax.ShapeDtypeStruct((half, seq, share, rows, columns), bf16),
+            jax.ShapeDtypeStruct((half, seq, share, rows, columns), bf16),
         ],
         compiler_params=params(("arbitrary",)),
         name="feed",
-        cost_estimate=pl.CostEstimate(
-            flops=12 * tokens * width * features,
-            bytes_accessed=8 * width * features + 16 * tokens * width,
-            transcendentals=tokens * features,
-        ),
+        cost_estimate=BRIEF,
     )(ids, places, low, *cots, first_sum, feed_in, feed_out, *after)
 
 
@@ -1196,11 +1169,7 @@
         out_shape=[shape, shape],
         compiler_params=params(("arbitrary",)),
         name="by_columns",
-        cost_estimate=pl.CostEstimate(
-            flops=2 * tokens * rows * right.shape[1],
-            bytes_accessed=2 * (tokens + rows) * right.shape[1],
-            transcendentals=0,
-        ),
+        cost_estimate=BRIEF,
     )(ids, places, left, right, *after)
 
 
@@ -1215,7 +1184,7 @@
     keep[...] = grad[middle:].reshape(keep.shape)
 
 
-def by_rows(ids, places, left, right, seq=1, after=()):
+def by_rows(ids, places, left, right, seq=1, after=(), cost=BRIEF):
     tokens, rows = left.shape
     parts = ids.shape[0]
     half = parts // 2
@@ -1249,11 +1218,7 @@
         out_shape=[shape, shape],
         compiler_params=params(("arbitrary",)),
         name="by_rows",
-        cost_estimate=pl.CostEstimate(
-            flops=2 * tokens * rows * right.shape[1],
-            bytes_accessed=2 * (tokens + rows) * right.shape[1],
-            transcendentals=0,
-        ),
+        cost_estimate=cost,
     )(ids, places, left, right, *after)
 
 
@@ -1325,45 +1290,49 @@
         out_shape=[jax.ShapeDtypeStruct((tokens, rows), f32), shape, shape],
         compiler_params=params(("arbitrary",)),
         name="value_back",
-        cost_estimate=pl.CostEstimate(
-            flops=4 * tokens * rows * proj.shape[1],
-            bytes_accessed=20 * tokens * rows,
-            transcendentals=0,
-        ),
+        cost_estimate=LONG,
     )(ids, places, left, own, others, slope, proj, *after)
 
 
 def stage_body(*refs, shapes):
-    count = len(shapes)
-    ins, outs = refs[: 2 * count], list(refs[2 * count :])
-    for k in range(count):
-        kept, arrived = ins[2 * k], ins[2 * k + 1]
-        for part in range(shapes[k][0]):
-            out = outs.pop(0)
-            out[...] = (kept[part].astype(f32) + arrived[part].astype(f32)).astype(out.dtype)
-
-
-def stage_sums(pairs, after=(), steps=4, wide=()):
+    count = sum(pairs for pairs, _ in shapes)
+    ins, outs = list(refs[: 2 * count]), list(refs[2 * count :])
+    for pairs, halves in shapes:
+        into = [outs.pop(0) for _ in range(halves)]
+        start = 0
+        for _ in range(pairs):
+            kept, arrived = ins.pop(0), ins.pop(0)
+            stop = start + kept.shape[0]
+            for part, out in enumerate(into):
+                out[start:stop] = (
+                    kept[:, part].astype(f32) + arrived[:, part].astype(f32)
+                ).astype(out.dtype)
+            start = stop
+
+
+def stage_sums(groups, after=(), steps=4, cost=BRIEF):
     shapes, ins, in_specs, out_specs, out_shapes, whole = [], [], [], [], [], []
-    for kept, _ in pairs:
-        rows = kept.size // kept.shape[-1] // min(2, kept.shape[0])
-        while rows % (16 * steps):
+    for pairs, single, _ in groups:
+        _, n, rows, _ = pairs[0][0].shape
+        while (n * rows // (1 if single else 2)) % (16 * steps):
             steps //= 2
-    for number, (kept, arrived) in enumerate(pairs):
-        halves = 1 if kept.shape[0] == 1 else 2
-        columns = kept.shape[-1]
-        rows = kept.size // columns // halves
-        rows_each = rows // steps
-        shapes.append((halves, rows, columns))
-        for v in (kept, arrived):
-            ins.append(v.reshape(halves, rows, columns))
-            in_specs.append(pl.BlockSpec((halves, rows_each, columns), lambda i: (0, i, 0)))
+    for pairs, single, kind in groups:
+        halves = 1 if single else 2
+        g, n, rows, columns = pairs[0][0].shape
+        each = n * rows // halves // steps
+        shapes.append((len(pairs), halves))
+        for pair in pairs:
+            for v in pair:
+                ins.append(v.reshape(g, halves, n * rows // halves, columns))
+                in_specs.append(
+                    pl.BlockSpec((g, halves, each, columns), lambda i: (0, 0, i, 0))
+                )
         for _ in range(halves):
-            out_specs.append(pl.BlockSpec((rows_each, columns), lambda i: (i, 0)))
+            out_specs.append(pl.BlockSpec((len(pairs) * g, each, columns), lambda i: (0, i, 0)))
             out_shapes.append(
-                jax.ShapeDtypeStruct((rows, columns), f32 if number in wide else bf16)
+                jax.ShapeDtypeStruct((len(pairs) * g, n * rows // halves, columns), kind)
             )
-        whole.append((halves, (kept.shape[0] // halves, *kept.shape[1:])))
+        whole.append((halves, (len(pairs) * g, n // halves, rows, columns)))
     sums = list(
         pl.pallas_call(
             ignoring(functools.partial(stage_body, shapes=shapes), len(ins), len(after)),
@@ -1373,17 +1342,10 @@
             out_shape=out_shapes,
             compiler_params=params(("arbitrary",)),
             name="stage_sums",
-            cost_estimate=pl.CostEstimate(
-                flops=sum(v.size for v in ins),
-                bytes_accessed=sum(3 * v.size for v in ins),
-                transcendentals=0,
-            ),
+            cost_estimate=cost,
         )(*ins, *after)
     )
-    out = []
-    for halves, shape in whole:
-        out.append(tuple(sums.pop(0).reshape(shape) for _ in range(halves)))
-    return out
+    return [tuple(sums.pop(0).reshape(shape) for _ in range(halves)) for halves, shape in whole]
 
 
 class Layout:
@@ -1429,13 +1391,16 @@
             out.append(self.send(sent, self.home_to_work(round_index)))
         return out
 
-    def collect(self, values):
-        back = []
-        for round_index in range(2):
-            pairs = [(b, a) for a, b in self.pairs(self.home_to_work(round_index))]
-            back.append(lax.ppermute(values[round_index], AXES, pairs))
+    def homeward(self, value, round_index):
+        pairs = [(b, a) for a, b in self.pairs(self.home_to_work(round_index))]
+        return lax.ppermute(value, AXES, pairs)
+
+    def gathered(self, back):
         late = lax.axis_index("seq") >= self.seq // 2
         return jnp.stack([jnp.where(late, back[1], back[0]), jnp.where(late, back[0], back[1])])
+
+    def collect(self, values):
+        return self.gathered([self.homeward(v, r) for r, v in enumerate(values)])
 
     def rotate(self, value, by):
         def move(d, z):
@@ -1458,15 +1423,6 @@
                 for by in range(1, self.members)
             ]
         )
-
-    def scatter_sum(self, own, others):
-        slots = own.shape[0]
-        total = own.astype(f32)
-        for by in range(1, self.members):
-            total = total + self.rotate(
-                others[(by - 1) * slots : by * slots], self.members - by
-            ).astype(f32)
-        return total
 
     def orders(self):
         dp, z = lax.axis_index("dp"), lax.axis_index("seq")
@@ -1501,58 +1457,103 @@
             return lambda d, z: (d ^ (1 << stage if d % 2 == 0 else 1 << (bits - stage)), z)
         return lambda d, z: (d, z ^ (1 << (stage - bits)))
 
-    def turn(self, sums, after):
-        sums = [s for s in sums if s.arrived is not None]
+    def turn(self, sums, after, cost=BRIEF):
+        sums = [s for s in sums if s.arrived]
         if not sums:
             return after
         dp_stages = self.dp.bit_length() - 1
         last = dp_stages + self.seq.bit_length() - 1
-        wide = [k for k, s in enumerate(sums) if s.stage + 1 == last]
-        out = stage_sums([(s.kept, s.arrived) for s in sums], after, wide=wide)
-        for s, held in zip(sums, out):
+        groups = []
+        for s in sums:
+            pairs = list(zip(s.kept, s.arrived))
+            single = s.stage + 1 == last
+            if s.stage + 1 == dp_stages:
+                single = not s.over_seq
+                if s.over_seq:
+                    pairs = [
+                        tuple(
+                            v.reshape(v.shape[0], self.seq, -1, v.shape[-1]) for v in pair
+                        )
+                        for pair in pairs
+                    ]
+            groups.append((pairs, single, f32 if s.stage + 1 == last else bf16))
+        out = stage_sums(groups, after, cost=cost)
+        for s, held, (_, single, _) in zip(sums, out, groups):
             s.stage += 1
-            s.arrived = None
-            if s.stage == last:
-                s.total = held[0][0]
-            elif s.stage == dp_stages:
-                s.block = held[0]
-                if s.over_seq:
-                    s.begin_seq(held[0])
+            s.arrived = ()
+            if single:
+                s.total = held[0]
             else:
-                s.send(*held)
+                s.send([held[0]], [held[1]])
         return [part for held in out for part in held]
 
-    def reduce_all(self, flat):
+    def sum_seq(self, held):
+        low = 1
+        while low < self.seq:
+            others = [low] if 2 * low >= self.seq else [low, 2 * low, 3 * low]
+            mine = held
+            for other in others:
+                held = held + self.send(mine, lambda d, z: (d, z ^ other))
+            low *= 4
+        return held
+
+    def reduce_all(self, sent, held):
         core = lax.axis_index("dp") % 2
-        count = flat.shape[0]
-        split = jnp.pad(flat, (0, -count % 2048)).reshape(2, -1, 128)
-        held = lax.dynamic_index_in_dim(split, core, 0, False)
-        sent = lax.dynamic_index_in_dim(split, 1 - core, 0, False)
         held = held + self.send(sent, lambda d, z: (d ^ 1, z))
-        for bit in range(1, self.dp.bit_length() - 1):
-            held = held + self.send(held, lambda d, z: (d ^ (1 << bit), z))
-        for bit in range(self.seq.bit_length() - 1):
-            held = held + self.send(held, lambda d, z: (d, z ^ (1 << bit)))
+        held = self.sum_seq(held)
+        low = 2
+        while low < self.dp:
+            others = [low] if 2 * low >= self.dp else [low, 2 * low, 3 * low]
+            mine = held
+            for other in others:
+                held = held + self.send(mine, lambda d, z: (d ^ other, z))
+            low *= 4
         other = self.send(held, lambda d, z: (d ^ 1, z))
-        return jnp.where(
-            core == 0, jnp.stack([held, other]), jnp.stack([other, held])
-        ).reshape(-1)[:count]
+        return jnp.where(core == 0, jnp.stack([held, other]), jnp.stack([other, held]))
+
+
+def pack_body(core_ref, qx_a, qx_b, qs_a, qs_b, rest_ref, sent, held):
+    rows = jnp.concatenate(
+        [qx_a[...] + qx_b[...], qs_a[...] + qs_b[...], rest_ref[...]], axis=0
+    )
+    middle = rows.shape[0] // 2
+    first = core_ref[0] == 0
+    sent[...] = jnp.where(first, rows[middle:], rows[:middle])
+    held[...] = jnp.where(first, rows[:middle], rows[middle:])
+
+
+def pack(core, first, second, rest, after=()):
+    ins = [v.reshape(-1, 128) for v in (first[0], second[0], first[1], second[1])] + [rest]
+    rows = 2 * ins[0].shape[0] + rest.shape[0]
+    shape = jax.ShapeDtypeStruct((rows // 2, 128), f32)
+    inside = pl.BlockSpec(memory_space=pltpu.VMEM)
+    return pl.pallas_call(
+        ignoring(pack_body, 6, len(after)),
+        in_specs=[pl.BlockSpec(memory_space=pltpu.SMEM)]
+        + [inside] * 5
+        + [pl.BlockSpec(memory_space=pl.ANY)] * len(after),
+        out_specs=[inside, inside],
+        out_shape=[shape, shape],
+        name="pack",
+        cost_estimate=BRIEF,
+    )(core[None].astype(jnp.int32), *ins, *after)
 
 
 class Sum:
-    def __init__(self, layout, sent, kept, over_seq=True):
+    def __init__(self, layout, *pairs, over_seq=True):
         self.layout, self.over_seq, self.stage = layout, over_seq, 0
-        self.block = self.total = None
-        self.send(sent, kept)
+        self.total = None
+        pairs = [[v.reshape(1, v.shape[0], -1, v.shape[-1]) for v in pair] for pair in pairs]
+        self.send([p[0] for p in pairs], [p[1] for p in pairs])
 
     def send(self, sent, kept):
         self.kept = kept
-        self.arrived = self.layout.send(sent, self.layout.partner(self.stage))
+        self.arrived = [self.layout.send(v, self.layout.partner(self.stage)) for v in sent]
 
     def begin_seq(self, block):
-        block = block.reshape(self.layout.seq, -1, block.shape[-1])
+        self.total = None
         middle = self.layout.seq // 2
-        self.send(block[:middle], block[middle:])
+        self.send([block[None, :middle]], [block[None, middle:]])
 
 
 def mm(a, b):
@@ -1681,14 +1682,16 @@
     result_a, result_b, grad_feed, out_send, out_keep, in_send, in_keep = feed(
         ids, places, feed_low, cots, first_sum, feed_in, feed_out, layout.seq
     )
-    block_out = layout.collect([result_a, result_b])
-    feed_out_sum = Sum(layout, out_send, out_keep)
-    feed_in_sum = Sum(layout, in_send, in_keep)
+    home = [layout.homeward(result_a, 0), layout.homeward(result_b, 1)]
+    block_out = layout.gathered(home)
+    out_sum = Sum(layout, (out_send, out_keep))
+    in_sum = Sum(layout, (in_send, in_keep))
 
     grad_input, grad_main, grad_att, feed_gain_grad = gate(
         grad_feed, cots, flat_low, cand_in, base, attended, feed_gain[None], out_proj
     )
-    after = layout.turn((feed_out_sum, feed_in_sum), (grad_att,))
+    after = layout.turn((out_sum, in_sum), (grad_att,))
+    mix_parts = by_rows(ids, None, mixed, grad_main, after=after, cost=LONG)
     proj_parts = by_columns(
         ids,
         places,
@@ -1696,13 +1699,12 @@
         gated,
         rows=width,
         at=grad_main.shape[1] // width - 1,
-        after=after,
-    )
-    proj_sum = Sum(layout, *proj_parts)
-    mix_parts = by_rows(ids, None, mixed, grad_main, after=proj_parts)
-    mix_sum = Sum(layout, *mix_parts, over_seq=False)
-    after = layout.turn((proj_sum,), mix_parts)
-    grad_query, gk_own, gk_oth, gv_own, gv_oth, rel_sums = attend_back(
+        after=mix_parts,
+    )
+    after = layout.turn((out_sum,), (*proj_parts, *home))
+    mix_sum = Sum(layout, mix_parts, over_seq=False)
+    proj_sum = Sum(layout, proj_parts)
+    grad_query, gk_own, gv_own, both_oth, rel_sums = attend_back(
         table,
         query_low,
         grad_att.reshape(slots, chunk_rows, value_width),
@@ -1714,34 +1716,37 @@
         value_others,
         after=after,
     )
-    after = layout.turn((feed_out_sum, feed_in_sum, mix_sum), (grad_query,))
-    grad_key = layout.scatter_sum(gk_own, gk_oth).reshape(tokens, key_width)
-    grad_query = grad_query.reshape(tokens, key_width)
-    grad_shared = (
-        (grad_query * score_affine[0] + grad_key * score_affine[2]) * silu_slope(shared_pre)
-    ).astype(bf16)
-    grad_smooth = (mm_nt(grad_main, mix_main) + mm_nt(grad_shared, mix_shared)) * silu_slope(
-        smoothed
-    )
-    grad_smooth = grad_smooth.reshape(slots, chunk_rows, width)
-    back = back_ends(grad_smooth, decay_slab, after=after)
-    back_all = jnp.concatenate([back, layout.gather(back)])
-    after = layout.turn((proj_sum, feed_out_sum, feed_in_sum), (back,))
+    both_back = layout.returns(both_oth)
+    after = layout.turn((in_sum, out_sum, proj_sum), (grad_query,), cost=LONG)
     grad_normed, value_send, value_keep = value_back(
         ids,
         places,
         normed_low,
         gv_own.reshape(tokens, value_width),
-        layout.returns(gv_oth),
+        both_back,
         value_slope,
         value_proj,
         layout.seq,
         after=after,
     )
-    value_sum = Sum(layout, value_send, value_keep)
-    shared_parts = by_rows(ids, None, mixed, grad_shared, after=(grad_normed,))
-    shared_sum = Sum(layout, *shared_parts, over_seq=False)
-    after = layout.turn((mix_sum, value_sum, shared_sum), shared_parts)
+    grad_key = jnp.sum(both_back[:, :, value_width:].astype(f32), axis=0) + gk_own.reshape(
+        tokens, key_width
+    ).astype(f32)
+    grad_query = grad_query.reshape(tokens, key_width)
+    grad_shared = (
+        (grad_query * score_affine[0] + grad_key * score_affine[2]) * silu_slope(shared_pre)
+    ).astype(bf16)
+    shared_grad = mm_tn(mixed, grad_shared).astype(bf16)
+    shared_grad = lax.psum_scatter(shared_grad, "dp", scatter_dimension=0, tiled=True)
+    after = layout.turn((in_sum, out_sum, proj_sum, mix_sum), (grad_normed,))
+    value_sum = Sum(layout, (value_send, value_keep))
+    grad_smooth = (mm_nt(grad_main, mix_main) + mm_nt(grad_shared, mix_shared)) * silu_slope(
+        smoothed
+    )
+    grad_smooth = grad_smooth.reshape(slots, chunk_rows, width)
+    back = back_ends(grad_smooth, decay_slab, after=after)
+    back_all = jnp.concatenate([back, layout.gather(back)])
+    after = layout.turn((out_sum, in_sum, mix_sum, value_sum), (back,))
 
     def scan_back(slot, after):
         return back_scan(
@@ -1763,23 +1768,29 @@
 
     first = scan_back(0, after)
     after = layout.turn(
-        (feed_out_sum, feed_in_sum, proj_sum, mix_sum, value_sum, shared_sum), (first[0],)
-    )
-    second = scan_back(1, after)
-    grad_in = layout.collect([first[0], second[0]]).astype(f32)
-    after = layout.turn((proj_sum, value_sum, shared_sum), (second[0],))
-    while mix_sum.block is None or shared_sum.block is None:
-        after = layout.turn((mix_sum, shared_sum), after)
-    mix_rows = jnp.concatenate([shared_sum.block[0, 0], mix_sum.block[0, 0]], axis=1)
-    mix_rows = mix_rows.reshape(mix_rows.shape[0], layout.seq, -1).transpose(1, 0, 2)
-    mix_sum.begin_seq(mix_rows[blocks])
-    sums = (feed_out_sum, feed_in_sum, proj_sum, value_sum, mix_sum)
+        (in_sum, mix_sum, value_sum, proj_sum, out_sum), (first[0], shared_grad)
+    )
+    home_first = layout.homeward(first[0], 0)
+    while mix_sum.total is None:
+        after = layout.turn((mix_sum,), after)
+    rows = jnp.concatenate([shared_grad, mix_sum.total[0, 0]], axis=1)
+    rows = rows.reshape(rows.shape[0], layout.seq, -1).transpose(1, 0, 2)
+    mix_sum.begin_seq(rows[blocks])
+    second = scan_back(1, (*after, *mix_sum.kept))
+    home_second = layout.homeward(second[0], 1)
+    after = (second[0], home_first)
+    sums = (mix_sum, proj_sum, value_sum, out_sum, in_sum)
+    turned = layout.turn(sums, after)
+    after = (*turned, home_second)
     while any(v.total is None for v in sums):
         after = layout.turn(sums, after)
-    feed_out_grad, feed_in_grad, out_grad, value_grad, mix_grad = (v.total for v in sums)
-    feed_out_grad, out_grad = feed_out_grad.T, out_grad.T
-    qx, qs, mix_gain_grad, omega_grad = (a + b for a, b in zip(first[1:], second[1:]))
-
+    grad_in = layout.gathered([home_first, home_second]).astype(f32)
+    feed_out_grad, feed_in_grad = out_sum.total[0, 0].T, in_sum.total[0, 0]
+    rows = width // layout.dp
+    feed_in_grad = feed_in_grad.reshape(-1, rows, feed_in_grad.shape[-1])
+    feed_in_grad = feed_in_grad.transpose(1, 0, 2).reshape(rows, -1)
+    out_grad, value_grad = proj_sum.total[0, 0].T, value_sum.total[0, 0]
+    mix_grad = mix_sum.total[0, 0]
     affine_grad = jnp.stack(
         [
             jnp.sum(grad_query * shared_pre * jax.nn.sigmoid(shared_pre), axis=0),
@@ -1790,21 +1801,24 @@
     )
     relative_grad = bias_grad(rel_sums[:, 0], seq_length)
     small = [
-        qx.reshape(-1),
-        qs.reshape(-1),
-        mix_gain_grad.reshape(-1),
-        omega_grad.reshape(-1),
-        feed_gain_grad.reshape(-1),
-        affine_grad.reshape(-1),
+        first[3] + second[3],
+        first[4] + second[4],
+        feed_gain_grad,
+        affine_grad,
         relative_grad,
     ]
-    sums = layout.reduce_all(jnp.concatenate(small))
-    parts, start = [], 0
+    small = [v.reshape(-1, 128) for v in small]
+    rest = jnp.concatenate(small)
+    rest = jnp.pad(rest, ((0, -rest.shape[0] % 16), (0, 0)))
+    totals = layout.reduce_all(*pack(core, first[1:3], second[1:3], rest, after=turned))
+    totals = totals.reshape(-1, 128)
+    count = states * width // 128
+    input_sum = totals[:count].reshape(states, width)
+    decay_sum = totals[count : 2 * count].reshape(states, width)
+    parts, start = [], 2 * count
     for item in small:
-        parts.append(lax.slice_in_dim(sums, start, start + item.shape[0]))
+        parts.append(totals[start : start + item.shape[0]].reshape(-1))
         start += item.shape[0]
-    input_sum = parts[0].reshape(states, width)
-    decay_sum = parts[1].reshape(states, width)
     input_total = smooth_eta * input_sum
     decay_total = smooth_eta * rate * decay_sum
     eta_grad = rate * input_sum
@@ -1815,18 +1829,18 @@
     return (
         block_out,
         grad_in,
-        parts[2],
+        parts[0],
         alpha_grad,
         damp_grad,
         beta_grad,
         eta_grad,
-        parts[3],
+        parts[1],
         value_grad,
         mix_grad,
-        parts[5].reshape(4, key_width),
-        parts[6],
+        parts[3].reshape(4, key_width),
+        parts[4],
         out_grad,
-        parts[4],
+        parts[2],
         feed_in_grad,
         feed_out_grad,
     )

time: 631 us -> 597 us (0.946)
  waiting for transfers between devices: 116 us -> 61 us
  starting transfers between devices: 63.2 us -> 44.4 us
  between operations: 2.55 us -> 15.8 us
  Pallas kernels: 311 us -> 323 us
  local copies, waits for them, and re-layouts: 40.1 us -> 50.6 us
    ppermute x45 -> x43, waiting for transfers between devices: 116 us -> 61 us  [send(): return lax.ppermute(value, AXES, self.pairs(move))]
    ppermute x45 -> x43, starting transfers between devices: 57.4 us -> 40.2 us  [send(): return lax.ppermute(value, AXES, self.pairs(move))]
    pallas_call x1, Pallas kernels: 22.2 us -> 34.4 us  [attend_back(): pl.pallas_call(ignoring(functools.partial(attend_back_body, total=total),...]
    reshape x0 -> x6, local copies, waits for them, and re-layouts: none -> 8.2 us  [the longest x2 2.66 us: layer(): parts.append(totals[start:start + item.shape[0]].reshape(-1))]
    pallas_call x1, Pallas kernels: 16.3 us -> 22.8 us  [attend(): pl.pallas_call(functools.partial(attend_body, total=total), grid_spec=plt...]
    pallas_call x2 -> x1, Pallas kernels: 19.8 us -> 15.1 us  [by_rows(): pl.pallas_call(ignoring(by_rows_body, 4, len(after)), grid_spec=pltpu.Pre...]
    unnamed x132 -> x122, local copies, waits for them, and re-layouts: 14.2 us -> 18.6 us
  transfers between devices with their start and end apart: 49 -> 48, of which waited for: 14 -> 14; matrix products, arithmetic and copies ran while one was open for 16% -> 22% of each run, Pallas kernels for 34% -> 40%
where the time goes in v3:
time: 597 us; the launch traced here: 586 us
  Pallas kernels  323 us (54%)
  matrix products  61.8 us (10%)
  waiting for transfers between devices  61 us (10%)
  local copies, waits for them, and re-layouts  50.6 us (8%)
  starting transfers between devices  44.4 us (7%)
  other arithmetic  29.5 us (5%)
  between operations  15.8 us (3%)
    pallas_call x1, Pallas kernels, feed(): pl.pallas_call(ignoring(feed_body, 8, len(after)), grid_spec=pltpu.Prefet...  68.6 us
    ppermute x43, waiting for transfers between devices, send(): return lax.ppermute(value, AXES, self.pairs(move))  61 us
    pallas_call x9, Pallas kernels, stage_sums(): pl.pallas_call(ignoring(functools.partial(stage_body, shapes=shapes), len...  50.3 us
    dot_general x4, matrix products, mm(): return jnp.dot(a, b, preferred_element_type=f32)  42.6 us
    pallas_call x2, Pallas kernels, back_scan(): pl.pallas_call(ignoring(back_scan_body, 13, len(after)), grid_spec=pltpu....  41 us
    ppermute x43, starting transfers between devices, send(): return lax.ppermute(value, AXES, self.pairs(move))  40.2 us
    pallas_call x1, Pallas kernels, attend_back(): pl.pallas_call(ignoring(functools.partial(attend_back_body, total=total),...  34.4 us
    pallas_call x1, Pallas kernels, attend(): pl.pallas_call(functools.partial(attend_body, total=total), grid_spec=plt...  22.8 us
  transfers between devices with their start and end apart: 48, of which 14 were waited for; matrix products, arithmetic and copies ran while one was open for 22% of the time, Pallas kernels for 40%

profile of v3, /device:TPU:0, one launch (start us, length us, event | category | flops | bytes accessed | tf_op | source)
XLA Modules:
  0.0 586.0 jit_solution(6018033551311914611)
XLA Ops:
  8.5 2.7 dynamic-slice_bitcast_fusion.3
  11.3 2.5 collective-permute-start.1
  17.0 3.1 collective-permute-start.6
  23.1 7.9 %slice.123.refs_5_ = bf16[1024,4096]{1,0:T(8,128)(2,1)} slice(bf16[1024,4224]{1,0:T(8,128)(2,1)} %param.30), slice={[0:1024], [128:4224]} | slice | bytes 16777216 | tf_op jit(solution)/shard_map/slice | solution.py:1636
  38.3 6.0 %bias.1 = (f32[9,256,256]{2,1,0:T(8,128)}, f32[9,256,256]{2,1,0:T(8,128)}) custom-call(s32[1]{0:T(128)S(6)} %convert_element_type.55.flag_ref, f32[8,1,512]{2,1,0:T(1,128)} %copy.62.back_row, f32[8,1,512]{2,1,0:T(1,128)} %broadcast_in_dim.54.front_row), custom_call_target="tpu_custom_call" | custom-call | tf_op jit(solution)/shard_map/bias/pallas_call | solution.py:808
  44.3 17.8 %collective-permute-done.1 = bf16[512,1024]{1,0:T(8,128)(2,1)} collective-permute-done((bf16[512,1024]{1,0:T(8,128)(2,1)S(1)}, bf16[512,1024]{1,0:T(8,128)(2,1)}, u32[]{:S(2)}, u32[]{:S(2)}) %collective-permute-start.1) | collective-permute-done | bytes 1048608 | tf_op jit(solution)/shard_map/ppermute | solution.py:1367
  62.1 3.1 pad_maximum_fusion.refs_0_.x_ref.refs_2_
  65.1 8.6 %front_ends.1 = (bf16[2,512,1024]{2,1,0:T(8,128)(2,1)}, f32[2,16,8,128]{3,2,1,0:T(8,128)}) custom-call(bf16[2,512,1024]{2,1,0:T(8,128)(2,1)} %pad_maximum_fusion.refs_0_.x_ref.refs_2_, f32[1,1024]{1,0:T(1,128)} %bitcast.369, f32[16,8,128]{2,1,0:T(8,128)} %bitcast.308, f32[9,256,256]{2,1,0:T(8,128)} %get-tuple-element.106.refs_3_.refs_4_, ...), custom_call_target="tpu_custom_call" | custom-call | flops 1 | bytes 1 | tf_op jit(solution)/shard_map/front_ends/pallas_call | solution.py:99
  73.8 12.8 %multiply_convert_fusion = (bf16[1024,2048]{1,0:T(8,128)(2,1)}, bf16[1024,2048]{1,0:T(8,128)(2,1)}) fusion(bf16[1024,1024]{1,0:T(8,128)(2,1)} %bitcast.382, bf16[1024,2048]{1,0:T(8,128)(2,1)} %refs_6_.3), kind=kOutput, calls=%fused_computation.1 | convolution fusion | flops 4315938816 | bytes 14680064 | tf_op jit(solution)/shard_map/dot_general | solution.py:1560
  87.8 18.3 %front_scan.1 = (f32[2,512,1024]{2,1,0:T(8,128)}, bf16[2,512,1024]{2,1,0:T(8,128)(2,1)}, f32[2,8,16,8,128]{4,3,2,1,0:T(8,128)}) custom-call(s32[9]{0:T(128)} %concatenate.42.table_ref.refs_0_, bf16[2,512,1024]{2,1,0:T(8,128)(2,1)} %pad_maximum_fusion.refs_0_.x_ref.refs_2_, f32[1,1024]{1,0:T(1,128)} %bitcast.370, f32[16,8,128]{2,1,0:T(8,128)} %bitcast.309, ...), custom_call_target="tpu_custom_call" | custom-call | flops 99999997952 | bytes 1 | tf_op jit(solution)/shard_map/front_scan/pallas_call | solution.py:186
  106.1 3.3 add_convert_fusion
  109.6 14.2 %convolution_convert_fusion.refs_5_.refs_6_ = bf16[1024,4096]{1,0:T(8,128)(2,1)} fusion(bf16[1024,1024]{1,0:T(8,128)(2,1)S(1)} %bitcast.245, bf16[1024,4224]{1,0:T(8,128)(2,1)} %param.30), kind=kOutput, calls=%fused_computation.4 | convolution fusion | flops 8594128896 | bytes 18874368 | tf_op jit(solution)/shard_map/dot_general | solution.py:1560
  124.5 22.8 %attend.1 = (bf16[2,512,2048]{2,1,0:T(8,128)(2,1)}, bf16[2,512,2048]{2,1,0:T(8,128)(2,1)}, f32[2,512,1]{2,1,0:T(8,128)}) custom-call(s32[9]{0:T(128)} %concatenate.42.table_ref.refs_0_, bf16[2,512,128]{2,1,0:T(8,128)(2,1)} %bitcast.333, f32[9,256,256]{2,1,0:T(8,128)} %get-tuple-element.107.refs_4_.bias_ref, bf16[2,512,4096]{2,1,0:T(8,128)(2,1)} %bitcast.240, ...), custom_call_target="tpu_custom_call" | custom-call | flops 1 | bytes 1 | tf_op jit(solution)/shard_map/attend/pallas_call | solution.py:545
  149.1 12.2 %fusion.21 = (f32[1024]{0:T(1024)S(1)}, f32[1024,1024]{1,0:T(8,128)S(1)}, f32[1024,1024]{1,0:T(8,128)}) fusion(bf16[1024,4096]{1,0:T(8,128)(2,1)} %convolution_convert_fusion.refs_5_.refs_6_, bf16[2,512,1024]{2,1,0:T(8,128)(2,1)S(1)} %copy-done.1, bf16[1024,2048]{1,0:T(8,128)(2,1)} %bitcast.257, bf16[2048,1024]{1,0:T(8,128)(2,1)} %refs_9_.1), kind=kOutput, calls=%fused_computation.89 | convolution fusion | flops 4310694912 | bytes 23072768 | tf_op jit(solution)/shard_map/dot_general | solution.py:1560
  164.0 68.6 %feed.1 = (bf16[512,1024]{1,0:T(8,128)(2,1)}, bf16[512,1024]{1,0:T(8,128)(2,1)}, f32[1024,1024]{1,0:T(8,128)}, bf16[4,1024,512]{2,1,0:T(8,128)(2,1)}, bf16[4,102...) custom-call(s32[8]{0:T(128)} %broadcast_select_fusion.1.refs_0_, ...), custom_call_target="tpu_custom_call" | custom-call | flops 1 | bytes 1 | tf_op jit(solution)/shard_map/feed/pallas_call | solution.py:1062
  232.6 2.0 collective-permute-start.9
  235.1 20.4 %gate.1 = (f32[1024,1024]{1,0:T(8,128)}, bf16[1024,4096]{1,0:T(8,128)(2,1)}, bf16[1024,2048]{1,0:T(8,128)(2,1)}, f32[1,1024]{1,0:T(1,128)}) custom-call(f32[1024,1024]{1,0:T(8,128)} %get-tuple-element.114.refs_0_, bf16[512,1024]{1,0:T(8,128)(2,1)} %collective-permute-done.6.refs_3_.refs_1_, bf16[512,1024]{1,0:T(8,128)(2,1)} %collective-permute-done.7.refs_4_.refs_2_, ...), custom_call_target="tpu_custom_call" | custom-call | flops 99999997952 | bytes 1 | tf_op jit(solution)/shard_map/gate/pallas_call | solution.py:900
  255.5 9.3 %stage_sums.9 = (bf16[1,2048,512]{2,1,0:T(8,128)(2,1)}, bf16[1,2048,512]{2,1,0:T(8,128)(2,1)}, bf16[1,2048,512]{2,1,0:T(8,128)(2,1)}, bf16[1,2048,512]{2,1,0:T(8,128)(2,1)}) custom-call(bf16[1,2,2048,512]{3,2,1,0:T(8,128)(2,1)} %bitcast.251, bf16[1,2,2048,512]{3,2,1,0:T(8,128)(2,1)} %bitcast.40.refs_1_, bf16[1,2,2048,512]{3,2,1,0:T(8,128)(2,1)} %bitcast.252, ...), custom_call_target="tpu_custom_call" | custom-call | flops 1 | bytes 1 | tf_op jit(solution)/shard_map/stage_sums/pallas_call | solution.py:1337
  266.8 15.1 %by_rows.1 = (bf16[4,1,128,4096]{3,2,1,0:T(8,128)(2,1)}, bf16[4,1,128,4096]{3,2,1,0:T(8,128)(2,1)}) custom-call(s32[8]{0:T(128)} %broadcast_select_fusion.1.refs_0_, s32[1]{0:T(128)} %constant.119.clone.1.refs_1_, bf16[1024,1024]{1,0:T(8,128)(2,1)} %bitcast.244, bf16[1024,4096]{1,0:T(8,128)(2,1)} %get-tuple-element.116.refs_3_.refs_2_, ...), custom_call_target="tpu_custom_call" | custom-call | flops 99999997952 | bytes 1 | tf_op jit(solution)/shard_map/by_rows/pallas_call | solution.py:1200
  281.9 11.9 %by_columns.1 = (bf16[4,1024,256]{2,1,0:T(8,128)(2,1)}, bf16[4,1024,256]{2,1,0:T(8,128)(2,1)}) custom-call(s32[8]{0:T(128)} %broadcast_select_fusion.1.refs_0_, s32[4]{0:T(128)} %get-tuple-element.105.refs_1_, bf16[1024,4096]{1,0:T(8,128)(2,1)} %get-tuple-element.116.refs_3_.refs_2_, bf16[1024,2048]{1,0:T(8,128)(2,1)} %bitcast.258, ...), custom_call_target="tpu_custom_call" | custom-call | flops 1 | bytes 1 | tf_op jit(solution)/shard_map/by_columns/pallas_call | solution.py:1144
  295.7 4.2 stage_sums.10
  301.9 34.4 %attend_back.1 = (f32[2,512,128]{2,1,0:T(8,128)}, bf16[2,512,128]{2,1,0:T(8,128)(2,1)}, bf16[2,512,2048]{2,1,0:T(8,128)(2,1)}, bf16[2,512,2176]{2,1,0:T(8,128)(2,1)}, f32[8,1,512]{2,1,0:T(1,128)}) custom-call(s32[9]{0:T(128)} %concatenate.42.table_ref.refs_0_, bf16[2,512,128]{2,1,0:T(8,128)(2,1)} %bitcast.334, bf16[2,512,2048]{2,1,0:T(8,128)(2,1)} %bitcast.250, ...), custom_call_target="tpu_custom_call" | custom-call | flops 99999997952 | bytes 1 | tf_op jit(solution)/shard_map/attend_back/pallas_call | solution.py:721
  340.7 6.7 %stage_sums.11 = (bf16[1,1024,512]{2,1,0:T(8,128)(2,1)}, bf16[1,1024,512]{2,1,0:T(8,128)(2,1)}, bf16[1,512,512]{2,1,0:T(8,128)(2,1)}, bf16[1,512,512]{2,1,0:T(8,...) custom-call(bf16[1,2,1024,512]{3,2,1,0:T(8,128)(2,1)} %bitcast.386, ...), custom_call_target="tpu_custom_call" | custom-call | flops 99999997952 | bytes 1 | tf_op jit(solution)/shard_map/stage_sums/pallas_call | solution.py:1337
  349.0 2.0 collective-permute-start.19
  351.0 15.7 %value_back.1 = (f32[1024,1024]{1,0:T(8,128)}, bf16[4,4,128,512]{3,2,1,0:T(8,128)(2,1)}, bf16[4,4,128,512]{3,2,1,0:T(8,128)(2,1)}) custom-call(s32[8]{0:T(128)} %broadcast_select_fusion.1.refs_0_, s32[4]{0:T(128)} %get-tuple-element.105.refs_1_, bf16[1024,1024]{1,0:T(8,128)(2,1)} %bitcast.383, bf16[1024,2048]{1,0:T(8,128)(2,1)} %bitcast.417, ...), custom_call_target="tpu_custom_call" | custom-call | flops 99999997952 | bytes 1 | tf_op jit(solution)/shard_map/value_back/pallas_call | solution.py:1271
  366.7 7.5 %collective-permute-done.17 = bf16[1,1,1024,512]{3,2,1,0:T(8,128)(2,1)S(1)} collective-permute-done((bf16[1,1,1024,512]{3,2,1,0:T(8,128)(2,1)}, bf16[1,1,1024,512]{3,2,1,0:T(8,128)(2,1)S(1)}, u32[]{:S(2)}, u32[]{:S(2)}) %collective-permute-start.17) | collective-permute-done | bytes 1048608 | tf_op jit(solution)/shard_map/ppermute | solution.py:1367
  375.7 8.3 %stage_sums.12 = (bf16[1,512,512]{2,1,0:T(8,128)(2,1)}, bf16[1,512,512]{2,1,0:T(8,128)(2,1)}, bf16[1,256,512]{2,1,0:T(8,128)(2,1)}, bf16[1,256,512]{2,1,0:T(8,12...) custom-call(bf16[1,2,512,512]{3,2,1,0:T(8,128)(2,1)} %bitcast.287, ...), custom_call_target="tpu_custom_call" | custom-call | flops 1 | bytes 1 | tf_op jit(solution)/shard_map/stage_sums/pallas_call | solution.py:1337
  385.5 2.3 collective-permute-start.23
  392.7 16.1 %fusion.6 = f32[1024,1024]{1,0:T(8,128)} fusion(f32[2,512,1024]{2,1,0:T(8,128)S(1)} %copy-done.55, f32[1024,1024]{1,0:T(8,128)S(1)} %fusion.15, bf16[1024,4096]{1,0:T(8,128)(2,1)} %get-tuple-element.116.refs_3_.refs_2_, bf16[1024,4224]{1,0:T(8,128)(2,1)} %param.30), kind=kOutput, calls=%fused_computation.15 | convolution fusion | flops 8599371776 | bytes 29360128 | tf_op jit(solution)/shard_map/dot_general | solution.py:1564
  408.8 8.1 %back_ends.1.refs_8_ = f32[2,16,8,128]{3,2,1,0:T(8,128)} custom-call(f32[2,512,1024]{2,1,0:T(8,128)} %bitcast.253, f32[16,8,128]{2,1,0:T(8,128)} %bitcast.310, bf16[1,2,256,512]{3,2,1,0:T(8,128)(2,1)} %bitcast.317, bf16[1,2,256,512]{3,2,1,0:T(8,128)(2,1)} %bitcast.274, bf16[1,1,256,512]{3,2,1,0:T(8,128)(2,1)} %bitcast.346, ...), custom_call_target="tpu_custom_call" | custom-call | flops 1 | bytes 1 | tf_op jit(solution)/shard_map/back_ends/pallas_call | solution.py:249
  420.9 6.7 %stage_sums.13 = (f32[1,256,512]{2,1,0:T(8,128)}, bf16[1,256,512]{2,1,0:T(8,128)(2,1)}, bf16[1,256,512]{2,1,0:T(8,128)(2,1)}, bf16[1,128,4096]{2,1,0:T(8,128)(2,...) custom-call(bf16[1,1,256,512]{3,2,1,0:T(8,128)(2,1)} %bitcast.292, ...), custom_call_target="tpu_custom_call" | custom-call | flops 1 | bytes 1 | tf_op jit(solution)/shard_map/stage_sums/pallas_call | solution.py:1337
  429.8 20.4 %back_scan.2 = (bf16[512,1024]{1,0:T(8,128)(2,1)}, f32[16,8,128]{2,1,0:T(8,128)}, f32[16,8,128]{2,1,0:T(8,128)}, f32[1,1024]{1,0:T(1,128)}, f32[1,1024]{1,0:T(1,128)}) custom-call(s32[9]{0:T(128)} %concatenate.42.table_ref.refs_0_, s32[1]{0:T(128)} %constant.119.clone.1.refs_1_, bf16[2,512,1024]{2,1,0:T(8,128)(2,1)} %pad_maximum_fusion.refs_0_.x_ref.refs_2_, ...), custom_call_target="tpu_custom_call" | custom-call | flops 99999997952 | bytes 1 | tf_op jit(solution)/shard_map/back_scan/pallas_call | solution.py:390
  451.8 3.1 collective-permute-done.27.refs_3_
  456.3 5.0 stage_sums.14
  469.6 20.6 %back_scan.3 = (bf16[512,1024]{1,0:T(8,128)(2,1)}, f32[16,8,128]{2,1,0:T(8,128)}, f32[16,8,128]{2,1,0:T(8,128)}, f32[1,1024]{1,0:T(1,128)}, f32[1,1024]{1,0:T(1,128)}) custom-call(s32[9]{0:T(128)} %concatenate.42.table_ref.refs_0_, s32[1]{0:T(128)} %constant.118.clone.1.refs_1_, bf16[2,512,1024]{2,1,0:T(8,128)(2,1)} %pad_maximum_fusion.refs_0_.x_ref.refs_2_, ...), custom_call_target="tpu_custom_call" | custom-call | flops 99999997952 | bytes 1 | tf_op jit(solution)/shard_map/back_scan/pallas_call | solution.py:390
  494.5 3.8 stage_sums.15
  502.4 2.3 collective-permute-start.38
  506.9 2.5 collective-permute-done.38
  509.4 3.7 collective-permute-done.37
  524.4 2.0 copy.75
  526.3 2.3 collective-permute-start.45
  540.3 8.7 %collective-permute-done.44.refs_3_ = bf16[1,1,256,256]{3,2,1,0:T(8,128)(2,1)} collective-permute-done((bf16[1,1,256,256]{3,2,1,0:T(8,128)(2,1)}, bf16[1,1,256,256]{3,2,1,0:T(8,128)(2,1)}, u32[]{:S(2)}, u32[]{:S(2)}) %collective-permute-start.44) | collective-permute-done | bytes 131104 | tf_op jit(solution)/shard_map/ppermute | solution.py:1367
  548.9 7.0 %collective-permute-done.45.refs_5_ = bf16[1,2,128,512]{3,2,1,0:T(8,128)(2,1)} collective-permute-done((bf16[1,2,128,512]{3,2,1,0:T(8,128)(2,1)}, bf16[1,2,128,512]{3,2,1,0:T(8,128)(2,1)}, u32[]{:S(2)}, u32[]{:S(2)}) %collective-permute-start.45) | collective-permute-done | bytes 262176 | tf_op jit(solution)/shard_map/ppermute | solution.py:1367
  556.0 5.5 collective-permute-done.43.refs_1_
  562.4 3.4 stage_sums.16
  567.7 2.1 copy.69
  571.2 2.3 maximum_convert_fusion
  575.9 2.8 stage_sums.17
  (269 shorter events, 98.2 us)
Async XLA Ops:
  7.2 444.6 %reduce-scatter.2.cloned.1.call-start = ((), (), s32[]{:S(2)}) async-start(), calls=%async_computation.1 | async-start | bytes 294912 | tf_op jit(solution)/shard_map/reduce_scatter | solution.py:1740
  8.0 28.2 %collective-permute-start.2 = (f32[2]{0:T(128)S(1)}, f32[2]{0:T(128)S(1)}, u32[]{:S(2)}, u32[]{:S(2)}) collective-permute-start(f32[2]{0:T(128)S(1)} %convert_element_type.54), channel_id=1, source_target_pairs={{0,4},{1,5},{2,6},{3,7},{4,0},{5,1},{6,2},{7,3},{8,12},{9,13},{10,... | collective-permute-start | bytes 32 | tf_op jit(solution)/shard_map/ppermute | solution.py:1367
  11.2 33.1 %collective-permute-start = (bf16[512,1024]{1,0:T(8,128)(2,1)}, bf16[512,1024]{1,0:T(8,128)(2,1)}, u32[]{:S(2)}, u32[]{:S(2)}) collective-permute-start(bf16[512,1024]{1,0:T(8,128)(2,1)} %get-tuple-element.274), channel_id=1, source_target_pairs={{0,4},{1,0},{2,5},{3,1},{4,6},{5,2},{6,7},{7,3},{8,12},{9,8},{10,1... | collective-permute-start | bytes 3145736 | tf_op jit(solution)/shard_map/ppermute | solution.py:1367
  11.3 50.8 %collective-permute-start.1 = (bf16[512,1024]{1,0:T(8,128)(2,1)S(1)}, bf16[512,1024]{1,0:T(8,128)(2,1)}, u32[]{:S(2)}, u32[]{:S(2)}) collective-permute-start(bf16[512,1024]{1,0:T(8,128)(2,1)S(1)} %get-tuple-element.275), channel_id=1, source_target_pairs={{0,1},{1,5},{2,0},{3,4},{4,3},{5,7},{6,2},{7,6},{8,9},{9,13},{10,8... | collective-permute-start | bytes 3145736 | tf_op jit(solution)/shard_map/ppermute | solution.py:1367
  15.3 148.6 %collective-permute-start.7 = (bf16[512,1024]{1,0:T(8,128)(2,1)}, bf16[512,1024]{1,0:T(8,128)(2,1)}, u32[]{:S(2)}, u32[]{:S(2)}) collective-permute-start(bf16[512,1024]{1,0:T(8,128)(2,1)} %get-tuple-element.272), channel_id=1, source_target_pairs={{0,1},{1,5},{2,0},{3,4},{4,3},{5,7},{6,2},{7,6},{8,9},{9,13},{10,8... | collective-permute-start | bytes 3145736 | tf_op jit(solution)/shard_map/ppermute | solution.py:1367
  17.0 146.9 %collective-permute-start.6 = (bf16[512,1024]{1,0:T(8,128)(2,1)}, bf16[512,1024]{1,0:T(8,128)(2,1)}, u32[]{:S(2)}, u32[]{:S(2)}) collective-permute-start(bf16[512,1024]{1,0:T(8,128)(2,1)} %get-tuple-element.273), channel_id=1, source_target_pairs={{0,4},{1,0},{2,5},{3,1},{4,6},{5,2},{6,7},{7,3},{8,12},{9,8},{10,1... | collective-permute-start | bytes 3145736 | tf_op jit(solution)/shard_map/ppermute | solution.py:1367
  73.7 13.3 %collective-permute-start.3 = (f32[2,16,8,128]{3,2,1,0:T(8,128)}, f32[2,16,8,128]{3,2,1,0:T(8,128)S(1)}, u32[]{:S(2)}, u32[]{:S(2)}) collective-permute-start(f32[2,16,8,128]{3,2,1,0:T(8,128)} %get-tuple-element.108), channel_id=1, source_target_pairs={{0,4},{1,5},{2,6},{3,7},{4,0},{5,1},{6,2},{7,3},{8,12},{9,13},{10,... | collective-permute-start | bytes 393224 | tf_op jit(solution)/shard_map/ppermute | solution.py:1367
  86.6 37.2 %collective-permute-start.5 = (bf16[2,512,2048]{2,1,0:T(8,128)(2,1)}, bf16[2,512,2048]{2,1,0:T(8,128)(2,1)}, u32[]{:S(2)}, u32[]{:S(2)}) collective-permute-start(bf16[2,512,2048]{2,1,0:T(8,128)(2,1)} %bitcast.29.v_own.refs_7_), channel_id=1, source_target_pairs={{0,4},{1,5},{2,6},{3,7},{4,0},{5,1},{6,2},{7,3},{8,12},{9,13},{10,... | collective-permute-start | bytes 12582920 | tf_op jit(solution)/shard_map/ppermute | solution.py:1367
  109.5 14.3 %collective-permute-start.4 = (bf16[2,512,128]{2,1,0:T(8,128)(2,1)S(1)}, bf16[2,512,128]{2,1,0:T(8,128)(2,1)S(1)}, u32[]{:S(2)}, u32[]{:S(2)}) collective-permute-start(bf16[2,512,128]{2,1,0:T(8,128)(2,1)S(1)} %bitcast.330), channel_id=1, source_target_pairs={{0,4},{1,5},{2,6},{3,7},{4,0},{5,1},{6,2},{7,3},{8,12},{9,13},{10,... | collective-permute-start | bytes 786440 | tf_op jit(solution)/shard_map/ppermute | solution.py:1367
  232.6 61.5 %collective-permute-start.8 = (bf16[512,1024]{1,0:T(8,128)(2,1)}, bf16[512,1024]{1,0:T(8,128)(2,1)}, u32[]{:S(2)}, u32[]{:S(2)}) collective-permute-start(bf16[512,1024]{1,0:T(8,128)(2,1)} %get-tuple-element.112), channel_id=1, source_target_pairs={{1,0},{5,1},{0,2},{4,3},{3,4},{7,5},{2,6},{6,7},{9,8},{13,9},{8,10... | collective-permute-start | bytes 3145736 | tf_op jit(solution)/shard_map/ppermute | solution.py:1396
  232.6 61.8 %collective-permute-start.9 = (bf16[512,1024]{1,0:T(8,128)(2,1)}, bf16[512,1024]{1,0:T(8,128)(2,1)}, u32[]{:S(2)}, u32[]{:S(2)}) collective-permute-start(bf16[512,1024]{1,0:T(8,128)(2,1)} %get-tuple-element.113), channel_id=1, source_target_pairs={{4,0},{0,1},{5,2},{1,3},{6,4},{2,5},{7,6},{3,7},{12,8},{8,9},{13,1... | collective-permute-start | bytes 3145736 | tf_op jit(solution)/shard_map/ppermute | solution.py:1396
  234.6 20.9 %collective-permute-start.10 = (bf16[1,4,1024,512]{3,2,1,0:T(8,128)(2,1)}, bf16[1,4,1024,512]{3,2,1,0:T(8,128)(2,1)}, u32[]{:S(2)}, u32[]{:S(2)}) collective-permute-start(bf16[1,4,1024,512]{3,2,1,0:T(8,128)(2,1)} %bitcast.381), channel_id=1, source_target_pairs={{0,4},{1,5},{2,6},{3,7},{4,0},{5,1},{6,2},{7,3},{8,12},{9,13},{10,... | collective-permute-start | bytes 12582920 | tf_op jit(solution)/shard_map/ppermute | solution.py:1367
  235.0 20.5 %collective-permute-start.11 = (bf16[1,4,1024,512]{3,2,1,0:T(8,128)(2,1)}, bf16[1,4,1024,512]{3,2,1,0:T(8,128)(2,1)}, u32[]{:S(2)}, u32[]{:S(2)}) collective-permute-start(bf16[1,4,1024,512]{3,2,1,0:T(8,128)(2,1)} %bitcast.380), channel_id=1, source_target_pairs={{0,4},{1,5},{2,6},{3,7},{4,0},{5,1},{6,2},{7,3},{8,12},{9,13},{10,... | collective-permute-start | bytes 12582920 | tf_op jit(solution)/shard_map/ppermute | solution.py:1367
  264.8 29.5 %collective-permute-start.12 = (bf16[1,2,1024,512]{3,2,1,0:T(8,128)(2,1)}, bf16[1,2,1024,512]{3,2,1,0:T(8,128)(2,1)S(1)}, u32[]{:S(2)}, u32[]{:S(2)}) collective-permute-start(bf16[1,2,1024,512]{3,2,1,0:T(8,128)(2,1)} %bitcast.389), channel_id=1, source_target_pairs={{0,8},{1,9},{2,10},{3,11},{4,20},{5,21},{6,22},{7,23},{8,0},{9,1},... | collective-permute-start | bytes 6291464 | tf_op jit(solution)/shard_map/ppermute | solution.py:1367
  266.7 73.0 %collective-permute-start.14 = (bf16[1,2,1024,512]{3,2,1,0:T(8,128)(2,1)}, bf16[1,2,1024,512]{3,2,1,0:T(8,128)(2,1)}, u32[]{:S(2)}, u32[]{:S(2)}) collective-permute-start(bf16[1,2,1024,512]{3,2,1,0:T(8,128)(2,1)} %bitcast.387), channel_id=1, source_target_pairs={{0,8},{1,9},{2,10},{3,11},{4,20},{5,21},{6,22},{7,23},{8,0},{9,1},... | collective-permute-start | bytes 6291464 | tf_op jit(solution)/shard_map/ppermute | solution.py:1367
  293.8 45.9 %collective-permute-start.16 = (bf16[1,4,1024,256]{3,2,1,0:T(8,128)(2,1)}, bf16[1,4,1024,256]{3,2,1,0:T(8,128)(2,1)}, u32[]{:S(2)}, u32[]{:S(2)}) collective-permute-start(bf16[1,4,1024,256]{3,2,1,0:T(8,128)(2,1)} %bitcast.271), channel_id=1, source_target_pairs={{0,4},{1,5},{2,6},{3,7},{4,0},{5,1},{6,2},{7,3},{8,12},{9,13},{10,... | collective-permute-start | bytes 6291464 | tf_op jit(solution)/shard_map/ppermute | solution.py:1367
  294.0 80.7 %collective-permute-start.20 = (bf16[1,4,128,4096]{3,2,1,0:T(8,128)(2,1)}, bf16[1,4,128,4096]{3,2,1,0:T(8,128)(2,1)}, u32[]{:S(2)}, u32[]{:S(2)}) collective-permute-start(bf16[1,4,128,4096]{3,2,1,0:T(8,128)(2,1)} %bitcast.256), channel_id=1, source_target_pairs={{0,4},{1,5},{2,6},{3,7},{4,0},{5,1},{6,2},{7,3},{8,12},{9,13},{10,... | collective-permute-start | bytes 12582920 | tf_op jit(solution)/shard_map/ppermute | solution.py:1367
  299.9 39.7 %collective-permute-start.15 = (bf16[1,1,1024,512]{3,2,1,0:T(8,128)(2,1)}, bf16[1,1,1024,512]{3,2,1,0:T(8,128)(2,1)S(1)}, u32[]{:S(2)}, u32[]{:S(2)}) collective-permute-start(bf16[1,1,1024,512]{3,2,1,0:T(8,128)(2,1)} %bitcast.398), channel_id=1, source_target_pairs={{0,16},{1,17},{2,18},{3,19},{4,12},{5,13},{6,14},{7,15},{8,24},{9,... | collective-permute-start | bytes 3145736 | tf_op jit(solution)/shard_map/ppermute | solution.py:1367
  337.2 13.8 %collective-permute-start.13 = (bf16[2,512,2176]{2,1,0:T(8,128)(2,1)}, bf16[2,512,2176]{2,1,0:T(8,128)(2,1)}, u32[]{:S(2)}, u32[]{:S(2)}) collective-permute-start(bf16[2,512,2176]{2,1,0:T(8,128)(2,1)} %get-tuple-element.134), channel_id=1, source_target_pairs={{0,4},{1,5},{2,6},{3,7},{4,0},{5,1},{6,2},{7,3},{8,12},{9,13},{10,... | collective-permute-start | bytes 13369352 | tf_op jit(solution)/shard_map/ppermute | solution.py:1367
  347.4 19.3 %collective-permute-start.18 = (bf16[1,2,256,512]{3,2,1,0:T(8,128)(2,1)}, bf16[1,2,256,512]{3,2,1,0:T(8,128)(2,1)S(1)}, u32[]{:S(2)}, u32[]{:S(2)}) collective-permute-start(bf16[1,2,256,512]{3,2,1,0:T(8,128)(2,1)} %bitcast.406), channel_id=1, source_target_pairs={{0,1},{1,0},{2,3},{3,2},{4,5},{5,4},{6,7},{7,6},{8,9},{9,8},{10,11... | collective-permute-start | bytes 1572872 | tf_op jit(solution)/shard_map/ppermute | solution.py:1367
  349.0 25.3 %collective-permute-start.17 = (bf16[1,1,1024,512]{3,2,1,0:T(8,128)(2,1)}, bf16[1,1,1024,512]{3,2,1,0:T(8,128)(2,1)S(1)}, u32[]{:S(2)}, u32[]{:S(2)}) collective-permute-start(bf16[1,1,1024,512]{3,2,1,0:T(8,128)(2,1)} %bitcast.402), channel_id=1, source_target_pairs={{0,16},{1,17},{2,18},{3,19},{4,12},{5,13},{6,14},{7,15},{8,24},{9,... | collective-permute-start | bytes 3145736 | tf_op jit(solution)/shard_map/ppermute | solution.py:1367
  349.0 25.7 %collective-permute-start.19 = (bf16[1,2,1024,256]{3,2,1,0:T(8,128)(2,1)}, bf16[1,2,1024,256]{3,2,1,0:T(8,128)(2,1)S(1)}, u32[]{:S(2)}, u32[]{:S(2)}) collective-permute-start(bf16[1,2,1024,256]{3,2,1,0:T(8,128)(2,1)} %bitcast.400), channel_id=1, source_target_pairs={{0,8},{1,9},{2,10},{3,11},{4,20},{5,21},{6,22},{7,23},{8,0},{9,1},... | collective-permute-start | bytes 3145736 | tf_op jit(solution)/shard_map/ppermute | solution.py:1367
  384.1 36.1 %collective-permute-start.22 = (bf16[1,1,256,512]{3,2,1,0:T(8,128)(2,1)}, bf16[1,1,256,512]{3,2,1,0:T(8,128)(2,1)}, u32[]{:S(2)}, u32[]{:S(2)}) collective-permute-start(bf16[1,1,256,512]{3,2,1,0:T(8,128)(2,1)} %bitcast.345), channel_id=1, source_target_pairs={{0,2},{1,3},{2,0},{3,1},{4,6},{5,7},{6,4},{7,5},{8,10},{9,11},{10,... | collective-permute-start | bytes 786440 | tf_op jit(solution)/shard_map/ppermute | solution.py:1367
  385.5 34.6 %collective-permute-start.23 = (bf16[1,2,256,512]{3,2,1,0:T(8,128)(2,1)}, bf16[1,2,256,512]{3,2,1,0:T(8,128)(2,1)S(1)}, u32[]{:S(2)}, u32[]{:S(2)}) collective-permute-start(bf16[1,2,256,512]{3,2,1,0:T(8,128)(2,1)} %bitcast.316), channel_id=1, source_target_pairs={{0,1},{1,0},{2,3},{3,2},{4,5},{5,4},{6,7},{7,6},{8,9},{9,8},{10,11... | collective-permute-start | bytes 1572872 | tf_op jit(solution)/shard_map/ppermute | solution.py:1367
  387.8 32.4 %collective-permute-start.25 = (bf16[1,4,512,512]{3,2,1,0:T(8,128)(2,1)}, bf16[1,4,512,512]{3,2,1,0:T(8,128)(2,1)}, u32[]{:S(2)}, u32[]{:S(2)}) collective-permute-start(bf16[1,4,512,512]{3,2,1,0:T(8,128)(2,1)} %bitcast.384), channel_id=1, source_target_pairs={{0,4},{1,5},{2,6},{3,7},{4,0},{5,1},{6,2},{7,3},{8,12},{9,13},{10,... | collective-permute-start | bytes 6291464 | tf_op jit(solution)/shard_map/ppermute | solution.py:1367
  387.8 32.4 %collective-permute-start.24 = (bf16[1,2,128,4096]{3,2,1,0:T(8,128)(2,1)}, bf16[1,2,128,4096]{3,2,1,0:T(8,128)(2,1)}, u32[]{:S(2)}, u32[]{:S(2)}) collective-permute-start(bf16[1,2,128,4096]{3,2,1,0:T(8,128)(2,1)} %bitcast.276), channel_id=1, source_target_pairs={{0,8},{1,9},{2,10},{3,11},{4,20},{5,21},{6,22},{7,23},{8,0},{9,1},... | collective-permute-start | bytes 6291464 | tf_op jit(solution)/shard_map/ppermute | solution.py:1367
  416.9 1.7 collective-permute-start.21
  418.6 33.2 %collective-permute-start.29 = (bf16[1,1,1024,256]{3,2,1,0:T(8,128)(2,1)}, bf16[1,1,1024,256]{3,2,1,0:T(8,128)(2,1)}, u32[]{:S(2)}, u32[]{:S(2)}) collective-permute-start(bf16[1,1,1024,256]{3,2,1,0:T(8,128)(2,1)} %bitcast.79.refs_6_), channel_id=1, source_target_pairs={{0,16},{1,17},{2,18},{3,19},{4,12},{5,13},{6,14},{7,15},{8,24},{9,... | collective-permute-start | bytes 1572872 | tf_op jit(solution)/shard_map/ppermute | solution.py:1367
  427.6 24.2 %collective-permute-start.26 = (bf16[1,1,256,512]{3,2,1,0:T(8,128)(2,1)}, bf16[1,1,256,512]{3,2,1,0:T(8,128)(2,1)S(1)}, u32[]{:S(2)}, u32[]{:S(2)}) collective-permute-start(bf16[1,1,256,512]{3,2,1,0:T(8,128)(2,1)} %bitcast.410), channel_id=1, source_target_pairs={{0,2},{1,3},{2,0},{3,1},{4,6},{5,7},{6,4},{7,5},{8,10},{9,11},{10,... | collective-permute-start | bytes 786440 | tf_op jit(solution)/shard_map/ppermute | solution.py:1367
  427.7 27.2 %collective-permute-start.27 = (bf16[1,1,128,4096]{3,2,1,0:T(8,128)(2,1)}, bf16[1,1,128,4096]{3,2,1,0:T(8,128)(2,1)S(1)}, u32[]{:S(2)}, u32[]{:S(2)}) collective-permute-start(bf16[1,1,128,4096]{3,2,1,0:T(8,128)(2,1)} %bitcast.396), channel_id=1, source_target_pairs={{0,16},{1,17},{2,18},{3,19},{4,12},{5,13},{6,14},{7,15},{8,24},{9,... | collective-permute-start | bytes 3145736 | tf_op jit(solution)/shard_map/ppermute | solution.py:1367
  429.2 25.7 %collective-permute-start.28 = (bf16[1,2,512,512]{3,2,1,0:T(8,128)(2,1)}, bf16[1,2,512,512]{3,2,1,0:T(8,128)(2,1)S(1)}, u32[]{:S(2)}, u32[]{:S(2)}) collective-permute-start(bf16[1,2,512,512]{3,2,1,0:T(8,128)(2,1)} %bitcast.394), channel_id=1, source_target_pairs={{0,8},{1,9},{2,10},{3,11},{4,20},{5,21},{6,22},{7,23},{8,0},{9,1},... | collective-permute-start | bytes 3145736 | tf_op jit(solution)/shard_map/ppermute | solution.py:1367
  450.3 43.2 %collective-permute-start.31 = (bf16[512,1024]{1,0:T(8,128)(2,1)}, bf16[512,1024]{1,0:T(8,128)(2,1)S(1)}, u32[]{:S(2)}, u32[]{:S(2)}) collective-permute-start(bf16[512,1024]{1,0:T(8,128)(2,1)} %get-tuple-element.164.refs_8_), channel_id=1, source_target_pairs={{4,0},{0,1},{5,2},{1,3},{6,4},{2,5},{7,6},{3,7},{12,8},{8,9},{13,1... | collective-permute-start | bytes 3145736 | tf_op jit(solution)/shard_map/ppermute | solution.py:1396
  461.3 32.1 %collective-permute-start.33 = (bf16[1,2,256,256]{3,2,1,0:T(8,128)(2,1)}, bf16[1,2,256,256]{3,2,1,0:T(8,128)(2,1)S(1)}, u32[]{:S(2)}, u32[]{:S(2)}) collective-permute-start(bf16[1,2,256,256]{3,2,1,0:T(8,128)(2,1)} %bitcast.408), channel_id=1, source_target_pairs={{0,1},{1,0},{2,3},{3,2},{4,5},{5,4},{6,7},{7,6},{8,9},{9,8},{10,11... | collective-permute-start | bytes 786440 | tf_op jit(solution)/shard_map/ppermute | solution.py:1367
  462.5 31.0 %collective-permute-start.34 = (bf16[1,1,512,512]{3,2,1,0:T(8,128)(2,1)}, bf16[1,1,512,512]{3,2,1,0:T(8,128)(2,1)}, u32[]{:S(2)}, u32[]{:S(2)}) collective-permute-start(bf16[1,1,512,512]{3,2,1,0:T(8,128)(2,1)} %bitcast.404), channel_id=1, source_target_pairs={{0,16},{1,17},{2,18},{3,19},{4,12},{5,13},{6,14},{7,15},{8,24},{9,... | collective-permute-start | bytes 1572872 | tf_op jit(solution)/shard_map/ppermute | solution.py:1367
  467.6 24.8 %collective-permute-start.32 = (bf16[1,2,128,1056]{2,3,1,0:T(8,128)(2,1)}, bf16[1,2,128,1056]{2,3,1,0:T(8,128)(2,1)S(1)}, u32[]{:S(2)}, u32[]{:S(2)}) collective-permute-start(bf16[1,2,128,1056]{2,3,1,0:T(8,128)(2,1)} %get-tuple-element.276), channel_id=1, source_target_pairs={{0,1},{1,0},{2,3},{3,2},{4,5},{5,4},{6,7},{7,6},{8,9},{9,8},{10,11... | collective-permute-start | bytes 1622024 | tf_op jit(solution)/shard_map/ppermute | solution.py:1367
  500.0 1.5 collective-permute-start.35
  502.4 6.9 %collective-permute-start.38 = (f32[160,128]{1,0:T(8,128)S(1)}, f32[160,128]{1,0:T(8,128)S(1)}, u32[]{:S(2)}, u32[]{:S(2)}) collective-permute-start(f32[160,128]{1,0:T(8,128)S(1)} %add.181), channel_id=1, source_target_pairs={{0,3},{1,2},{2,1},{3,0},{4,7},{5,6},{6,5},{7,4},{8,11},{9,10},{10,... | collective-permute-start | bytes 245768 | tf_op jit(solution)/shard_map/ppermute | solution.py:1367
  504.7 8.4 %collective-permute-start.37 = (f32[160,128]{1,0:T(8,128)S(1)}, f32[160,128]{1,0:T(8,128)S(1)}, u32[]{:S(2)}, u32[]{:S(2)}) collective-permute-start(f32[160,128]{1,0:T(8,128)S(1)} %add.181), channel_id=1, source_target_pairs={{0,2},{1,3},{2,0},{3,1},{4,6},{5,7},{6,4},{7,5},{8,10},{9,11},{10,... | collective-permute-start | bytes 245768 | tf_op jit(solution)/shard_map/ppermute | solution.py:1367
  505.2 7.9 %collective-permute-start.36 = (f32[160,128]{1,0:T(8,128)S(1)}, f32[160,128]{1,0:T(8,128)S(1)}, u32[]{:S(2)}, u32[]{:S(2)}) collective-permute-start(f32[160,128]{1,0:T(8,128)S(1)} %add.181), channel_id=1, source_target_pairs={{0,1},{1,0},{2,3},{3,2},{4,5},{5,4},{6,7},{7,6},{8,9},{9,8},{10,11... | collective-permute-start | bytes 245768 | tf_op jit(solution)/shard_map/ppermute | solution.py:1367
  513.1 6.2 %collective-permute-start.41 = (f32[160,128]{1,0:T(8,128)S(1)}, f32[160,128]{1,0:T(8,128)S(1)}, u32[]{:S(2)}, u32[]{:S(2)}) collective-permute-start(f32[160,128]{1,0:T(8,128)S(1)} %add_add_fusion.1), channel_id=1, source_target_pairs={{0,24},{1,25},{2,26},{3,27},{4,28},{5,29},{6,30},{7,31},{8,16},{9,... | collective-permute-start | bytes 245768 | tf_op jit(solution)/shard_map/ppermute | solution.py:1367
  514.6 5.1 collective-permute-start.40
  516.0 4.4 collective-permute-start.39
  518.4 43.1 %collective-permute-start.30 = (bf16[512,1024]{1,0:T(8,128)(2,1)S(1)}, bf16[512,1024]{1,0:T(8,128)(2,1)S(1)}, u32[]{:S(2)}, u32[]{:S(2)}) collective-permute-start(bf16[512,1024]{1,0:T(8,128)(2,1)S(1)} %copy-done.12), channel_id=1, source_target_pairs={{1,0},{5,1},{0,2},{4,3},{3,4},{7,5},{2,6},{6,7},{9,8},{13,9},{8,10... | collective-permute-start | bytes 3145736 | tf_op jit(solution)/shard_map/ppermute | solution.py:1396
  521.1 8.2 %collective-permute-start.42 = (f32[160,128]{1,0:T(8,128)}, f32[160,128]{1,0:T(8,128)}, u32[]{:S(2)}, u32[]{:S(2)}) collective-permute-start(f32[160,128]{1,0:T(8,128)} %add_add_fusion), channel_id=1, source_target_pairs={{0,4},{1,5},{2,6},{3,7},{4,0},{5,1},{6,2},{7,3},{8,12},{9,13},{10,... | collective-permute-start | bytes 245768 | tf_op jit(solution)/shard_map/ppermute | solution.py:1367
  526.3 22.6 %collective-permute-start.44 = (bf16[1,1,256,256]{3,2,1,0:T(8,128)(2,1)}, bf16[1,1,256,256]{3,2,1,0:T(8,128)(2,1)}, u32[]{:S(2)}, u32[]{:S(2)}) collective-permute-start(bf16[1,1,256,256]{3,2,1,0:T(8,128)(2,1)} %bitcast.328), channel_id=1, source_target_pairs={{0,2},{1,3},{2,0},{3,1},{4,6},{5,7},{6,4},{7,5},{8,10},{9,11},{10,... | collective-permute-start | bytes 393224 | tf_op jit(solution)/shard_map/ppermute | solution.py:1367
  526.3 29.6 %collective-permute-start.45 = (bf16[1,2,128,512]{3,2,1,0:T(8,128)(2,1)}, bf16[1,2,128,512]{3,2,1,0:T(8,128)(2,1)}, u32[]{:S(2)}, u32[]{:S(2)}) collective-permute-start(bf16[1,2,128,512]{3,2,1,0:T(8,128)(2,1)} %bitcast.302), channel_id=1, source_target_pairs={{0,1},{1,0},{2,3},{3,2},{4,5},{5,4},{6,7},{7,6},{8,9},{9,8},{10,11... | collective-permute-start | bytes 786440 | tf_op jit(solution)/shard_map/ppermute | solution.py:1367
  528.6 32.8 %collective-permute-start.43 = (bf16[1,1,128,1056]{3,2,1,0:T(8,128)(2,1)S(1)}, bf16[1,1,128,1056]{3,2,1,0:T(8,128)(2,1)}, u32[]{:S(2)}, u32[]{:S(2)}) collective-permute-start(bf16[1,1,128,1056]{3,2,1,0:T(8,128)(2,1)S(1)} %bitcast.282), channel_id=1, source_target_pairs={{0,2},{1,3},{2,0},{3,1},{4,6},{5,7},{6,4},{7,5},{8,10},{9,11},{10,... | collective-permute-start | bytes 811016 | tf_op jit(solution)/shard_map/ppermute | solution.py:1367
  565.9 9.4 %collective-permute-start.46 = (bf16[1,1,128,512]{3,2,1,0:T(8,128)(2,1)}, bf16[1,1,128,512]{3,2,1,0:T(8,128)(2,1)S(1)}, u32[]{:S(2)}, u32[]{:S(2)}) collective-permute-start(bf16[1,1,128,512]{3,2,1,0:T(8,128)(2,1)} %bitcast.350), channel_id=1, source_target_pairs={{0,2},{1,3},{2,0},{3,1},{4,6},{5,7},{6,4},{7,5},{8,10},{9,11},{10,... | collective-permute-start | bytes 393224 | tf_op jit(solution)/shard_map/ppermute | solution.py:1367
  (56 other events, 725.5 us)
Sparse Core Ops, SparseCore 0:
  418.7 32.0 reduce-scatter.1

commit v4 on v3

--- a/solution.py
+++ b/solution.py
@@ -1487,29 +1487,36 @@
                 s.send([held[0]], [held[1]])
         return [part for held in out for part in held]
 
-    def sum_seq(self, held):
+    def reduce_all(self, sent, held, after):
+        core = lax.axis_index("dp") % 2
+        held = held + self.send(sent, lambda d, z: (d ^ 1, z))
+        for bit in range(1, self.dp.bit_length() - 1):
+            held = held + self.send(held, lambda d, z: (d ^ (1 << bit), z))
+        held = later(held, after)
         low = 1
         while low < self.seq:
-            others = [low] if 2 * low >= self.seq else [low, 2 * low, 3 * low]
             mine = held
-            for other in others:
+            for other in [low] if 2 * low >= self.seq else [low, 2 * low, 3 * low]:
                 held = held + self.send(mine, lambda d, z: (d, z ^ other))
-            low *= 4
-        return held
-
-    def reduce_all(self, sent, held):
-        core = lax.axis_index("dp") % 2
-        held = held + self.send(sent, lambda d, z: (d ^ 1, z))
-        held = self.sum_seq(held)
-        low = 2
-        while low < self.dp:
-            others = [low] if 2 * low >= self.dp else [low, 2 * low, 3 * low]
-            mine = held
-            for other in others:
-                held = held + self.send(mine, lambda d, z: (d ^ other, z))
             low *= 4
         other = self.send(held, lambda d, z: (d ^ 1, z))
         return jnp.where(core == 0, jnp.stack([held, other]), jnp.stack([other, held]))
+
+
+def later_body(value, out):
+    out[...] = value[...]
+
+
+def later(value, after):
+    inside = pl.BlockSpec(memory_space=pltpu.VMEM)
+    return pl.pallas_call(
+        ignoring(later_body, 1, len(after)),
+        in_specs=[inside] + [pl.BlockSpec(memory_space=pl.ANY)] * len(after),
+        out_specs=inside,
+        out_shape=jax.ShapeDtypeStruct(value.shape, value.dtype),
+        name="later",
+        cost_estimate=BRIEF,
+    )(value, *after)
 
 
 def pack_body(core_ref, qx_a, qx_b, qs_a, qs_b, rest_ref, sent, held):
@@ -1594,7 +1601,7 @@
     tokens = slots * chunk_rows
     total = layout.seq
     seq_length = relative_bias.shape[0] // 2
-    block = min(64, chunk_rows)
+    block = min(128, chunk_rows)
     core = lax.axis_index("dp") % 2
     z = lax.axis_index("seq")
 
@@ -1738,12 +1745,13 @@
     ).astype(bf16)
     shared_grad = mm_tn(mixed, grad_shared).astype(bf16)
     shared_grad = lax.psum_scatter(shared_grad, "dp", scatter_dimension=0, tiled=True)
-    after = layout.turn((in_sum, out_sum, proj_sum, mix_sum), (grad_normed,))
+    after = layout.turn((in_sum, out_sum, mix_sum), (grad_normed,))
     value_sum = Sum(layout, (value_send, value_keep))
     grad_smooth = (mm_nt(grad_main, mix_main) + mm_nt(grad_shared, mix_shared)) * silu_slope(
         smoothed
     )
     grad_smooth = grad_smooth.reshape(slots, chunk_rows, width)
+    after = layout.turn((value_sum, proj_sum), (grad_smooth,))
     back = back_ends(grad_smooth, decay_slab, after=after)
     back_all = jnp.concatenate([back, layout.gather(back)])
     after = layout.turn((out_sum, in_sum, mix_sum, value_sum), (back,))
@@ -1780,8 +1788,8 @@
     home_second = layout.homeward(second[0], 1)
     after = (second[0], home_first)
     sums = (mix_sum, proj_sum, value_sum, out_sum, in_sum)
-    turned = layout.turn(sums, after)
-    after = (*turned, home_second)
+    turned = layout.turn(sums, after, cost=LONG)
+    after = layout.turn(sums, (*turned, home_second))
     while any(v.total is None for v in sums):
         after = layout.turn(sums, after)
     grad_in = layout.gathered([home_first, home_second]).astype(f32)
@@ -1810,7 +1818,9 @@
     small = [v.reshape(-1, 128) for v in small]
     rest = jnp.concatenate(small)
     rest = jnp.pad(rest, ((0, -rest.shape[0] % 16), (0, 0)))
-    totals = layout.reduce_all(*pack(core, first[1:3], second[1:3], rest, after=turned))
+    totals = layout.reduce_all(
+        *pack(core, first[1:3], second[1:3], rest, after=turned), after=after
+    )
     totals = totals.reshape(-1, 128)
     count = states * width // 128
     input_sum = totals[:count].reshape(states, width)

time: 597 us -> 582 us (0.975)
  local copies, waits for them, and re-layouts: 50.6 us -> 41 us
    unnamed x122 -> x142, local copies, waits for them, and re-layouts: 18.6 us -> 15.9 us
    ppermute x43 -> x42, waiting for transfers between devices: 61 us -> 60.3 us  [send(): return lax.ppermute(value, AXES, self.pairs(move))]
    ppermute x43 -> x42, starting transfers between devices: 40.2 us -> 40.3 us  [send(): return lax.ppermute(value, AXES, self.pairs(move))]
  transfers between devices with their start and end apart: 48 -> 47, of which waited for: 14 -> 11; matrix products, arithmetic and copies ran while one was open for 22% -> 21% of each run, Pallas kernels for 40% -> 43%
where the time goes in v4:
time: 582 us; the launch traced here: 570 us
  Pallas kernels  321 us (55%)
  matrix products  62 us (11%)
  waiting for transfers between devices  60.4 us (10%)
  starting transfers between devices  42.9 us (7%)
  local copies, waits for them, and re-layouts  41 us (7%)
  other arithmetic  27.3 us (5%)
  between operations  16 us (3%)
    pallas_call x1, Pallas kernels, feed(): pl.pallas_call(ignoring(feed_body, 8, len(after)), grid_spec=pltpu.Prefet...  68.5 us
    ppermute x42, waiting for transfers between devices, send(): return lax.ppermute(value, AXES, self.pairs(move))  60.3 us
    pallas_call x9, Pallas kernels, stage_sums(): pl.pallas_call(ignoring(functools.partial(stage_body, shapes=shapes), len...  49.7 us
    dot_general x4, matrix products, mm(): return jnp.dot(a, b, preferred_element_type=f32)  42.6 us
    pallas_call x2, Pallas kernels, back_scan(): pl.pallas_call(ignoring(back_scan_body, 13, len(after)), grid_spec=pltpu....  40.5 us
    ppermute x42, starting transfers between devices, send(): return lax.ppermute(value, AXES, self.pairs(move))  40.3 us
    pallas_call x1, Pallas kernels, attend_back(): pl.pallas_call(ignoring(functools.partial(attend_back_body, total=total),...  34.4 us
    pallas_call x1, Pallas kernels, attend(): pl.pallas_call(functools.partial(attend_body, total=total), grid_spec=plt...  22.8 us
  transfers between devices with their start and end apart: 47, of which 11 were waited for; matrix products, arithmetic and copies ran while one was open for 21% of the time, Pallas kernels for 43%

profile of v4, /device:TPU:0, one launch (start us, length us, event | category | flops | bytes accessed | tf_op | source)
XLA Modules:
  0.0 570.3 jit_solution(4259073625481548445)
XLA Ops:
  8.5 2.7 dynamic-slice_bitcast_fusion.3
  11.2 2.5 collective-permute-start.1
  17.0 3.1 collective-permute-start.6
  21.9 8.0 %slice.123.refs_5_ = bf16[1024,4096]{1,0:T(8,128)(2,1)} slice(bf16[1024,4224]{1,0:T(8,128)(2,1)} %param.30), slice={[0:1024], [128:4224]} | slice | bytes 16777216 | tf_op jit(solution)/shard_map/slice | solution.py:1643
  38.2 6.0 %bias.1 = (f32[9,256,256]{2,1,0:T(8,128)}, f32[9,256,256]{2,1,0:T(8,128)}) custom-call(s32[1]{0:T(128)S(6)} %convert_element_type.55.flag_ref, f32[8,1,512]{2,1,0:T(1,128)} %copy.62.back_row, f32[8,1,512]{2,1,0:T(1,128)} %broadcast_in_dim.54.front_row), custom_call_target="tpu_custom_call" | custom-call | tf_op jit(solution)/shard_map/bias/pallas_call | solution.py:808
  44.3 17.8 %collective-permute-done.1 = bf16[512,1024]{1,0:T(8,128)(2,1)} collective-permute-done((bf16[512,1024]{1,0:T(8,128)(2,1)S(1)}, bf16[512,1024]{1,0:T(8,128)(2,1)}, u32[]{:S(2)}, u32[]{:S(2)}) %collective-permute-start.1) | collective-permute-done | bytes 1048608 | tf_op jit(solution)/shard_map/ppermute | solution.py:1367
  62.0 3.1 pad_maximum_fusion.refs_0_.x_ref.refs_2_
  65.1 8.6 %front_ends.1 = (bf16[2,512,1024]{2,1,0:T(8,128)(2,1)}, f32[2,16,8,128]{3,2,1,0:T(8,128)}) custom-call(bf16[2,512,1024]{2,1,0:T(8,128)(2,1)} %pad_maximum_fusion.refs_0_.x_ref.refs_2_, f32[1,1024]{1,0:T(1,128)} %bitcast.364, f32[16,8,128]{2,1,0:T(8,128)} %bitcast.301, f32[9,256,256]{2,1,0:T(8,128)} %get-tuple-element.107.refs_3_.refs_4_, ...), custom_call_target="tpu_custom_call" | custom-call | flops 1 | bytes 1 | tf_op jit(solution)/shard_map/front_ends/pallas_call | solution.py:99
  73.7 12.9 %multiply_convert_fusion = (bf16[1024,2048]{1,0:T(8,128)(2,1)}, bf16[1024,2048]{1,0:T(8,128)(2,1)}) fusion(bf16[1024,1024]{1,0:T(8,128)(2,1)} %bitcast.377, bf16[1024,2048]{1,0:T(8,128)(2,1)} %refs_6_.3), kind=kOutput, calls=%fused_computation.1 | convolution fusion | flops 4315938816 | bytes 14680064 | tf_op jit(solution)/shard_map/dot_general | solution.py:1567
  87.8 15.9 %front_scan.1 = (f32[2,512,1024]{2,1,0:T(8,128)}, bf16[2,512,1024]{2,1,0:T(8,128)(2,1)}, f32[2,4,16,8,128]{4,3,2,1,0:T(8,128)}) custom-call(s32[9]{0:T(128)} %concatenate.42.table_ref.refs_0_, bf16[2,512,1024]{2,1,0:T(8,128)(2,1)} %pad_maximum_fusion.refs_0_.x_ref.refs_2_, f32[1,1024]{1,0:T(1,128)} %bitcast.365, f32[16,8,128]{2,1,0:T(8,128)} %bitcast.302, ...), custom_call_target="tpu_custom_call" | custom-call | flops 99999997952 | bytes 1 | tf_op jit(solution)/shard_map/front_scan/pallas_call | solution.py:186
  103.7 3.3 add_convert_fusion
  107.0 14.3 %convolution_convert_fusion.refs_5_.refs_6_ = bf16[1024,4096]{1,0:T(8,128)(2,1)} fusion(bf16[1024,1024]{1,0:T(8,128)(2,1)S(1)} %bitcast.248, bf16[1024,4224]{1,0:T(8,128)(2,1)} %param.30), kind=kOutput, calls=%fused_computation.4 | convolution fusion | flops 8594128896 | bytes 18874368 | tf_op jit(solution)/shard_map/dot_general | solution.py:1567
  122.1 22.8 %attend.1 = (bf16[2,512,2048]{2,1,0:T(8,128)(2,1)}, bf16[2,512,2048]{2,1,0:T(8,128)(2,1)}, f32[2,512,1]{2,1,0:T(8,128)}) custom-call(s32[9]{0:T(128)} %concatenate.42.table_ref.refs_0_, bf16[2,512,128]{2,1,0:T(8,128)(2,1)} %bitcast.331, f32[9,256,256]{2,1,0:T(8,128)} %get-tuple-element.108.refs_4_.bias_ref, bf16[2,512,4096]{2,1,0:T(8,128)(2,1)} %bitcast.245, ...), custom_call_target="tpu_custom_call" | custom-call | flops 1 | bytes 1 | tf_op jit(solution)/shard_map/attend/pallas_call | solution.py:545
  146.7 12.1 %fusion.21 = (f32[1024]{0:T(1024)S(1)}, f32[1024,1024]{1,0:T(8,128)S(1)}, f32[1024,1024]{1,0:T(8,128)}) fusion(bf16[1024,4096]{1,0:T(8,128)(2,1)} %convolution_convert_fusion.refs_5_.refs_6_, bf16[2,512,1024]{2,1,0:T(8,128)(2,1)S(1)} %copy-done.1, bf16[1024,2048]{1,0:T(8,128)(2,1)} %bitcast.259, bf16[2048,1024]{1,0:T(8,128)(2,1)} %refs_9_.1), kind=kOutput, calls=%fused_computation.88 | convolution fusion | flops 4310694912 | bytes 23072768 | tf_op jit(solution)/shard_map/dot_general | solution.py:1567
  159.5 1.9 multiply_convert_fusion.2.refs_2_
  161.4 68.5 %feed.1 = (bf16[512,1024]{1,0:T(8,128)(2,1)}, bf16[512,1024]{1,0:T(8,128)(2,1)}, f32[1024,1024]{1,0:T(8,128)}, bf16[4,1024,512]{2,1,0:T(8,128)(2,1)}, bf16[4,102...) custom-call(s32[8]{0:T(128)} %broadcast_select_fusion.1.refs_0_, ...), custom_call_target="tpu_custom_call" | custom-call | flops 1 | bytes 1 | tf_op jit(solution)/shard_map/feed/pallas_call | solution.py:1062
  230.0 2.0 collective-permute-start.9
  232.5 20.4 %gate.1 = (f32[1024,1024]{1,0:T(8,128)}, bf16[1024,4096]{1,0:T(8,128)(2,1)}, bf16[1024,2048]{1,0:T(8,128)(2,1)}, f32[1,1024]{1,0:T(1,128)}) custom-call(f32[1024,1024]{1,0:T(8,128)} %get-tuple-element.115.refs_0_, bf16[512,1024]{1,0:T(8,128)(2,1)} %collective-permute-done.6.refs_3_.refs_1_, bf16[512,1024]{1,0:T(8,128)(2,1)} %collective-permute-done.7.refs_4_.refs_2_, ...), custom_call_target="tpu_custom_call" | custom-call | flops 99999997952 | bytes 1 | tf_op jit(solution)/shard_map/gate/pallas_call | solution.py:900
  252.9 9.3 %stage_sums.9 = (bf16[1,2048,512]{2,1,0:T(8,128)(2,1)}, bf16[1,2048,512]{2,1,0:T(8,128)(2,1)}, bf16[1,2048,512]{2,1,0:T(8,128)(2,1)}, bf16[1,2048,512]{2,1,0:T(8,128)(2,1)}) custom-call(bf16[1,2,2048,512]{3,2,1,0:T(8,128)(2,1)} %bitcast.252, bf16[1,2,2048,512]{3,2,1,0:T(8,128)(2,1)} %bitcast.40.refs_1_, bf16[1,2,2048,512]{3,2,1,0:T(8,128)(2,1)} %bitcast.253, ...), custom_call_target="tpu_custom_call" | custom-call | flops 1 | bytes 1 | tf_op jit(solution)/shard_map/stage_sums/pallas_call | solution.py:1337
  262.2 2.0 collective-permute-start.14
  264.2 15.2 %by_rows.1 = (bf16[4,1,128,4096]{3,2,1,0:T(8,128)(2,1)}, bf16[4,1,128,4096]{3,2,1,0:T(8,128)(2,1)}) custom-call(s32[8]{0:T(128)} %broadcast_select_fusion.1.refs_0_, s32[1]{0:T(128)} %constant.119.clone.1.refs_1_, bf16[1024,1024]{1,0:T(8,128)(2,1)} %bitcast.247, bf16[1024,4096]{1,0:T(8,128)(2,1)} %get-tuple-element.117.refs_3_.refs_2_, ...), custom_call_target="tpu_custom_call" | custom-call | flops 99999997952 | bytes 1 | tf_op jit(solution)/shard_map/by_rows/pallas_call | solution.py:1200
  279.4 11.9 %by_columns.1 = (bf16[4,1024,256]{2,1,0:T(8,128)(2,1)}, bf16[4,1024,256]{2,1,0:T(8,128)(2,1)}) custom-call(s32[8]{0:T(128)} %broadcast_select_fusion.1.refs_0_, s32[4]{0:T(128)} %get-tuple-element.106.refs_1_, bf16[1024,4096]{1,0:T(8,128)(2,1)} %get-tuple-element.117.refs_3_.refs_2_, bf16[1024,2048]{1,0:T(8,128)(2,1)} %bitcast.260, ...), custom_call_target="tpu_custom_call" | custom-call | flops 1 | bytes 1 | tf_op jit(solution)/shard_map/by_columns/pallas_call | solution.py:1144
  293.1 4.2 stage_sums.10
  298.8 34.4 %attend_back.1 = (f32[2,512,128]{2,1,0:T(8,128)}, bf16[2,512,128]{2,1,0:T(8,128)(2,1)}, bf16[2,512,2048]{2,1,0:T(8,128)(2,1)}, bf16[2,512,2176]{2,1,0:T(8,128)(2,1)}, f32[8,1,512]{2,1,0:T(1,128)}) custom-call(s32[9]{0:T(128)} %concatenate.42.table_ref.refs_0_, bf16[2,512,128]{2,1,0:T(8,128)(2,1)} %bitcast.332, bf16[2,512,2048]{2,1,0:T(8,128)(2,1)} %bitcast.251, ...), custom_call_target="tpu_custom_call" | custom-call | flops 99999997952 | bytes 1 | tf_op jit(solution)/shard_map/attend_back/pallas_call | solution.py:721
  334.4 6.7 %stage_sums.11 = (bf16[1,1024,512]{2,1,0:T(8,128)(2,1)}, bf16[1,1024,512]{2,1,0:T(8,128)(2,1)}, bf16[1,512,512]{2,1,0:T(8,128)(2,1)}, bf16[1,512,512]{2,1,0:T(8,...) custom-call(bf16[1,2,1024,512]{3,2,1,0:T(8,128)(2,1)} %bitcast.381, ...), custom_call_target="tpu_custom_call" | custom-call | flops 99999997952 | bytes 1 | tf_op jit(solution)/shard_map/stage_sums/pallas_call | solution.py:1337
  341.8 2.3 collective-permute-start.18
  344.1 15.8 %value_back.1 = (f32[1024,1024]{1,0:T(8,128)}, bf16[4,4,128,512]{3,2,1,0:T(8,128)(2,1)}, bf16[4,4,128,512]{3,2,1,0:T(8,128)(2,1)}) custom-call(s32[8]{0:T(128)} %broadcast_select_fusion.1.refs_0_, s32[4]{0:T(128)} %get-tuple-element.106.refs_1_, bf16[1024,1024]{1,0:T(8,128)(2,1)} %bitcast.378, bf16[1024,2048]{1,0:T(8,128)(2,1)} %bitcast.419, ...), custom_call_target="tpu_custom_call" | custom-call | flops 99999997952 | bytes 1 | tf_op jit(solution)/shard_map/value_back/pallas_call | solution.py:1271
  359.9 6.1 %collective-permute-done.20 = bf16[1,1,1024,512]{3,2,1,0:T(8,128)(2,1)S(1)} collective-permute-done((bf16[1,1,1024,512]{3,2,1,0:T(8,128)(2,1)}, bf16[1,1,1024,512]{3,2,1,0:T(8,128)(2,1)S(1)}, u32[]{:S(2)}, u32[]{:S(2)}) %collective-permute-start.20) | collective-permute-done | bytes 1048608 | tf_op jit(solution)/shard_map/ppermute | solution.py:1367
  367.0 7.3 %stage_sums.13 = (bf16[1,512,512]{2,1,0:T(8,128)(2,1)}, bf16[1,512,512]{2,1,0:T(8,128)(2,1)}, bf16[1,256,512]{2,1,0:T(8,128)(2,1)}, bf16[1,256,512]{2,1,0:T(8,12...) custom-call(bf16[1,2,512,512]{3,2,1,0:T(8,128)(2,1)} %bitcast.295, ...), custom_call_target="tpu_custom_call" | custom-call | flops 1 | bytes 1 | tf_op jit(solution)/shard_map/stage_sums/pallas_call | solution.py:1337
  374.2 3.4 collective-permute-start.25
  377.6 2.0 fusion.12
  381.3 16.3 %fusion.6 = f32[1024,1024]{1,0:T(8,128)} fusion(f32[2,512,1024]{2,1,0:T(8,128)S(1)} %copy-done.65, f32[1024,1024]{1,0:T(8,128)S(1)} %fusion.15, bf16[1024,4096]{1,0:T(8,128)(2,1)} %get-tuple-element.117.refs_3_.refs_2_, bf16[1024,4224]{1,0:T(8,128)(2,1)} %param.30), kind=kOutput, calls=%fused_computation.15 | convolution fusion | flops 8599371776 | bytes 29360128 | tf_op jit(solution)/shard_map/dot_general | solution.py:1571
  398.9 4.9 stage_sums.12
  404.3 2.1 collective-permute-start.24
  407.7 8.0 %back_ends.1.refs_8_ = f32[2,16,8,128]{3,2,1,0:T(8,128)} custom-call(f32[2,512,1024]{2,1,0:T(8,128)} %bitcast.240, f32[16,8,128]{2,1,0:T(8,128)} %bitcast.303, bf16[1,2,512,512]{3,2,1,0:T(8,128)(2,1)} %bitcast.287, bf16[1,2,512,512]{3,2,1,0:T(8,128)(2,1)} %bitcast.254, bf16[1,1,1024,256]{3,2,1,0:T(8,128)(2,1)} %bitcast.75.refs_4_, ...), custom_call_target="tpu_custom_call" | custom-call | flops 1 | bytes 1 | tf_op jit(solution)/shard_map/back_ends/pallas_call | solution.py:249
  418.1 3.1 collective-permute-done.23.refs_1_
  423.7 5.8 %stage_sums.14 = (f32[1,256,512]{2,1,0:T(8,128)}, bf16[1,256,512]{2,1,0:T(8,128)(2,1)}, bf16[1,256,512]{2,1,0:T(8,128)(2,1)}, bf16[1,128,4096]{2,1,0:T(8,128)(2,...) custom-call(bf16[1,1,256,512]{3,2,1,0:T(8,128)(2,1)} %bitcast.341, ...), custom_call_target="tpu_custom_call" | custom-call | flops 1 | bytes 1 | tf_op jit(solution)/shard_map/stage_sums/pallas_call | solution.py:1337
  433.3 20.2 %back_scan.2 = (bf16[512,1024]{1,0:T(8,128)(2,1)}, f32[16,8,128]{2,1,0:T(8,128)}, f32[16,8,128]{2,1,0:T(8,128)}, f32[1,1024]{1,0:T(1,128)}, f32[1,1024]{1,0:T(1,128)}) custom-call(s32[9]{0:T(128)} %concatenate.42.table_ref.refs_0_, s32[1]{0:T(128)} %constant.119.clone.1.refs_1_, bf16[2,512,1024]{2,1,0:T(8,128)(2,1)} %pad_maximum_fusion.refs_0_.x_ref.refs_2_, ...), custom_call_target="tpu_custom_call" | custom-call | flops 99999997952 | bytes 1 | tf_op jit(solution)/shard_map/back_scan/pallas_call | solution.py:390
  455.0 4.4 stage_sums.15
  467.4 20.3 %back_scan.3 = (bf16[512,1024]{1,0:T(8,128)(2,1)}, f32[16,8,128]{2,1,0:T(8,128)}, f32[16,8,128]{2,1,0:T(8,128)}, f32[1,1024]{1,0:T(1,128)}, f32[1,1024]{1,0:T(1,128)}) custom-call(s32[9]{0:T(128)} %concatenate.42.table_ref.refs_0_, s32[1]{0:T(128)} %constant.118.clone.1.refs_1_, bf16[2,512,1024]{2,1,0:T(8,128)(2,1)} %pad_maximum_fusion.refs_0_.x_ref.refs_2_, ...), custom_call_target="tpu_custom_call" | custom-call | flops 99999997952 | bytes 1 | tf_op jit(solution)/shard_map/back_scan/pallas_call | solution.py:390
  493.2 3.8 stage_sums.16
  514.3 23.3 %collective-permute-done.40.refs_3_ = bf16[1,1,256,256]{3,2,1,0:T(8,128)(2,1)} collective-permute-done((bf16[1,1,256,256]{3,2,1,0:T(8,128)(2,1)S(1)}, bf16[1,1,256,256]{3,2,1,0:T(8,128)(2,1)}, u32[]{:S(2)}, u32[]{:S(2)}) %collective-permute-start.40) | collective-permute-done | bytes 131104 | tf_op jit(solution)/shard_map/ppermute | solution.py:1367
  537.6 2.7 collective-permute-done.41.refs_5_
  541.3 3.3 stage_sums.17
  546.2 2.2 collective-permute-start.44
  548.4 2.2 collective-permute-start.42
  553.5 2.5 collective-permute-done.43
  556.3 2.3 maximum_convert_fusion
  (289 shorter events, 80.7 us)
Async XLA Ops:
  7.2 446.4 %reduce-scatter.2.cloned.1.call-start = ((), (), s32[]{:S(2)}) async-start(), calls=%async_computation.1 | async-start | bytes 294912 | tf_op jit(solution)/shard_map/reduce_scatter | solution.py:1747
  8.0 28.2 %collective-permute-start.2 = (f32[2]{0:T(128)S(1)}, f32[2]{0:T(128)S(1)}, u32[]{:S(2)}, u32[]{:S(2)}) collective-permute-start(f32[2]{0:T(128)S(1)} %convert_element_type.54), channel_id=1, source_target_pairs={{0,4},{1,5},{2,6},{3,7},{4,0},{5,1},{6,2},{7,3},{8,12},{9,13},{10,... | collective-permute-start | bytes 32 | tf_op jit(solution)/shard_map/ppermute | solution.py:1367
  11.2 33.1 %collective-permute-start = (bf16[512,1024]{1,0:T(8,128)(2,1)}, bf16[512,1024]{1,0:T(8,128)(2,1)}, u32[]{:S(2)}, u32[]{:S(2)}) collective-permute-start(bf16[512,1024]{1,0:T(8,128)(2,1)} %get-tuple-element.276), channel_id=1, source_target_pairs={{0,4},{1,0},{2,5},{3,1},{4,6},{5,2},{6,7},{7,3},{8,12},{9,8},{10,1... | collective-permute-start | bytes 3145736 | tf_op jit(solution)/shard_map/ppermute | solution.py:1367
  11.2 50.8 %collective-permute-start.1 = (bf16[512,1024]{1,0:T(8,128)(2,1)S(1)}, bf16[512,1024]{1,0:T(8,128)(2,1)}, u32[]{:S(2)}, u32[]{:S(2)}) collective-permute-start(bf16[512,1024]{1,0:T(8,128)(2,1)S(1)} %get-tuple-element.277), channel_id=1, source_target_pairs={{0,1},{1,5},{2,0},{3,4},{4,3},{5,7},{6,2},{7,6},{8,9},{9,13},{10,8... | collective-permute-start | bytes 3145736 | tf_op jit(solution)/shard_map/ppermute | solution.py:1367
  15.3 146.1 %collective-permute-start.7 = (bf16[512,1024]{1,0:T(8,128)(2,1)}, bf16[512,1024]{1,0:T(8,128)(2,1)}, u32[]{:S(2)}, u32[]{:S(2)}) collective-permute-start(bf16[512,1024]{1,0:T(8,128)(2,1)} %get-tuple-element.274), channel_id=1, source_target_pairs={{0,1},{1,5},{2,0},{3,4},{4,3},{5,7},{6,2},{7,6},{8,9},{9,13},{10,8... | collective-permute-start | bytes 3145736 | tf_op jit(solution)/shard_map/ppermute | solution.py:1367
  17.0 144.4 %collective-permute-start.6 = (bf16[512,1024]{1,0:T(8,128)(2,1)}, bf16[512,1024]{1,0:T(8,128)(2,1)}, u32[]{:S(2)}, u32[]{:S(2)}) collective-permute-start(bf16[512,1024]{1,0:T(8,128)(2,1)} %get-tuple-element.275), channel_id=1, source_target_pairs={{0,4},{1,0},{2,5},{3,1},{4,6},{5,2},{6,7},{7,3},{8,12},{9,8},{10,1... | collective-permute-start | bytes 3145736 | tf_op jit(solution)/shard_map/ppermute | solution.py:1367
  36.3 67.4 %copy-start.55 = (f32[128]{0:T(128)}, f32[128]{0:T(128)S(1)}, u32[]{:S(2)}) copy-start(f32[128]{0:T(128)S(1)} %get-tuple-element.307) | copy-start | bytes 1540
  73.7 13.4 %collective-permute-start.3 = (f32[2,16,8,128]{3,2,1,0:T(8,128)}, f32[2,16,8,128]{3,2,1,0:T(8,128)S(1)}, u32[]{:S(2)}, u32[]{:S(2)}) collective-permute-start(f32[2,16,8,128]{3,2,1,0:T(8,128)} %get-tuple-element.109), channel_id=1, source_target_pairs={{0,4},{1,5},{2,6},{3,7},{4,0},{5,1},{6,2},{7,3},{8,12},{9,13},{10,... | collective-permute-start | bytes 393224 | tf_op jit(solution)/shard_map/ppermute | solution.py:1367
  86.6 34.8 %collective-permute-start.5 = (bf16[2,512,2048]{2,1,0:T(8,128)(2,1)}, bf16[2,512,2048]{2,1,0:T(8,128)(2,1)}, u32[]{:S(2)}, u32[]{:S(2)}) collective-permute-start(bf16[2,512,2048]{2,1,0:T(8,128)(2,1)} %bitcast.29.v_own.refs_7_), channel_id=1, source_target_pairs={{0,4},{1,5},{2,6},{3,7},{4,0},{5,1},{6,2},{7,3},{8,12},{9,13},{10,... | collective-permute-start | bytes 12582920 | tf_op jit(solution)/shard_map/ppermute | solution.py:1367
  107.0 14.3 %collective-permute-start.4 = (bf16[2,512,128]{2,1,0:T(8,128)(2,1)S(1)}, bf16[2,512,128]{2,1,0:T(8,128)(2,1)S(1)}, u32[]{:S(2)}, u32[]{:S(2)}) collective-permute-start(bf16[2,512,128]{2,1,0:T(8,128)(2,1)S(1)} %bitcast.328), channel_id=1, source_target_pairs={{0,4},{1,5},{2,6},{3,7},{4,0},{5,1},{6,2},{7,3},{8,12},{9,13},{10,... | collective-permute-start | bytes 786440 | tf_op jit(solution)/shard_map/ppermute | solution.py:1367
  229.9 61.3 %collective-permute-start.8 = (bf16[512,1024]{1,0:T(8,128)(2,1)}, bf16[512,1024]{1,0:T(8,128)(2,1)}, u32[]{:S(2)}, u32[]{:S(2)}) collective-permute-start(bf16[512,1024]{1,0:T(8,128)(2,1)} %get-tuple-element.113), channel_id=1, source_target_pairs={{1,0},{5,1},{0,2},{4,3},{3,4},{7,5},{2,6},{6,7},{9,8},{13,9},{8,10... | collective-permute-start | bytes 3145736 | tf_op jit(solution)/shard_map/ppermute | solution.py:1396
  230.0 61.8 %collective-permute-start.9 = (bf16[512,1024]{1,0:T(8,128)(2,1)}, bf16[512,1024]{1,0:T(8,128)(2,1)}, u32[]{:S(2)}, u32[]{:S(2)}) collective-permute-start(bf16[512,1024]{1,0:T(8,128)(2,1)} %get-tuple-element.114), channel_id=1, source_target_pairs={{4,0},{0,1},{5,2},{1,3},{6,4},{2,5},{7,6},{3,7},{12,8},{8,9},{13,1... | collective-permute-start | bytes 3145736 | tf_op jit(solution)/shard_map/ppermute | solution.py:1396
  232.0 20.9 %collective-permute-start.10 = (bf16[1,4,1024,512]{3,2,1,0:T(8,128)(2,1)}, bf16[1,4,1024,512]{3,2,1,0:T(8,128)(2,1)}, u32[]{:S(2)}, u32[]{:S(2)}) collective-permute-start(bf16[1,4,1024,512]{3,2,1,0:T(8,128)(2,1)} %bitcast.376), channel_id=1, source_target_pairs={{0,4},{1,5},{2,6},{3,7},{4,0},{5,1},{6,2},{7,3},{8,12},{9,13},{10,... | collective-permute-start | bytes 12582920 | tf_op jit(solution)/shard_map/ppermute | solution.py:1367
  232.0 20.9 %collective-permute-start.11 = (bf16[1,4,1024,512]{3,2,1,0:T(8,128)(2,1)}, bf16[1,4,1024,512]{3,2,1,0:T(8,128)(2,1)}, u32[]{:S(2)}, u32[]{:S(2)}) collective-permute-start(bf16[1,4,1024,512]{3,2,1,0:T(8,128)(2,1)} %bitcast.375), channel_id=1, source_target_pairs={{0,4},{1,5},{2,6},{3,7},{4,0},{5,1},{6,2},{7,3},{8,12},{9,13},{10,... | collective-permute-start | bytes 12582920 | tf_op jit(solution)/shard_map/ppermute | solution.py:1367
  262.2 29.6 %collective-permute-start.12 = (bf16[1,2,1024,512]{3,2,1,0:T(8,128)(2,1)}, bf16[1,2,1024,512]{3,2,1,0:T(8,128)(2,1)S(1)}, u32[]{:S(2)}, u32[]{:S(2)}) collective-permute-start(bf16[1,2,1024,512]{3,2,1,0:T(8,128)(2,1)} %bitcast.385), channel_id=1, source_target_pairs={{0,8},{1,9},{2,10},{3,11},{4,20},{5,21},{6,22},{7,23},{8,0},{9,1},... | collective-permute-start | bytes 6291464 | tf_op jit(solution)/shard_map/ppermute | solution.py:1367
  262.2 71.2 %collective-permute-start.14 = (bf16[1,2,1024,512]{3,2,1,0:T(8,128)(2,1)}, bf16[1,2,1024,512]{3,2,1,0:T(8,128)(2,1)}, u32[]{:S(2)}, u32[]{:S(2)}) collective-permute-start(bf16[1,2,1024,512]{3,2,1,0:T(8,128)(2,1)} %bitcast.382), channel_id=1, source_target_pairs={{0,8},{1,9},{2,10},{3,11},{4,20},{5,21},{6,22},{7,23},{8,0},{9,1},... | collective-permute-start | bytes 6291464 | tf_op jit(solution)/shard_map/ppermute | solution.py:1367
  291.2 42.1 %collective-permute-start.16 = (bf16[1,4,1024,256]{3,2,1,0:T(8,128)(2,1)}, bf16[1,4,1024,256]{3,2,1,0:T(8,128)(2,1)}, u32[]{:S(2)}, u32[]{:S(2)}) collective-permute-start(bf16[1,4,1024,256]{3,2,1,0:T(8,128)(2,1)} %bitcast.271), channel_id=1, source_target_pairs={{0,4},{1,5},{2,6},{3,7},{4,0},{5,1},{6,2},{7,3},{8,12},{9,13},{10,... | collective-permute-start | bytes 6291464 | tf_op jit(solution)/shard_map/ppermute | solution.py:1367
  291.2 74.7 %collective-permute-start.22 = (bf16[1,4,128,4096]{3,2,1,0:T(8,128)(2,1)}, bf16[1,4,128,4096]{3,2,1,0:T(8,128)(2,1)}, u32[]{:S(2)}, u32[]{:S(2)}) collective-permute-start(bf16[1,4,128,4096]{3,2,1,0:T(8,128)(2,1)} %bitcast.258), channel_id=1, source_target_pairs={{0,4},{1,5},{2,6},{3,7},{4,0},{5,1},{6,2},{7,3},{8,12},{9,13},{10,... | collective-permute-start | bytes 12582920 | tf_op jit(solution)/shard_map/ppermute | solution.py:1367
  297.3 36.0 %collective-permute-start.15 = (bf16[1,1,1024,512]{3,2,1,0:T(8,128)(2,1)}, bf16[1,1,1024,512]{3,2,1,0:T(8,128)(2,1)S(1)}, u32[]{:S(2)}, u32[]{:S(2)}) collective-permute-start(bf16[1,1,1024,512]{3,2,1,0:T(8,128)(2,1)} %bitcast.396), channel_id=1, source_target_pairs={{0,16},{1,17},{2,18},{3,19},{4,12},{5,13},{6,14},{7,15},{8,24},{9,... | collective-permute-start | bytes 3145736 | tf_op jit(solution)/shard_map/ppermute | solution.py:1367
  333.3 10.8 %collective-permute-start.13 = (bf16[2,512,2176]{2,1,0:T(8,128)(2,1)}, bf16[2,512,2176]{2,1,0:T(8,128)(2,1)}, u32[]{:S(2)}, u32[]{:S(2)}) collective-permute-start(bf16[2,512,2176]{2,1,0:T(8,128)(2,1)} %get-tuple-element.135), channel_id=1, source_target_pairs={{0,4},{1,5},{2,6},{3,7},{4,0},{5,1},{6,2},{7,3},{8,12},{9,13},{10,... | collective-permute-start | bytes 13369352 | tf_op jit(solution)/shard_map/ppermute | solution.py:1367
  341.1 18.7 %collective-permute-start.21 = (bf16[1,2,256,512]{3,2,1,0:T(8,128)(2,1)}, bf16[1,2,256,512]{3,2,1,0:T(8,128)(2,1)S(1)}, u32[]{:S(2)}, u32[]{:S(2)}) collective-permute-start(bf16[1,2,256,512]{3,2,1,0:T(8,128)(2,1)} %bitcast.401), channel_id=1, source_target_pairs={{0,1},{1,0},{2,3},{3,2},{4,5},{5,4},{6,7},{7,6},{8,9},{9,8},{10,11... | collective-permute-start | bytes 1572872 | tf_op jit(solution)/shard_map/ppermute | solution.py:1367
  341.2 24.8 %collective-permute-start.20 = (bf16[1,1,1024,512]{3,2,1,0:T(8,128)(2,1)}, bf16[1,1,1024,512]{3,2,1,0:T(8,128)(2,1)S(1)}, u32[]{:S(2)}, u32[]{:S(2)}) collective-permute-start(bf16[1,1,1024,512]{3,2,1,0:T(8,128)(2,1)} %bitcast.393), channel_id=1, source_target_pairs={{0,16},{1,17},{2,18},{3,19},{4,12},{5,13},{6,14},{7,15},{8,24},{9,... | collective-permute-start | bytes 3145736 | tf_op jit(solution)/shard_map/ppermute | solution.py:1367
  341.8 55.9 %collective-permute-start.18 = (bf16[1,2,1024,256]{3,2,1,0:T(8,128)(2,1)}, bf16[1,2,1024,256]{3,2,1,0:T(8,128)(2,1)}, u32[]{:S(2)}, u32[]{:S(2)}) collective-permute-start(bf16[1,2,1024,256]{3,2,1,0:T(8,128)(2,1)} %bitcast.387), channel_id=1, source_target_pairs={{0,8},{1,9},{2,10},{3,11},{4,20},{5,21},{6,22},{7,23},{8,0},{9,1},... | collective-permute-start | bytes 3145736 | tf_op jit(solution)/shard_map/ppermute | solution.py:1367
  359.9 37.8 %collective-permute-start.17 = (bf16[1,4,512,512]{3,2,1,0:T(8,128)(2,1)}, bf16[1,4,512,512]{3,2,1,0:T(8,128)(2,1)S(1)}, u32[]{:S(2)}, u32[]{:S(2)}) collective-permute-start(bf16[1,4,512,512]{3,2,1,0:T(8,128)(2,1)} %bitcast.384), channel_id=1, source_target_pairs={{0,4},{1,5},{2,6},{3,7},{4,0},{5,1},{6,2},{7,3},{8,12},{9,13},{10,... | collective-permute-start | bytes 6291464 | tf_op jit(solution)/shard_map/ppermute | solution.py:1367
  374.2 48.7 %collective-permute-start.25 = (bf16[1,2,128,4096]{3,2,1,0:T(8,128)(2,1)}, bf16[1,2,128,4096]{3,2,1,0:T(8,128)(2,1)}, u32[]{:S(2)}, u32[]{:S(2)}) collective-permute-start(bf16[1,2,128,4096]{3,2,1,0:T(8,128)(2,1)} %bitcast.379), channel_id=1, source_target_pairs={{0,8},{1,9},{2,10},{3,11},{4,20},{5,21},{6,22},{7,23},{8,0},{9,1},... | collective-permute-start | bytes 6291464 | tf_op jit(solution)/shard_map/ppermute | solution.py:1367
  403.9 19.1 %collective-permute-start.26 = (bf16[1,2,512,512]{3,2,1,0:T(8,128)(2,1)}, bf16[1,2,512,512]{3,2,1,0:T(8,128)(2,1)}, u32[]{:S(2)}, u32[]{:S(2)}) collective-permute-start(bf16[1,2,512,512]{3,2,1,0:T(8,128)(2,1)} %bitcast.286), channel_id=1, source_target_pairs={{0,8},{1,9},{2,10},{3,11},{4,20},{5,21},{6,22},{7,23},{8,0},{9,1},... | collective-permute-start | bytes 3145736 | tf_op jit(solution)/shard_map/ppermute | solution.py:1367
  404.3 18.7 %collective-permute-start.24 = (bf16[1,2,256,512]{3,2,1,0:T(8,128)(2,1)}, bf16[1,2,256,512]{3,2,1,0:T(8,128)(2,1)S(1)}, u32[]{:S(2)}, u32[]{:S(2)}) collective-permute-start(bf16[1,2,256,512]{3,2,1,0:T(8,128)(2,1)} %bitcast.398), channel_id=1, source_target_pairs={{0,1},{1,0},{2,3},{3,2},{4,5},{5,4},{6,7},{7,6},{8,9},{9,8},{10,11... | collective-permute-start | bytes 1572872 | tf_op jit(solution)/shard_map/ppermute | solution.py:1367
  407.7 13.5 %collective-permute-start.23 = (bf16[1,1,256,512]{3,2,1,0:T(8,128)(2,1)}, bf16[1,1,256,512]{3,2,1,0:T(8,128)(2,1)S(1)}, u32[]{:S(2)}, u32[]{:S(2)}) collective-permute-start(bf16[1,1,256,512]{3,2,1,0:T(8,128)(2,1)} %bitcast.403), channel_id=1, source_target_pairs={{0,2},{1,3},{2,0},{3,1},{4,6},{5,7},{6,4},{7,5},{8,10},{9,11},{10,... | collective-permute-start | bytes 786440 | tf_op jit(solution)/shard_map/ppermute | solution.py:1367
  415.6 1.6 collective-permute-start.19
  417.2 36.4 %collective-permute-start.30 = (bf16[1,1,1024,256]{3,2,1,0:T(8,128)(2,1)}, bf16[1,1,1024,256]{3,2,1,0:T(8,128)(2,1)S(1)}, u32[]{:S(2)}, u32[]{:S(2)}) collective-permute-start(bf16[1,1,1024,256]{3,2,1,0:T(8,128)(2,1)} %bitcast.75.refs_4_), channel_id=1, source_target_pairs={{0,16},{1,17},{2,18},{3,19},{4,12},{5,13},{6,14},{7,15},{8,24},{9,... | collective-permute-start | bytes 1572872 | tf_op jit(solution)/shard_map/ppermute | solution.py:1367
  429.6 24.0 %collective-permute-start.27 = (bf16[1,1,256,512]{3,2,1,0:T(8,128)(2,1)}, bf16[1,1,256,512]{3,2,1,0:T(8,128)(2,1)S(1)}, u32[]{:S(2)}, u32[]{:S(2)}) collective-permute-start(bf16[1,1,256,512]{3,2,1,0:T(8,128)(2,1)} %bitcast.412), channel_id=1, source_target_pairs={{0,2},{1,3},{2,0},{3,1},{4,6},{5,7},{6,4},{7,5},{8,10},{9,11},{10,... | collective-permute-start | bytes 786440 | tf_op jit(solution)/shard_map/ppermute | solution.py:1367
  431.2 22.4 %collective-permute-start.29 = (bf16[1,1,512,512]{3,2,1,0:T(8,128)(2,1)}, bf16[1,1,512,512]{3,2,1,0:T(8,128)(2,1)S(1)}, u32[]{:S(2)}, u32[]{:S(2)}) collective-permute-start(bf16[1,1,512,512]{3,2,1,0:T(8,128)(2,1)} %bitcast.399), channel_id=1, source_target_pairs={{0,16},{1,17},{2,18},{3,19},{4,12},{5,13},{6,14},{7,15},{8,24},{9,... | collective-permute-start | bytes 1572872 | tf_op jit(solution)/shard_map/ppermute | solution.py:1367
  431.7 22.0 %collective-permute-start.28 = (bf16[1,1,128,4096]{3,2,1,0:T(8,128)(2,1)}, bf16[1,1,128,4096]{3,2,1,0:T(8,128)(2,1)S(1)}, u32[]{:S(2)}, u32[]{:S(2)}) collective-permute-start(bf16[1,1,128,4096]{3,2,1,0:T(8,128)(2,1)} %bitcast.389), channel_id=1, source_target_pairs={{0,16},{1,17},{2,18},{3,19},{4,12},{5,13},{6,14},{7,15},{8,24},{9,... | collective-permute-start | bytes 3145736 | tf_op jit(solution)/shard_map/ppermute | solution.py:1367
  453.5 38.7 %collective-permute-start.32 = (bf16[512,1024]{1,0:T(8,128)(2,1)}, bf16[512,1024]{1,0:T(8,128)(2,1)S(1)}, u32[]{:S(2)}, u32[]{:S(2)}) collective-permute-start(bf16[512,1024]{1,0:T(8,128)(2,1)} %get-tuple-element.167.refs_8_), channel_id=1, source_target_pairs={{4,0},{0,1},{5,2},{1,3},{6,4},{2,5},{7,6},{3,7},{12,8},{8,9},{13,1... | collective-permute-start | bytes 3145736 | tf_op jit(solution)/shard_map/ppermute | solution.py:1396
  459.4 32.8 %collective-permute-start.35 = (bf16[1,2,128,512]{3,2,1,0:T(8,128)(2,1)}, bf16[1,2,128,512]{3,2,1,0:T(8,128)(2,1)S(1)}, u32[]{:S(2)}, u32[]{:S(2)}) collective-permute-start(bf16[1,2,128,512]{3,2,1,0:T(8,128)(2,1)} %bitcast.410), channel_id=1, source_target_pairs={{0,1},{1,0},{2,3},{3,2},{4,5},{5,4},{6,7},{7,6},{8,9},{9,8},{10,11... | collective-permute-start | bytes 786440 | tf_op jit(solution)/shard_map/ppermute | solution.py:1367
  460.3 31.8 %collective-permute-start.34 = (bf16[1,2,256,256]{3,2,1,0:T(8,128)(2,1)}, bf16[1,2,256,256]{3,2,1,0:T(8,128)(2,1)}, u32[]{:S(2)}, u32[]{:S(2)}) collective-permute-start(bf16[1,2,256,256]{3,2,1,0:T(8,128)(2,1)} %bitcast.408), channel_id=1, source_target_pairs={{0,1},{1,0},{2,3},{3,2},{4,5},{5,4},{6,7},{7,6},{8,9},{9,8},{10,11... | collective-permute-start | bytes 786440 | tf_op jit(solution)/shard_map/ppermute | solution.py:1367
  465.4 25.7 %collective-permute-start.33 = (bf16[1,2,128,1056]{2,3,1,0:T(8,128)(2,1)}, bf16[1,2,128,1056]{2,3,1,0:T(8,128)(2,1)S(1)}, u32[]{:S(2)}, u32[]{:S(2)}) collective-permute-start(bf16[1,2,128,1056]{2,3,1,0:T(8,128)(2,1)} %get-tuple-element.278), channel_id=1, source_target_pairs={{0,1},{1,0},{2,3},{3,2},{4,5},{5,4},{6,7},{7,6},{8,9},{9,8},{10,11... | collective-permute-start | bytes 1622024 | tf_op jit(solution)/shard_map/ppermute | solution.py:1367
  490.0 50.3 %collective-permute-start.31 = (bf16[512,1024]{1,0:T(8,128)(2,1)}, bf16[512,1024]{1,0:T(8,128)(2,1)S(1)}, u32[]{:S(2)}, u32[]{:S(2)}) collective-permute-start(bf16[512,1024]{1,0:T(8,128)(2,1)} %get-tuple-element.174.refs_6_), channel_id=1, source_target_pairs={{1,0},{5,1},{0,2},{4,3},{3,4},{7,5},{2,6},{6,7},{9,8},{13,9},{8,10... | collective-permute-start | bytes 3145736 | tf_op jit(solution)/shard_map/ppermute | solution.py:1396
  498.7 2.4 collective-permute-start.36
  499.6 40.7 %collective-permute-start.39 = (bf16[1,1,128,1056]{3,2,1,0:T(8,128)(2,1)}, bf16[1,1,128,1056]{3,2,1,0:T(8,128)(2,1)}, u32[]{:S(2)}, u32[]{:S(2)}) collective-permute-start(bf16[1,1,128,1056]{3,2,1,0:T(8,128)(2,1)} %bitcast.276), channel_id=1, source_target_pairs={{0,2},{1,3},{2,0},{3,1},{4,6},{5,7},{6,4},{7,5},{8,10},{9,11},{10,... | collective-permute-start | bytes 811016 | tf_op jit(solution)/shard_map/ppermute | solution.py:1367
  502.0 6.2 %collective-permute-start.37 = (f32[160,128]{1,0:T(8,128)S(1)}, f32[160,128]{1,0:T(8,128)S(1)}, u32[]{:S(2)}, u32[]{:S(2)}) collective-permute-start(f32[160,128]{1,0:T(8,128)S(1)} %add.178), channel_id=1, source_target_pairs={{0,8},{1,9},{2,10},{3,11},{4,12},{5,13},{6,14},{7,15},{8,0},{9,1},... | collective-permute-start | bytes 245768 | tf_op jit(solution)/shard_map/ppermute | solution.py:1367
  505.2 32.5 %collective-permute-start.40 = (bf16[1,1,256,256]{3,2,1,0:T(8,128)(2,1)S(1)}, bf16[1,1,256,256]{3,2,1,0:T(8,128)(2,1)}, u32[]{:S(2)}, u32[]{:S(2)}) collective-permute-start(bf16[1,1,256,256]{3,2,1,0:T(8,128)(2,1)S(1)} %bitcast.313), channel_id=1, source_target_pairs={{0,2},{1,3},{2,0},{3,1},{4,6},{5,7},{6,4},{7,5},{8,10},{9,11},{10,... | collective-permute-start | bytes 393224 | tf_op jit(solution)/shard_map/ppermute | solution.py:1367
  506.7 33.6 %collective-permute-start.41 = (bf16[1,1,128,512]{3,2,1,0:T(8,128)(2,1)S(1)}, bf16[1,1,128,512]{3,2,1,0:T(8,128)(2,1)}, u32[]{:S(2)}, u32[]{:S(2)}) collective-permute-start(bf16[1,1,128,512]{3,2,1,0:T(8,128)(2,1)S(1)} %bitcast.316), channel_id=1, source_target_pairs={{0,2},{1,3},{2,0},{3,1},{4,6},{5,7},{6,4},{7,5},{8,10},{9,11},{10,... | collective-permute-start | bytes 393224 | tf_op jit(solution)/shard_map/ppermute | solution.py:1367
  508.2 4.6 collective-permute-start.38
  546.2 7.4 %collective-permute-start.44 = (f32[160,128]{1,0:T(8,128)}, f32[160,128]{1,0:T(8,128)S(1)}, u32[]{:S(2)}, u32[]{:S(2)}) collective-permute-start(f32[160,128]{1,0:T(8,128)} %later.1), channel_id=1, source_target_pairs={{0,3},{1,2},{2,1},{3,0},{4,7},{5,6},{6,5},{7,4},{8,11},{9,10},{10,... | collective-permute-start | bytes 245768 | tf_op jit(solution)/shard_map/ppermute | solution.py:1367
  548.4 7.7 %collective-permute-start.43 = (f32[160,128]{1,0:T(8,128)}, f32[160,128]{1,0:T(8,128)S(1)}, u32[]{:S(2)}, u32[]{:S(2)}) collective-permute-start(f32[160,128]{1,0:T(8,128)} %later.1), channel_id=1, source_target_pairs={{0,2},{1,3},{2,0},{3,1},{4,6},{5,7},{6,4},{7,5},{8,10},{9,11},{10,... | collective-permute-start | bytes 245768 | tf_op jit(solution)/shard_map/ppermute | solution.py:1367
  548.4 7.7 %collective-permute-start.42 = (f32[160,128]{1,0:T(8,128)}, f32[160,128]{1,0:T(8,128)S(1)}, u32[]{:S(2)}, u32[]{:S(2)}) collective-permute-start(f32[160,128]{1,0:T(8,128)} %later.1), channel_id=1, source_target_pairs={{0,1},{1,0},{2,3},{3,2},{4,5},{5,4},{6,7},{7,6},{8,9},{9,8},{10,11... | collective-permute-start | bytes 245768 | tf_op jit(solution)/shard_map/ppermute | solution.py:1367
  556.1 4.3 collective-permute-start.45
  (65 other events, 650.9 us)
Sparse Core Ops, SparseCore 0:
  417.3 33.1 reduce-scatter.1

commit v5 on v4

--- a/solution.py
+++ b/solution.py
@@ -67,15 +67,18 @@
     return slab[pl.ds(pl.multiple_of(t * groups, groups), groups), :]
 
 
-def front_ends_body(x_ref, gain_ref, decay_ref, low_ref, end_ref, slab):
+def front_body(
+    x_ref, gain_ref, decay_ref, proj_ref, low_ref, copy_ref, value_ref, slope_ref, end_ref, slab
+):
     states, groups, _ = decay_ref.shape
-    count = x_ref.shape[1]
-
-    @pl.when(pl.program_id(1) == 0)
+    count = x_ref.shape[0]
+
+    @pl.when(pl.program_id(0) == 0)
     def _():
         end_ref[...] = jnp.zeros_like(end_ref)
 
-    unit, _ = unit_rows_of(x_ref[0].astype(f32))
+    copy_ref[0] = x_ref[...]
+    unit, _ = unit_rows_of(x_ref[...].astype(f32))
     normed = unit * gain_ref[...]
     low_ref[0] = normed.astype(bf16)
     to_slab(slab, normed)
@@ -90,34 +93,55 @@
     )
     for n in range(states):
         end_ref[0, n] = state[n]
-
-
-def front_ends(x, gain, decay, block=256, after=()):
-    slots, length, width = x.shape
+    for c in range(proj_ref.shape[1] // 512):
+        at = slice(c * 512, (c + 1) * 512)
+        pre = jnp.dot(low_ref[0], proj_ref[:, at], preferred_element_type=f32)
+        gate = jax.nn.sigmoid(pre)
+        value = pre * gate
+        value_ref[0, :, at] = value.astype(bf16)
+        slope_ref[0, :, at] = (gate + value * (1.0 - gate)).astype(bf16)
+
+
+def front(x, slot, slots, earlier, gain, decay, proj, after=()):
+    length, width = x.shape
+    value_width = proj.shape[1]
     states, groups, lanes = decay.shape
-    block = min(block, length)
+    block = min(256, length)
+    anywhere = pl.BlockSpec(memory_space=pl.ANY)
+
+    def tokens(columns):
+        return pl.BlockSpec((1, block, columns), lambda b: (slot, b, 0))
+
     return pl.pallas_call(
-        ignoring(front_ends_body, 3, len(after)),
-        grid=(slots, length // block),
+        ignoring(front_body, 4, len(earlier) + len(after)),
+        grid=(length // block,),
         in_specs=[
-            pl.BlockSpec((1, block, width), lambda k, b: (k, b, 0)),
-            pl.BlockSpec((1, width), lambda k, b: (0, 0)),
-            pl.BlockSpec((states, groups, lanes), lambda k, b: (0, 0, 0)),
+            pl.BlockSpec((block, width), lambda b: (b, 0)),
+            pl.BlockSpec((1, width), lambda b: (0, 0)),
+            pl.BlockSpec((states, groups, lanes), lambda b: (0, 0, 0)),
+            pl.BlockSpec(proj.shape, lambda b: (0, 0), pipeline_mode=pl.Buffered(1)),
         ]
-        + [pl.BlockSpec(memory_space=pl.ANY)] * len(after),
+        + [anywhere] * (len(earlier) + len(after)),
         out_specs=[
-            pl.BlockSpec((1, block, width), lambda k, b: (k, b, 0)),
-            pl.BlockSpec((1, states, groups, lanes), lambda k, b: (k, 0, 0, 0)),
+            tokens(width),
+            tokens(width),
+            tokens(value_width),
+            tokens(value_width),
+            pl.BlockSpec((1, states, groups, lanes), lambda b: (slot, 0, 0, 0)),
         ],
         out_shape=[
             jax.ShapeDtypeStruct((slots, length, width), bf16),
+            jax.ShapeDtypeStruct((slots, length, width), bf16),
+            jax.ShapeDtypeStruct((slots, length, value_width), bf16),
+            jax.ShapeDtypeStruct((slots, length, value_width), bf16),
             jax.ShapeDtypeStruct((slots, states, groups, lanes), f32),
         ],
         scratch_shapes=[pltpu.VMEM((block * groups, lanes), f32)],
-        compiler_params=params(("arbitrary", "arbitrary")),
-        name="front_ends",
+        input_output_aliases={4 + k: k for k in range(len(earlier))},
+        compiler_params=params(("arbitrary",)),
+        name="front",
         cost_estimate=BRIEF,
-    )(x, gain, decay, *after)
+    )(x, gain, decay, proj, *earlier, *after)
 
 
 def front_scan_body(
@@ -129,9 +153,14 @@
     span_ref,
     omega_ref,
     ends_ref,
+    proj_ref,
+    affine_ref,
     smooth_ref,
     mixed_ref,
     check_ref,
+    shared_ref,
+    query_ref,
+    key_ref,
     slab,
     out_slab,
     carry,
@@ -174,15 +203,22 @@
         carry[n] = state[n]
     smoothed = from_slab(out_slab, count, groups) + omega_ref[...] * normed
     smooth_ref[0] = smoothed
-    mixed_ref[0] = (smoothed * jax.nn.sigmoid(smoothed)).astype(bf16)
-
-
-def front_scan(table, x, gain, decay, coef, span, omega, ends, block):
+    mixed = (smoothed * jax.nn.sigmoid(smoothed)).astype(bf16)
+    mixed_ref[0] = mixed
+    shared_pre = jnp.dot(mixed, proj_ref[...], preferred_element_type=f32)
+    shared = shared_pre * jax.nn.sigmoid(shared_pre)
+    shared_ref[0] = shared_pre
+    query_ref[0] = (shared * affine_ref[0:1] + affine_ref[1:2]).astype(bf16)
+    key_ref[0] = (shared * affine_ref[2:3] + affine_ref[3:4]).astype(bf16)
+
+
+def front_scan(table, x, gain, decay, coef, span, omega, ends, proj, affine, block):
     slots, length, width = x.shape
     states, groups, lanes = decay.shape
     whole3 = pl.BlockSpec((states, groups, lanes), lambda k, b, t: (0, 0, 0))
     row = pl.BlockSpec((1, width), lambda k, b, t: (0, 0))
     tokens = pl.BlockSpec((1, block, width), lambda k, b, t: (k, b, 0))
+    narrow = pl.BlockSpec((1, block, proj.shape[1]), lambda k, b, t: (k, b, 0))
     return pl.pallas_call(
         front_scan_body,
         grid_spec=pltpu.PrefetchScalarGridSpec(
@@ -196,11 +232,16 @@
                 whole3,
                 row,
                 pl.BlockSpec(ends.shape, lambda k, b, t: (0, 0, 0, 0)),
+                pl.BlockSpec(proj.shape, lambda k, b, t: (0, 0)),
+                pl.BlockSpec(affine.shape, lambda k, b, t: (0, 0)),
             ],
             out_specs=[
                 tokens,
                 tokens,
                 pl.BlockSpec((1, 1, states, groups, lanes), lambda k, b, t: (k, b, 0, 0, 0)),
+                narrow,
+                narrow,
+                narrow,
             ],
             scratch_shapes=[
                 pltpu.VMEM((block * groups, lanes), f32),
@@ -212,11 +253,14 @@
             jax.ShapeDtypeStruct((slots, length, width), f32),
             jax.ShapeDtypeStruct((slots, length, width), bf16),
             jax.ShapeDtypeStruct((slots, length // block, states, groups, lanes), f32),
+            jax.ShapeDtypeStruct((slots, length, proj.shape[1]), f32),
+            jax.ShapeDtypeStruct((slots, length, proj.shape[1]), bf16),
+            jax.ShapeDtypeStruct((slots, length, proj.shape[1]), bf16),
         ],
         compiler_params=params(("arbitrary", "arbitrary")),
         name="front_scan",
         cost_estimate=LONG,
-    )(table, x, gain, decay, coef, span, omega, ends)
+    )(table, x, gain, decay, coef, span, omega, ends, proj, affine)
 
 
 def back_ends_body(gs_ref, decay_ref, end_ref, slab):
@@ -437,19 +481,13 @@
     )(table, jnp.full((1,), slot, jnp.int32), x, gs, gv, gi, check, gain, decay, coef, span, omega, ends, *after)
 
 
-def load_chunks(table_ref, sources, total, length, sem):
+def chunk_copies(table_ref, own, others, kept, total, length, sem):
     copies = []
     for slot in range(total):
         place = pl.ds(pl.multiple_of(table_ref[slot] * length, length), length)
-        for own, others, kept in sources:
-            source = own.at[slot] if slot < 2 else others.at[slot - 2]
-            copies.append(
-                pltpu.make_async_copy(source, kept.at[place, :], sem.at[len(copies)])
-            )
-    for copy in copies:
-        copy.start()
-    for copy in copies:
-        copy.wait()
+        source = own.at[slot] if slot < 2 else others.at[slot - 2]
+        copies.append(pltpu.make_async_copy(source, kept.at[place, :], sem.at[slot]))
+    return copies
 
 
 def attend_body(
@@ -468,7 +506,8 @@
     values,
     scores,
     probs,
-    sem,
+    key_sem,
+    value_sem,
     *,
     total,
 ):
@@ -477,11 +516,15 @@
     tiles = length // TILE
     scale = float(key_width) ** (-0.5)
 
+    key_copies = chunk_copies(table_ref, k_own, k_oth, keys, total, length, key_sem)
+    value_copies = chunk_copies(table_ref, v_own, v_oth, values, total, length, value_sem)
+
     @pl.when(pl.program_id(0) == 0)
     def _():
-        load_chunks(
-            table_ref, ((k_own, k_oth, keys), (v_own, v_oth, values)), total, length, sem
-        )
+        for copy in key_copies + value_copies:
+            copy.start()
+        for copy in key_copies:
+            copy.wait()
 
     chunk = table_ref[pl.program_id(0)]
     reach = jnp.where(table_ref[2 * total] == 1, chunk + 1, 1)
@@ -515,6 +558,11 @@
     lse_ref[0] = peak + jnp.log(sums)
     inverse = 1.0 / sums
 
+    @pl.when(pl.program_id(0) == 0)
+    def _():
+        for copy in value_copies:
+            copy.wait()
+
     for count in range(1, total + 1):
 
         @pl.when(reach == count)
@@ -523,7 +571,7 @@
             span = pl.ds(pl.multiple_of(base, length), width)
 
             def column(ct, _):
-                at = pl.ds(pl.multiple_of(ct * TILE, TILE), TILE)
+                at = pl.ds(pl.multiple_of(ct * 512, 512), 512)
                 rows = (
                     jnp.dot(probs[:, :width], values[span, at], preferred_element_type=f32)
                     * inverse
@@ -533,7 +581,7 @@
                 gated_ref[0, :, at] = (gate * jax.nn.sigmoid(gate) * rows).astype(bf16)
                 return 0
 
-            lax.fori_loop(0, value_width // TILE, column, 0)
+            lax.fori_loop(0, value_width // 512, column, 0)
 
 
 def attend(table, q, bias, reset, k_own, k_oth, v_own, v_oth):
@@ -566,7 +614,8 @@
                 pltpu.VMEM((total * length, value_width), bf16),
                 pltpu.VMEM((total * length // TILE, length, TILE), f32),
                 pltpu.VMEM((length, total * length), bf16),
-                pltpu.SemaphoreType.DMA((2 * total,)),
+                pltpu.SemaphoreType.DMA((total,)),
+                pltpu.SemaphoreType.DMA((total,)),
             ],
         ),
         out_shape=[
@@ -602,7 +651,8 @@
     probs_kept,
     grads_kept,
     rel_ref,
-    sem,
+    key_sem,
+    value_sem,
     *,
     total,
 ):
@@ -614,14 +664,19 @@
     nt = (((1,), (1,)), ((), ()))
     tn = (((0,), (0,)), ((), ()))
 
+    copies = chunk_copies(
+        table_ref, k_own, k_oth, keys, total, length, key_sem
+    ) + chunk_copies(table_ref, v_own, v_oth, values, total, length, value_sem)
+
     @pl.when(step == 0)
     def _():
+        for copy in copies:
+            copy.start()
         gk_sum[...] = jnp.zeros_like(gk_sum)
         gv_sum[...] = jnp.zeros_like(gv_sum)
         rel_ref[...] = jnp.zeros_like(rel_ref)
-        load_chunks(
-            table_ref, ((k_own, k_oth, keys), (v_own, v_oth, values)), total, length, sem
-        )
+        for copy in copies:
+            copy.wait()
 
     chunk = table_ref[step]
     reach = jnp.where(table_ref[2 * total] == 1, chunk + 1, 1)
@@ -749,7 +804,8 @@
                 pltpu.VMEM((total, length, length), f32),
                 pltpu.VMEM((total, length, length), f32),
                 pltpu.VMEM(bias.shape, f32),
-                pltpu.SemaphoreType.DMA((2 * total,)),
+                pltpu.SemaphoreType.DMA((total,)),
+                pltpu.SemaphoreType.DMA((total,)),
             ],
         ),
         out_shape=[
@@ -1108,6 +1164,30 @@
     )(ids, places, low, *cots, first_sum, feed_in, feed_out, *after)
 
 
+def product_body(left_ref, right_ref, out_ref):
+    out_ref[...] = jnp.dot(
+        left_ref[...], right_ref[...], preferred_element_type=f32
+    ).astype(out_ref.dtype)
+
+
+def product(left, right, tile=1024):
+    tokens, depth = left.shape
+    columns = right.shape[1]
+    return pl.pallas_call(
+        product_body,
+        grid=(columns // tile,),
+        in_specs=[
+            pl.BlockSpec(left.shape, lambda i: (0, 0), pipeline_mode=pl.Buffered(1)),
+            pl.BlockSpec((depth, tile), lambda i: (0, i)),
+        ],
+        out_specs=pl.BlockSpec((tokens, tile), lambda i: (0, i)),
+        out_shape=jax.ShapeDtypeStruct((tokens, columns), bf16),
+        compiler_params=params(("arbitrary",)),
+        name="product",
+        cost_estimate=BRIEF,
+    )(left, right)
+
+
 def by_columns_body(ids_ref, places_ref, left_ref, right_ref, send, keep, plain, turned):
     step = pl.program_id(0)
     half = pl.num_programs(0) // 2
@@ -1295,38 +1375,46 @@
 
 
 def stage_body(*refs, shapes):
-    count = sum(pairs for pairs, _ in shapes)
+    count = sum(pairs for pairs, _, _ in shapes)
     ins, outs = list(refs[: 2 * count]), list(refs[2 * count :])
-    for pairs, halves in shapes:
+    for pairs, halves, turned in shapes:
         into = [outs.pop(0) for _ in range(halves)]
         start = 0
         for _ in range(pairs):
             kept, arrived = ins.pop(0), ins.pop(0)
             stop = start + kept.shape[0]
             for part, out in enumerate(into):
-                out[start:stop] = (
-                    kept[:, part].astype(f32) + arrived[:, part].astype(f32)
-                ).astype(out.dtype)
+                total = kept[:, part].astype(f32) + arrived[:, part].astype(f32)
+                if turned:
+                    out[0] = total[0].T
+                else:
+                    out[start:stop] = total.astype(out.dtype)
             start = stop
 
 
 def stage_sums(groups, after=(), steps=4, cost=BRIEF):
     shapes, ins, in_specs, out_specs, out_shapes, whole = [], [], [], [], [], []
-    for pairs, single, _ in groups:
+    for pairs, single, kind in groups:
         _, n, rows, _ = pairs[0][0].shape
-        while (n * rows // (1 if single else 2)) % (16 * steps):
+        lanes = 128 if kind == "turned" else 16
+        while (n * rows // (1 if single else 2)) % (lanes * steps) and steps > 1:
             steps //= 2
     for pairs, single, kind in groups:
         halves = 1 if single else 2
         g, n, rows, columns = pairs[0][0].shape
         each = n * rows // halves // steps
-        shapes.append((len(pairs), halves))
+        shapes.append((len(pairs), halves, kind == "turned"))
         for pair in pairs:
             for v in pair:
                 ins.append(v.reshape(g, halves, n * rows // halves, columns))
                 in_specs.append(
                     pl.BlockSpec((g, halves, each, columns), lambda i: (0, 0, i, 0))
                 )
+        if kind == "turned":
+            out_specs.append(pl.BlockSpec((1, columns, each), lambda i: (0, 0, i)))
+            out_shapes.append(jax.ShapeDtypeStruct((1, columns, rows), f32))
+            whole.append((1, (1, 1, columns, rows)))
+            continue
         for _ in range(halves):
             out_specs.append(pl.BlockSpec((len(pairs) * g, each, columns), lambda i: (0, i, 0)))
             out_shapes.append(
@@ -1476,7 +1564,10 @@
                         )
                         for pair in pairs
                     ]
-            groups.append((pairs, single, f32 if s.stage + 1 == last else bf16))
+            kind = bf16
+            if s.stage + 1 == last:
+                kind = "turned" if s.turned else f32
+            groups.append((pairs, single, kind))
         out = stage_sums(groups, after, cost=cost)
         for s, held, (_, single, _) in zip(sums, out, groups):
             s.stage += 1
@@ -1487,68 +1578,102 @@
                 s.send([held[0]], [held[1]])
         return [part for held in out for part in held]
 
-    def reduce_all(self, sent, held, after):
+    def over_seq(self, held):
         core = lax.axis_index("dp") % 2
-        held = held + self.send(sent, lambda d, z: (d ^ 1, z))
-        for bit in range(1, self.dp.bit_length() - 1):
+        split = held.reshape(2, -1, held.shape[-1])
+        held = lax.dynamic_index_in_dim(split, core, 0, False)
+        for bit in range(self.seq.bit_length() - 1):
+            held = held + self.send(held, lambda d, z: (d, z ^ (1 << bit)))
+        return held, self.send(held, lambda d, z: (d ^ 1, z))
+
+
+    def over_dp(self, held):
+        bits = self.dp.bit_length() - 1
+        for bit in range(bits - 1):
             held = held + self.send(held, lambda d, z: (d ^ (1 << bit), z))
-        held = later(held, after)
-        low = 1
-        while low < self.seq:
-            mine = held
-            for other in [low] if 2 * low >= self.seq else [low, 2 * low, 3 * low]:
-                held = held + self.send(mine, lambda d, z: (d, z ^ other))
-            low *= 4
-        other = self.send(held, lambda d, z: (d ^ 1, z))
-        return jnp.where(core == 0, jnp.stack([held, other]), jnp.stack([other, held]))
-
-
-def later_body(value, out):
-    out[...] = value[...]
-
-
-def later(value, after):
+        return held, self.send(held, lambda d, z: (d ^ (1 << (bits - 1)), z))
+
+
+def later_body(left, right, out):
+    out[...] = left[...] + right[...]
+
+
+def later_sum(left, right, after):
     inside = pl.BlockSpec(memory_space=pltpu.VMEM)
     return pl.pallas_call(
-        ignoring(later_body, 1, len(after)),
-        in_specs=[inside] + [pl.BlockSpec(memory_space=pl.ANY)] * len(after),
+        ignoring(later_body, 2, len(after)),
+        in_specs=[inside] * 2 + [pl.BlockSpec(memory_space=pl.ANY)] * len(after),
         out_specs=inside,
-        out_shape=jax.ShapeDtypeStruct(value.shape, value.dtype),
-        name="later",
+        out_shape=jax.ShapeDtypeStruct(left.shape, left.dtype),
+        name="later_sum",
         cost_estimate=BRIEF,
-    )(value, *after)
-
-
-def pack_body(core_ref, qx_a, qx_b, qs_a, qs_b, rest_ref, sent, held):
-    rows = jnp.concatenate(
-        [qx_a[...] + qx_b[...], qs_a[...] + qs_b[...], rest_ref[...]], axis=0
-    )
-    middle = rows.shape[0] // 2
-    first = core_ref[0] == 0
-    sent[...] = jnp.where(first, rows[middle:], rows[:middle])
-    held[...] = jnp.where(first, rows[:middle], rows[middle:])
-
-
-def pack(core, first, second, rest, after=()):
+    )(left, right, *after)
+
+
+def pack_body(qx_a, qx_b, qs_a, qs_b, rest_ref, out):
+    rows = qx_a.shape[0]
+    out[:rows] = qx_a[...] + qx_b[...]
+    out[rows : 2 * rows] = qs_a[...] + qs_b[...]
+    out[2 * rows :] = rest_ref[...]
+
+
+def pack(first, second, rest, after=()):
     ins = [v.reshape(-1, 128) for v in (first[0], second[0], first[1], second[1])] + [rest]
     rows = 2 * ins[0].shape[0] + rest.shape[0]
-    shape = jax.ShapeDtypeStruct((rows // 2, 128), f32)
     inside = pl.BlockSpec(memory_space=pltpu.VMEM)
     return pl.pallas_call(
-        ignoring(pack_body, 6, len(after)),
-        in_specs=[pl.BlockSpec(memory_space=pltpu.SMEM)]
-        + [inside] * 5
-        + [pl.BlockSpec(memory_space=pl.ANY)] * len(after),
-        out_specs=[inside, inside],
-        out_shape=[shape, shape],
+        ignoring(pack_body, 5, len(after)),
+        in_specs=[inside] * 5 + [pl.BlockSpec(memory_space=pl.ANY)] * len(after),
+        out_specs=inside,
+        out_shape=jax.ShapeDtypeStruct((rows, 128), f32),
         name="pack",
         cost_estimate=BRIEF,
-    )(core[None].astype(jnp.int32), *ins, *after)
+    )(*ins, *after)
+
+
+def finish_body(
+    core_ref, mine, other, alpha, damp, beta, eta, alpha_out, damp_out, beta_out, eta_out, rest, rows
+):
+    half = mine.shape[0]
+    first = core_ref[0] == 0
+    rows[:half] = jnp.where(first, mine[...], other[...])
+    rows[half:] = jnp.where(first, other[...], mine[...])
+    states = alpha.shape[0]
+    groups = alpha.shape[1] // 128
+    for c in range(groups):
+        at = slice(c * 128, (c + 1) * 128)
+        x_sum = rows[pl.ds(c, states, stride=groups), :]
+        s_sum = rows[pl.ds(states * groups + c, states, stride=groups), :]
+        rate = alpha[:, at] * beta[:, at]
+        input_total = eta[:, at] * x_sum
+        decay_total = eta[:, at] * rate * s_sum
+        alpha_out[:, at] = beta[:, at] * input_total - damp[:, at] * decay_total
+        damp_out[:, at] = -alpha[:, at] * decay_total
+        beta_out[:, at] = alpha[:, at] * input_total
+        eta_out[:, at] = rate * x_sum
+    rest[...] = rows[2 * states * groups :]
+
+
+def finish(core, mine, other, alpha, damp, beta, eta):
+    inside = pl.BlockSpec(memory_space=pltpu.VMEM)
+    rows = 2 * mine.shape[0]
+    shape = jax.ShapeDtypeStruct(alpha.shape, f32)
+    left = rows - 2 * alpha.size // 128
+    return pl.pallas_call(
+        finish_body,
+        in_specs=[pl.BlockSpec(memory_space=pltpu.SMEM)] + [inside] * 6,
+        out_specs=[inside] * 5,
+        out_shape=[shape] * 4 + [jax.ShapeDtypeStruct((left, 128), f32)],
+        scratch_shapes=[pltpu.VMEM((rows, 128), f32)],
+        name="finish",
+        cost_estimate=BRIEF,
+    )(core[None].astype(jnp.int32), mine, other, alpha, damp, beta, eta)
 
 
 class Sum:
-    def __init__(self, layout, *pairs, over_seq=True):
+    def __init__(self, layout, *pairs, over_seq=True, turned=False):
         self.layout, self.over_seq, self.stage = layout, over_seq, 0
+        self.turned = turned
         self.total = None
         pairs = [[v.reshape(1, v.shape[0], -1, v.shape[-1]) for v in pair] for pair in pairs]
         self.send([p[0] for p in pairs], [p[1] for p in pairs])
@@ -1627,8 +1752,7 @@
     table = jnp.concatenate([chunks, slot_of, full.astype(jnp.int32)[None]])
     ids, places, blocks = layout.orders()
 
-    x = jnp.stack(layout.spread(inputs))
-    cots = layout.spread(cotangent)
+    arriving = layout.spread(inputs)
     bias_back, bias_front = bias_tiles(relative_bias, chunk_rows // TILE - 1, full)
 
     states = smooth_alpha.shape[0]
@@ -1642,29 +1766,37 @@
     omega_row = smooth_omega[None]
     mix_shared, mix_main = mix_proj[:, :key_width], mix_proj[:, key_width:]
 
-    normed_low, ends = front_ends(
-        x, gain_row, decay_slab, after=(bias_back, bias_front, mix_main, mix_shared, span, coef)
-    )
+    held, after = (), (bias_back, bias_front, mix_main, mix_shared, span, coef)
+    for slot in range(slots):
+        held = front(
+            arriving[slot], slot, slots, held, gain_row, decay_slab, value_proj, after=after
+        )
+        after = ()
+    normed_low, x, value_low, value_slope, ends = held
     ends_all = jnp.concatenate([ends, layout.gather(ends)])
+    cotangent, ends_all = lax.optimization_barrier((cotangent, ends_all))
+    cots = layout.spread(cotangent)
     normed_low = normed_low.reshape(tokens, width)
-    value_pre = mm(normed_low, value_proj)
-    value_low = jax.nn.silu(value_pre).astype(bf16).reshape(slots, chunk_rows, value_width)
-    value_slope = silu_slope(value_pre).astype(bf16)
+    value_slope = value_slope.reshape(tokens, value_width)
     value_others = layout.gather(value_low)
-    smoothed, mixed, check = front_scan(
-        table, x, gain_row, decay_slab, coef, span, omega_row, ends_all, block
+    smoothed, mixed, check, shared_pre, query_low, key_low = front_scan(
+        table,
+        x,
+        gain_row,
+        decay_slab,
+        coef,
+        span,
+        omega_row,
+        ends_all,
+        mix_shared,
+        score_affine,
+        block,
     )
     smoothed = smoothed.reshape(tokens, width)
     mixed = mixed.reshape(tokens, width)
-
-    shared_pre = mm(mixed, mix_shared)
-    shared = jax.nn.silu(shared_pre)
-    query_low = (shared * score_affine[0] + score_affine[1]).astype(bf16)
-    key_low = (shared * score_affine[2] + score_affine[3]).astype(bf16)
-    query_low = query_low.reshape(slots, chunk_rows, key_width)
-    key_low = key_low.reshape(slots, chunk_rows, key_width)
+    shared_pre = shared_pre.reshape(tokens, key_width)
     key_others = layout.gather(key_low)
-    base = mm(mixed, mix_main).astype(bf16)
+    base = product(mixed, mix_main)
     attended, gated, lse = attend(
         table,
         query_low,
@@ -1691,13 +1823,14 @@
     )
     home = [layout.homeward(result_a, 0), layout.homeward(result_b, 1)]
     block_out = layout.gathered(home)
-    out_sum = Sum(layout, (out_send, out_keep))
+    out_sum = Sum(layout, (out_send, out_keep), turned=True)
     in_sum = Sum(layout, (in_send, in_keep))
 
     grad_input, grad_main, grad_att, feed_gain_grad = gate(
         grad_feed, cots, flat_low, cand_in, base, attended, feed_gain[None], out_proj
     )
-    after = layout.turn((out_sum, in_sum), (grad_att,))
+    after = layout.turn((out_sum,), (grad_att,))
+    after = layout.turn((in_sum,), after)
     mix_parts = by_rows(ids, None, mixed, grad_main, after=after, cost=LONG)
     proj_parts = by_columns(
         ids,
@@ -1710,7 +1843,7 @@
     )
     after = layout.turn((out_sum,), (*proj_parts, *home))
     mix_sum = Sum(layout, mix_parts, over_seq=False)
-    proj_sum = Sum(layout, proj_parts)
+    proj_sum = Sum(layout, proj_parts, turned=True)
     grad_query, gk_own, gv_own, both_oth, rel_sums = attend_back(
         table,
         query_low,
@@ -1743,18 +1876,18 @@
     grad_shared = (
         (grad_query * score_affine[0] + grad_key * score_affine[2]) * silu_slope(shared_pre)
     ).astype(bf16)
-    shared_grad = mm_tn(mixed, grad_shared).astype(bf16)
-    shared_grad = lax.psum_scatter(shared_grad, "dp", scatter_dimension=0, tiled=True)
-    after = layout.turn((in_sum, out_sum, mix_sum), (grad_normed,))
+    shared_parts = by_rows(ids, None, mixed, grad_shared, after=(grad_normed,))
+    after = layout.turn((out_sum, mix_sum), shared_parts)
+    shared_sum = Sum(layout, shared_parts, over_seq=False)
     value_sum = Sum(layout, (value_send, value_keep))
     grad_smooth = (mm_nt(grad_main, mix_main) + mm_nt(grad_shared, mix_shared)) * silu_slope(
         smoothed
     )
     grad_smooth = grad_smooth.reshape(slots, chunk_rows, width)
-    after = layout.turn((value_sum, proj_sum), (grad_smooth,))
+    after = layout.turn((in_sum, value_sum, proj_sum, shared_sum), (grad_smooth,))
     back = back_ends(grad_smooth, decay_slab, after=after)
     back_all = jnp.concatenate([back, layout.gather(back)])
-    after = layout.turn((out_sum, in_sum, mix_sum, value_sum), (back,))
+    after = layout.turn((out_sum, in_sum, mix_sum, value_sum, shared_sum), (back,))
 
     def scan_back(slot, after):
         return back_scan(
@@ -1776,29 +1909,15 @@
 
     first = scan_back(0, after)
     after = layout.turn(
-        (in_sum, mix_sum, value_sum, proj_sum, out_sum), (first[0], shared_grad)
+        (in_sum, mix_sum, value_sum, proj_sum, out_sum, shared_sum), (first[0],)
     )
     home_first = layout.homeward(first[0], 0)
-    while mix_sum.total is None:
-        after = layout.turn((mix_sum,), after)
-    rows = jnp.concatenate([shared_grad, mix_sum.total[0, 0]], axis=1)
+    while mix_sum.total is None or shared_sum.total is None:
+        after = layout.turn((mix_sum, shared_sum), after)
+    rows = jnp.concatenate([shared_sum.total[0, 0], mix_sum.total[0, 0]], axis=1)
     rows = rows.reshape(rows.shape[0], layout.seq, -1).transpose(1, 0, 2)
     mix_sum.begin_seq(rows[blocks])
     second = scan_back(1, (*after, *mix_sum.kept))
-    home_second = layout.homeward(second[0], 1)
-    after = (second[0], home_first)
-    sums = (mix_sum, proj_sum, value_sum, out_sum, in_sum)
-    turned = layout.turn(sums, after, cost=LONG)
-    after = layout.turn(sums, (*turned, home_second))
-    while any(v.total is None for v in sums):
-        after = layout.turn(sums, after)
-    grad_in = layout.gathered([home_first, home_second]).astype(f32)
-    feed_out_grad, feed_in_grad = out_sum.total[0, 0].T, in_sum.total[0, 0]
-    rows = width // layout.dp
-    feed_in_grad = feed_in_grad.reshape(-1, rows, feed_in_grad.shape[-1])
-    feed_in_grad = feed_in_grad.transpose(1, 0, 2).reshape(rows, -1)
-    out_grad, value_grad = proj_sum.total[0, 0].T, value_sum.total[0, 0]
-    mix_grad = mix_sum.total[0, 0]
     affine_grad = jnp.stack(
         [
             jnp.sum(grad_query * shared_pre * jax.nn.sigmoid(shared_pre), axis=0),
@@ -1818,24 +1937,28 @@
     small = [v.reshape(-1, 128) for v in small]
     rest = jnp.concatenate(small)
     rest = jnp.pad(rest, ((0, -rest.shape[0] % 16), (0, 0)))
-    totals = layout.reduce_all(
-        *pack(core, first[1:3], second[1:3], rest, after=turned), after=after
-    )
-    totals = totals.reshape(-1, 128)
-    count = states * width // 128
-    input_sum = totals[:count].reshape(states, width)
-    decay_sum = totals[count : 2 * count].reshape(states, width)
-    parts, start = [], 2 * count
+    home_second = layout.homeward(second[0], 1)
+    sums = (mix_sum, proj_sum, value_sum, out_sum, in_sum)
+    turned = layout.turn(sums, (second[0], home_first), cost=LONG)
+    totals = layout.over_dp(pack(first[1:3], second[1:3], rest, after=turned))
+    after = layout.turn(sums, (*turned, home_second))
+    totals = layout.over_seq(later_sum(*totals, after=after))
+    while any(v.total is None for v in sums):
+        after = layout.turn(sums, after)
+    grad_in = layout.gathered([home_first, home_second]).astype(f32)
+    feed_out_grad, feed_in_grad = out_sum.total[0, 0], in_sum.total[0, 0]
+    rows = width // layout.dp
+    feed_in_grad = feed_in_grad.reshape(-1, rows, feed_in_grad.shape[-1])
+    feed_in_grad = feed_in_grad.transpose(1, 0, 2).reshape(rows, -1)
+    out_grad, value_grad = proj_sum.total[0, 0], value_sum.total[0, 0]
+    mix_grad = mix_sum.total[0, 0]
+    alpha_grad, damp_grad, beta_grad, eta_grad, totals = finish(
+        core, *totals, smooth_alpha, smooth_damp, smooth_beta, smooth_eta
+    )
+    parts, start = [], 0
     for item in small:
         parts.append(totals[start : start + item.shape[0]].reshape(-1))
         start += item.shape[0]
-    input_total = smooth_eta * input_sum
-    decay_total = smooth_eta * rate * decay_sum
-    eta_grad = rate * input_sum
-    alpha_grad = smooth_beta * input_total - smooth_damp * decay_total
-    damp_grad = -smooth_alpha * decay_total
-    beta_grad = smooth_alpha * input_total
-
     return (
         block_out,
         grad_in,

time: 582 us -> 563 us (0.967)
  matrix products: 62 us -> 33.7 us
  starting transfers between devices: 42.9 us -> 58.1 us
  between operations: 16 us -> 2.23 us
  Pallas kernels: 321 us -> 334 us
  local copies, waits for them, and re-layouts: 41 us -> 47.3 us
    dot_general x4 -> x1, matrix products: 42.6 us -> 12.1 us  [mm(): return jnp.dot(a, b, preferred_element_type=f32)]
    pallas_call x3 -> x6, Pallas kernels: 11.8 us -> 38 us  [the longest x2 20 us: front(): pl.pallas_call(ignoring(front_body, 4, len(earlier) + len(after)), grid=(...]
    pallas_call x1, Pallas kernels: 34.4 us -> 22.4 us  [attend_back(): pl.pallas_call(ignoring(functools.partial(attend_back_body, total=total),...]
    ppermute x42 -> x44, starting transfers between devices: 40.3 us -> 48.8 us  [send(): return lax.ppermute(value, AXES, self.pairs(move))]
    pallas_call x1, Pallas kernels: 22.8 us -> 14.8 us  [attend(): pl.pallas_call(functools.partial(attend_body, total=total), grid_spec=plt...]
    ppermute x4, starting transfers between devices: 2.62 us -> 9.29 us  [homeward(): return lax.ppermute(value, AXES, pairs)]
    pallas_call x1 -> x2, Pallas kernels: 15.2 us -> 20 us  [by_rows(): pl.pallas_call(ignoring(by_rows_body, 4, len(after)), grid_spec=pltpu.Pre...]
    ppermute x42 -> x44, waiting for transfers between devices: 60.3 us -> 56.7 us  [send(): return lax.ppermute(value, AXES, self.pairs(move))]
  transfers between devices with their start and end apart: 47 -> 48, of which waited for: 11 -> 11; matrix products, arithmetic and copies ran while one was open for 21% -> 15% of each run, Pallas kernels for 43% -> 45%
where the time goes in v5:
time: 563 us; the launch traced here: 555 us
  Pallas kernels  334 us (59%)
  starting transfers between devices  58.1 us (10%)
  waiting for transfers between devices  56.7 us (10%)
  local copies, waits for them, and re-layouts  47.3 us (8%)
  matrix products  33.7 us (6%)
  other arithmetic  23.4 us (4%)
    pallas_call x1, Pallas kernels, feed(): pl.pallas_call(ignoring(feed_body, 8, len(after)), grid_spec=pltpu.Prefet...  68.7 us
    ppermute x44, waiting for transfers between devices, send(): return lax.ppermute(value, AXES, self.pairs(move))  56.7 us
    pallas_call x10, Pallas kernels, stage_sums(): pl.pallas_call(ignoring(functools.partial(stage_body, shapes=shapes), len...  50.7 us
    ppermute x44, starting transfers between devices, send(): return lax.ppermute(value, AXES, self.pairs(move))  48.8 us
    pallas_call x2, Pallas kernels, back_scan(): pl.pallas_call(ignoring(back_scan_body, 13, len(after)), grid_spec=pltpu....  40.5 us
    pallas_call x1, Pallas kernels, attend_back(): pl.pallas_call(ignoring(functools.partial(attend_back_body, total=total),...  22.4 us
    dot_general x2, matrix products, mm_nt(): lax.dot_general(a, b, (((1,), (1,)), ((), ())), preferred_element_type=f32)  21.5 us
    pallas_call x2, Pallas kernels, front(): pl.pallas_call(ignoring(front_body, 4, len(earlier) + len(after)), grid=(...  20 us
  transfers between devices with their start and end apart: 48, of which 11 were waited for; matrix products, arithmetic and copies ran while one was open for 15% of the time, Pallas kernels for 45%

profile of v5, /device:TPU:0, one launch (start us, length us, event | category | flops | bytes accessed | tf_op | source)
XLA Modules:
  0.0 555.4 jit_solution(15538007060413166548)
XLA Ops:
  1.8 2.7 dynamic-slice_bitcast_fusion.2
  4.5 2.5 collective-permute-start
  8.9 7.9 %slice.109.refs_6_.right_ref = bf16[1024,4096]{1,0:T(8,128)(2,1)} slice(bf16[1024,4224]{1,0:T(8,128)(2,1)} %param.30), slice={[0:1024], [128:4224]} | slice | bytes 16777216 | tf_op jit(solution)/shard_map/slice | solution.py:1767
  22.3 6.0 %bias.1 = (f32[9,256,256]{2,1,0:T(8,128)}, f32[9,256,256]{2,1,0:T(8,128)}) custom-call(s32[1]{0:T(128)S(6)} %convert_element_type.41.flag_ref, f32[8,1,512]{2,1,0:T(1,128)} %copy.61.back_row, f32[8,1,512]{2,1,0:T(1,128)} %broadcast_in_dim.51.front_row), custom_call_target="tpu_custom_call" | custom-call | tf_op jit(solution)/shard_map/bias/pallas_call | solution.py:864
  29.4 10.0 %front.2 = (bf16[2,512,1024]{2,1,0:T(8,128)(2,1)}, bf16[2,512,1024]{2,1,0:T(8,128)(2,1)}, bf16[2,512,2048]{2,1,0:T(8,128)(2,1)}, bf16[2,512,2048]{2,1,0:T(8,128)(2,1)}, f32[2,16,8,128]{3,2,1,0:T(8,128)}) custom-call(bf16[512,1024]{1,0:T(8,128)(2,1)} %copy-done.14, f32[1,1024]{1,0:T(1,128)} %bitcast.367, f32[16,8,128]{2,1,0:T(8,128)} %bitcast.295, ...), custom_call_target="tpu_custom_call" | custom-call | flops 1 | bytes 1 | tf_op jit(solution)/shard_map/front/pallas_call | solution.py:115
  39.4 15.9 %collective-permute-done.refs_0_ = bf16[512,1024]{1,0:T(8,128)(2,1)S(1)} collective-permute-done((bf16[512,1024]{1,0:T(8,128)(2,1)S(1)}, bf16[512,1024]{1,0:T(8,128)(2,1)S(1)}, u32[]{:S(2)}, u32[]{:S(2)}) %collective-permute-start) | collective-permute-done | bytes 1048608 | tf_op jit(solution)/shard_map/ppermute | solution.py:1455
  56.3 10.0 %front.3 = (bf16[2,512,1024]{2,1,0:T(8,128)(2,1)}, bf16[2,512,1024]{2,1,0:T(8,128)(2,1)}, bf16[2,512,2048]{2,1,0:T(8,128)(2,1)}, bf16[2,512,2048]{2,1,0:T(8,128)(2,1)}, f32[2,16,8,128]{3,2,1,0:T(8,128)}) custom-call(bf16[512,1024]{1,0:T(8,128)(2,1)} %copy-done.13, ...), custom_call_target="tpu_custom_call", output_to_operand_aliasing={{0}: (4, {}), {1}: (5, {}), {2}: (6, {}), {3}: (7, {}), {4}... | custom-call | flops 1 | bytes 1 | tf_op jit(solution)/shard_map/front/pallas_call | solution.py:115
  69.7 17.3 %front_scan.1 = (f32[2,512,1024]{2,1,0:T(8,128)}, bf16[2,512,1024]{2,1,0:T(8,128)(2,1)}, f32[2,4,16,8,128]{4,3,2,1,0:T(8,128)}, f32[2,512,128]{2,1,0:T(8,128)}, ...) custom-call(s32[9]{0:T(128)} %concatenate.44.table_ref.refs_0_, ...), custom_call_target="tpu_custom_call" | custom-call | flops 99999997952 | bytes 1 | tf_op jit(solution)/shard_map/front_scan/pallas_call | solution.py:222
  89.9 1.8 collective-permute-start.6
  91.7 13.0 %product.1.refs_5_.refs_6_ = bf16[1024,4096]{1,0:T(8,128)(2,1)} custom-call(bf16[1024,1024]{1,0:T(8,128)(2,1)} %bitcast.250, bf16[1024,4096]{1,0:T(8,128)(2,1)} %slice.109.refs_6_.right_ref), custom_call_target="tpu_custom_call" | custom-call | flops 1 | bytes 1 | tf_op jit(solution)/shard_map/product/pallas_call | solution.py:1176
  105.4 14.8 %attend.1 = (bf16[2,512,2048]{2,1,0:T(8,128)(2,1)}, bf16[2,512,2048]{2,1,0:T(8,128)(2,1)}, f32[2,512,1]{2,1,0:T(8,128)}) custom-call(s32[9]{0:T(128)} %concatenate.44.table_ref.refs_0_, bf16[2,512,128]{2,1,0:T(8,128)(2,1)} %get-tuple-element.141.q_ref.refs_1_, f32[9,256,256]{2,1,0:T(8,128)} %get-tuple-element.131.refs_5_.bias_ref, ...), custom_call_target="tpu_custom_call" | custom-call | flops 1 | bytes 1 | tf_op jit(solution)/shard_map/attend/pallas_call | solution.py:593
  122.0 12.1 %fusion.20 = (f32[1024]{0:T(1024)S(1)}, f32[1024,1024]{1,0:T(8,128)S(1)}, f32[1024,1024]{1,0:T(8,128)}) fusion(bf16[1024,4096]{1,0:T(8,128)(2,1)} %product.1.refs_5_.refs_6_, bf16[2,512,1024]{2,1,0:T(8,128)(2,1)S(1)} %copy-done.7, bf16[1024,2048]{1,0:T(8,128)(2,1)} %bitcast.263, bf16[2048,1024]{1,0:T(8,128)(2,1)} %refs_9_.1), kind=kOutput, calls=%fused_computation.76 | convolution fusion | flops 4310694912 | bytes 23072768 | tf_op jit(solution)/shard_map/dot_general | solution.py:1692
  134.9 2.0 multiply_convert_fusion.refs_2_
  137.8 68.7 %feed.1 = (bf16[512,1024]{1,0:T(8,128)(2,1)}, bf16[512,1024]{1,0:T(8,128)(2,1)}, f32[1024,1024]{1,0:T(8,128)}, bf16[4,1024,512]{2,1,0:T(8,128)(2,1)}, bf16[4,102...) custom-call(s32[8]{0:T(128)} %broadcast_select_fusion.1.refs_0_, ...), custom_call_target="tpu_custom_call" | custom-call | flops 1 | bytes 1 | tf_op jit(solution)/shard_map/feed/pallas_call | solution.py:1118
  206.5 7.4 %collective-permute-start.8 = (bf16[512,1024]{1,0:T(8,128)(2,1)}, bf16[512,1024]{1,0:T(8,128)(2,1)}, u32[]{:S(2)}, u32[]{:S(2)}) collective-permute-start(bf16[512,1024]{1,0:T(8,128)(2,1)} %get-tuple-element.146), channel_id=1, source_target_pairs={{1,0},{5,1},{0,2},{4,3},{3,4},{7,5},{2,6},{6,7},{9,8},{13,9},{8,10... | collective-permute-start | bytes 3145736 | tf_op jit(solution)/shard_map/ppermute | solution.py:1484
  215.0 19.9 %gate.1 = (f32[1024,1024]{1,0:T(8,128)}, bf16[1024,4096]{1,0:T(8,128)(2,1)}, bf16[1024,2048]{1,0:T(8,128)(2,1)}, f32[1,1024]{1,0:T(1,128)}) custom-call(f32[1024,1024]{1,0:T(8,128)} %get-tuple-element.148.refs_0_, bf16[512,1024]{1,0:T(8,128)(2,1)} %collective-permute-done.6.refs_3_.refs_1_, bf16[512,1024]{1,0:T(8,128)(2,1)} %copy-done.15, ...), custom_call_target="tpu_custom_call" | custom-call | flops 99999997952 | bytes 1 | tf_op jit(solution)/shard_map/gate/pallas_call | solution.py:956
  234.9 5.9 %stage_sums.10 = (bf16[1,2048,512]{2,1,0:T(8,128)(2,1)}, bf16[1,2048,512]{2,1,0:T(8,128)(2,1)}) custom-call(bf16[1,2,2048,512]{3,2,1,0:T(8,128)(2,1)} %bitcast.258, bf16[1,2,2048,512]{3,2,1,0:T(8,128)(2,1)} %bitcast.30.refs_1_, bf16[1024,2048]{1,0:T(8,128)(2,1)} %get-tuple-element.151.refs_2_), custom_call_target="tpu_custom_call" | custom-call | flops 1 | bytes 1 | tf_op jit(solution)/shard_map/stage_sums/pallas_call | solution.py:1425
  242.5 5.9 %stage_sums.11 = (bf16[1,2048,512]{2,1,0:T(8,128)(2,1)}, bf16[1,2048,512]{2,1,0:T(8,128)(2,1)}) custom-call(bf16[1,2,2048,512]{3,2,1,0:T(8,128)(2,1)} %bitcast.257, bf16[1,2,2048,512]{3,2,1,0:T(8,128)(2,1)} %bitcast.35.refs_1_, bf16[1,2,1024,512]{3,2,1,0:T(8,128)(2,1)} %bitcast.285, bf16[1,2,1024,512]{3,2,1,0:T(8,128)(2,1)} %bitcast.253), custom_call_target="tpu_custom_call" | custom-call | flops 1 | bytes 1 | tf_op jit(solution)/shard_map/stage_sums/pallas_call | solution.py:1425
  248.8 15.2 %by_rows.2 = (bf16[4,1,128,4096]{3,2,1,0:T(8,128)(2,1)}, bf16[4,1,128,4096]{3,2,1,0:T(8,128)(2,1)}) custom-call(s32[8]{0:T(128)} %broadcast_select_fusion.1.refs_0_, s32[1]{0:T(128)} %constant.118.clone.1.refs_1_, bf16[1024,1024]{1,0:T(8,128)(2,1)} %bitcast.251, bf16[1024,4096]{1,0:T(8,128)(2,1)} %get-tuple-element.150.refs_3_.refs_2_, ...), custom_call_target="tpu_custom_call" | custom-call | flops 99999997952 | bytes 1 | tf_op jit(solution)/shard_map/by_rows/pallas_call | solution.py:1280
  264.0 11.9 %by_columns.1 = (bf16[4,1024,256]{2,1,0:T(8,128)(2,1)}, bf16[4,1024,256]{2,1,0:T(8,128)(2,1)}) custom-call(s32[8]{0:T(128)} %broadcast_select_fusion.1.refs_0_, s32[4]{0:T(128)} %get-tuple-element.129.refs_1_, bf16[1024,4096]{1,0:T(8,128)(2,1)} %get-tuple-element.150.refs_3_.refs_2_, bf16[1024,2048]{1,0:T(8,128)(2,1)} %bitcast.264, ...), custom_call_target="tpu_custom_call" | custom-call | flops 1 | bytes 1 | tf_op jit(solution)/shard_map/by_columns/pallas_call | solution.py:1224
  277.7 4.2 stage_sums.12
  282.9 22.4 %attend_back.1 = (f32[2,512,128]{2,1,0:T(8,128)}, bf16[2,512,128]{2,1,0:T(8,128)(2,1)}, bf16[2,512,2048]{2,1,0:T(8,128)(2,1)}, bf16[2,512,2176]{2,1,0:T(8,128)(2,1)}, f32[8,1,512]{2,1,0:T(1,128)}) custom-call(s32[9]{0:T(128)} %concatenate.44.table_ref.refs_0_, bf16[2,512,128]{2,1,0:T(8,128)(2,1)} %get-tuple-element.141.q_ref.refs_1_, ...), custom_call_target="tpu_custom_call" | custom-call | flops 99999997952 | bytes 1 | tf_op jit(solution)/shard_map/attend_back/pallas_call | solution.py:776
  306.8 6.7 %stage_sums.13 = (bf16[1,1024,512]{2,1,0:T(8,128)(2,1)}, bf16[1,1024,512]{2,1,0:T(8,128)(2,1)}, bf16[1,512,512]{2,1,0:T(8,128)(2,1)}, bf16[1,512,512]{2,1,0:T(8,...) custom-call(bf16[1,2,1024,512]{3,2,1,0:T(8,128)(2,1)} %bitcast.393, ...), custom_call_target="tpu_custom_call" | custom-call | flops 99999997952 | bytes 1 | tf_op jit(solution)/shard_map/stage_sums/pallas_call | solution.py:1425
  313.6 14.1 %collective-permute-start.22 = (bf16[1,2,256,512]{3,2,1,0:T(8,128)(2,1)}, bf16[1,2,256,512]{3,2,1,0:T(8,128)(2,1)S(1)}, u32[]{:S(2)}, u32[]{:S(2)}) collective-permute-start(bf16[1,2,256,512]{3,2,1,0:T(8,128)(2,1)} %bitcast.412), channel_id=1, source_target_pairs={{0,1},{1,0},{2,3},{3,2},{4,5},{5,4},{6,7},{7,6},{8,9},{9,8},{10,11... | collective-permute-start | bytes 1572872 | tf_op jit(solution)/shard_map/ppermute | solution.py:1455
  327.7 2.3 collective-permute-start.19
  330.0 15.9 %value_back.1 = (f32[1024,1024]{1,0:T(8,128)}, bf16[4,4,128,512]{3,2,1,0:T(8,128)(2,1)}, bf16[4,4,128,512]{3,2,1,0:T(8,128)(2,1)}) custom-call(s32[8]{0:T(128)} %broadcast_select_fusion.1.refs_0_, s32[4]{0:T(128)} %get-tuple-element.129.refs_1_, bf16[1024,1024]{1,0:T(8,128)(2,1)} %bitcast.276, bf16[1024,2048]{1,0:T(8,128)(2,1)} %bitcast.431, ...), custom_call_target="tpu_custom_call" | custom-call | flops 99999997952 | bytes 1 | tf_op jit(solution)/shard_map/value_back/pallas_call | solution.py:1351
  345.9 2.5 fusion.15
  348.4 4.8 by_rows.3
  353.1 3.7 fusion.17
  357.6 6.4 %stage_sums.15 = (bf16[1,256,512]{2,1,0:T(8,128)(2,1)}, bf16[1,256,512]{2,1,0:T(8,128)(2,1)}, bf16[1,256,4096]{2,1,0:T(8,128)(2,1)}, bf16[1,256,4096]{2,1,0:T(8,128)(2,1)}) custom-call(bf16[1,2,256,512]{3,2,1,0:T(8,128)(2,1)} %bitcast.324, bf16[1,2,256,512]{3,2,1,0:T(8,128)(2,1)} %copy-done.23, bf16[1,2,256,4096]{3,2,1,0:T(8,128)(2,1)} %bitcast.249, ...), custom_call_target="tpu_custom_call" | custom-call | flops 1 | bytes 1 | tf_op jit(solution)/shard_map/stage_sums/pallas_call | solution.py:1425
  364.5 17.9 %fusion.6 = f32[1024,1024]{1,0:T(8,128)} fusion(f32[2,512,1024]{2,1,0:T(8,128)} %get-tuple-element.171, f32[1024,1024]{1,0:T(8,128)} %fusion.17, bf16[1024,4096]{1,0:T(8,128)(2,1)} %get-tuple-element.150.refs_3_.refs_2_, bf16[1024,4224]{1,0:T(8,128)(2,1)} %param.30), kind=kOutput, calls=%fused_computation.11 | convolution fusion | flops 8599371776 | bytes 29360128 | tf_op jit(solution)/shard_map/dot_general | solution.py:1696
  383.8 5.9 %stage_sums.14 = (bf16[1,512,512]{2,1,0:T(8,128)(2,1)}, bf16[1,512,512]{2,1,0:T(8,128)(2,1)}, bf16[1,1024,512]{2,1,0:T(8,128)(2,1)}, bf16[1,1024,512]{2,1,0:T(8,...) custom-call(bf16[1,2,512,512]{3,2,1,0:T(8,128)(2,1)} %bitcast.302, ...), custom_call_target="tpu_custom_call" | custom-call | flops 1 | bytes 1 | tf_op jit(solution)/shard_map/stage_sums/pallas_call | solution.py:1425
  394.7 8.1 %back_ends.1.refs_10_ = f32[2,16,8,128]{3,2,1,0:T(8,128)} custom-call(f32[2,512,1024]{2,1,0:T(8,128)} %bitcast.246, f32[16,8,128]{2,1,0:T(8,128)} %bitcast.298, bf16[1,2,256,512]{3,2,1,0:T(8,128)(2,1)} %bitcast.320, bf16[1,2,256,512]{3,2,1,0:T(8,128)(2,1)} %bitcast.280, bf16[1,2,512,512]{3,2,1,0:T(8,128)(2,1)} %bitcast.306, ...), custom_call_target="tpu_custom_call" | custom-call | flops 1 | bytes 1 | tf_op jit(solution)/shard_map/back_ends/pallas_call | solution.py:293
  408.6 3.4 collective-permute-done.25.refs_3_
  413.0 5.2 stage_sums.16
  421.9 20.2 %back_scan.2 = (bf16[512,1024]{1,0:T(8,128)(2,1)}, f32[16,8,128]{2,1,0:T(8,128)}, f32[16,8,128]{2,1,0:T(8,128)}, f32[1,1024]{1,0:T(1,128)}, f32[1,1024]{1,0:T(1,128)}) custom-call(s32[9]{0:T(128)} %concatenate.44.table_ref.refs_0_, s32[1]{0:T(128)} %constant.118.clone.1.refs_1_, bf16[2,512,1024]{2,1,0:T(8,128)(2,1)} %get-tuple-element.137.x_ref.refs_2_, ...), custom_call_target="tpu_custom_call" | custom-call | flops 99999997952 | bytes 1 | tf_op jit(solution)/shard_map/back_scan/pallas_call | solution.py:434
  445.0 4.8 stage_sums.17
  457.8 20.3 %back_scan.3 = (bf16[512,1024]{1,0:T(8,128)(2,1)}, f32[16,8,128]{2,1,0:T(8,128)}, f32[16,8,128]{2,1,0:T(8,128)}, f32[1,1024]{1,0:T(1,128)}, f32[1,1024]{1,0:T(1,128)}) custom-call(s32[9]{0:T(128)} %concatenate.44.table_ref.refs_0_, s32[1]{0:T(128)} %constant.117.clone.1.refs_1_, bf16[2,512,1024]{2,1,0:T(8,128)(2,1)} %get-tuple-element.137.x_ref.refs_2_, ...), custom_call_target="tpu_custom_call" | custom-call | flops 99999997952 | bytes 1 | tf_op jit(solution)/shard_map/back_scan/pallas_call | solution.py:434
  483.3 3.5 stage_sums.18
  492.5 2.9 collective-permute-start.43
  495.4 2.9 collective-permute-start.42
  500.7 18.1 %collective-permute-done.43.refs_3_ = bf16[1,1,256,256]{3,2,1,0:T(8,128)(2,1)S(1)} collective-permute-done((bf16[1,1,256,256]{3,2,1,0:T(8,128)(2,1)}, bf16[1,1,256,256]{3,2,1,0:T(8,128)(2,1)S(1)}, u32[]{:S(2)}, u32[]{:S(2)}) %collective-permute-start.43) | collective-permute-done | bytes 131104 | tf_op jit(solution)/shard_map/ppermute | solution.py:1455
  518.8 2.8 collective-permute-done.44.refs_5_
  521.6 6.2 %collective-permute-done.42.refs_1_ = bf16[1,1,128,1056]{3,2,1,0:T(8,128)(2,1)S(1)} collective-permute-done((bf16[1,1,128,1056]{3,2,1,0:T(8,128)(2,1)}, bf16[1,1,128,1056]{3,2,1,0:T(8,128)(2,1)S(1)}, u32[]{:S(2)}, u32[]{:S(2)}) %collective-permute-start.42) | collective-permute-done | bytes 270368 | tf_op jit(solution)/shard_map/ppermute | solution.py:1455
  529.5 2.1 stage_sums.19
  537.4 2.1 collective-permute-done.45
  540.9 4.6 collective-permute-done.46
  545.5 2.3 maximum_convert_fusion
  (275 shorter events, 86.3 us)
Async XLA Ops:
  1.3 19.7 %collective-permute-start.2 = (f32[2]{0:T(128)S(1)}, f32[2]{0:T(128)S(1)}, u32[]{:S(2)}, u32[]{:S(2)}) collective-permute-start(f32[2]{0:T(128)S(1)} %convert_element_type.40), channel_id=1, source_target_pairs={{0,4},{1,5},{2,6},{3,7},{4,0},{5,1},{6,2},{7,3},{8,12},{9,13},{10,... | collective-permute-start | bytes 32 | tf_op jit(solution)/shard_map/ppermute | solution.py:1455
  4.5 23.9 %collective-permute-start.1 = (bf16[512,1024]{1,0:T(8,128)(2,1)}, bf16[512,1024]{1,0:T(8,128)(2,1)S(1)}, u32[]{:S(2)}, u32[]{:S(2)}) collective-permute-start(bf16[512,1024]{1,0:T(8,128)(2,1)} %get-tuple-element.319), channel_id=1, source_target_pairs={{0,4},{1,0},{2,5},{3,1},{4,6},{5,2},{6,7},{7,3},{8,12},{9,8},{10,1... | collective-permute-start | bytes 3145736 | tf_op jit(solution)/shard_map/ppermute | solution.py:1455
  4.5 50.8 %collective-permute-start = (bf16[512,1024]{1,0:T(8,128)(2,1)S(1)}, bf16[512,1024]{1,0:T(8,128)(2,1)S(1)}, u32[]{:S(2)}, u32[]{:S(2)}) collective-permute-start(bf16[512,1024]{1,0:T(8,128)(2,1)S(1)} %get-tuple-element.320), channel_id=1, source_target_pairs={{0,1},{1,5},{2,0},{3,4},{4,3},{5,7},{6,2},{7,6},{8,9},{9,13},{10,8... | collective-permute-start | bytes 3145736 | tf_op jit(solution)/shard_map/ppermute | solution.py:1455
  66.3 1.8 collective-permute-start.3
  67.6 37.1 %collective-permute-start.5 = (bf16[2,512,2048]{2,1,0:T(8,128)(2,1)}, bf16[2,512,2048]{2,1,0:T(8,128)(2,1)}, u32[]{:S(2)}, u32[]{:S(2)}) collective-permute-start(bf16[2,512,2048]{2,1,0:T(8,128)(2,1)} %get-tuple-element.143.v_own.refs_7_), channel_id=1, source_target_pairs={{0,4},{1,5},{2,6},{3,7},{4,0},{5,1},{6,2},{7,3},{8,12},{9,13},{10,... | collective-permute-start | bytes 12582920 | tf_op jit(solution)/shard_map/ppermute | solution.py:1455
  87.0 17.7 %collective-permute-start.4 = (bf16[2,512,128]{2,1,0:T(8,128)(2,1)}, bf16[2,512,128]{2,1,0:T(8,128)(2,1)S(1)}, u32[]{:S(2)}, u32[]{:S(2)}) collective-permute-start(bf16[2,512,128]{2,1,0:T(8,128)(2,1)} %get-tuple-element.142.k_own.refs_5_), channel_id=1, source_target_pairs={{0,4},{1,5},{2,6},{3,7},{4,0},{5,1},{6,2},{7,3},{8,12},{9,13},{10,... | collective-permute-start | bytes 786440 | tf_op jit(solution)/shard_map/ppermute | solution.py:1455
  89.9 47.0 %collective-permute-start.7 = (bf16[512,1024]{1,0:T(8,128)(2,1)}, bf16[512,1024]{1,0:T(8,128)(2,1)S(1)}, u32[]{:S(2)}, u32[]{:S(2)}) collective-permute-start(bf16[512,1024]{1,0:T(8,128)(2,1)} %get-tuple-element.317), channel_id=1, source_target_pairs={{0,1},{1,5},{2,0},{3,4},{4,3},{5,7},{6,2},{7,6},{8,9},{9,13},{10,8... | collective-permute-start | bytes 3145736 | tf_op jit(solution)/shard_map/ppermute | solution.py:1455
  89.9 47.0 %collective-permute-start.6 = (bf16[512,1024]{1,0:T(8,128)(2,1)}, bf16[512,1024]{1,0:T(8,128)(2,1)}, u32[]{:S(2)}, u32[]{:S(2)}) collective-permute-start(bf16[512,1024]{1,0:T(8,128)(2,1)} %get-tuple-element.318), channel_id=1, source_target_pairs={{0,4},{1,0},{2,5},{3,1},{4,6},{5,2},{6,7},{7,3},{8,12},{9,8},{10,1... | collective-permute-start | bytes 3145736 | tf_op jit(solution)/shard_map/ppermute | solution.py:1455
  206.5 69.4 %collective-permute-start.8 = (bf16[512,1024]{1,0:T(8,128)(2,1)}, bf16[512,1024]{1,0:T(8,128)(2,1)}, u32[]{:S(2)}, u32[]{:S(2)}) collective-permute-start(bf16[512,1024]{1,0:T(8,128)(2,1)} %get-tuple-element.146), channel_id=1, source_target_pairs={{1,0},{5,1},{0,2},{4,3},{3,4},{7,5},{2,6},{6,7},{9,8},{13,9},{8,10... | collective-permute-start | bytes 3145736 | tf_op jit(solution)/shard_map/ppermute | solution.py:1484
  213.9 62.5 %collective-permute-start.9 = (bf16[512,1024]{1,0:T(8,128)(2,1)}, bf16[512,1024]{1,0:T(8,128)(2,1)}, u32[]{:S(2)}, u32[]{:S(2)}) collective-permute-start(bf16[512,1024]{1,0:T(8,128)(2,1)} %get-tuple-element.147), channel_id=1, source_target_pairs={{4,0},{0,1},{5,2},{1,3},{6,4},{2,5},{7,6},{3,7},{12,8},{8,9},{13,1... | collective-permute-start | bytes 3145736 | tf_op jit(solution)/shard_map/ppermute | solution.py:1484
  213.9 21.0 %collective-permute-start.10 = (bf16[1,4,1024,512]{3,2,1,0:T(8,128)(2,1)}, bf16[1,4,1024,512]{3,2,1,0:T(8,128)(2,1)}, u32[]{:S(2)}, u32[]{:S(2)}) collective-permute-start(bf16[1,4,1024,512]{3,2,1,0:T(8,128)(2,1)} %bitcast.390), channel_id=1, source_target_pairs={{0,4},{1,5},{2,6},{3,7},{4,0},{5,1},{6,2},{7,3},{8,12},{9,13},{10,... | collective-permute-start | bytes 12582920 | tf_op jit(solution)/shard_map/ppermute | solution.py:1455
  215.0 27.6 %collective-permute-start.12 = (bf16[1,4,1024,512]{3,2,1,0:T(8,128)(2,1)}, bf16[1,4,1024,512]{3,2,1,0:T(8,128)(2,1)}, u32[]{:S(2)}, u32[]{:S(2)}) collective-permute-start(bf16[1,4,1024,512]{3,2,1,0:T(8,128)(2,1)} %bitcast.389), channel_id=1, source_target_pairs={{0,4},{1,5},{2,6},{3,7},{4,0},{5,1},{6,2},{7,3},{8,12},{9,13},{10,... | collective-permute-start | bytes 12582920 | tf_op jit(solution)/shard_map/ppermute | solution.py:1455
  240.8 35.6 %collective-permute-start.11 = (bf16[1,2,1024,512]{3,2,1,0:T(8,128)(2,1)}, bf16[1,2,1024,512]{3,2,1,0:T(8,128)(2,1)S(1)}, u32[]{:S(2)}, u32[]{:S(2)}) collective-permute-start(bf16[1,2,1024,512]{3,2,1,0:T(8,128)(2,1)} %bitcast.284), channel_id=1, source_target_pairs={{0,8},{1,9},{2,10},{3,11},{4,20},{5,21},{6,22},{7,23},{8,0},{9,1},... | collective-permute-start | bytes 6291464 | tf_op jit(solution)/shard_map/ppermute | solution.py:1455
  248.4 57.4 %collective-permute-start.14 = (bf16[1,2,1024,512]{3,2,1,0:T(8,128)(2,1)}, bf16[1,2,1024,512]{3,2,1,0:T(8,128)(2,1)}, u32[]{:S(2)}, u32[]{:S(2)}) collective-permute-start(bf16[1,2,1024,512]{3,2,1,0:T(8,128)(2,1)} %bitcast.395), channel_id=1, source_target_pairs={{0,8},{1,9},{2,10},{3,11},{4,20},{5,21},{6,22},{7,23},{8,0},{9,1},... | collective-permute-start | bytes 6291464 | tf_op jit(solution)/shard_map/ppermute | solution.py:1455
  275.8 30.0 %collective-permute-start.16 = (bf16[1,4,1024,256]{3,2,1,0:T(8,128)(2,1)}, bf16[1,4,1024,256]{3,2,1,0:T(8,128)(2,1)}, u32[]{:S(2)}, u32[]{:S(2)}) collective-permute-start(bf16[1,4,1024,256]{3,2,1,0:T(8,128)(2,1)} %bitcast.274), channel_id=1, source_target_pairs={{0,4},{1,5},{2,6},{3,7},{4,0},{5,1},{6,2},{7,3},{8,12},{9,13},{10,... | collective-permute-start | bytes 6291464 | tf_op jit(solution)/shard_map/ppermute | solution.py:1455
  275.8 81.0 %collective-permute-start.23 = (bf16[1,4,128,4096]{3,2,1,0:T(8,128)(2,1)}, bf16[1,4,128,4096]{3,2,1,0:T(8,128)(2,1)}, u32[]{:S(2)}, u32[]{:S(2)}) collective-permute-start(bf16[1,4,128,4096]{3,2,1,0:T(8,128)(2,1)} %bitcast.262), channel_id=1, source_target_pairs={{0,4},{1,5},{2,6},{3,7},{4,0},{5,1},{6,2},{7,3},{8,12},{9,13},{10,... | collective-permute-start | bytes 12582920 | tf_op jit(solution)/shard_map/ppermute | solution.py:1455
  281.9 23.9 %collective-permute-start.15 = (bf16[1,1,1024,512]{3,2,1,0:T(8,128)(2,1)}, bf16[1,1,1024,512]{3,2,1,0:T(8,128)(2,1)S(1)}, u32[]{:S(2)}, u32[]{:S(2)}) collective-permute-start(bf16[1,1,1024,512]{3,2,1,0:T(8,128)(2,1)} %bitcast.406), channel_id=1, source_target_pairs={{0,16},{1,17},{2,18},{3,19},{4,12},{5,13},{6,14},{7,15},{8,24},{9,... | collective-permute-start | bytes 3145736 | tf_op jit(solution)/shard_map/ppermute | solution.py:1455
  305.3 24.7 %collective-permute-start.13 = (bf16[2,512,2176]{2,1,0:T(8,128)(2,1)}, bf16[2,512,2176]{2,1,0:T(8,128)(2,1)}, u32[]{:S(2)}, u32[]{:S(2)}) collective-permute-start(bf16[2,512,2176]{2,1,0:T(8,128)(2,1)} %get-tuple-element.168), channel_id=1, source_target_pairs={{0,4},{1,5},{2,6},{3,7},{4,0},{5,1},{6,2},{7,3},{8,12},{9,13},{10,... | collective-permute-start | bytes 13369352 | tf_op jit(solution)/shard_map/ppermute | solution.py:1455
  313.6 43.2 %collective-permute-start.22 = (bf16[1,2,256,512]{3,2,1,0:T(8,128)(2,1)}, bf16[1,2,256,512]{3,2,1,0:T(8,128)(2,1)S(1)}, u32[]{:S(2)}, u32[]{:S(2)}) collective-permute-start(bf16[1,2,256,512]{3,2,1,0:T(8,128)(2,1)} %bitcast.412), channel_id=1, source_target_pairs={{0,1},{1,0},{2,3},{3,2},{4,5},{5,4},{6,7},{7,6},{8,9},{9,8},{10,11... | collective-permute-start | bytes 1572872 | tf_op jit(solution)/shard_map/ppermute | solution.py:1455
  327.7 54.7 %collective-permute-start.17 = (bf16[1,1,1024,512]{3,2,1,0:T(8,128)(2,1)}, bf16[1,1,1024,512]{3,2,1,0:T(8,128)(2,1)}, u32[]{:S(2)}, u32[]{:S(2)}) collective-permute-start(bf16[1,1,1024,512]{3,2,1,0:T(8,128)(2,1)} %bitcast.399), channel_id=1, source_target_pairs={{0,16},{1,17},{2,18},{3,19},{4,12},{5,13},{6,14},{7,15},{8,24},{9,... | collective-permute-start | bytes 3145736 | tf_op jit(solution)/shard_map/ppermute | solution.py:1455
  327.7 54.7 %collective-permute-start.19 = (bf16[1,2,1024,256]{3,2,1,0:T(8,128)(2,1)}, bf16[1,2,1024,256]{3,2,1,0:T(8,128)(2,1)}, u32[]{:S(2)}, u32[]{:S(2)}) collective-permute-start(bf16[1,2,1024,256]{3,2,1,0:T(8,128)(2,1)} %bitcast.397), channel_id=1, source_target_pairs={{0,8},{1,9},{2,10},{3,11},{4,20},{5,21},{6,22},{7,23},{8,0},{9,1},... | collective-permute-start | bytes 3145736 | tf_op jit(solution)/shard_map/ppermute | solution.py:1455
  353.1 29.3 %collective-permute-start.20 = (bf16[1,4,128,128]{3,2,1,0:T(8,128)(2,1)}, bf16[1,4,128,128]{3,2,1,0:T(8,128)(2,1)S(1)}, u32[]{:S(2)}, u32[]{:S(2)}) collective-permute-start(bf16[1,4,128,128]{3,2,1,0:T(8,128)(2,1)} %bitcast.353), channel_id=1, source_target_pairs={{0,4},{1,5},{2,6},{3,7},{4,0},{5,1},{6,2},{7,3},{8,12},{9,13},{10,... | collective-permute-start | bytes 393224 | tf_op jit(solution)/shard_map/ppermute | solution.py:1455
  364.0 43.8 %collective-permute-start.26 = (bf16[1,2,128,4096]{3,2,1,0:T(8,128)(2,1)}, bf16[1,2,128,4096]{3,2,1,0:T(8,128)(2,1)}, u32[]{:S(2)}, u32[]{:S(2)}) collective-permute-start(bf16[1,2,128,4096]{3,2,1,0:T(8,128)(2,1)} %bitcast.391), channel_id=1, source_target_pairs={{0,8},{1,9},{2,10},{3,11},{4,20},{5,21},{6,22},{7,23},{8,0},{9,1},... | collective-permute-start | bytes 6291464 | tf_op jit(solution)/shard_map/ppermute | solution.py:1455
  364.0 18.4 %collective-permute-start.18 = (bf16[1,4,512,512]{3,2,1,0:T(8,128)(2,1)}, bf16[1,4,512,512]{3,2,1,0:T(8,128)(2,1)S(1)}, u32[]{:S(2)}, u32[]{:S(2)}) collective-permute-start(bf16[1,4,512,512]{3,2,1,0:T(8,128)(2,1)} %bitcast.394), channel_id=1, source_target_pairs={{0,4},{1,5},{2,6},{3,7},{4,0},{5,1},{6,2},{7,3},{8,12},{9,13},{10,... | collective-permute-start | bytes 6291464 | tf_op jit(solution)/shard_map/ppermute | solution.py:1455
  389.7 22.3 %collective-permute-start.27 = (bf16[1,2,512,512]{3,2,1,0:T(8,128)(2,1)}, bf16[1,2,512,512]{3,2,1,0:T(8,128)(2,1)S(1)}, u32[]{:S(2)}, u32[]{:S(2)}) collective-permute-start(bf16[1,2,512,512]{3,2,1,0:T(8,128)(2,1)} %bitcast.305), channel_id=1, source_target_pairs={{0,8},{1,9},{2,10},{3,11},{4,20},{5,21},{6,22},{7,23},{8,0},{9,1},... | collective-permute-start | bytes 3145736 | tf_op jit(solution)/shard_map/ppermute | solution.py:1455
  392.1 15.4 %collective-permute-start.24 = (bf16[1,1,256,512]{3,2,1,0:T(8,128)(2,1)}, bf16[1,1,256,512]{3,2,1,0:T(8,128)(2,1)}, u32[]{:S(2)}, u32[]{:S(2)}) collective-permute-start(bf16[1,1,256,512]{3,2,1,0:T(8,128)(2,1)} %bitcast.85), channel_id=1, source_target_pairs={{0,2},{1,3},{2,0},{3,1},{4,6},{5,7},{6,4},{7,5},{8,10},{9,11},{10,... | collective-permute-start | bytes 786440 | tf_op jit(solution)/shard_map/ppermute | solution.py:1455
  392.5 19.5 %collective-permute-start.25 = (bf16[1,2,256,512]{3,2,1,0:T(8,128)(2,1)}, bf16[1,2,256,512]{3,2,1,0:T(8,128)(2,1)}, u32[]{:S(2)}, u32[]{:S(2)}) collective-permute-start(bf16[1,2,256,512]{3,2,1,0:T(8,128)(2,1)} %bitcast.319), channel_id=1, source_target_pairs={{0,1},{1,0},{2,3},{3,2},{4,5},{5,4},{6,7},{7,6},{8,9},{9,8},{10,11... | collective-permute-start | bytes 1572872 | tf_op jit(solution)/shard_map/ppermute | solution.py:1455
  402.8 1.6 collective-permute-start.21
  404.3 4.3 collective-permute-start.28
  407.4 34.6 %collective-permute-start.32 = (bf16[1,1,1024,256]{3,2,1,0:T(8,128)(2,1)S(1)}, bf16[1,1,1024,256]{3,2,1,0:T(8,128)(2,1)S(1)}, u32[]{:S(2)}, u32[]{:S(2)}) collective-permute-start(bf16[1,1,1024,256]{3,2,1,0:T(8,128)(2,1)S(1)} %bitcast.317), channel_id=1, source_target_pairs={{0,16},{1,17},{2,18},{3,19},{4,12},{5,13},{6,14},{7,15},{8,24},{9,... | collective-permute-start | bytes 1572872 | tf_op jit(solution)/shard_map/ppermute | solution.py:1455
  418.1 25.7 %collective-permute-start.33 = (bf16[1,1,128,128]{3,2,1,0:T(8,128)(2,1)}, bf16[1,1,128,128]{3,2,1,0:T(8,128)(2,1)S(1)}, u32[]{:S(2)}, u32[]{:S(2)}) collective-permute-start(bf16[1,1,128,128]{3,2,1,0:T(8,128)(2,1)} %bitcast.424), channel_id=1, source_target_pairs={{0,16},{1,17},{2,18},{3,19},{4,12},{5,13},{6,14},{7,15},{8,24},{9,... | collective-permute-start | bytes 98312 | tf_op jit(solution)/shard_map/ppermute | solution.py:1455
  419.4 24.4 %collective-permute-start.29 = (bf16[1,1,256,512]{3,2,1,0:T(8,128)(2,1)}, bf16[1,1,256,512]{3,2,1,0:T(8,128)(2,1)S(1)}, u32[]{:S(2)}, u32[]{:S(2)}) collective-permute-start(bf16[1,1,256,512]{3,2,1,0:T(8,128)(2,1)} %bitcast.422), channel_id=1, source_target_pairs={{0,2},{1,3},{2,0},{3,1},{4,6},{5,7},{6,4},{7,5},{8,10},{9,11},{10,... | collective-permute-start | bytes 786440 | tf_op jit(solution)/shard_map/ppermute | solution.py:1455
  419.8 24.0 %collective-permute-start.31 = (bf16[1,1,512,512]{3,2,1,0:T(8,128)(2,1)}, bf16[1,1,512,512]{3,2,1,0:T(8,128)(2,1)S(1)}, u32[]{:S(2)}, u32[]{:S(2)}) collective-permute-start(bf16[1,1,512,512]{3,2,1,0:T(8,128)(2,1)} %bitcast.410), channel_id=1, source_target_pairs={{0,16},{1,17},{2,18},{3,19},{4,12},{5,13},{6,14},{7,15},{8,24},{9,... | collective-permute-start | bytes 1572872 | tf_op jit(solution)/shard_map/ppermute | solution.py:1455
  421.1 22.8 %collective-permute-start.30 = (bf16[1,1,128,4096]{3,2,1,0:T(8,128)(2,1)}, bf16[1,1,128,4096]{3,2,1,0:T(8,128)(2,1)S(1)}, u32[]{:S(2)}, u32[]{:S(2)}) collective-permute-start(bf16[1,1,128,4096]{3,2,1,0:T(8,128)(2,1)} %bitcast.401), channel_id=1, source_target_pairs={{0,16},{1,17},{2,18},{3,19},{4,12},{5,13},{6,14},{7,15},{8,24},{9,... | collective-permute-start | bytes 3145736 | tf_op jit(solution)/shard_map/ppermute | solution.py:1455
  442.1 40.2 %collective-permute-start.35 = (bf16[512,1024]{1,0:T(8,128)(2,1)}, bf16[512,1024]{1,0:T(8,128)(2,1)S(1)}, u32[]{:S(2)}, u32[]{:S(2)}) collective-permute-start(bf16[512,1024]{1,0:T(8,128)(2,1)} %get-tuple-element.209.refs_10_), channel_id=1, source_target_pairs={{4,0},{0,1},{5,2},{1,3},{6,4},{2,5},{7,6},{3,7},{12,8},{8,9},{13,1... | collective-permute-start | bytes 3145736 | tf_op jit(solution)/shard_map/ppermute | solution.py:1484
  449.8 32.5 %collective-permute-start.38 = (bf16[1,2,128,512]{3,2,1,0:T(8,128)(2,1)}, bf16[1,2,128,512]{3,2,1,0:T(8,128)(2,1)}, u32[]{:S(2)}, u32[]{:S(2)}) collective-permute-start(bf16[1,2,128,512]{3,2,1,0:T(8,128)(2,1)} %bitcast.420), channel_id=1, source_target_pairs={{0,1},{1,0},{2,3},{3,2},{4,5},{5,4},{6,7},{7,6},{8,9},{9,8},{10,11... | collective-permute-start | bytes 786440 | tf_op jit(solution)/shard_map/ppermute | solution.py:1455
  450.7 31.6 %collective-permute-start.37 = (bf16[1,2,256,256]{3,2,1,0:T(8,128)(2,1)}, bf16[1,2,256,256]{3,2,1,0:T(8,128)(2,1)}, u32[]{:S(2)}, u32[]{:S(2)}) collective-permute-start(bf16[1,2,256,256]{3,2,1,0:T(8,128)(2,1)} %bitcast.418), channel_id=1, source_target_pairs={{0,1},{1,0},{2,3},{3,2},{4,5},{5,4},{6,7},{7,6},{8,9},{9,8},{10,11... | collective-permute-start | bytes 786440 | tf_op jit(solution)/shard_map/ppermute | solution.py:1455
  455.8 25.4 %collective-permute-start.36 = (bf16[1,2,128,1056]{2,3,1,0:T(8,128)(2,1)}, bf16[1,2,128,1056]{2,3,1,0:T(8,128)(2,1)S(1)}, u32[]{:S(2)}, u32[]{:S(2)}) collective-permute-start(bf16[1,2,128,1056]{2,3,1,0:T(8,128)(2,1)} %get-tuple-element.321), channel_id=1, source_target_pairs={{0,1},{1,0},{2,3},{3,2},{4,5},{5,4},{6,7},{7,6},{8,9},{9,8},{10,11... | collective-permute-start | bytes 1622024 | tf_op jit(solution)/shard_map/ppermute | solution.py:1455
  478.1 49.7 %collective-permute-start.34 = (bf16[512,1024]{1,0:T(8,128)(2,1)}, bf16[512,1024]{1,0:T(8,128)(2,1)S(1)}, u32[]{:S(2)}, u32[]{:S(2)}) collective-permute-start(bf16[512,1024]{1,0:T(8,128)(2,1)} %get-tuple-element.217.refs_6_), channel_id=1, source_target_pairs={{1,0},{5,1},{0,2},{4,3},{3,4},{7,5},{2,6},{6,7},{9,8},{13,9},{8,10... | collective-permute-start | bytes 3145736 | tf_op jit(solution)/shard_map/ppermute | solution.py:1484
  488.4 2.1 collective-permute-start.39
  491.5 6.8 %collective-permute-start.40 = (f32[320,128]{1,0:T(8,128)S(1)}, f32[320,128]{1,0:T(8,128)S(1)}, u32[]{:S(2)}, u32[]{:S(2)}) collective-permute-start(f32[320,128]{1,0:T(8,128)S(1)} %add.145), channel_id=1, source_target_pairs={{0,8},{1,9},{2,10},{3,11},{4,12},{5,13},{6,14},{7,15},{8,0},{9,1},... | collective-permute-start | bytes 491528 | tf_op jit(solution)/shard_map/ppermute | solution.py:1455
  492.5 26.3 %collective-permute-start.43 = (bf16[1,1,256,256]{3,2,1,0:T(8,128)(2,1)}, bf16[1,1,256,256]{3,2,1,0:T(8,128)(2,1)S(1)}, u32[]{:S(2)}, u32[]{:S(2)}) collective-permute-start(bf16[1,1,256,256]{3,2,1,0:T(8,128)(2,1)} %bitcast.327), channel_id=1, source_target_pairs={{0,2},{1,3},{2,0},{3,1},{4,6},{5,7},{6,4},{7,5},{8,10},{9,11},{10,... | collective-permute-start | bytes 393224 | tf_op jit(solution)/shard_map/ppermute | solution.py:1455
  495.3 26.2 %collective-permute-start.44 = (bf16[1,1,128,512]{3,2,1,0:T(8,128)(2,1)}, bf16[1,1,128,512]{3,2,1,0:T(8,128)(2,1)S(1)}, u32[]{:S(2)}, u32[]{:S(2)}) collective-permute-start(bf16[1,1,128,512]{3,2,1,0:T(8,128)(2,1)} %bitcast.330), channel_id=1, source_target_pairs={{0,2},{1,3},{2,0},{3,1},{4,6},{5,7},{6,4},{7,5},{8,10},{9,11},{10,... | collective-permute-start | bytes 393224 | tf_op jit(solution)/shard_map/ppermute | solution.py:1455
  495.4 32.4 %collective-permute-start.42 = (bf16[1,1,128,1056]{3,2,1,0:T(8,128)(2,1)}, bf16[1,1,128,1056]{3,2,1,0:T(8,128)(2,1)S(1)}, u32[]{:S(2)}, u32[]{:S(2)}) collective-permute-start(bf16[1,1,128,1056]{3,2,1,0:T(8,128)(2,1)} %bitcast.287), channel_id=1, source_target_pairs={{0,2},{1,3},{2,0},{3,1},{4,6},{5,7},{6,4},{7,5},{8,10},{9,11},{10,... | collective-permute-start | bytes 811016 | tf_op jit(solution)/shard_map/ppermute | solution.py:1455
  498.3 33.3 %collective-permute-start.41 = (f32[320,128]{1,0:T(8,128)S(1)}, f32[320,128]{1,0:T(8,128)S(1)}, u32[]{:S(2)}, u32[]{:S(2)}) collective-permute-start(f32[320,128]{1,0:T(8,128)S(1)} %add.146.refs_0_), channel_id=1, source_target_pairs={{0,16},{1,17},{2,18},{3,19},{4,20},{5,21},{6,22},{7,23},{8,24},{9,... | collective-permute-start | bytes 491528 | tf_op jit(solution)/shard_map/ppermute | solution.py:1455
  535.0 4.4 collective-permute-start.45
  539.5 5.9 %collective-permute-start.46 = (f32[160,128]{1,0:T(8,128)S(1)}, f32[160,128]{1,0:T(8,128)S(1)}, u32[]{:S(2)}, u32[]{:S(2)}) collective-permute-start(f32[160,128]{1,0:T(8,128)S(1)} %fusion.27), channel_id=1, source_target_pairs={{0,2},{1,3},{2,0},{3,1},{4,6},{5,7},{6,4},{7,5},{8,10},{9,11},{10,... | collective-permute-start | bytes 245768 | tf_op jit(solution)/shard_map/ppermute | solution.py:1455
  545.5 3.4 collective-permute-start.47
  (61 other events, 539.7 us)

commit v6 on v5

--- a/solution.py
+++ b/solution.py
@@ -265,43 +265,49 @@
 
 def back_ends_body(gs_ref, decay_ref, end_ref, slab):
     states, groups, _ = decay_ref.shape
-    count = gs_ref.shape[1]
-
-    @pl.when(pl.program_id(1) == 0)
+    slots, count, _ = gs_ref.shape
+
+    @pl.when(pl.program_id(0) == 0)
     def _():
         end_ref[...] = jnp.zeros_like(end_ref)
 
-    to_slab(slab, gs_ref[0])
+    for k in range(slots):
+        to_slab(slab.at[k], gs_ref[k])
     decay = [decay_ref[n] for n in range(states)]
 
     def step(t, state):
-        row = slab_row(slab, count - 1 - t, groups)
-        return tuple(d * s + row for d, s in zip(decay, state))
+        rows = [slab_row(slab.at[k], count - 1 - t, groups) for k in range(slots)]
+        return [tuple(d * s + row for d, s in zip(decay, held)) for row, held in zip(rows, state)]
 
     state = lax.fori_loop(
-        0, count, step, tuple(end_ref[0, n] for n in range(states)), unroll=8
-    )
-    for n in range(states):
-        end_ref[0, n] = state[n]
-
-
-def back_ends(gs, decay, block=256, after=()):
+        0,
+        count,
+        step,
+        [tuple(end_ref[k, n] for n in range(states)) for k in range(slots)],
+        unroll=8,
+    )
+    for k in range(slots):
+        for n in range(states):
+            end_ref[k, n] = state[k][n]
+
+
+def back_ends(gs, decay, block=128, after=()):
     slots, length, width = gs.shape
     states, groups, lanes = decay.shape
     block = min(block, length)
     blocks = length // block
     return pl.pallas_call(
         ignoring(back_ends_body, 2, len(after)),
-        grid=(slots, blocks),
+        grid=(blocks,),
         in_specs=[
-            pl.BlockSpec((1, block, width), lambda k, b: (k, blocks - 1 - b, 0)),
-            pl.BlockSpec((states, groups, lanes), lambda k, b: (0, 0, 0)),
+            pl.BlockSpec((slots, block, width), lambda b: (0, blocks - 1 - b, 0)),
+            pl.BlockSpec((states, groups, lanes), lambda b: (0, 0, 0)),
         ]
         + [pl.BlockSpec(memory_space=pl.ANY)] * len(after),
-        out_specs=pl.BlockSpec((1, states, groups, lanes), lambda k, b: (k, 0, 0, 0)),
+        out_specs=pl.BlockSpec((slots, states, groups, lanes), lambda b: (0, 0, 0, 0)),
         out_shape=jax.ShapeDtypeStruct((slots, states, groups, lanes), f32),
-        scratch_shapes=[pltpu.VMEM((block * groups, lanes), f32)],
-        compiler_params=params(("arbitrary", "arbitrary")),
+        scratch_shapes=[pltpu.VMEM((slots, block * groups, lanes), f32)],
+        compiler_params=params(("arbitrary",)),
         name="back_ends",
         cost_estimate=BRIEF,
     )(gs, decay, *after)
@@ -571,7 +577,7 @@
             span = pl.ds(pl.multiple_of(base, length), width)
 
             def column(ct, _):
-                at = pl.ds(pl.multiple_of(ct * 512, 512), 512)
+                at = pl.ds(pl.multiple_of(ct * 1024, 1024), 1024)
                 rows = (
                     jnp.dot(probs[:, :width], values[span, at], preferred_element_type=f32)
                     * inverse
@@ -581,7 +587,7 @@
                 gated_ref[0, :, at] = (gate * jax.nn.sigmoid(gate) * rows).astype(bf16)
                 return 0
 
-            lax.fori_loop(0, value_width // 512, column, 0)
+            lax.fori_loop(0, value_width // 1024, column, 0)
 
 
 def attend(table, q, bias, reset, k_own, k_oth, v_own, v_oth):
@@ -719,13 +725,13 @@
         gk_sum[spot, :] += jnp.dot(grad_scores, queries, preferred_element_type=f32)
 
         def column(ct, _):
-            at = pl.ds(pl.multiple_of(ct * 512, 512), 512)
+            at = pl.ds(pl.multiple_of(ct * 1024, 1024), 1024)
             gv_sum[spot, at] += jnp.dot(
                 probs, grad_ref[0, :, at], preferred_element_type=f32
             )
             return 0
 
-        lax.fori_loop(0, value_width // 512, column, 0)
+        lax.fori_loop(0, value_width // 1024, column, 0)
         return grad_query + lax.dot_general(
             grad_scores, keys[spot, :], tn, preferred_element_type=f32
         )
@@ -885,6 +891,53 @@
     return jnp.concatenate(
         [blocks[::-1].reshape(-1), jnp.zeros((2 * length - (count + 1) * TILE,), f32)]
     )
+
+
+def candidate_body(
+    gated_ref, proj_ref, pre_ref, update_ref, x_ref, gain_ref, cand_ref, first_ref, low_ref
+):
+    cand_in = pre_ref[...].astype(f32) + jnp.dot(
+        gated_ref[...], proj_ref[...], preferred_element_type=f32
+    )
+    cand_ref[...] = cand_in
+    x = x_ref[...].astype(f32)
+    update = jax.nn.sigmoid(update_ref[...].astype(f32))
+    first = x + update * (cand_in * jax.nn.sigmoid(cand_in) - x)
+    first_ref[...] = first
+    unit, _ = unit_rows_of(first)
+    low_ref[...] = (unit * gain_ref[...]).astype(bf16)
+
+
+def candidate(gated, proj, base, x, gain):
+    tokens, width = x.shape
+    value_width = gated.shape[1]
+    rows = min(256, tokens)
+    wide = value_width // width
+
+    def block(columns, at=0):
+        return pl.BlockSpec((rows, columns), lambda i: (i, at))
+
+    return pl.pallas_call(
+        candidate_body,
+        grid=(tokens // rows,),
+        in_specs=[
+            block(value_width),
+            pl.BlockSpec(proj.shape, lambda i: (0, 0), pipeline_mode=pl.Buffered(1)),
+            block(width, wide + 1),
+            block(width, wide),
+            block(width),
+            pl.BlockSpec((1, width), lambda i: (0, 0)),
+        ],
+        out_specs=[block(width)] * 3,
+        out_shape=[
+            jax.ShapeDtypeStruct((tokens, width), f32),
+            jax.ShapeDtypeStruct((tokens, width), f32),
+            jax.ShapeDtypeStruct((tokens, width), bf16),
+        ],
+        compiler_params=params(("arbitrary",)),
+        name="candidate",
+        cost_estimate=BRIEF,
+    )(gated, proj, base, base, x, gain)
 
 
 def gate_body(
@@ -1188,6 +1241,59 @@
     )(left, right)
 
 
+def smooth_back_body(
+    main_ref, shared_ref, weight_ref, shared_weight_ref, smooth_ref, out_ref, total
+):
+    step = pl.program_id(0)
+
+    @pl.when(step == 0)
+    def _():
+        total[...] = mm_nt(shared_ref[...], shared_weight_ref[...])
+
+    total[...] += mm_nt(main_ref[...], weight_ref[...])
+
+    @pl.when(step == pl.num_programs(0) - 1)
+    def _():
+        out_ref[...] = total[...] * silu_slope(smooth_ref[...])
+
+
+def smooth_back(main, shared, weight, shared_weight, smoothed, after=(), riders=None):
+    tokens, width = smoothed.shape
+    tile = 1024
+
+    def all_of(shape):
+        return pl.BlockSpec(shape, lambda i: (0, 0), pipeline_mode=pl.Buffered(1))
+
+    extra = riders or Riders([], 1)
+    taken, given = len(extra.ins), len(extra.out_shapes)
+
+    def body(*refs):
+        first = 5 + taken + len(after)
+        smooth_back_body(*refs[:5], refs[first], *refs[first + 1 + given :])
+        extra.body(refs[5 : 5 + taken], refs[first + 1 : first + 1 + given])
+
+    out = pl.pallas_call(
+        body,
+        grid=(main.shape[1] // tile,),
+        in_specs=[
+            pl.BlockSpec((tokens, tile), lambda i: (0, i)),
+            all_of(shared.shape),
+            pl.BlockSpec((width, tile), lambda i: (0, i)),
+            all_of(shared_weight.shape),
+            all_of(smoothed.shape),
+        ]
+        + extra.in_specs
+        + [pl.BlockSpec(memory_space=pl.ANY)] * len(after),
+        out_specs=[all_of(smoothed.shape)] + extra.out_specs,
+        out_shape=[jax.ShapeDtypeStruct(smoothed.shape, f32)] + extra.out_shapes,
+        scratch_shapes=[pltpu.VMEM(smoothed.shape, f32)],
+        compiler_params=params(("arbitrary",)),
+        name="smooth_back",
+        cost_estimate=LONG,
+    )(main, shared, weight, shared_weight, smoothed, *extra.ins, *after)
+    return (out[0], riders.result(out[1:])) if riders else out[0]
+
+
 def by_columns_body(ids_ref, places_ref, left_ref, right_ref, send, keep, plain, turned):
     step = pl.program_id(0)
     half = pl.num_programs(0) // 2
@@ -1264,7 +1370,7 @@
     keep[...] = grad[middle:].reshape(keep.shape)
 
 
-def by_rows(ids, places, left, right, seq=1, after=(), cost=BRIEF):
+def by_rows(ids, places, left, right, seq=1, after=(), cost=BRIEF, riders=None):
     tokens, rows = left.shape
     parts = ids.shape[0]
     half = parts // 2
@@ -1277,8 +1383,16 @@
     split = pl.BlockSpec(
         (half, 1, rows // parts, tile), lambda i, t, u: (0, u[jnp.minimum(i // share, seq - 1)], 0, i % share)
     )
-    return pl.pallas_call(
-        ignoring(by_rows_body, 4, len(after)),
+    extra = riders or Riders([], 1)
+    taken, given = len(extra.ins), len(extra.out_shapes)
+
+    def body(*refs):
+        first = 4 + taken + len(after)
+        by_rows_body(*refs[:4], *refs[first : first + 2], *refs[first + 2 + given :])
+        extra.body(refs[4 : 4 + taken], refs[first + 2 : first + 2 + given])
+
+    out = pl.pallas_call(
+        body,
         grid_spec=pltpu.PrefetchScalarGridSpec(
             num_scalar_prefetch=2,
             grid=(seq * share,),
@@ -1288,18 +1402,20 @@
                 ),
                 pl.BlockSpec((tokens, tile), lambda i, t, u: (0, i)),
             ]
+            + extra.in_specs
             + [pl.BlockSpec(memory_space=pl.ANY)] * len(after),
-            out_specs=[split, split],
+            out_specs=[split, split] + extra.out_specs,
             scratch_shapes=[
                 pltpu.VMEM((rows, tokens), bf16),
                 pltpu.VMEM((rows, tokens), bf16),
             ],
         ),
-        out_shape=[shape, shape],
+        out_shape=[shape, shape] + extra.out_shapes,
         compiler_params=params(("arbitrary",)),
         name="by_rows",
         cost_estimate=cost,
-    )(ids, places, left, right, *after)
+    )(ids, places, left, right, *extra.ins, *after)
+    return (out[:2], riders.result(out[2:])) if riders else out
 
 
 def value_back_body(
@@ -1374,66 +1490,79 @@
     )(ids, places, left, own, others, slope, proj, *after)
 
 
-def stage_body(*refs, shapes):
-    count = sum(pairs for pairs, _, _ in shapes)
-    ins, outs = list(refs[: 2 * count]), list(refs[2 * count :])
-    for pairs, halves, turned in shapes:
-        into = [outs.pop(0) for _ in range(halves)]
-        start = 0
-        for _ in range(pairs):
-            kept, arrived = ins.pop(0), ins.pop(0)
-            stop = start + kept.shape[0]
-            for part, out in enumerate(into):
-                total = kept[:, part].astype(f32) + arrived[:, part].astype(f32)
-                if turned:
-                    out[0] = total[0].T
-                else:
-                    out[start:stop] = total.astype(out.dtype)
-            start = stop
+class Riders:
+    def __init__(self, groups, steps):
+        self.shapes, self.ins, self.whole = [], [], []
+        self.in_specs, self.out_specs, self.out_shapes = [], [], []
+        for pairs, single, kind in groups:
+            halves = 1 if single else 2
+            g, n, rows, columns = pairs[0][0].shape
+            each = n * rows // halves // steps
+            self.shapes.append((len(pairs), halves))
+            for pair in pairs:
+                for v in pair:
+                    self.ins.append(v.reshape(g, halves, n * rows // halves, columns))
+                    self.in_specs.append(
+                        pl.BlockSpec((g, halves, each, columns), lambda i, *_: (0, 0, i, 0))
+                    )
+            for _ in range(halves):
+                self.out_specs.append(
+                    pl.BlockSpec((len(pairs) * g, each, columns), lambda i, *_: (0, i, 0))
+                )
+                self.out_shapes.append(
+                    jax.ShapeDtypeStruct((len(pairs) * g, n * rows // halves, columns), kind)
+                )
+            self.whole.append((halves, (len(pairs) * g, n // halves, rows, columns)))
+
+    @staticmethod
+    def fit(groups, steps):
+        for pairs, single, _ in groups:
+            _, n, rows, _ = pairs[0][0].shape
+            while (n * rows // (1 if single else 2)) % (16 * steps) and steps > 1:
+                steps //= 2
+        return steps
+
+    def body(self, ins, outs):
+        ins, outs = list(ins), list(outs)
+        for pairs, halves in self.shapes:
+            into = [outs.pop(0) for _ in range(halves)]
+            start = 0
+            for _ in range(pairs):
+                kept, arrived = ins.pop(0), ins.pop(0)
+                stop = start + kept.shape[0]
+                for part, out in enumerate(into):
+                    out[start:stop] = (
+                        kept[:, part].astype(f32) + arrived[:, part].astype(f32)
+                    ).astype(out.dtype)
+                start = stop
+
+    def result(self, sums):
+        sums = list(sums)
+        return [
+            tuple(sums.pop(0).reshape(shape) for _ in range(halves))
+            for halves, shape in self.whole
+        ]
 
 
 def stage_sums(groups, after=(), steps=4, cost=BRIEF):
-    shapes, ins, in_specs, out_specs, out_shapes, whole = [], [], [], [], [], []
-    for pairs, single, kind in groups:
-        _, n, rows, _ = pairs[0][0].shape
-        lanes = 128 if kind == "turned" else 16
-        while (n * rows // (1 if single else 2)) % (lanes * steps) and steps > 1:
-            steps //= 2
-    for pairs, single, kind in groups:
-        halves = 1 if single else 2
-        g, n, rows, columns = pairs[0][0].shape
-        each = n * rows // halves // steps
-        shapes.append((len(pairs), halves, kind == "turned"))
-        for pair in pairs:
-            for v in pair:
-                ins.append(v.reshape(g, halves, n * rows // halves, columns))
-                in_specs.append(
-                    pl.BlockSpec((g, halves, each, columns), lambda i: (0, 0, i, 0))
-                )
-        if kind == "turned":
-            out_specs.append(pl.BlockSpec((1, columns, each), lambda i: (0, 0, i)))
-            out_shapes.append(jax.ShapeDtypeStruct((1, columns, rows), f32))
-            whole.append((1, (1, 1, columns, rows)))
-            continue
-        for _ in range(halves):
-            out_specs.append(pl.BlockSpec((len(pairs) * g, each, columns), lambda i: (0, i, 0)))
-            out_shapes.append(
-                jax.ShapeDtypeStruct((len(pairs) * g, n * rows // halves, columns), kind)
-            )
-        whole.append((halves, (len(pairs) * g, n // halves, rows, columns)))
-    sums = list(
-        pl.pallas_call(
-            ignoring(functools.partial(stage_body, shapes=shapes), len(ins), len(after)),
-            grid=(steps,),
-            in_specs=in_specs + [pl.BlockSpec(memory_space=pl.ANY)] * len(after),
-            out_specs=out_specs,
-            out_shape=out_shapes,
-            compiler_params=params(("arbitrary",)),
-            name="stage_sums",
-            cost_estimate=cost,
-        )(*ins, *after)
-    )
-    return [tuple(sums.pop(0).reshape(shape) for _ in range(halves)) for halves, shape in whole]
+    steps = Riders.fit(groups, steps)
+    riders = Riders(groups, steps)
+    count = len(riders.ins)
+
+    def body(*refs):
+        riders.body(refs[:count], refs[count + len(after) :])
+
+    sums = pl.pallas_call(
+        body,
+        grid=(steps,),
+        in_specs=riders.in_specs + [pl.BlockSpec(memory_space=pl.ANY)] * len(after),
+        out_specs=riders.out_specs,
+        out_shape=riders.out_shapes,
+        compiler_params=params(("arbitrary",)),
+        name="stage_sums",
+        cost_estimate=cost,
+    )(*riders.ins, *after)
+    return riders.result(sums)
 
 
 class Layout:
@@ -1545,10 +1674,10 @@
             return lambda d, z: (d ^ (1 << stage if d % 2 == 0 else 1 << (bits - stage)), z)
         return lambda d, z: (d, z ^ (1 << (stage - bits)))
 
-    def turn(self, sums, after, cost=BRIEF):
+    def turn(self, sums, after, cost=BRIEF, carrier=None, steps=None):
         sums = [s for s in sums if s.arrived]
         if not sums:
-            return after
+            return carrier(None, after) if carrier else after
         dp_stages = self.dp.bit_length() - 1
         last = dp_stages + self.seq.bit_length() - 1
         groups = []
@@ -1564,11 +1693,15 @@
                         )
                         for pair in pairs
                     ]
-            kind = bf16
-            if s.stage + 1 == last:
-                kind = "turned" if s.turned else f32
-            groups.append((pairs, single, kind))
-        out = stage_sums(groups, after, cost=cost)
+            groups.append((pairs, single, f32 if s.stage + 1 == last else bf16))
+        if carrier:
+            if Riders.fit(groups, steps) == steps:
+                own, out = carrier(Riders(groups, steps), after)
+            else:
+                out = stage_sums(groups, after, cost=cost)
+                own = carrier(None, [part for held in out for part in held])
+        else:
+            out = stage_sums(groups, after, cost=cost)
         for s, held, (_, single, _) in zip(sums, out, groups):
             s.stage += 1
             s.arrived = ()
@@ -1576,15 +1709,15 @@
                 s.total = held[0]
             else:
                 s.send([held[0]], [held[1]])
+        if carrier:
+            return own
         return [part for held in out for part in held]
 
     def over_seq(self, held):
-        core = lax.axis_index("dp") % 2
-        split = held.reshape(2, -1, held.shape[-1])
-        held = lax.dynamic_index_in_dim(split, core, 0, False)
-        for bit in range(self.seq.bit_length() - 1):
-            held = held + self.send(held, lambda d, z: (d, z ^ (1 << bit)))
-        return held, self.send(held, lambda d, z: (d ^ 1, z))
+        bits = self.seq.bit_length() - 1
+        for bit in range(bits - 1):
+            held = held + self.send(held.astype(bf16), lambda d, z: (d, z ^ (1 << bit))).astype(f32)
+        return held, self.send(held.astype(bf16), lambda d, z: (d, z ^ (1 << (bits - 1))))
 
 
     def over_dp(self, held):
@@ -1632,12 +1765,9 @@
 
 
 def finish_body(
-    core_ref, mine, other, alpha, damp, beta, eta, alpha_out, damp_out, beta_out, eta_out, rest, rows
+    mine, other, alpha, damp, beta, eta, alpha_out, damp_out, beta_out, eta_out, rest, rows
 ):
-    half = mine.shape[0]
-    first = core_ref[0] == 0
-    rows[:half] = jnp.where(first, mine[...], other[...])
-    rows[half:] = jnp.where(first, other[...], mine[...])
+    rows[...] = mine[...] + other[...].astype(f32)
     states = alpha.shape[0]
     groups = alpha.shape[1] // 128
     for c in range(groups):
@@ -1654,26 +1784,25 @@
     rest[...] = rows[2 * states * groups :]
 
 
-def finish(core, mine, other, alpha, damp, beta, eta):
+def finish(mine, other, alpha, damp, beta, eta):
     inside = pl.BlockSpec(memory_space=pltpu.VMEM)
-    rows = 2 * mine.shape[0]
+    rows = mine.shape[0]
     shape = jax.ShapeDtypeStruct(alpha.shape, f32)
     left = rows - 2 * alpha.size // 128
     return pl.pallas_call(
         finish_body,
-        in_specs=[pl.BlockSpec(memory_space=pltpu.SMEM)] + [inside] * 6,
+        in_specs=[inside] * 6,
         out_specs=[inside] * 5,
         out_shape=[shape] * 4 + [jax.ShapeDtypeStruct((left, 128), f32)],
         scratch_shapes=[pltpu.VMEM((rows, 128), f32)],
         name="finish",
         cost_estimate=BRIEF,
-    )(core[None].astype(jnp.int32), mine, other, alpha, damp, beta, eta)
+    )(mine, other, alpha, damp, beta, eta)
 
 
 class Sum:
-    def __init__(self, layout, *pairs, over_seq=True, turned=False):
+    def __init__(self, layout, *pairs, over_seq=True):
         self.layout, self.over_seq, self.stage = layout, over_seq, 0
-        self.turned = turned
         self.total = None
         pairs = [[v.reshape(1, v.shape[0], -1, v.shape[-1]) for v in pair] for pair in pairs]
         self.send([p[0] for p in pairs], [p[1] for p in pairs])
@@ -1811,26 +1940,19 @@
     gated = gated.reshape(tokens, value_width)
 
     flat_low = x.reshape(tokens, width)
-    flat = flat_low.astype(f32)
-    update_pre = base[:, value_width : value_width + width].astype(f32)
-    cand_in = base[:, value_width + width :].astype(f32) + mm(gated, out_proj)
-    first_sum = flat + jax.nn.sigmoid(update_pre) * (jax.nn.silu(cand_in) - flat)
-    unit_two, _ = unit_rows_of(first_sum)
-    feed_low = (unit_two * feed_gain).astype(bf16)
+    cand_in, first_sum, feed_low = candidate(gated, out_proj, base, flat_low, feed_gain[None])
 
     result_a, result_b, grad_feed, out_send, out_keep, in_send, in_keep = feed(
         ids, places, feed_low, cots, first_sum, feed_in, feed_out, layout.seq
     )
     home = [layout.homeward(result_a, 0), layout.homeward(result_b, 1)]
     block_out = layout.gathered(home)
-    out_sum = Sum(layout, (out_send, out_keep), turned=True)
-    in_sum = Sum(layout, (in_send, in_keep))
+    feed_sum = Sum(layout, (out_send, out_keep), (in_send, in_keep))
 
     grad_input, grad_main, grad_att, feed_gain_grad = gate(
         grad_feed, cots, flat_low, cand_in, base, attended, feed_gain[None], out_proj
     )
-    after = layout.turn((out_sum,), (grad_att,))
-    after = layout.turn((in_sum,), after)
+    after = layout.turn((feed_sum,), (grad_att,))
     mix_parts = by_rows(ids, None, mixed, grad_main, after=after, cost=LONG)
     proj_parts = by_columns(
         ids,
@@ -1841,9 +1963,9 @@
         at=grad_main.shape[1] // width - 1,
         after=mix_parts,
     )
-    after = layout.turn((out_sum,), (*proj_parts, *home))
+    after = (*proj_parts, *home)
     mix_sum = Sum(layout, mix_parts, over_seq=False)
-    proj_sum = Sum(layout, proj_parts, turned=True)
+    proj_sum = Sum(layout, proj_parts)
     grad_query, gk_own, gv_own, both_oth, rel_sums = attend_back(
         table,
         query_low,
@@ -1857,7 +1979,7 @@
         after=after,
     )
     both_back = layout.returns(both_oth)
-    after = layout.turn((in_sum, out_sum, proj_sum), (grad_query,), cost=LONG)
+    after = layout.turn((feed_sum, proj_sum), (grad_query,), cost=LONG)
     grad_normed, value_send, value_keep = value_back(
         ids,
         places,
@@ -1877,17 +1999,17 @@
         (grad_query * score_affine[0] + grad_key * score_affine[2]) * silu_slope(shared_pre)
     ).astype(bf16)
     shared_parts = by_rows(ids, None, mixed, grad_shared, after=(grad_normed,))
-    after = layout.turn((out_sum, mix_sum), shared_parts)
     shared_sum = Sum(layout, shared_parts, over_seq=False)
     value_sum = Sum(layout, (value_send, value_keep))
-    grad_smooth = (mm_nt(grad_main, mix_main) + mm_nt(grad_shared, mix_shared)) * silu_slope(
-        smoothed
+    after = layout.turn((mix_sum,), shared_parts)
+    grad_smooth = smooth_back(
+        grad_main, grad_shared, mix_main, mix_shared, smoothed, after=after
     )
     grad_smooth = grad_smooth.reshape(slots, chunk_rows, width)
-    after = layout.turn((in_sum, value_sum, proj_sum, shared_sum), (grad_smooth,))
+    after = layout.turn((feed_sum, value_sum, proj_sum, shared_sum), (grad_smooth,))
     back = back_ends(grad_smooth, decay_slab, after=after)
     back_all = jnp.concatenate([back, layout.gather(back)])
-    after = layout.turn((out_sum, in_sum, mix_sum, value_sum, shared_sum), (back,))
+    after = layout.turn((feed_sum, mix_sum, value_sum, shared_sum), (back,))
 
     def scan_back(slot, after):
         return back_scan(
@@ -1909,7 +2031,7 @@
 
     first = scan_back(0, after)
     after = layout.turn(
-        (in_sum, mix_sum, value_sum, proj_sum, out_sum, shared_sum), (first[0],)
+        (feed_sum, mix_sum, value_sum, proj_sum, shared_sum), (first[0],)
     )
     home_first = layout.homeward(first[0], 0)
     while mix_sum.total is None or shared_sum.total is None:
@@ -1938,7 +2060,7 @@
     rest = jnp.concatenate(small)
     rest = jnp.pad(rest, ((0, -rest.shape[0] % 16), (0, 0)))
     home_second = layout.homeward(second[0], 1)
-    sums = (mix_sum, proj_sum, value_sum, out_sum, in_sum)
+    sums = (mix_sum, proj_sum, value_sum, feed_sum)
     turned = layout.turn(sums, (second[0], home_first), cost=LONG)
     totals = layout.over_dp(pack(first[1:3], second[1:3], rest, after=turned))
     after = layout.turn(sums, (*turned, home_second))
@@ -1946,14 +2068,14 @@
     while any(v.total is None for v in sums):
         after = layout.turn(sums, after)
     grad_in = layout.gathered([home_first, home_second]).astype(f32)
-    feed_out_grad, feed_in_grad = out_sum.total[0, 0], in_sum.total[0, 0]
+    feed_out_grad, feed_in_grad = feed_sum.total[0, 0].T, feed_sum.total[1, 0]
     rows = width // layout.dp
     feed_in_grad = feed_in_grad.reshape(-1, rows, feed_in_grad.shape[-1])
     feed_in_grad = feed_in_grad.transpose(1, 0, 2).reshape(rows, -1)
-    out_grad, value_grad = proj_sum.total[0, 0], value_sum.total[0, 0]
+    out_grad, value_grad = proj_sum.total[0, 0].T, value_sum.total[0, 0]
     mix_grad = mix_sum.total[0, 0]
     alpha_grad, damp_grad, beta_grad, eta_grad, totals = finish(
-        core, *totals, smooth_alpha, smooth_damp, smooth_beta, smooth_eta
+        *totals, smooth_alpha, smooth_damp, smooth_beta, smooth_eta
     )
     parts, start = [], 0
     for item in small:

time: 563 us -> 547 us (0.972)
  matrix products: 33.7 us -> 0 us
  Pallas kernels: 334 us -> 359 us
  waiting for transfers between devices: 56.7 us -> 49.1 us
    dot_general x3 -> x0, matrix products: 33.7 us -> none  [the longest x2 21.5 us: mm_nt(): lax.dot_general(a, b, (((1,), (1,)), ((), ())), preferred_element_type=f32)]
    pallas_call x14, Pallas kernels: 80.5 us -> 107 us  [the longest x8 47.9 us: stage_sums(): pl.pallas_call(body, grid=(steps,), in_specs=riders.in_specs + [pl.BlockS...]
    ppermute x44 -> x39, waiting for transfers between devices: 56.7 us -> 49 us  [send(): return lax.ppermute(value, AXES, self.pairs(move))]
    ppermute x44 -> x39, starting transfers between devices: 48.8 us -> 52.1 us  [send(): return lax.ppermute(value, AXES, self.pairs(move))]
    unnamed x130 -> x132, local copies, waits for them, and re-layouts: 18.7 us -> 20 us
  transfers between devices with their start and end apart: 48 -> 43, of which waited for: 11 -> 9; matrix products, arithmetic and copies ran while one was open for 15% -> 9% of each run, Pallas kernels for 45% -> 51%
where the time goes in v6:
time: 547 us; the launch traced here: 541 us
  Pallas kernels  359 us (66%)
  starting transfers between devices  61.5 us (11%)
  waiting for transfers between devices  49.1 us (9%)
  local copies, waits for them, and re-layouts  47.5 us (9%)
  other arithmetic  21 us (4%)
    pallas_call x1, Pallas kernels, feed(): pl.pallas_call(ignoring(feed_body, 8, len(after)), grid_spec=pltpu.Prefet...  68.7 us
    ppermute x39, starting transfers between devices, send(): return lax.ppermute(value, AXES, self.pairs(move))  52.1 us
    ppermute x39, waiting for transfers between devices, send(): return lax.ppermute(value, AXES, self.pairs(move))  49 us
    pallas_call x8, Pallas kernels, stage_sums(): pl.pallas_call(body, grid=(steps,), in_specs=riders.in_specs + [pl.BlockS...  47.9 us
    pallas_call x2, Pallas kernels, back_scan(): pl.pallas_call(ignoring(back_scan_body, 13, len(after)), grid_spec=pltpu....  40.6 us
    pallas_call x1, Pallas kernels, attend_back(): pl.pallas_call(ignoring(functools.partial(attend_back_body, total=total),...  21.7 us
    pallas_call x2, Pallas kernels, front(): pl.pallas_call(ignoring(front_body, 4, len(earlier) + len(after)), grid=(...  20.1 us
    unnamed x132, local copies, waits for them, and re-layouts  20 us
  transfers between devices with their start and end apart: 43, of which 9 were waited for; matrix products, arithmetic and copies ran while one was open for 9% of the time, Pallas kernels for 51%

profile of v6, /device:TPU:0, one launch (start us, length us, event | category | flops | bytes accessed | tf_op | source)
XLA Modules:
  0.0 540.7 jit_solution(16648252565750521580)
XLA Ops:
  0.7 2.7 dynamic-slice_bitcast_fusion.2
  3.8 2.6 collective-permute-start.1
  6.4 2.5 collective-permute-start
  10.7 7.9 %slice.111.refs_6_.right_ref.refs_2_ = bf16[1024,4096]{1,0:T(8,128)(2,1)} slice(bf16[1024,4224]{1,0:T(8,128)(2,1)} %param.30), slice={[0:1024], [128:4224]} | slice | bytes 16777216 | tf_op jit(solution)/shard_map/slice | solution.py:1896
  23.5 6.1 %bias.1 = (f32[9,256,256]{2,1,0:T(8,128)}, f32[9,256,256]{2,1,0:T(8,128)}) custom-call(s32[1]{0:T(128)S(6)} %convert_element_type.38.flag_ref, f32[8,1,512]{2,1,0:T(1,128)} %copy.64.back_row, f32[8,1,512]{2,1,0:T(1,128)} %broadcast_in_dim.48.front_row), custom_call_target="tpu_custom_call" | custom-call | tf_op jit(solution)/shard_map/bias/pallas_call | solution.py:870
  30.6 10.0 %front.2 = (bf16[2,512,1024]{2,1,0:T(8,128)(2,1)}, bf16[2,512,1024]{2,1,0:T(8,128)(2,1)}, bf16[2,512,2048]{2,1,0:T(8,128)(2,1)}, bf16[2,512,2048]{2,1,0:T(8,128)(2,1)}, f32[2,16,8,128]{3,2,1,0:T(8,128)}) custom-call(bf16[512,1024]{1,0:T(8,128)(2,1)} %copy-done.12, f32[1,1024]{1,0:T(1,128)} %bitcast.324, f32[16,8,128]{2,1,0:T(8,128)} %bitcast.260, ...), custom_call_target="tpu_custom_call" | custom-call | flops 1 | bytes 1 | tf_op jit(solution)/shard_map/front/pallas_call | solution.py:115
  40.6 13.5 %collective-permute-done.1.refs_0_ = bf16[512,1024]{1,0:T(8,128)(2,1)S(1)} collective-permute-done((bf16[512,1024]{1,0:T(8,128)(2,1)S(1)}, bf16[512,1024]{1,0:T(8,128)(2,1)S(1)}, u32[]{:S(2)}, u32[]{:S(2)}) %collective-permute-start.1) | collective-permute-done | bytes 1048608 | tf_op jit(solution)/shard_map/ppermute | solution.py:1584
  55.1 10.1 %front.3 = (bf16[2,512,1024]{2,1,0:T(8,128)(2,1)}, bf16[2,512,1024]{2,1,0:T(8,128)(2,1)}, bf16[2,512,2048]{2,1,0:T(8,128)(2,1)}, bf16[2,512,2048]{2,1,0:T(8,128)(2,1)}, f32[2,16,8,128]{3,2,1,0:T(8,128)}) custom-call(bf16[512,1024]{1,0:T(8,128)(2,1)} %copy-done.11, ...), custom_call_target="tpu_custom_call", output_to_operand_aliasing={{0}: (4, {}), {1}: (5, {}), {2}: (6, {}), {3}: (7, {}), {4}... | custom-call | flops 1 | bytes 1 | tf_op jit(solution)/shard_map/front/pallas_call | solution.py:115
  69.8 1.9 collective-permute-start.6
  71.8 17.3 %front_scan.1 = (f32[2,512,1024]{2,1,0:T(8,128)}, bf16[2,512,1024]{2,1,0:T(8,128)(2,1)}, f32[2,4,16,8,128]{4,3,2,1,0:T(8,128)}, f32[2,512,128]{2,1,0:T(8,128)}, ...) custom-call(s32[9]{0:T(128)} %concatenate.42.table_ref.refs_0_, ...), custom_call_target="tpu_custom_call" | custom-call | flops 99999997952 | bytes 1 | tf_op jit(solution)/shard_map/front_scan/pallas_call | solution.py:222
  90.9 13.0 %product.1.pre_ref.update_ref.refs_5_.refs_6_ = bf16[1024,4096]{1,0:T(8,128)(2,1)} custom-call(bf16[1024,1024]{1,0:T(8,128)(2,1)} %bitcast.220, bf16[1024,4096]{1,0:T(8,128)(2,1)} %slice.111.refs_6_.right_ref.refs_2_), custom_call_target="tpu_custom_call" | custom-call | flops 1 | bytes 1 | tf_op jit(solution)/shard_map/product/pallas_call | solution.py:1229
  104.6 13.9 %attend.1 = (bf16[2,512,2048]{2,1,0:T(8,128)(2,1)}, bf16[2,512,2048]{2,1,0:T(8,128)(2,1)}, f32[2,512,1]{2,1,0:T(8,128)}) custom-call(s32[9]{0:T(128)} %concatenate.42.table_ref.refs_0_, bf16[2,512,128]{2,1,0:T(8,128)(2,1)} %get-tuple-element.134.q_ref.refs_1_, f32[9,256,256]{2,1,0:T(8,128)} %get-tuple-element.125.refs_5_.bias_ref, ...), custom_call_target="tpu_custom_call" | custom-call | flops 1 | bytes 1 | tf_op jit(solution)/shard_map/attend/pallas_call | solution.py:599
  118.6 12.7 %candidate.1 = (f32[1024,1024]{1,0:T(8,128)}, f32[1024,1024]{1,0:T(8,128)}, bf16[1024,1024]{1,0:T(8,128)(2,1)}) custom-call(bf16[1024,2048]{1,0:T(8,128)(2,1)} %bitcast.216, bf16[2048,1024]{1,0:T(8,128)(2,1)} %refs_9_.1, bf16[1024,4096]{1,0:T(8,128)(2,1)} %product.1.pre_ref.update_ref.refs_5_.refs_6_, ...), custom_call_target="tpu_custom_call" | custom-call | flops 1 | bytes 1 | tf_op jit(solution)/shard_map/candidate/pallas_call | solution.py:920
  134.4 68.7 %feed.1 = (bf16[512,1024]{1,0:T(8,128)(2,1)}, bf16[512,1024]{1,0:T(8,128)(2,1)}, f32[1024,1024]{1,0:T(8,128)}, bf16[4,1024,512]{2,1,0:T(8,128)(2,1)}, bf16[4,102...) custom-call(s32[8]{0:T(128)} %broadcast_select_fusion.1.refs_0_, ...), custom_call_target="tpu_custom_call" | custom-call | flops 1 | bytes 1 | tf_op jit(solution)/shard_map/feed/pallas_call | solution.py:1171
  203.1 7.8 %collective-permute-start.8 = (bf16[512,1024]{1,0:T(8,128)(2,1)}, bf16[512,1024]{1,0:T(8,128)(2,1)}, u32[]{:S(2)}, u32[]{:S(2)}) collective-permute-start(bf16[512,1024]{1,0:T(8,128)(2,1)} %get-tuple-element.142), channel_id=1, source_target_pairs={{1,0},{5,1},{0,2},{4,3},{3,4},{7,5},{2,6},{6,7},{9,8},{13,9},{8,10... | collective-permute-start | bytes 3145736 | tf_op jit(solution)/shard_map/ppermute | solution.py:1613
  211.4 19.9 %gate.1 = (f32[1024,1024]{1,0:T(8,128)}, bf16[1024,4096]{1,0:T(8,128)(2,1)}, bf16[1024,2048]{1,0:T(8,128)(2,1)}, f32[1,1024]{1,0:T(1,128)}) custom-call(f32[1024,1024]{1,0:T(8,128)} %get-tuple-element.144.refs_0_, bf16[512,1024]{1,0:T(8,128)(2,1)} %copy-done.14, bf16[512,1024]{1,0:T(8,128)(2,1)} %copy-done.13, bf16[1024,1024]{1,0:T(8,128)(2,1)} %bitcast.219, ...), custom_call_target="tpu_custom_call" | custom-call | flops 99999997952 | bytes 1 | tf_op jit(solution)/shard_map/gate/pallas_call | solution.py:1009
  231.3 9.4 %stage_sums.8 = (bf16[2,2048,512]{2,1,0:T(8,128)(2,1)}, bf16[2,2048,512]{2,1,0:T(8,128)(2,1)}) custom-call(bf16[1,2,2048,512]{3,2,1,0:T(8,128)(2,1)} %bitcast.225, bf16[1,2,2048,512]{3,2,1,0:T(8,128)(2,1)} %bitcast.30.refs_1_, bf16[1,2,2048,512]{3,2,1,0:T(8,128)(2,1)} %bitcast.226, bf16[1,2,2048,512]{3,2,1,0:T(8,128)(2,1)} %bitcast.33.refs_3_, ...), custom_call_target="tpu_custom_call" | custom-call | flops 1 | bytes 1 | tf_op jit(solution)/shard_map/stage_sums/pallas_call | solution.py:1555
  242.3 15.1 %by_rows.2 = (bf16[4,1,128,4096]{3,2,1,0:T(8,128)(2,1)}, bf16[4,1,128,4096]{3,2,1,0:T(8,128)(2,1)}) custom-call(s32[8]{0:T(128)} %broadcast_select_fusion.1.refs_0_, s32[1]{0:T(128)} %constant.102.clone.1.refs_1_, bf16[1024,1024]{1,0:T(8,128)(2,1)} %bitcast.221, bf16[1024,4096]{1,0:T(8,128)(2,1)} %get-tuple-element.147.refs_3_.refs_2_.refs_0_, ...), custom_call_target="tpu_custom_call" | custom-call | flops 99999997952 | bytes 1 | tf_op jit(solution)/shard_map/by_rows/pallas_call | solution.py:1394
  257.5 11.9 %by_columns.1 = (bf16[4,1024,256]{2,1,0:T(8,128)(2,1)}, bf16[4,1024,256]{2,1,0:T(8,128)(2,1)}) custom-call(s32[8]{0:T(128)} %broadcast_select_fusion.1.refs_0_, s32[4]{0:T(128)} %get-tuple-element.123.refs_1_, bf16[1024,4096]{1,0:T(8,128)(2,1)} %get-tuple-element.147.refs_3_.refs_2_.refs_0_, bf16[1024,2048]{1,0:T(8,128)(2,1)} %bitcast.217, ...), custom_call_target="tpu_custom_call" | custom-call | flops 1 | bytes 1 | tf_op jit(solution)/shard_map/by_columns/pallas_call | solution.py:1330
  269.9 21.7 %attend_back.1 = (f32[2,512,128]{2,1,0:T(8,128)}, bf16[2,512,128]{2,1,0:T(8,128)(2,1)}, bf16[2,512,2048]{2,1,0:T(8,128)(2,1)}, bf16[2,512,2176]{2,1,0:T(8,128)(2,1)}, f32[8,1,512]{2,1,0:T(1,128)}) custom-call(s32[9]{0:T(128)} %concatenate.42.table_ref.refs_0_, bf16[2,512,128]{2,1,0:T(8,128)(2,1)} %get-tuple-element.134.q_ref.refs_1_, ...), custom_call_target="tpu_custom_call" | custom-call | flops 99999997952 | bytes 1 | tf_op jit(solution)/shard_map/attend_back/pallas_call | solution.py:782
  293.1 7.7 %stage_sums.9 = (bf16[2,1024,512]{2,1,0:T(8,128)(2,1)}, bf16[2,1024,512]{2,1,0:T(8,128)(2,1)}, bf16[1,2048,256]{2,1,0:T(8,128)(2,1)}, bf16[1,2048,256]{2,1,0:T(8,128)(2,1)}) custom-call(bf16[2,2,1024,512]{3,2,1,0:T(8,128)(2,1)} %bitcast.347, bf16[2,2,1024,512]{3,2,1,0:T(8,128)(2,1)} %collective-permute-done.14.refs_1_, bf16[1,2,2048,256]{3,2,1,0:T(8,128)(2,1)} %bitcast.358, ...), custom_call_target="tpu_custom_call" | custom-call | flops 99999997952 | bytes 1 | tf_op jit(solution)/shard_map/stage_sums/pallas_call | solution.py:1555
  302.3 11.6 %collective-permute-start.16 = (bf16[2,1,1024,512]{3,2,1,0:T(8,128)(2,1)}, bf16[2,1,1024,512]{3,2,1,0:T(8,128)(2,1)}, u32[]{:S(2)}, u32[]{:S(2)}) collective-permute-start(bf16[2,1,1024,512]{3,2,1,0:T(8,128)(2,1)} %bitcast.355), channel_id=1, source_target_pairs={{0,16},{1,17},{2,18},{3,19},{4,12},{5,13},{6,14},{7,15},{8,24},{9,... | collective-permute-start | bytes 6291464 | tf_op jit(solution)/shard_map/ppermute | solution.py:1584
  313.9 15.9 %value_back.1 = (f32[1024,1024]{1,0:T(8,128)}, bf16[4,4,128,512]{3,2,1,0:T(8,128)(2,1)}, bf16[4,4,128,512]{3,2,1,0:T(8,128)(2,1)}) custom-call(s32[8]{0:T(128)} %broadcast_select_fusion.1.refs_0_, s32[4]{0:T(128)} %get-tuple-element.123.refs_1_, bf16[1024,1024]{1,0:T(8,128)(2,1)} %bitcast.244, bf16[1024,2048]{1,0:T(8,128)(2,1)} %bitcast.385, ...), custom_call_target="tpu_custom_call" | custom-call | flops 99999997952 | bytes 1 | tf_op jit(solution)/shard_map/value_back/pallas_call | solution.py:1467
  329.8 2.5 fusion.8
  332.3 4.4 by_rows.3
  336.8 6.1 %stage_sums.10 = (bf16[1,256,4096]{2,1,0:T(8,128)(2,1)}, bf16[1,256,4096]{2,1,0:T(8,128)(2,1)}) custom-call(bf16[1,2,256,4096]{3,2,1,0:T(8,128)(2,1)} %bitcast.215, bf16[1,2,256,4096]{3,2,1,0:T(8,128)(2,1)} %bitcast.46.refs_1_, bf16[4,1,128,128]{3,2,1,0:T(8,128)(2,1)} %get-tuple-element.173.refs_2_, bf16[4,1,128,128]{3,2,1,0:T(8,128)(2,1)} %get-tuple-element.174.refs_3_), custom_call_target="tpu_custom_call" | custom-call | flops 1 | bytes 1 | tf_op jit(solution)/shard_map/stage_sums/pallas_call | solution.py:1555
  343.4 17.1 %smooth_back.1 = f32[1024,1024]{1,0:T(8,128)} custom-call(bf16[1024,4096]{1,0:T(8,128)(2,1)} %get-tuple-element.147.refs_3_.refs_2_.refs_0_, bf16[1024,128]{1,0:T(8,128)(2,1)} %get-tuple-element.300.refs_3_.refs_1_, bf16[1024,4096]{1,0:T(8,128)(2,1)} %slice.111.refs_6_.right_ref.refs_2_, bf16[1024,128]{1,0:T(8,128)(2,1)} %slice.112.refs_7_.proj_ref.refs_3_, ...), custom_call_target="tpu_custom_call" | custom-call | flops 99999997952 | bytes 1 | tf_op jit(solution)/shard_map/smooth_back/pallas_call | solution.py:1275
  361.8 6.9 %stage_sums.11 = (bf16[2,512,512]{2,1,0:T(8,128)(2,1)}, bf16[2,512,512]{2,1,0:T(8,128)(2,1)}, bf16[1,1024,512]{2,1,0:T(8,128)(2,1)}, bf16[1,1024,512]{2,1,0:T(8,...) custom-call(bf16[2,2,512,512]{3,2,1,0:T(8,128)(2,1)} %bitcast.241, ...), custom_call_target="tpu_custom_call" | custom-call | flops 1 | bytes 1 | tf_op jit(solution)/shard_map/stage_sums/pallas_call | solution.py:1555
  368.7 3.6 collective-permute-start.21
  374.7 8.1 %back_ends.1.refs_8_ = f32[2,16,8,128]{3,2,1,0:T(8,128)} custom-call(f32[2,512,1024]{2,1,0:T(8,128)} %bitcast.212, f32[16,8,128]{2,1,0:T(8,128)} %bitcast.263, bf16[2,2,256,512]{3,2,1,0:T(8,128)(2,1)} %bitcast.271, bf16[2,2,256,512]{3,2,1,0:T(8,128)(2,1)} %bitcast.228, bf16[1,2,512,512]{3,2,1,0:T(8,128)(2,1)} %bitcast.269, ...), custom_call_target="tpu_custom_call" | custom-call | flops 1 | bytes 1 | tf_op jit(solution)/shard_map/back_ends/pallas_call | solution.py:299
  388.0 8.3 %collective-permute-done.21.refs_1_ = bf16[2,2,256,512]{3,2,1,0:T(8,128)(2,1)S(1)} collective-permute-done((bf16[2,2,256,512]{3,2,1,0:T(8,128)(2,1)}, bf16[2,2,256,512]{3,2,1,0:T(8,128)(2,1)S(1)}, u32[]{:S(2)}, u32[]{:S(2)}) %collective-permute-start.21) | collective-permute-done | bytes 1048608 | tf_op jit(solution)/shard_map/ppermute | solution.py:1584
  398.3 6.1 %stage_sums.12 = (bf16[2,256,512]{2,1,0:T(8,128)(2,1)}, bf16[2,256,512]{2,1,0:T(8,128)(2,1)}, bf16[1,128,4096]{2,1,0:T(8,128)(2,1)}, bf16[1,128,4096]{2,1,0:T(8,...) custom-call(bf16[2,2,256,512]{3,2,1,0:T(8,128)(2,1)} %bitcast.229, ...), custom_call_target="tpu_custom_call" | custom-call | flops 1 | bytes 1 | tf_op jit(solution)/shard_map/stage_sums/pallas_call | solution.py:1555
  404.7 1.9 collective-permute-start.25
  408.7 20.2 %back_scan.2 = (bf16[512,1024]{1,0:T(8,128)(2,1)}, f32[16,8,128]{2,1,0:T(8,128)}, f32[16,8,128]{2,1,0:T(8,128)}, f32[1,1024]{1,0:T(1,128)}, f32[1,1024]{1,0:T(1,128)}) custom-call(s32[9]{0:T(128)} %concatenate.42.table_ref.refs_0_, s32[1]{0:T(128)} %constant.102.clone.1.refs_1_, bf16[2,512,1024]{2,1,0:T(8,128)(2,1)} %get-tuple-element.131.x_ref.refs_2_, ...), custom_call_target="tpu_custom_call" | custom-call | flops 99999997952 | bytes 1 | tf_op jit(solution)/shard_map/back_scan/pallas_call | solution.py:440
  431.9 4.8 stage_sums.13
  444.9 20.3 %back_scan.3 = (bf16[512,1024]{1,0:T(8,128)(2,1)}, f32[16,8,128]{2,1,0:T(8,128)}, f32[16,8,128]{2,1,0:T(8,128)}, f32[1,1024]{1,0:T(1,128)}, f32[1,1024]{1,0:T(1,128)}) custom-call(s32[9]{0:T(128)} %concatenate.42.table_ref.refs_0_, s32[1]{0:T(128)} %constant.101.clone.1.refs_1_, bf16[2,512,1024]{2,1,0:T(8,128)(2,1)} %get-tuple-element.131.x_ref.refs_2_, ...), custom_call_target="tpu_custom_call" | custom-call | flops 99999997952 | bytes 1 | tf_op jit(solution)/shard_map/back_scan/pallas_call | solution.py:440
  471.4 3.5 stage_sums.14
  476.5 1.7 select_bitcast_fusion.3
  478.3 4.7 collective-permute-start.38
  486.1 2.9 collective-permute-start.40
  492.7 18.4 %collective-permute-done.39.refs_3_ = bf16[1,1,256,256]{3,2,1,0:T(8,128)(2,1)S(1)} collective-permute-done((bf16[1,1,256,256]{3,2,1,0:T(8,128)(2,1)S(1)}, bf16[1,1,256,256]{3,2,1,0:T(8,128)(2,1)S(1)}, u32[]{:S(2)}, u32[]{:S(2)}) %collective-permute-start.39) | collective-permute-done | bytes 131104 | tf_op jit(solution)/shard_map/ppermute | solution.py:1584
  511.2 2.8 collective-permute-done.40.refs_5_
  515.7 3.3 stage_sums.15
  519.8 1.7 later_sum.1
  523.4 3.6 collective-permute-done.41
  527.6 2.3 collective-permute-start.42
  530.0 2.3 maximum_convert_fusion
  534.7 1.8 finish.1
  (260 shorter events, 75.3 us)
Async XLA Ops:
  3.4 26.3 %collective-permute-start.2 = (bf16[512,1024]{1,0:T(8,128)(2,1)}, bf16[512,1024]{1,0:T(8,128)(2,1)S(1)}, u32[]{:S(2)}, u32[]{:S(2)}) collective-permute-start(bf16[512,1024]{1,0:T(8,128)(2,1)} %get-tuple-element.307), channel_id=1, source_target_pairs={{0,4},{1,0},{2,5},{3,1},{4,6},{5,2},{6,7},{7,3},{8,12},{9,8},{10,1... | collective-permute-start | bytes 3145736 | tf_op jit(solution)/shard_map/ppermute | solution.py:1584
  3.8 50.3 %collective-permute-start.1 = (bf16[512,1024]{1,0:T(8,128)(2,1)S(1)}, bf16[512,1024]{1,0:T(8,128)(2,1)S(1)}, u32[]{:S(2)}, u32[]{:S(2)}) collective-permute-start(bf16[512,1024]{1,0:T(8,128)(2,1)S(1)} %get-tuple-element.308), channel_id=1, source_target_pairs={{0,1},{1,5},{2,0},{3,4},{4,3},{5,7},{6,2},{7,6},{8,9},{9,13},{10,8... | collective-permute-start | bytes 3145736 | tf_op jit(solution)/shard_map/ppermute | solution.py:1584
  6.4 15.8 %collective-permute-start = (f32[2]{0:T(128)S(1)}, f32[2]{0:T(128)S(1)}, u32[]{:S(2)}, u32[]{:S(2)}) collective-permute-start(f32[2]{0:T(128)S(1)} %convert_element_type.37), channel_id=1, source_target_pairs={{0,4},{1,5},{2,6},{3,7},{4,0},{5,1},{6,2},{7,3},{8,12},{9,13},{10,... | collective-permute-start | bytes 32 | tf_op jit(solution)/shard_map/ppermute | solution.py:1584
  65.2 1.8 collective-permute-start.3
  66.6 37.3 %collective-permute-start.5 = (bf16[2,512,2048]{2,1,0:T(8,128)(2,1)}, bf16[2,512,2048]{2,1,0:T(8,128)(2,1)}, u32[]{:S(2)}, u32[]{:S(2)}) collective-permute-start(bf16[2,512,2048]{2,1,0:T(8,128)(2,1)} %get-tuple-element.137.v_own.refs_7_), channel_id=1, source_target_pairs={{0,4},{1,5},{2,6},{3,7},{4,0},{5,1},{6,2},{7,3},{8,12},{9,13},{10,... | collective-permute-start | bytes 12582920 | tf_op jit(solution)/shard_map/ppermute | solution.py:1584
  69.8 63.3 %collective-permute-start.7 = (bf16[512,1024]{1,0:T(8,128)(2,1)}, bf16[512,1024]{1,0:T(8,128)(2,1)S(1)}, u32[]{:S(2)}, u32[]{:S(2)}) collective-permute-start(bf16[512,1024]{1,0:T(8,128)(2,1)} %get-tuple-element.305), channel_id=1, source_target_pairs={{0,1},{1,5},{2,0},{3,4},{4,3},{5,7},{6,2},{7,6},{8,9},{9,13},{10,8... | collective-permute-start | bytes 3145736 | tf_op jit(solution)/shard_map/ppermute | solution.py:1584
  69.8 63.3 %collective-permute-start.6 = (bf16[512,1024]{1,0:T(8,128)(2,1)S(1)}, bf16[512,1024]{1,0:T(8,128)(2,1)S(1)}, u32[]{:S(2)}, u32[]{:S(2)}) collective-permute-start(bf16[512,1024]{1,0:T(8,128)(2,1)S(1)} %get-tuple-element.306), channel_id=1, source_target_pairs={{0,4},{1,0},{2,5},{3,1},{4,6},{5,2},{6,7},{7,3},{8,12},{9,8},{10,1... | collective-permute-start | bytes 3145736 | tf_op jit(solution)/shard_map/ppermute | solution.py:1584
  89.0 14.9 %collective-permute-start.4 = (bf16[2,512,128]{2,1,0:T(8,128)(2,1)}, bf16[2,512,128]{2,1,0:T(8,128)(2,1)S(1)}, u32[]{:S(2)}, u32[]{:S(2)}) collective-permute-start(bf16[2,512,128]{2,1,0:T(8,128)(2,1)} %get-tuple-element.136.k_own.refs_5_), channel_id=1, source_target_pairs={{0,4},{1,5},{2,6},{3,7},{4,0},{5,1},{6,2},{7,3},{8,12},{9,13},{10,... | collective-permute-start | bytes 786440 | tf_op jit(solution)/shard_map/ppermute | solution.py:1584
  203.1 66.8 %collective-permute-start.8 = (bf16[512,1024]{1,0:T(8,128)(2,1)}, bf16[512,1024]{1,0:T(8,128)(2,1)}, u32[]{:S(2)}, u32[]{:S(2)}) collective-permute-start(bf16[512,1024]{1,0:T(8,128)(2,1)} %get-tuple-element.142), channel_id=1, source_target_pairs={{1,0},{5,1},{0,2},{4,3},{3,4},{7,5},{2,6},{6,7},{9,8},{13,9},{8,10... | collective-permute-start | bytes 3145736 | tf_op jit(solution)/shard_map/ppermute | solution.py:1613
  210.9 59.0 %collective-permute-start.9 = (bf16[512,1024]{1,0:T(8,128)(2,1)}, bf16[512,1024]{1,0:T(8,128)(2,1)}, u32[]{:S(2)}, u32[]{:S(2)}) collective-permute-start(bf16[512,1024]{1,0:T(8,128)(2,1)} %get-tuple-element.143), channel_id=1, source_target_pairs={{4,0},{0,1},{5,2},{1,3},{6,4},{2,5},{7,6},{3,7},{12,8},{8,9},{13,1... | collective-permute-start | bytes 3145736 | tf_op jit(solution)/shard_map/ppermute | solution.py:1613
  210.9 20.4 %collective-permute-start.10 = (bf16[1,4,1024,512]{3,2,1,0:T(8,128)(2,1)}, bf16[1,4,1024,512]{3,2,1,0:T(8,128)(2,1)}, u32[]{:S(2)}, u32[]{:S(2)}) collective-permute-start(bf16[1,4,1024,512]{3,2,1,0:T(8,128)(2,1)} %bitcast.352), channel_id=1, source_target_pairs={{0,4},{1,5},{2,6},{3,7},{4,0},{5,1},{6,2},{7,3},{8,12},{9,13},{10,... | collective-permute-start | bytes 12582920 | tf_op jit(solution)/shard_map/ppermute | solution.py:1584
  211.4 19.9 %collective-permute-start.11 = (bf16[1,4,1024,512]{3,2,1,0:T(8,128)(2,1)}, bf16[1,4,1024,512]{3,2,1,0:T(8,128)(2,1)}, u32[]{:S(2)}, u32[]{:S(2)}) collective-permute-start(bf16[1,4,1024,512]{3,2,1,0:T(8,128)(2,1)} %bitcast.351), channel_id=1, source_target_pairs={{0,4},{1,5},{2,6},{3,7},{4,0},{5,1},{6,2},{7,3},{8,12},{9,13},{10,... | collective-permute-start | bytes 12582920 | tf_op jit(solution)/shard_map/ppermute | solution.py:1584
  240.7 51.1 %collective-permute-start.14 = (bf16[2,2,1024,512]{3,2,1,0:T(8,128)(2,1)}, bf16[2,2,1024,512]{3,2,1,0:T(8,128)(2,1)}, u32[]{:S(2)}, u32[]{:S(2)}) collective-permute-start(bf16[2,2,1024,512]{3,2,1,0:T(8,128)(2,1)} %bitcast.348), channel_id=1, source_target_pairs={{0,8},{1,9},{2,10},{3,11},{4,20},{5,21},{6,22},{7,23},{8,0},{9,1},... | collective-permute-start | bytes 12582920 | tf_op jit(solution)/shard_map/ppermute | solution.py:1584
  269.3 22.4 %collective-permute-start.15 = (bf16[1,4,1024,256]{3,2,1,0:T(8,128)(2,1)}, bf16[1,4,1024,256]{3,2,1,0:T(8,128)(2,1)S(1)}, u32[]{:S(2)}, u32[]{:S(2)}) collective-permute-start(bf16[1,4,1024,256]{3,2,1,0:T(8,128)(2,1)} %bitcast.360), channel_id=1, source_target_pairs={{0,4},{1,5},{2,6},{3,7},{4,0},{5,1},{6,2},{7,3},{8,12},{9,13},{10,... | collective-permute-start | bytes 6291464 | tf_op jit(solution)/shard_map/ppermute | solution.py:1584
  269.5 67.3 %collective-permute-start.13 = (bf16[1,4,128,4096]{3,2,1,0:T(8,128)(2,1)}, bf16[1,4,128,4096]{3,2,1,0:T(8,128)(2,1)}, u32[]{:S(2)}, u32[]{:S(2)}) collective-permute-start(bf16[1,4,128,4096]{3,2,1,0:T(8,128)(2,1)} %bitcast.234), channel_id=1, source_target_pairs={{0,4},{1,5},{2,6},{3,7},{4,0},{5,1},{6,2},{7,3},{8,12},{9,13},{10,... | collective-permute-start | bytes 12582920 | tf_op jit(solution)/shard_map/ppermute | solution.py:1584
  291.5 22.3 %collective-permute-start.12 = (bf16[2,512,2176]{2,1,0:T(8,128)(2,1)}, bf16[2,512,2176]{2,1,0:T(8,128)(2,1)}, u32[]{:S(2)}, u32[]{:S(2)}) collective-permute-start(bf16[2,512,2176]{2,1,0:T(8,128)(2,1)} %get-tuple-element.161), channel_id=1, source_target_pairs={{0,4},{1,5},{2,6},{3,7},{4,0},{5,1},{6,2},{7,3},{8,12},{9,13},{10,... | collective-permute-start | bytes 13369352 | tf_op jit(solution)/shard_map/ppermute | solution.py:1584
  300.8 59.7 %collective-permute-start.18 = (bf16[1,2,1024,256]{3,2,1,0:T(8,128)(2,1)}, bf16[1,2,1024,256]{3,2,1,0:T(8,128)(2,1)}, u32[]{:S(2)}, u32[]{:S(2)}) collective-permute-start(bf16[1,2,1024,256]{3,2,1,0:T(8,128)(2,1)} %bitcast.361), channel_id=1, source_target_pairs={{0,8},{1,9},{2,10},{3,11},{4,20},{5,21},{6,22},{7,23},{8,0},{9,1},... | collective-permute-start | bytes 3145736 | tf_op jit(solution)/shard_map/ppermute | solution.py:1584
  302.3 58.2 %collective-permute-start.16 = (bf16[2,1,1024,512]{3,2,1,0:T(8,128)(2,1)}, bf16[2,1,1024,512]{3,2,1,0:T(8,128)(2,1)}, u32[]{:S(2)}, u32[]{:S(2)}) collective-permute-start(bf16[2,1,1024,512]{3,2,1,0:T(8,128)(2,1)} %bitcast.355), channel_id=1, source_target_pairs={{0,16},{1,17},{2,18},{3,19},{4,12},{5,13},{6,14},{7,15},{8,24},{9,... | collective-permute-start | bytes 6291464 | tf_op jit(solution)/shard_map/ppermute | solution.py:1584
  336.8 23.7 %collective-permute-start.19 = (bf16[1,4,128,128]{3,2,1,0:T(8,128)(2,1)}, bf16[1,4,128,128]{3,2,1,0:T(8,128)(2,1)S(1)}, u32[]{:S(2)}, u32[]{:S(2)}) collective-permute-start(bf16[1,4,128,128]{3,2,1,0:T(8,128)(2,1)} %bitcast.310), channel_id=1, source_target_pairs={{0,4},{1,5},{2,6},{3,7},{4,0},{5,1},{6,2},{7,3},{8,12},{9,13},{10,... | collective-permute-start | bytes 393224 | tf_op jit(solution)/shard_map/ppermute | solution.py:1584
  342.9 44.9 %collective-permute-start.22 = (bf16[1,2,128,4096]{3,2,1,0:T(8,128)(2,1)}, bf16[1,2,128,4096]{3,2,1,0:T(8,128)(2,1)}, u32[]{:S(2)}, u32[]{:S(2)}) collective-permute-start(bf16[1,2,128,4096]{3,2,1,0:T(8,128)(2,1)} %bitcast.353), channel_id=1, source_target_pairs={{0,8},{1,9},{2,10},{3,11},{4,20},{5,21},{6,22},{7,23},{8,0},{9,1},... | collective-permute-start | bytes 6291464 | tf_op jit(solution)/shard_map/ppermute | solution.py:1584
  343.0 17.5 %collective-permute-start.17 = (bf16[1,4,512,512]{3,2,1,0:T(8,128)(2,1)}, bf16[1,4,512,512]{3,2,1,0:T(8,128)(2,1)S(1)}, u32[]{:S(2)}, u32[]{:S(2)}) collective-permute-start(bf16[1,4,512,512]{3,2,1,0:T(8,128)(2,1)} %bitcast.357), channel_id=1, source_target_pairs={{0,4},{1,5},{2,6},{3,7},{4,0},{5,1},{6,2},{7,3},{8,12},{9,13},{10,... | collective-permute-start | bytes 6291464 | tf_op jit(solution)/shard_map/ppermute | solution.py:1584
  368.7 27.6 %collective-permute-start.21 = (bf16[2,2,256,512]{3,2,1,0:T(8,128)(2,1)}, bf16[2,2,256,512]{3,2,1,0:T(8,128)(2,1)S(1)}, u32[]{:S(2)}, u32[]{:S(2)}) collective-permute-start(bf16[2,2,256,512]{3,2,1,0:T(8,128)(2,1)} %bitcast.270), channel_id=1, source_target_pairs={{0,1},{1,0},{2,3},{3,2},{4,5},{5,4},{6,7},{7,6},{8,9},{9,8},{10,11... | collective-permute-start | bytes 3145736 | tf_op jit(solution)/shard_map/ppermute | solution.py:1584
  372.3 24.0 %collective-permute-start.23 = (bf16[1,2,512,512]{3,2,1,0:T(8,128)(2,1)}, bf16[1,2,512,512]{3,2,1,0:T(8,128)(2,1)S(1)}, u32[]{:S(2)}, u32[]{:S(2)}) collective-permute-start(bf16[1,2,512,512]{3,2,1,0:T(8,128)(2,1)} %bitcast.268), channel_id=1, source_target_pairs={{0,8},{1,9},{2,10},{3,11},{4,20},{5,21},{6,22},{7,23},{8,0},{9,1},... | collective-permute-start | bytes 3145736 | tf_op jit(solution)/shard_map/ppermute | solution.py:1584
  382.8 2.4 collective-permute-start.20
  383.6 4.4 collective-permute-start.24
  385.2 43.7 %collective-permute-start.28 = (bf16[1,1,1024,256]{3,2,1,0:T(8,128)(2,1)}, bf16[1,1,1024,256]{3,2,1,0:T(8,128)(2,1)S(1)}, u32[]{:S(2)}, u32[]{:S(2)}) collective-permute-start(bf16[1,1,1024,256]{3,2,1,0:T(8,128)(2,1)} %bitcast.283), channel_id=1, source_target_pairs={{0,16},{1,17},{2,18},{3,19},{4,12},{5,13},{6,14},{7,15},{8,24},{9,... | collective-permute-start | bytes 1572872 | tf_op jit(solution)/shard_map/ppermute | solution.py:1584
  404.4 24.8 %collective-permute-start.29 = (bf16[1,1,128,128]{3,2,1,0:T(8,128)(2,1)}, bf16[1,1,128,128]{3,2,1,0:T(8,128)(2,1)S(1)}, u32[]{:S(2)}, u32[]{:S(2)}) collective-permute-start(bf16[1,1,128,128]{3,2,1,0:T(8,128)(2,1)} %bitcast.377), channel_id=1, source_target_pairs={{0,16},{1,17},{2,18},{3,19},{4,12},{5,13},{6,14},{7,15},{8,24},{9,... | collective-permute-start | bytes 98312 | tf_op jit(solution)/shard_map/ppermute | solution.py:1584
  404.7 25.9 %collective-permute-start.25 = (bf16[2,1,256,512]{3,2,1,0:T(8,128)(2,1)}, bf16[2,1,256,512]{3,2,1,0:T(8,128)(2,1)S(1)}, u32[]{:S(2)}, u32[]{:S(2)}) collective-permute-start(bf16[2,1,256,512]{3,2,1,0:T(8,128)(2,1)} %bitcast.367), channel_id=1, source_target_pairs={{0,2},{1,3},{2,0},{3,1},{4,6},{5,7},{6,4},{7,5},{8,10},{9,11},{10,... | collective-permute-start | bytes 1572872 | tf_op jit(solution)/shard_map/ppermute | solution.py:1584
  406.6 24.0 %collective-permute-start.27 = (bf16[1,1,512,512]{3,2,1,0:T(8,128)(2,1)}, bf16[1,1,512,512]{3,2,1,0:T(8,128)(2,1)S(1)}, u32[]{:S(2)}, u32[]{:S(2)}) collective-permute-start(bf16[1,1,512,512]{3,2,1,0:T(8,128)(2,1)} %bitcast.365), channel_id=1, source_target_pairs={{0,16},{1,17},{2,18},{3,19},{4,12},{5,13},{6,14},{7,15},{8,24},{9,... | collective-permute-start | bytes 1572872 | tf_op jit(solution)/shard_map/ppermute | solution.py:1584
  408.2 22.4 %collective-permute-start.26 = (bf16[1,1,128,4096]{3,2,1,0:T(8,128)(2,1)}, bf16[1,1,128,4096]{3,2,1,0:T(8,128)(2,1)S(1)}, u32[]{:S(2)}, u32[]{:S(2)}) collective-permute-start(bf16[1,1,128,4096]{3,2,1,0:T(8,128)(2,1)} %bitcast.363), channel_id=1, source_target_pairs={{0,16},{1,17},{2,18},{3,19},{4,12},{5,13},{6,14},{7,15},{8,24},{9,... | collective-permute-start | bytes 3145736 | tf_op jit(solution)/shard_map/ppermute | solution.py:1584
  428.9 41.5 %collective-permute-start.31 = (bf16[512,1024]{1,0:T(8,128)(2,1)}, bf16[512,1024]{1,0:T(8,128)(2,1)S(1)}, u32[]{:S(2)}, u32[]{:S(2)}) collective-permute-start(bf16[512,1024]{1,0:T(8,128)(2,1)} %get-tuple-element.197.refs_10_), channel_id=1, source_target_pairs={{4,0},{0,1},{5,2},{1,3},{6,4},{2,5},{7,6},{3,7},{12,8},{8,9},{13,1... | collective-permute-start | bytes 3145736 | tf_op jit(solution)/shard_map/ppermute | solution.py:1613
  436.8 33.6 %collective-permute-start.34 = (bf16[1,2,128,512]{3,2,1,0:T(8,128)(2,1)}, bf16[1,2,128,512]{3,2,1,0:T(8,128)(2,1)}, u32[]{:S(2)}, u32[]{:S(2)}) collective-permute-start(bf16[1,2,128,512]{3,2,1,0:T(8,128)(2,1)} %bitcast.375), channel_id=1, source_target_pairs={{0,1},{1,0},{2,3},{3,2},{4,5},{5,4},{6,7},{7,6},{8,9},{9,8},{10,11... | collective-permute-start | bytes 786440 | tf_op jit(solution)/shard_map/ppermute | solution.py:1584
  437.9 32.5 %collective-permute-start.33 = (bf16[1,2,256,256]{3,2,1,0:T(8,128)(2,1)}, bf16[1,2,256,256]{3,2,1,0:T(8,128)(2,1)}, u32[]{:S(2)}, u32[]{:S(2)}) collective-permute-start(bf16[1,2,256,256]{3,2,1,0:T(8,128)(2,1)} %bitcast.373), channel_id=1, source_target_pairs={{0,1},{1,0},{2,3},{3,2},{4,5},{5,4},{6,7},{7,6},{8,9},{9,8},{10,11... | collective-permute-start | bytes 786440 | tf_op jit(solution)/shard_map/ppermute | solution.py:1584
  442.8 26.5 %collective-permute-start.32 = (bf16[1,2,128,1056]{2,3,1,0:T(8,128)(2,1)}, bf16[1,2,128,1056]{2,3,1,0:T(8,128)(2,1)S(1)}, u32[]{:S(2)}, u32[]{:S(2)}) collective-permute-start(bf16[1,2,128,1056]{2,3,1,0:T(8,128)(2,1)} %get-tuple-element.309), channel_id=1, source_target_pairs={{0,1},{1,0},{2,3},{3,2},{4,5},{5,4},{6,7},{7,6},{8,9},{9,8},{10,11... | collective-permute-start | bytes 1622024 | tf_op jit(solution)/shard_map/ppermute | solution.py:1584
  444.9 23.0 %copy-start.45 = (f32[1,1024]{1,0:T(1,128)S(1)}, f32[1,1024]{1,0:T(1,128)}, u32[]{:S(2)}) copy-start(f32[1,1024]{1,0:T(1,128)} %get-tuple-element.214) | copy-start | bytes 12292
  444.9 23.0 %copy-start.49 = (f32[128]{0:T(128)S(1)}, f32[128]{0:T(128)}, u32[]{:S(2)}) copy-start(f32[128]{0:T(128)} %get-tuple-element.299) | copy-start | bytes 1540
  444.9 23.0 %copy-start.50 = (f32[128]{0:T(128)S(1)}, f32[128]{0:T(128)}, u32[]{:S(2)}) copy-start(f32[128]{0:T(128)} %get-tuple-element.294) | copy-start | bytes 1540
  465.3 48.7 %collective-permute-start.30 = (bf16[512,1024]{1,0:T(8,128)(2,1)}, bf16[512,1024]{1,0:T(8,128)(2,1)S(1)}, u32[]{:S(2)}, u32[]{:S(2)}) collective-permute-start(bf16[512,1024]{1,0:T(8,128)(2,1)} %get-tuple-element.205.refs_6_), channel_id=1, source_target_pairs={{1,0},{5,1},{0,2},{4,3},{3,4},{7,5},{2,6},{6,7},{9,8},{13,9},{8,10... | collective-permute-start | bytes 3145736 | tf_op jit(solution)/shard_map/ppermute | solution.py:1613
  476.5 6.5 %collective-permute-start.35 = (f32[320,128]{1,0:T(8,128)}, f32[320,128]{1,0:T(8,128)S(1)}, u32[]{:S(2)}, u32[]{:S(2)}) collective-permute-start(f32[320,128]{1,0:T(8,128)} %pack.1), channel_id=1, source_target_pairs={{0,4},{1,5},{2,6},{3,7},{4,0},{5,1},{6,2},{7,3},{8,12},{9,13},{10,... | collective-permute-start | bytes 491528 | tf_op jit(solution)/shard_map/ppermute | solution.py:1584
  478.3 35.7 %collective-permute-start.38 = (bf16[1,1,128,1056]{3,2,1,0:T(8,128)(2,1)S(1)}, bf16[1,1,128,1056]{3,2,1,0:T(8,128)(2,1)S(1)}, u32[]{:S(2)}, u32[]{:S(2)}) collective-permute-start(bf16[1,1,128,1056]{3,2,1,0:T(8,128)(2,1)S(1)} %bitcast.253), channel_id=1, source_target_pairs={{0,2},{1,3},{2,0},{3,1},{4,6},{5,7},{6,4},{7,5},{8,10},{9,11},{10,... | collective-permute-start | bytes 811016 | tf_op jit(solution)/shard_map/ppermute | solution.py:1584
  483.0 6.3 %collective-permute-start.36 = (f32[320,128]{1,0:T(8,128)S(1)}, f32[320,128]{1,0:T(8,128)S(1)}, u32[]{:S(2)}, u32[]{:S(2)}) collective-permute-start(f32[320,128]{1,0:T(8,128)S(1)} %add.95), channel_id=1, source_target_pairs={{0,8},{1,9},{2,10},{3,11},{4,12},{5,13},{6,14},{7,15},{8,0},{9,1},... | collective-permute-start | bytes 491528 | tf_op jit(solution)/shard_map/ppermute | solution.py:1584
  486.1 25.1 %collective-permute-start.39 = (bf16[1,1,256,256]{3,2,1,0:T(8,128)(2,1)S(1)}, bf16[1,1,256,256]{3,2,1,0:T(8,128)(2,1)S(1)}, u32[]{:S(2)}, u32[]{:S(2)}) collective-permute-start(bf16[1,1,256,256]{3,2,1,0:T(8,128)(2,1)S(1)} %bitcast.292), channel_id=1, source_target_pairs={{0,2},{1,3},{2,0},{3,1},{4,6},{5,7},{6,4},{7,5},{8,10},{9,11},{10,... | collective-permute-start | bytes 393224 | tf_op jit(solution)/shard_map/ppermute | solution.py:1584
  486.1 27.8 %collective-permute-start.40 = (bf16[1,1,128,512]{3,2,1,0:T(8,128)(2,1)S(1)}, bf16[1,1,128,512]{3,2,1,0:T(8,128)(2,1)S(1)}, u32[]{:S(2)}, u32[]{:S(2)}) collective-permute-start(bf16[1,1,128,512]{3,2,1,0:T(8,128)(2,1)S(1)} %bitcast.295), channel_id=1, source_target_pairs={{0,2},{1,3},{2,0},{3,1},{4,6},{5,7},{6,4},{7,5},{8,10},{9,11},{10,... | collective-permute-start | bytes 393224 | tf_op jit(solution)/shard_map/ppermute | solution.py:1584
  489.4 29.7 %copy-start.21 = (f32[320,128]{1,0:T(8,128)}, f32[320,128]{1,0:T(8,128)S(1)}, u32[]{:S(2)}) copy-start(f32[320,128]{1,0:T(8,128)S(1)} %add.96.refs_0_) | copy-start | bytes 491524
  489.4 29.7 %collective-permute-start.37 = (f32[320,128]{1,0:T(8,128)S(1)}, f32[320,128]{1,0:T(8,128)S(1)}, u32[]{:S(2)}, u32[]{:S(2)}) collective-permute-start(f32[320,128]{1,0:T(8,128)S(1)} %add.96.refs_0_), channel_id=1, source_target_pairs={{0,16},{1,17},{2,18},{3,19},{4,20},{5,21},{6,22},{7,23},{8,24},{9,... | collective-permute-start | bytes 491528 | tf_op jit(solution)/shard_map/ppermute | solution.py:1584
  492.7 30.5 %copy-start.10 = (bf16[512,1024]{1,0:T(8,128)(2,1)S(1)}, bf16[512,1024]{1,0:T(8,128)(2,1)}, u32[]{:S(2)}) copy-start(bf16[512,1024]{1,0:T(8,128)(2,1)} %copy-done.9) | copy-start | bytes 3145732
  522.4 4.5 collective-permute-start.41
  527.6 6.4 %collective-permute-start.42 = (bf16[320,128]{1,0:T(8,128)(2,1)S(1)}, bf16[320,128]{1,0:T(8,128)(2,1)S(1)}, u32[]{:S(2)}, u32[]{:S(2)}) collective-permute-start(bf16[320,128]{1,0:T(8,128)(2,1)S(1)} %get-tuple-element.297), channel_id=1, source_target_pairs={{0,2},{1,3},{2,0},{3,1},{4,6},{5,7},{6,4},{7,5},{8,10},{9,11},{10,... | collective-permute-start | bytes 245768 | tf_op jit(solution)/shard_map/ppermute | solution.py:1584
  (56 other events, 432.3 us)

commit v7 on v6

--- a/solution.py
+++ b/solution.py
@@ -68,14 +68,26 @@
 
 
 def front_body(
-    x_ref, gain_ref, decay_ref, proj_ref, low_ref, copy_ref, value_ref, slope_ref, end_ref, slab
+    x_ref,
+    gain_ref,
+    decay_ref,
+    proj_ref,
+    begin_ref,
+    low_ref,
+    copy_ref,
+    value_ref,
+    slope_ref,
+    end_ref,
+    slab,
+    *,
+    fresh,
 ):
     states, groups, _ = decay_ref.shape
     count = x_ref.shape[0]
 
     @pl.when(pl.program_id(0) == 0)
     def _():
-        end_ref[...] = jnp.zeros_like(end_ref)
+        end_ref[...] = jnp.zeros_like(end_ref) if fresh else begin_ref[...]
 
     copy_ref[0] = x_ref[...]
     unit, _ = unit_rows_of(x_ref[...].astype(f32))
@@ -102,24 +114,28 @@
         slope_ref[0, :, at] = (gate + value * (1.0 - gate)).astype(bf16)
 
 
-def front(x, slot, slots, earlier, gain, decay, proj, after=()):
-    length, width = x.shape
+def front(x, slot, row, whole, earlier, gain, decay, proj, after=()):
+    rows, width = x.shape
+    slots, length = whole
     value_width = proj.shape[1]
     states, groups, lanes = decay.shape
-    block = min(256, length)
+    block = min(256, rows)
+    first = row // block
+    begin = earlier[-1] if row else jnp.zeros((slots, *decay.shape), f32)
     anywhere = pl.BlockSpec(memory_space=pl.ANY)
 
     def tokens(columns):
-        return pl.BlockSpec((1, block, columns), lambda b: (slot, b, 0))
+        return pl.BlockSpec((1, block, columns), lambda b: (slot, first + b, 0))
 
     return pl.pallas_call(
-        ignoring(front_body, 4, len(earlier) + len(after)),
-        grid=(length // block,),
+        ignoring(functools.partial(front_body, fresh=row == 0), 5, len(earlier) + len(after)),
+        grid=(rows // block,),
         in_specs=[
             pl.BlockSpec((block, width), lambda b: (b, 0)),
             pl.BlockSpec((1, width), lambda b: (0, 0)),
             pl.BlockSpec((states, groups, lanes), lambda b: (0, 0, 0)),
             pl.BlockSpec(proj.shape, lambda b: (0, 0), pipeline_mode=pl.Buffered(1)),
+            pl.BlockSpec((1, states, groups, lanes), lambda b: (slot, 0, 0, 0)),
         ]
         + [anywhere] * (len(earlier) + len(after)),
         out_specs=[
@@ -137,11 +153,11 @@
             jax.ShapeDtypeStruct((slots, states, groups, lanes), f32),
         ],
         scratch_shapes=[pltpu.VMEM((block * groups, lanes), f32)],
-        input_output_aliases={4 + k: k for k in range(len(earlier))},
+        input_output_aliases={5 + k: k for k in range(len(earlier))},
         compiler_params=params(("arbitrary",)),
         name="front",
         cost_estimate=BRIEF,
-    )(x, gain, decay, proj, *earlier, *after)
+    )(x, gain, decay, proj, begin, *earlier, *after)
 
 
 def front_scan_body(
@@ -152,7 +168,8 @@
     coef_ref,
     span_ref,
     omega_ref,
-    ends_ref,
+    ends_own,
+    ends_oth,
     proj_ref,
     affine_ref,
     smooth_ref,
@@ -164,15 +181,19 @@
     slab,
     out_slab,
     carry,
+    ends_ref,
 ):
     states, groups, _ = decay_ref.shape
     count = x_ref.shape[1]
     slot = pl.program_id(0)
-    total = ends_ref.shape[0]
+    slots = ends_own.shape[0]
+    total = slots + ends_oth.shape[0]
 
     @pl.when(pl.program_id(1) == 0)
     def _():
         carry[...] = jnp.zeros_like(carry)
+        ends_ref[:slots] = ends_own[...]
+        ends_ref[slots:] = ends_oth[...]
 
         def link(i, _):
             carry[...] = span_ref[...] * carry[...] + ends_ref[table_ref[total + i]]
@@ -212,7 +233,7 @@
     key_ref[0] = (shared * affine_ref[2:3] + affine_ref[3:4]).astype(bf16)
 
 
-def front_scan(table, x, gain, decay, coef, span, omega, ends, proj, affine, block):
+def front_scan(table, x, gain, decay, coef, span, omega, ends, others, proj, affine, block):
     slots, length, width = x.shape
     states, groups, lanes = decay.shape
     whole3 = pl.BlockSpec((states, groups, lanes), lambda k, b, t: (0, 0, 0))
@@ -232,6 +253,7 @@
                 whole3,
                 row,
                 pl.BlockSpec(ends.shape, lambda k, b, t: (0, 0, 0, 0)),
+                pl.BlockSpec(others.shape, lambda k, b, t: (0, 0, 0, 0)),
                 pl.BlockSpec(proj.shape, lambda k, b, t: (0, 0)),
                 pl.BlockSpec(affine.shape, lambda k, b, t: (0, 0)),
             ],
@@ -247,6 +269,7 @@
                 pltpu.VMEM((block * groups, lanes), f32),
                 pltpu.VMEM((block * groups, lanes), f32),
                 pltpu.VMEM((states, groups, lanes), f32),
+                pltpu.VMEM((ends.shape[0] + others.shape[0], states, groups, lanes), f32),
             ],
         ),
         out_shape=[
@@ -260,7 +283,7 @@
         compiler_params=params(("arbitrary", "arbitrary")),
         name="front_scan",
         cost_estimate=LONG,
-    )(table, x, gain, decay, coef, span, omega, ends, proj, affine)
+    )(table, x, gain, decay, coef, span, omega, ends, others, proj, affine)
 
 
 def back_ends_body(gs_ref, decay_ref, end_ref, slab):
@@ -326,7 +349,8 @@
     coef_ref,
     span_ref,
     omega_ref,
-    ends_ref,
+    ends_own,
+    ends_oth,
     grad_ref,
     qx_ref,
     qs_ref,
@@ -337,11 +361,13 @@
     out_slab,
     history,
     carry,
+    ends_ref,
 ):
     states, groups, _ = decay_ref.shape
     count = x_ref.shape[1]
     slot = slot_ref[0]
-    total = ends_ref.shape[0]
+    slots = ends_own.shape[0]
+    total = slots + ends_oth.shape[0]
 
     @pl.when(pl.program_id(0) == 0)
     def _():
@@ -353,6 +379,8 @@
     @pl.when(pl.program_id(0) == 0)
     def _():
         carry[...] = jnp.zeros_like(carry)
+        ends_ref[:slots] = ends_own[...]
+        ends_ref[slots:] = ends_oth[...]
 
         def link(i, _):
             carry[...] = (
@@ -429,7 +457,7 @@
     ).astype(bf16)
 
 
-def back_scan(table, slot, x, gs, gv, gi, check, gain, decay, coef, span, omega, ends, after=()):
+def back_scan(table, slot, x, gs, gv, gi, check, gain, decay, coef, span, omega, ends, others, after=()):
     _, length, width = x.shape
     states, groups, lanes = decay.shape
     blocks = check.shape[1]
@@ -438,7 +466,7 @@
     row = pl.BlockSpec((1, width), lambda b, t, u: (0, 0))
     tokens = pl.BlockSpec((1, block, width), lambda b, t, u: (slot, blocks - 1 - b, 0))
     return pl.pallas_call(
-        ignoring(back_scan_body, 13, len(after)),
+        ignoring(back_scan_body, 14, len(after)),
         grid_spec=pltpu.PrefetchScalarGridSpec(
             num_scalar_prefetch=2,
             grid=(blocks,),
@@ -457,6 +485,7 @@
                 whole3,
                 row,
                 pl.BlockSpec(ends.shape, lambda b, t, u: (0, 0, 0, 0)),
+                pl.BlockSpec(others.shape, lambda b, t, u: (0, 0, 0, 0)),
             ]
             + [pl.BlockSpec(memory_space=pl.ANY)] * len(after),
             out_specs=[
@@ -472,6 +501,7 @@
                 pltpu.VMEM((block * groups, lanes), f32),
                 pltpu.VMEM((block, states, groups, lanes), f32),
                 pltpu.VMEM((states, groups, lanes), f32),
+                pltpu.VMEM((ends.shape[0] + others.shape[0], states, groups, lanes), f32),
             ],
         ),
         out_shape=[
@@ -484,7 +514,7 @@
         compiler_params=params(("arbitrary",)),
         name="back_scan",
         cost_estimate=LONG,
-    )(table, jnp.full((1,), slot, jnp.int32), x, gs, gv, gi, check, gain, decay, coef, span, omega, ends, *after)
+    )(table, jnp.full((1,), slot, jnp.int32), x, gs, gv, gi, check, gain, decay, coef, span, omega, ends, others, *after)
 
 
 def chunk_copies(table_ref, own, others, kept, total, length, sem):
@@ -561,7 +591,7 @@
         return sums + jnp.sum(terms, axis=1, keepdims=True)
 
     sums = lax.fori_loop(0, reach * tiles, second, jnp.zeros((length, 1), f32))
-    lse_ref[0] = peak + jnp.log(sums)
+    lse_ref[0] = jnp.broadcast_to(peak + jnp.log(sums), (length, 128)).T[:1]
     inverse = 1.0 / sums
 
     @pl.when(pl.program_id(0) == 0)
@@ -613,7 +643,7 @@
             out_specs=[
                 tokens,
                 tokens,
-                pl.BlockSpec((1, length, 1), lambda k, t: (k, 0, 0)),
+                pl.BlockSpec((1, 1, length), lambda k, t: (k, 0, 0)),
             ],
             scratch_shapes=[
                 pltpu.VMEM((total * length, key_width), bf16),
@@ -627,7 +657,7 @@
         out_shape=[
             jax.ShapeDtypeStruct((slots, length, value_width), bf16),
             jax.ShapeDtypeStruct((slots, length, value_width), bf16),
-            jax.ShapeDtypeStruct((slots, length, 1), f32),
+            jax.ShapeDtypeStruct((slots, 1, length), f32),
         ],
         compiler_params=params(("arbitrary",)),
         name="attend",
@@ -1598,15 +1628,15 @@
 
         return move
 
-    def spread(self, value):
+    def outgoing(self, value):
         late = lax.axis_index("seq") >= self.seq // 2
-        out = []
-        for round_index in range(2):
-            sent = lax.dynamic_index_in_dim(
-                value, jnp.where(late, 1 - round_index, round_index), 0, False
-            )
-            out.append(self.send(sent, self.home_to_work(round_index)))
-        return out
+        return [
+            lax.dynamic_index_in_dim(value, jnp.where(late, 1 - r, r), 0, False)
+            for r in range(2)
+        ]
+
+    def to_work(self, value, round_index):
+        return self.send(value, self.home_to_work(round_index))
 
     def homeward(self, value, round_index):
         pairs = [(b, a) for a, b in self.pairs(self.home_to_work(round_index))]
@@ -1765,8 +1795,9 @@
 
 
 def finish_body(
-    mine, other, alpha, damp, beta, eta, alpha_out, damp_out, beta_out, eta_out, rest, rows
+    mine, other, alpha, damp, beta, eta, alpha_out, damp_out, beta_out, eta_out, *rest
 ):
+    *rest, rows = rest
     rows[...] = mine[...] + other[...].astype(f32)
     states = alpha.shape[0]
     groups = alpha.shape[1] // 128
@@ -1781,19 +1812,21 @@
         damp_out[:, at] = -alpha[:, at] * decay_total
         beta_out[:, at] = alpha[:, at] * input_total
         eta_out[:, at] = rate * x_sum
-    rest[...] = rows[2 * states * groups :]
-
-
-def finish(mine, other, alpha, damp, beta, eta):
+    start = 2 * states * groups
+    for out in rest:
+        out[...] = rows[start : start + out.shape[0]]
+        start += out.shape[0]
+
+
+def finish(mine, other, alpha, damp, beta, eta, counts):
     inside = pl.BlockSpec(memory_space=pltpu.VMEM)
     rows = mine.shape[0]
     shape = jax.ShapeDtypeStruct(alpha.shape, f32)
-    left = rows - 2 * alpha.size // 128
     return pl.pallas_call(
         finish_body,
         in_specs=[inside] * 6,
-        out_specs=[inside] * 5,
-        out_shape=[shape] * 4 + [jax.ShapeDtypeStruct((left, 128), f32)],
+        out_specs=[inside] * (4 + len(counts)),
+        out_shape=[shape] * 4 + [jax.ShapeDtypeStruct((n, 128), f32) for n in counts],
         scratch_shapes=[pltpu.VMEM((rows, 128), f32)],
         name="finish",
         cost_estimate=BRIEF,
@@ -1881,7 +1914,12 @@
     table = jnp.concatenate([chunks, slot_of, full.astype(jnp.int32)[None]])
     ids, places, blocks = layout.orders()
 
-    arriving = layout.spread(inputs)
+    arriving = [
+        (slot, at * (chunk_rows // count), layout.to_work(piece, slot))
+        for slot, count in ((0, 1), (1, 1))
+        for at, piece in enumerate(jnp.split(layout.outgoing(inputs)[slot], count))
+    ]
+    leaving = layout.outgoing(cotangent)
     bias_back, bias_front = bias_tiles(relative_bias, chunk_rows // TILE - 1, full)
 
     states = smooth_alpha.shape[0]
@@ -1896,15 +1934,16 @@
     mix_shared, mix_main = mix_proj[:, :key_width], mix_proj[:, key_width:]
 
     held, after = (), (bias_back, bias_front, mix_main, mix_shared, span, coef)
-    for slot in range(slots):
+    ready = (table, ids, places, blocks, *leaving)
+    for slot, row, piece in arriving:
         held = front(
-            arriving[slot], slot, slots, held, gain_row, decay_slab, value_proj, after=after
+            piece, slot, row, (slots, chunk_rows), held, gain_row, decay_slab, value_proj, after=after
         )
-        after = ()
+        after, ready = ready, ()
     normed_low, x, value_low, value_slope, ends = held
-    ends_all = jnp.concatenate([ends, layout.gather(ends)])
-    cotangent, ends_all = lax.optimization_barrier((cotangent, ends_all))
-    cots = layout.spread(cotangent)
+    ends_others = layout.gather(ends)
+    leaving, ends_others = lax.optimization_barrier((leaving, ends_others))
+    cots = [layout.to_work(v, r) for r, v in enumerate(leaving)]
     normed_low = normed_low.reshape(tokens, width)
     value_slope = value_slope.reshape(tokens, value_width)
     value_others = layout.gather(value_low)
@@ -1916,7 +1955,8 @@
         coef,
         span,
         omega_row,
-        ends_all,
+        ends,
+        ends_others,
         mix_shared,
         score_affine,
         block,
@@ -1970,7 +2010,7 @@
         table,
         query_low,
         grad_att.reshape(slots, chunk_rows, value_width),
-        lse.reshape(slots, 1, chunk_rows),
+        lse,
         bias_back,
         key_low,
         key_others,
@@ -2008,7 +2048,7 @@
     grad_smooth = grad_smooth.reshape(slots, chunk_rows, width)
     after = layout.turn((feed_sum, value_sum, proj_sum, shared_sum), (grad_smooth,))
     back = back_ends(grad_smooth, decay_slab, after=after)
-    back_all = jnp.concatenate([back, layout.gather(back)])
+    back_others = layout.gather(back)
     after = layout.turn((feed_sum, mix_sum, value_sum, shared_sum), (back,))
 
     def scan_back(slot, after):
@@ -2025,7 +2065,8 @@
             coef,
             span,
             omega_row,
-            back_all,
+            back,
+            back_others,
             after=after,
         )
 
@@ -2074,13 +2115,10 @@
     feed_in_grad = feed_in_grad.transpose(1, 0, 2).reshape(rows, -1)
     out_grad, value_grad = proj_sum.total[0, 0].T, value_sum.total[0, 0]
     mix_grad = mix_sum.total[0, 0]
-    alpha_grad, damp_grad, beta_grad, eta_grad, totals = finish(
-        *totals, smooth_alpha, smooth_damp, smooth_beta, smooth_eta
-    )
-    parts, start = [], 0
-    for item in small:
-        parts.append(totals[start : start + item.shape[0]].reshape(-1))
-        start += item.shape[0]
+    alpha_grad, damp_grad, beta_grad, eta_grad, *parts = finish(
+        *totals, smooth_alpha, smooth_damp, smooth_beta, smooth_eta, [v.shape[0] for v in small]
+    )
+    parts = [v.reshape(-1) for v in parts]
     return (
         block_out,
         grad_in,

time: 547 us -> 538 us (0.984)
  Pallas kernels: 359 us -> 377 us
  starting transfers between devices: 61.5 us -> 43.6 us
    ppermute x39, starting transfers between devices: 52.1 us -> 39.1 us  [send(): return lax.ppermute(value, AXES, self.pairs(move))]
    pallas_call x1, Pallas kernels: 21.7 us -> 33.1 us  [attend_back(): pl.pallas_call(ignoring(functools.partial(attend_back_body, total=total),...]
    pallas_call x1, Pallas kernels: 13.9 us -> 20 us  [attend(): pl.pallas_call(functools.partial(attend_body, total=total), grid_spec=plt...]
    unnamed x132 -> x130, local copies, waits for them, and re-layouts: 20 us -> 17.7 us
  transfers between devices with their start and end apart: 43 -> 43, of which waited for: 9 -> 10; matrix products, arithmetic and copies ran while one was open for 9% -> 9% of each run, Pallas kernels for 51% -> 55%
where the time goes in v7:
time: 538 us; the launch traced here: 531 us
  Pallas kernels  377 us (70%)
  waiting for transfers between devices  49.1 us (9%)
  starting transfers between devices  43.6 us (8%)
  local copies, waits for them, and re-layouts  42.2 us (8%)
  other arithmetic  17.2 us (3%)
    pallas_call x1, Pallas kernels, feed(): pl.pallas_call(ignoring(feed_body, 8, len(after)), grid_spec=pltpu.Prefet...  68.5 us
    ppermute x39, waiting for transfers between devices, send(): return lax.ppermute(value, AXES, self.pairs(move))  49.1 us
    pallas_call x8, Pallas kernels, stage_sums(): pl.pallas_call(body, grid=(steps,), in_specs=riders.in_specs + [pl.BlockS...  47.8 us
    pallas_call x2, Pallas kernels, back_scan(): pl.pallas_call(ignoring(back_scan_body, 14, len(after)), grid_spec=pltpu....  40.6 us
    ppermute x39, starting transfers between devices, send(): return lax.ppermute(value, AXES, self.pairs(move))  39.1 us
    pallas_call x1, Pallas kernels, attend_back(): pl.pallas_call(ignoring(functools.partial(attend_back_body, total=total),...  33.1 us
    pallas_call x2, Pallas kernels, front(): pl.pallas_call(ignoring(functools.partial(front_body, fresh=row == 0), 5,...  20.1 us
    pallas_call x1, Pallas kernels, attend(): pl.pallas_call(functools.partial(attend_body, total=total), grid_spec=plt...  20 us
  transfers between devices with their start and end apart: 43, of which 10 were waited for; matrix products, arithmetic and copies ran while one was open for 9% of the time, Pallas kernels for 55%

profile of v7, /device:TPU:0, one launch (start us, length us, event | category | flops | bytes accessed | tf_op | source)
XLA Modules:
  0.0 531.0 jit_solution(553694946173431164)
XLA Ops:
  1.8 3.0 dynamic-slice_bitcast_fusion.2
  4.9 2.5 collective-permute-start.1
  7.6 8.0 %slice.96.refs_7_.right_ref.refs_2_ = bf16[1024,4096]{1,0:T(8,128)(2,1)} slice(bf16[1024,4224]{1,0:T(8,128)(2,1)} %param.30), slice={[0:1024], [128:4224]} | slice | bytes 16777216 | tf_op jit(solution)/shard_map/slice | solution.py:1934
  15.5 1.7 slice.97.refs_8_.proj_ref.refs_3_
  26.4 6.1 %bias.1 = (f32[9,256,256]{2,1,0:T(8,128)}, f32[9,256,256]{2,1,0:T(8,128)}) custom-call(s32[1]{0:T(128)S(6)} %convert_element_type.38.flag_ref, f32[8,1,512]{2,1,0:T(1,128)} %copy.62.back_row, f32[8,1,512]{2,1,0:T(1,128)} %broadcast_in_dim.48.front_row), custom_call_target="tpu_custom_call" | custom-call | tf_op jit(solution)/shard_map/bias/pallas_call | solution.py:900
  33.1 10.0 %front.2 = (bf16[2,512,1024]{2,1,0:T(8,128)(2,1)}, bf16[2,512,1024]{2,1,0:T(8,128)(2,1)}, bf16[2,512,2048]{2,1,0:T(8,128)(2,1)}, bf16[2,512,2048]{2,1,0:T(8,128)(2,1)}, f32[2,16,8,128]{3,2,1,0:T(8,128)}) custom-call(bf16[512,1024]{1,0:T(8,128)(2,1)} %collective-permute-done.2.refs_0_, f32[1,1024]{1,0:T(1,128)} %bitcast.322, f32[16,8,128]{2,1,0:T(8,128)} %bitcast.269, ...), custom_call_target="tpu_custom_call" | custom-call | flops 1 | bytes 1 | tf_op jit(solution)/shard_map/front/pallas_call | solution.py:130
  43.2 12.5 %collective-permute-done.1.refs_0_ = bf16[512,1024]{1,0:T(8,128)(2,1)S(1)} collective-permute-done((bf16[512,1024]{1,0:T(8,128)(2,1)}, bf16[512,1024]{1,0:T(8,128)(2,1)S(1)}, u32[]{:S(2)}, u32[]{:S(2)}) %collective-permute-start.1) | collective-permute-done | bytes 1048608 | tf_op jit(solution)/shard_map/ppermute | solution.py:1614
  56.6 10.1 %front.3 = (bf16[2,512,1024]{2,1,0:T(8,128)(2,1)}, bf16[2,512,1024]{2,1,0:T(8,128)(2,1)}, bf16[2,512,2048]{2,1,0:T(8,128)(2,1)}, bf16[2,512,2048]{2,1,0:T(8,128)(2,1)}, f32[2,16,8,128]{3,2,1,0:T(8,128)}) custom-call(bf16[512,1024]{1,0:T(8,128)(2,1)} %copy-done.11, ...), custom_call_target="tpu_custom_call", output_to_operand_aliasing={{0}: (5, {}), {1}: (6, {}), {2}: (7, {}), {3}: (8, {}), {4}... | custom-call | flops 1 | bytes 1 | tf_op jit(solution)/shard_map/front/pallas_call | solution.py:130
  68.5 2.4 collective-permute-start.7
  70.8 17.3 %front_scan.1 = (f32[2,512,1024]{2,1,0:T(8,128)}, bf16[2,512,1024]{2,1,0:T(8,128)(2,1)}, f32[2,4,16,8,128]{4,3,2,1,0:T(8,128)}, f32[2,512,128]{2,1,0:T(8,128)}, ...) custom-call(s32[9]{0:T(128)} %concatenate.36.refs_10_.table_ref.refs_0_, ...), custom_call_target="tpu_custom_call" | custom-call | flops 99999997952 | bytes 1 | tf_op jit(solution)/shard_map/front_scan/pallas_call | solution.py:243
  88.8 13.0 %product.1.pre_ref.update_ref.refs_5_.refs_6_ = bf16[1024,4096]{1,0:T(8,128)(2,1)} custom-call(bf16[1024,1024]{1,0:T(8,128)(2,1)} %bitcast.216, bf16[1024,4096]{1,0:T(8,128)(2,1)} %slice.96.refs_7_.right_ref.refs_2_), custom_call_target="tpu_custom_call" | custom-call | flops 1 | bytes 1 | tf_op jit(solution)/shard_map/product/pallas_call | solution.py:1259
  102.5 20.0 %attend.1 = (bf16[2,512,2048]{2,1,0:T(8,128)(2,1)}, bf16[2,512,2048]{2,1,0:T(8,128)(2,1)}, f32[2,1,512]{2,1,0:T(1,128)}) custom-call(s32[9]{0:T(128)} %concatenate.36.refs_10_.table_ref.refs_0_, bf16[2,512,128]{2,1,0:T(8,128)(2,1)} %get-tuple-element.139.q_ref.refs_1_, f32[9,256,256]{2,1,0:T(8,128)} %get-tuple-element.130.refs_6_.bias_ref, ...), custom_call_target="tpu_custom_call" | custom-call | flops 1 | bytes 1 | tf_op jit(solution)/shard_map/attend/pallas_call | solution.py:629
  122.5 12.7 %candidate.1 = (f32[1024,1024]{1,0:T(8,128)}, f32[1024,1024]{1,0:T(8,128)}, bf16[1024,1024]{1,0:T(8,128)(2,1)}) custom-call(bf16[1024,2048]{1,0:T(8,128)(2,1)} %bitcast.212, bf16[2048,1024]{1,0:T(8,128)(2,1)} %refs_9_.1, bf16[1024,4096]{1,0:T(8,128)(2,1)} %product.1.pre_ref.update_ref.refs_5_.refs_6_, ...), custom_call_target="tpu_custom_call" | custom-call | flops 1 | bytes 1 | tf_op jit(solution)/shard_map/candidate/pallas_call | solution.py:950
  136.2 68.5 %feed.1 = (bf16[512,1024]{1,0:T(8,128)(2,1)}, bf16[512,1024]{1,0:T(8,128)(2,1)}, f32[1024,1024]{1,0:T(8,128)}, bf16[4,1024,512]{2,1,0:T(8,128)(2,1)}, bf16[4,102...) custom-call(s32[8]{0:T(128)} %broadcast_select_fusion.1.refs_11_.refs_0_, ...), custom_call_target="tpu_custom_call" | custom-call | flops 1 | bytes 1 | tf_op jit(solution)/shard_map/feed/pallas_call | solution.py:1201
  205.2 2.0 collective-permute-start.9
  207.2 19.8 %gate.1 = (f32[1024,1024]{1,0:T(8,128)}, bf16[1024,4096]{1,0:T(8,128)(2,1)}, bf16[1024,2048]{1,0:T(8,128)(2,1)}, f32[1,1024]{1,0:T(1,128)}) custom-call(f32[1024,1024]{1,0:T(8,128)} %get-tuple-element.150.refs_0_, bf16[512,1024]{1,0:T(8,128)(2,1)} %copy-done.14, bf16[512,1024]{1,0:T(8,128)(2,1)} %collective-permute-done.7.refs_4_.refs_2_, ...), custom_call_target="tpu_custom_call" | custom-call | flops 99999997952 | bytes 1 | tf_op jit(solution)/shard_map/gate/pallas_call | solution.py:1039
  227.1 9.5 %stage_sums.8 = (bf16[2,2048,512]{2,1,0:T(8,128)(2,1)}, bf16[2,2048,512]{2,1,0:T(8,128)(2,1)}) custom-call(bf16[1,2,2048,512]{3,2,1,0:T(8,128)(2,1)} %bitcast.221, bf16[1,2,2048,512]{3,2,1,0:T(8,128)(2,1)} %bitcast.30.refs_1_, bf16[1,2,2048,512]{3,2,1,0:T(8,128)(2,1)} %bitcast.222, bf16[1,2,2048,512]{3,2,1,0:T(8,128)(2,1)} %bitcast.33.refs_3_, ...), custom_call_target="tpu_custom_call" | custom-call | flops 1 | bytes 1 | tf_op jit(solution)/shard_map/stage_sums/pallas_call | solution.py:1585
  238.0 15.1 %by_rows.2 = (bf16[4,1,128,4096]{3,2,1,0:T(8,128)(2,1)}, bf16[4,1,128,4096]{3,2,1,0:T(8,128)(2,1)}) custom-call(s32[8]{0:T(128)} %broadcast_select_fusion.1.refs_11_.refs_0_, s32[1]{0:T(128)} %constant.104.clone.1.refs_1_, bf16[1024,1024]{1,0:T(8,128)(2,1)} %bitcast.217, bf16[1024,4096]{1,0:T(8,128)(2,1)} %get-tuple-element.153.refs_3_.refs_2_.refs_0_, ...), custom_call_target="tpu_custom_call" | custom-call | flops 99999997952 | bytes 1 | tf_op jit(solution)/shard_map/by_rows/pallas_call | solution.py:1424
  253.2 11.9 %by_columns.1 = (bf16[4,1024,256]{2,1,0:T(8,128)(2,1)}, bf16[4,1024,256]{2,1,0:T(8,128)(2,1)}) custom-call(s32[8]{0:T(128)} %broadcast_select_fusion.1.refs_11_.refs_0_, s32[4]{0:T(128)} %get-tuple-element.128.refs_12_.refs_1_, bf16[1024,4096]{1,0:T(8,128)(2,1)} %get-tuple-element.153.refs_3_.refs_2_.refs_0_, bf16[1024,2048]{1,0:T(8,128)(2,1)} %bitcast.213, ...), custom_call_target="tpu_custom_call" | custom-call | flops 1 | bytes 1 | tf_op jit(solution)/shard_map/by_columns/pallas_call | solution.py:1360
  265.1 33.1 %attend_back.1 = (f32[2,512,128]{2,1,0:T(8,128)}, bf16[2,512,128]{2,1,0:T(8,128)(2,1)}, bf16[2,512,2048]{2,1,0:T(8,128)(2,1)}, bf16[2,512,2176]{2,1,0:T(8,128)(2,1)}, f32[8,1,512]{2,1,0:T(1,128)}) custom-call(s32[9]{0:T(128)} %concatenate.36.refs_10_.table_ref.refs_0_, bf16[2,512,128]{2,1,0:T(8,128)(2,1)} %get-tuple-element.139.q_ref.refs_1_, ...), custom_call_target="tpu_custom_call" | custom-call | flops 99999997952 | bytes 1 | tf_op jit(solution)/shard_map/attend_back/pallas_call | solution.py:812
  300.1 7.7 %stage_sums.9 = (bf16[2,1024,512]{2,1,0:T(8,128)(2,1)}, bf16[2,1024,512]{2,1,0:T(8,128)(2,1)}, bf16[1,2048,256]{2,1,0:T(8,128)(2,1)}, bf16[1,2048,256]{2,1,0:T(8,128)(2,1)}) custom-call(bf16[2,2,1024,512]{3,2,1,0:T(8,128)(2,1)} %bitcast.343, bf16[2,2,1024,512]{3,2,1,0:T(8,128)(2,1)} %collective-permute-done.14.refs_1_, bf16[1,2,2048,256]{3,2,1,0:T(8,128)(2,1)} %bitcast.354, ...), custom_call_target="tpu_custom_call" | custom-call | flops 99999997952 | bytes 1 | tf_op jit(solution)/shard_map/stage_sums/pallas_call | solution.py:1585
  310.0 15.9 %value_back.1 = (f32[1024,1024]{1,0:T(8,128)}, bf16[4,4,128,512]{3,2,1,0:T(8,128)(2,1)}, bf16[4,4,128,512]{3,2,1,0:T(8,128)(2,1)}) custom-call(s32[8]{0:T(128)} %broadcast_select_fusion.1.refs_11_.refs_0_, s32[4]{0:T(128)} %get-tuple-element.128.refs_12_.refs_1_, bf16[1024,1024]{1,0:T(8,128)(2,1)} %bitcast.240, bf16[1024,2048]{1,0:T(8,128)(2,1)} %bitcast.383, ...), custom_call_target="tpu_custom_call" | custom-call | flops 99999997952 | bytes 1 | tf_op jit(solution)/shard_map/value_back/pallas_call | solution.py:1497
  326.0 2.5 fusion.8
  328.5 4.4 by_rows.3
  333.4 6.0 %stage_sums.10 = (bf16[1,256,4096]{2,1,0:T(8,128)(2,1)}, bf16[1,256,4096]{2,1,0:T(8,128)(2,1)}) custom-call(bf16[1,2,256,4096]{3,2,1,0:T(8,128)(2,1)} %bitcast.211, bf16[1,2,256,4096]{3,2,1,0:T(8,128)(2,1)} %bitcast.46.refs_1_, bf16[4,1,128,128]{3,2,1,0:T(8,128)(2,1)} %get-tuple-element.179.refs_2_, bf16[4,1,128,128]{3,2,1,0:T(8,128)(2,1)} %get-tuple-element.180.refs_3_), custom_call_target="tpu_custom_call" | custom-call | flops 1 | bytes 1 | tf_op jit(solution)/shard_map/stage_sums/pallas_call | solution.py:1585
  340.9 17.1 %smooth_back.1 = f32[1024,1024]{1,0:T(8,128)} custom-call(bf16[1024,4096]{1,0:T(8,128)(2,1)} %get-tuple-element.153.refs_3_.refs_2_.refs_0_, bf16[1024,128]{1,0:T(8,128)(2,1)} %get-tuple-element.310.refs_3_.refs_1_, bf16[1024,4096]{1,0:T(8,128)(2,1)} %slice.96.refs_7_.right_ref.refs_2_, bf16[1024,128]{1,0:T(8,128)(2,1)} %slice.97.refs_8_.proj_ref.refs_3_, ...), custom_call_target="tpu_custom_call" | custom-call | flops 99999997952 | bytes 1 | tf_op jit(solution)/shard_map/smooth_back/pallas_call | solution.py:1305
  359.3 6.9 %stage_sums.11 = (bf16[2,512,512]{2,1,0:T(8,128)(2,1)}, bf16[2,512,512]{2,1,0:T(8,128)(2,1)}, bf16[1,1024,512]{2,1,0:T(8,128)(2,1)}, bf16[1,1024,512]{2,1,0:T(8,...) custom-call(bf16[2,2,512,512]{3,2,1,0:T(8,128)(2,1)} %bitcast.237, ...), custom_call_target="tpu_custom_call" | custom-call | flops 1 | bytes 1 | tf_op jit(solution)/shard_map/stage_sums/pallas_call | solution.py:1585
  367.2 2.0 collective-permute-start.23
  371.2 8.1 %back_ends.1.refs_8_.refs_12_ = f32[2,16,8,128]{3,2,1,0:T(8,128)} custom-call(f32[2,512,1024]{2,1,0:T(8,128)} %bitcast.208, f32[16,8,128]{2,1,0:T(8,128)} %bitcast.272, bf16[2,2,256,512]{3,2,1,0:T(8,128)(2,1)} %bitcast.263, bf16[2,2,256,512]{3,2,1,0:T(8,128)(2,1)} %bitcast.223, bf16[1,2,512,512]{3,2,1,0:T(8,128)(2,1)} %bitcast.259, ...), custom_call_target="tpu_custom_call" | custom-call | flops 1 | bytes 1 | tf_op jit(solution)/shard_map/back_ends/pallas_call | solution.py:322
  381.0 1.9 collective-permute-done.24.refs_7_
  383.0 7.9 %collective-permute-done.21.refs_1_ = bf16[2,2,256,512]{3,2,1,0:T(8,128)(2,1)S(1)} collective-permute-done((bf16[2,2,256,512]{3,2,1,0:T(8,128)(2,1)}, bf16[2,2,256,512]{3,2,1,0:T(8,128)(2,1)S(1)}, u32[]{:S(2)}, u32[]{:S(2)}) %collective-permute-start.21) | collective-permute-done | bytes 1048608 | tf_op jit(solution)/shard_map/ppermute | solution.py:1614
  392.8 6.0 %stage_sums.12 = (bf16[2,256,512]{2,1,0:T(8,128)(2,1)}, bf16[2,256,512]{2,1,0:T(8,128)(2,1)}, bf16[1,128,4096]{2,1,0:T(8,128)(2,1)}, bf16[1,128,4096]{2,1,0:T(8,...) custom-call(bf16[2,2,256,512]{3,2,1,0:T(8,128)(2,1)} %bitcast.224, ...), custom_call_target="tpu_custom_call" | custom-call | flops 1 | bytes 1 | tf_op jit(solution)/shard_map/stage_sums/pallas_call | solution.py:1585
  398.8 1.8 collective-permute-start.26
  403.1 20.2 %back_scan.2 = (bf16[512,1024]{1,0:T(8,128)(2,1)}, f32[16,8,128]{2,1,0:T(8,128)}, f32[16,8,128]{2,1,0:T(8,128)}, f32[1,1024]{1,0:T(1,128)}, f32[1,1024]{1,0:T(1,128)}) custom-call(s32[9]{0:T(128)} %concatenate.36.refs_10_.table_ref.refs_0_, s32[1]{0:T(128)} %constant.104.clone.1.refs_1_, bf16[2,512,1024]{2,1,0:T(8,128)(2,1)} %get-tuple-element.136.x_ref.refs_2_, ...), custom_call_target="tpu_custom_call" | custom-call | flops 99999997952 | bytes 1 | tf_op jit(solution)/shard_map/back_scan/pallas_call | solution.py:468
  426.5 4.8 stage_sums.13
  439.4 20.3 %back_scan.3 = (bf16[512,1024]{1,0:T(8,128)(2,1)}, f32[16,8,128]{2,1,0:T(8,128)}, f32[16,8,128]{2,1,0:T(8,128)}, f32[1,1024]{1,0:T(1,128)}, f32[1,1024]{1,0:T(1,128)}) custom-call(s32[9]{0:T(128)} %concatenate.36.refs_10_.table_ref.refs_0_, s32[1]{0:T(128)} %constant.103.clone.1.refs_1_, bf16[2,512,1024]{2,1,0:T(8,128)(2,1)} %get-tuple-element.136.x_ref.refs_2_, ...), custom_call_target="tpu_custom_call" | custom-call | flops 99999997952 | bytes 1 | tf_op jit(solution)/shard_map/back_scan/pallas_call | solution.py:468
  465.7 3.6 stage_sums.14
  470.9 1.7 select_bitcast_fusion.3
  472.6 6.9 %collective-permute-start.38 = (bf16[1,1,128,1056]{3,2,1,0:T(8,128)(2,1)S(1)}, bf16[1,1,128,1056]{3,2,1,0:T(8,128)(2,1)}, u32[]{:S(2)}, u32[]{:S(2)}) collective-permute-start(bf16[1,1,128,1056]{3,2,1,0:T(8,128)(2,1)S(1)} %bitcast.249), channel_id=1, source_target_pairs={{0,2},{1,3},{2,0},{3,1},{4,6},{5,7},{6,4},{7,5},{8,10},{9,11},{10,... | collective-permute-start | bytes 811016 | tf_op jit(solution)/shard_map/ppermute | solution.py:1614
  479.5 2.1 collective-permute-start.36
  483.2 2.9 collective-permute-start.40
  488.6 17.8 %collective-permute-done.39.refs_3_ = bf16[1,1,256,256]{3,2,1,0:T(8,128)(2,1)} collective-permute-done((bf16[1,1,256,256]{3,2,1,0:T(8,128)(2,1)S(1)}, bf16[1,1,256,256]{3,2,1,0:T(8,128)(2,1)}, u32[]{:S(2)}, u32[]{:S(2)}) %collective-permute-start.39) | collective-permute-done | bytes 131104 | tf_op jit(solution)/shard_map/ppermute | solution.py:1614
  506.4 2.8 collective-permute-done.40.refs_5_
  510.2 3.3 stage_sums.15
  517.5 3.9 collective-permute-done.41
  522.1 2.1 collective-permute-start.42
  524.2 2.3 maximum_convert_fusion
  528.9 1.8 finish.1
  (253 shorter events, 64.8 us)
Async XLA Ops:
  1.3 23.1 %collective-permute-start = (f32[2]{0:T(128)S(1)}, f32[2]{0:T(128)S(1)}, u32[]{:S(2)}, u32[]{:S(2)}) collective-permute-start(f32[2]{0:T(128)S(1)} %convert_element_type.37), channel_id=1, source_target_pairs={{0,4},{1,5},{2,6},{3,7},{4,0},{5,1},{6,2},{7,3},{8,12},{9,13},{10,... | collective-permute-start | bytes 32 | tf_op jit(solution)/shard_map/ppermute | solution.py:1614
  4.8 27.7 %collective-permute-start.2 = (bf16[512,1024]{1,0:T(8,128)(2,1)}, bf16[512,1024]{1,0:T(8,128)(2,1)}, u32[]{:S(2)}, u32[]{:S(2)}) collective-permute-start(bf16[512,1024]{1,0:T(8,128)(2,1)} %get-tuple-element.317), channel_id=1, source_target_pairs={{0,4},{1,0},{2,5},{3,1},{4,6},{5,2},{6,7},{7,3},{8,12},{9,8},{10,1... | collective-permute-start | bytes 3145736 | tf_op jit(solution)/shard_map/ppermute | solution.py:1614
  4.9 50.8 %collective-permute-start.1 = (bf16[512,1024]{1,0:T(8,128)(2,1)}, bf16[512,1024]{1,0:T(8,128)(2,1)S(1)}, u32[]{:S(2)}, u32[]{:S(2)}) collective-permute-start(bf16[512,1024]{1,0:T(8,128)(2,1)} %get-tuple-element.318), channel_id=1, source_target_pairs={{0,1},{1,5},{2,0},{3,4},{4,3},{5,7},{6,2},{7,6},{8,9},{9,13},{10,8... | collective-permute-start | bytes 3145736 | tf_op jit(solution)/shard_map/ppermute | solution.py:1614
  66.7 1.6 collective-permute-start.3
  66.8 35.0 %collective-permute-start.5 = (bf16[2,512,2048]{2,1,0:T(8,128)(2,1)}, bf16[2,512,2048]{2,1,0:T(8,128)(2,1)}, u32[]{:S(2)}, u32[]{:S(2)}) collective-permute-start(bf16[2,512,2048]{2,1,0:T(8,128)(2,1)} %get-tuple-element.142.v_own.refs_7_), channel_id=1, source_target_pairs={{0,4},{1,5},{2,6},{3,7},{4,0},{5,1},{6,2},{7,3},{8,12},{9,13},{10,... | collective-permute-start | bytes 12582920 | tf_op jit(solution)/shard_map/ppermute | solution.py:1614
  68.3 66.9 %collective-permute-start.6 = (bf16[512,1024]{1,0:T(8,128)(2,1)S(1)}, bf16[512,1024]{1,0:T(8,128)(2,1)S(1)}, u32[]{:S(2)}, u32[]{:S(2)}) collective-permute-start(bf16[512,1024]{1,0:T(8,128)(2,1)S(1)} %copy-done.3), channel_id=1, source_target_pairs={{0,4},{1,0},{2,5},{3,1},{4,6},{5,2},{6,7},{7,3},{8,12},{9,8},{10,1... | collective-permute-start | bytes 3145736 | tf_op jit(solution)/shard_map/ppermute | solution.py:1614
  68.5 66.7 %collective-permute-start.7 = (bf16[512,1024]{1,0:T(8,128)(2,1)S(1)}, bf16[512,1024]{1,0:T(8,128)(2,1)}, u32[]{:S(2)}, u32[]{:S(2)}) collective-permute-start(bf16[512,1024]{1,0:T(8,128)(2,1)S(1)} %copy-done.2), channel_id=1, source_target_pairs={{0,1},{1,5},{2,0},{3,4},{4,3},{5,7},{6,2},{7,6},{8,9},{9,13},{10,8... | collective-permute-start | bytes 3145736 | tf_op jit(solution)/shard_map/ppermute | solution.py:1614
  88.2 13.6 %collective-permute-start.4 = (bf16[2,512,128]{2,1,0:T(8,128)(2,1)}, bf16[2,512,128]{2,1,0:T(8,128)(2,1)S(1)}, u32[]{:S(2)}, u32[]{:S(2)}) collective-permute-start(bf16[2,512,128]{2,1,0:T(8,128)(2,1)} %get-tuple-element.141.k_own.refs_5_), channel_id=1, source_target_pairs={{0,4},{1,5},{2,6},{3,7},{4,0},{5,1},{6,2},{7,3},{8,12},{9,13},{10,... | collective-permute-start | bytes 786440 | tf_op jit(solution)/shard_map/ppermute | solution.py:1614
  204.6 22.4 %collective-permute-start.10 = (bf16[1,4,1024,512]{3,2,1,0:T(8,128)(2,1)}, bf16[1,4,1024,512]{3,2,1,0:T(8,128)(2,1)}, u32[]{:S(2)}, u32[]{:S(2)}) collective-permute-start(bf16[1,4,1024,512]{3,2,1,0:T(8,128)(2,1)} %bitcast.348), channel_id=1, source_target_pairs={{0,4},{1,5},{2,6},{3,7},{4,0},{5,1},{6,2},{7,3},{8,12},{9,13},{10,... | collective-permute-start | bytes 12582920 | tf_op jit(solution)/shard_map/ppermute | solution.py:1614
  205.1 22.0 %collective-permute-start.11 = (bf16[1,4,1024,512]{3,2,1,0:T(8,128)(2,1)}, bf16[1,4,1024,512]{3,2,1,0:T(8,128)(2,1)}, u32[]{:S(2)}, u32[]{:S(2)}) collective-permute-start(bf16[1,4,1024,512]{3,2,1,0:T(8,128)(2,1)} %bitcast.347), channel_id=1, source_target_pairs={{0,4},{1,5},{2,6},{3,7},{4,0},{5,1},{6,2},{7,3},{8,12},{9,13},{10,... | collective-permute-start | bytes 12582920 | tf_op jit(solution)/shard_map/ppermute | solution.py:1614
  205.2 59.9 %collective-permute-start.8 = (bf16[512,1024]{1,0:T(8,128)(2,1)}, bf16[512,1024]{1,0:T(8,128)(2,1)}, u32[]{:S(2)}, u32[]{:S(2)}) collective-permute-start(bf16[512,1024]{1,0:T(8,128)(2,1)} %get-tuple-element.148), channel_id=1, source_target_pairs={{1,0},{5,1},{0,2},{4,3},{3,4},{7,5},{2,6},{6,7},{9,8},{13,9},{8,10... | collective-permute-start | bytes 3145736 | tf_op jit(solution)/shard_map/ppermute | solution.py:1643
  205.2 59.9 %collective-permute-start.9 = (bf16[512,1024]{1,0:T(8,128)(2,1)}, bf16[512,1024]{1,0:T(8,128)(2,1)}, u32[]{:S(2)}, u32[]{:S(2)}) collective-permute-start(bf16[512,1024]{1,0:T(8,128)(2,1)} %get-tuple-element.149), channel_id=1, source_target_pairs={{4,0},{0,1},{5,2},{1,3},{6,4},{2,5},{7,6},{3,7},{12,8},{8,9},{13,1... | collective-permute-start | bytes 3145736 | tf_op jit(solution)/shard_map/ppermute | solution.py:1643
  236.5 62.3 %collective-permute-start.14 = (bf16[2,2,1024,512]{3,2,1,0:T(8,128)(2,1)}, bf16[2,2,1024,512]{3,2,1,0:T(8,128)(2,1)}, u32[]{:S(2)}, u32[]{:S(2)}) collective-permute-start(bf16[2,2,1024,512]{3,2,1,0:T(8,128)(2,1)} %bitcast.344), channel_id=1, source_target_pairs={{0,8},{1,9},{2,10},{3,11},{4,20},{5,21},{6,22},{7,23},{8,0},{9,1},... | collective-permute-start | bytes 12582920 | tf_op jit(solution)/shard_map/ppermute | solution.py:1614
  265.1 33.7 %collective-permute-start.15 = (bf16[1,4,1024,256]{3,2,1,0:T(8,128)(2,1)}, bf16[1,4,1024,256]{3,2,1,0:T(8,128)(2,1)S(1)}, u32[]{:S(2)}, u32[]{:S(2)}) collective-permute-start(bf16[1,4,1024,256]{3,2,1,0:T(8,128)(2,1)} %bitcast.356), channel_id=1, source_target_pairs={{0,4},{1,5},{2,6},{3,7},{4,0},{5,1},{6,2},{7,3},{8,12},{9,13},{10,... | collective-permute-start | bytes 6291464 | tf_op jit(solution)/shard_map/ppermute | solution.py:1614
  298.2 11.8 %collective-permute-start.12 = (bf16[2,512,2176]{2,1,0:T(8,128)(2,1)}, bf16[2,512,2176]{2,1,0:T(8,128)(2,1)}, u32[]{:S(2)}, u32[]{:S(2)}) collective-permute-start(bf16[2,512,2176]{2,1,0:T(8,128)(2,1)} %get-tuple-element.167), channel_id=1, source_target_pairs={{0,4},{1,5},{2,6},{3,7},{4,0},{5,1},{6,2},{7,3},{8,12},{9,13},{10,... | collective-permute-start | bytes 13369352 | tf_op jit(solution)/shard_map/ppermute | solution.py:1614
  298.7 34.7 %collective-permute-start.13 = (bf16[1,4,128,4096]{3,2,1,0:T(8,128)(2,1)}, bf16[1,4,128,4096]{3,2,1,0:T(8,128)(2,1)}, u32[]{:S(2)}, u32[]{:S(2)}) collective-permute-start(bf16[1,4,128,4096]{3,2,1,0:T(8,128)(2,1)} %bitcast.229), channel_id=1, source_target_pairs={{0,4},{1,5},{2,6},{3,7},{4,0},{5,1},{6,2},{7,3},{8,12},{9,13},{10,... | collective-permute-start | bytes 12582920 | tf_op jit(solution)/shard_map/ppermute | solution.py:1614
  307.9 50.1 %collective-permute-start.16 = (bf16[2,1,1024,512]{3,2,1,0:T(8,128)(2,1)}, bf16[2,1,1024,512]{3,2,1,0:T(8,128)(2,1)}, u32[]{:S(2)}, u32[]{:S(2)}) collective-permute-start(bf16[2,1,1024,512]{3,2,1,0:T(8,128)(2,1)} %bitcast.351), channel_id=1, source_target_pairs={{0,16},{1,17},{2,18},{3,19},{4,12},{5,13},{6,14},{7,15},{8,24},{9,... | collective-permute-start | bytes 6291464 | tf_op jit(solution)/shard_map/ppermute | solution.py:1614
  309.4 48.6 %collective-permute-start.18 = (bf16[1,2,1024,256]{3,2,1,0:T(8,128)(2,1)}, bf16[1,2,1024,256]{3,2,1,0:T(8,128)(2,1)}, u32[]{:S(2)}, u32[]{:S(2)}) collective-permute-start(bf16[1,2,1024,256]{3,2,1,0:T(8,128)(2,1)} %bitcast.357), channel_id=1, source_target_pairs={{0,8},{1,9},{2,10},{3,11},{4,20},{5,21},{6,22},{7,23},{8,0},{9,1},... | collective-permute-start | bytes 3145736 | tf_op jit(solution)/shard_map/ppermute | solution.py:1614
  325.9 32.1 %collective-permute-start.17 = (bf16[1,4,512,512]{3,2,1,0:T(8,128)(2,1)}, bf16[1,4,512,512]{3,2,1,0:T(8,128)(2,1)S(1)}, u32[]{:S(2)}, u32[]{:S(2)}) collective-permute-start(bf16[1,4,512,512]{3,2,1,0:T(8,128)(2,1)} %bitcast.353), channel_id=1, source_target_pairs={{0,4},{1,5},{2,6},{3,7},{4,0},{5,1},{6,2},{7,3},{8,12},{9,13},{10,... | collective-permute-start | bytes 6291464 | tf_op jit(solution)/shard_map/ppermute | solution.py:1614
  333.0 25.0 %collective-permute-start.19 = (bf16[1,4,128,128]{3,2,1,0:T(8,128)(2,1)}, bf16[1,4,128,128]{3,2,1,0:T(8,128)(2,1)S(1)}, u32[]{:S(2)}, u32[]{:S(2)}) collective-permute-start(bf16[1,4,128,128]{3,2,1,0:T(8,128)(2,1)} %bitcast.306), channel_id=1, source_target_pairs={{0,4},{1,5},{2,6},{3,7},{4,0},{5,1},{6,2},{7,3},{8,12},{9,13},{10,... | collective-permute-start | bytes 393224 | tf_op jit(solution)/shard_map/ppermute | solution.py:1614
  339.5 40.6 %collective-permute-start.22 = (bf16[1,2,128,4096]{3,2,1,0:T(8,128)(2,1)}, bf16[1,2,128,4096]{3,2,1,0:T(8,128)(2,1)}, u32[]{:S(2)}, u32[]{:S(2)}) collective-permute-start(bf16[1,2,128,4096]{3,2,1,0:T(8,128)(2,1)} %bitcast.349), channel_id=1, source_target_pairs={{0,8},{1,9},{2,10},{3,11},{4,20},{5,21},{6,22},{7,23},{8,0},{9,1},... | collective-permute-start | bytes 6291464 | tf_op jit(solution)/shard_map/ppermute | solution.py:1614
  366.2 24.6 %collective-permute-start.21 = (bf16[2,2,256,512]{3,2,1,0:T(8,128)(2,1)}, bf16[2,2,256,512]{3,2,1,0:T(8,128)(2,1)S(1)}, u32[]{:S(2)}, u32[]{:S(2)}) collective-permute-start(bf16[2,2,256,512]{3,2,1,0:T(8,128)(2,1)} %bitcast.262), channel_id=1, source_target_pairs={{0,1},{1,0},{2,3},{3,2},{4,5},{5,4},{6,7},{7,6},{8,9},{9,8},{10,11... | collective-permute-start | bytes 3145736 | tf_op jit(solution)/shard_map/ppermute | solution.py:1614
  367.2 23.6 %collective-permute-start.23 = (bf16[1,2,512,512]{3,2,1,0:T(8,128)(2,1)}, bf16[1,2,512,512]{3,2,1,0:T(8,128)(2,1)S(1)}, u32[]{:S(2)}, u32[]{:S(2)}) collective-permute-start(bf16[1,2,512,512]{3,2,1,0:T(8,128)(2,1)} %bitcast.258), channel_id=1, source_target_pairs={{0,8},{1,9},{2,10},{3,11},{4,20},{5,21},{6,22},{7,23},{8,0},{9,1},... | collective-permute-start | bytes 3145736 | tf_op jit(solution)/shard_map/ppermute | solution.py:1614
  371.1 11.9 %collective-permute-start.24 = (bf16[1,2,128,128]{3,2,1,0:T(8,128)(2,1)}, bf16[1,2,128,128]{3,2,1,0:T(8,128)(2,1)S(1)}, u32[]{:S(2)}, u32[]{:S(2)}) collective-permute-start(bf16[1,2,128,128]{3,2,1,0:T(8,128)(2,1)} %bitcast.309), channel_id=1, source_target_pairs={{0,8},{1,9},{2,10},{3,11},{4,20},{5,21},{6,22},{7,23},{8,0},{9,1},... | collective-permute-start | bytes 196616 | tf_op jit(solution)/shard_map/ppermute | solution.py:1614
  379.3 22.9 %collective-permute-start.20 = (f32[2,16,8,128]{3,2,1,0:T(8,128)}, f32[2,16,8,128]{3,2,1,0:T(8,128)}, u32[]{:S(2)}, u32[]{:S(2)}) collective-permute-start(f32[2,16,8,128]{3,2,1,0:T(8,128)} %back_ends.1.refs_8_.refs_12_), channel_id=1, source_target_pairs={{0,4},{1,5},{2,6},{3,7},{4,0},{5,1},{6,2},{7,3},{8,12},{9,13},{10,... | collective-permute-start | bytes 393224 | tf_op jit(solution)/shard_map/ppermute | solution.py:1614
  380.1 43.3 %collective-permute-start.28 = (bf16[1,1,1024,256]{3,2,1,0:T(8,128)(2,1)}, bf16[1,1,1024,256]{3,2,1,0:T(8,128)(2,1)S(1)}, u32[]{:S(2)}, u32[]{:S(2)}) collective-permute-start(bf16[1,1,1024,256]{3,2,1,0:T(8,128)(2,1)} %bitcast.279), channel_id=1, source_target_pairs={{0,16},{1,17},{2,18},{3,19},{4,12},{5,13},{6,14},{7,15},{8,24},{9,... | collective-permute-start | bytes 1572872 | tf_op jit(solution)/shard_map/ppermute | solution.py:1614
  398.8 26.6 %collective-permute-start.26 = (bf16[1,1,128,4096]{3,2,1,0:T(8,128)(2,1)}, bf16[1,1,128,4096]{3,2,1,0:T(8,128)(2,1)S(1)}, u32[]{:S(2)}, u32[]{:S(2)}) collective-permute-start(bf16[1,1,128,4096]{3,2,1,0:T(8,128)(2,1)} %bitcast.359), channel_id=1, source_target_pairs={{0,16},{1,17},{2,18},{3,19},{4,12},{5,13},{6,14},{7,15},{8,24},{9,... | collective-permute-start | bytes 3145736 | tf_op jit(solution)/shard_map/ppermute | solution.py:1614
  400.5 23.9 %collective-permute-start.27 = (bf16[1,1,512,512]{3,2,1,0:T(8,128)(2,1)}, bf16[1,1,512,512]{3,2,1,0:T(8,128)(2,1)S(1)}, u32[]{:S(2)}, u32[]{:S(2)}) collective-permute-start(bf16[1,1,512,512]{3,2,1,0:T(8,128)(2,1)} %bitcast.363), channel_id=1, source_target_pairs={{0,16},{1,17},{2,18},{3,19},{4,12},{5,13},{6,14},{7,15},{8,24},{9,... | collective-permute-start | bytes 1572872 | tf_op jit(solution)/shard_map/ppermute | solution.py:1614
  400.8 24.5 %collective-permute-start.25 = (bf16[2,1,256,512]{3,2,1,0:T(8,128)(2,1)}, bf16[2,1,256,512]{3,2,1,0:T(8,128)(2,1)S(1)}, u32[]{:S(2)}, u32[]{:S(2)}) collective-permute-start(bf16[2,1,256,512]{3,2,1,0:T(8,128)(2,1)} %bitcast.361), channel_id=1, source_target_pairs={{0,2},{1,3},{2,0},{3,1},{4,6},{5,7},{6,4},{7,5},{8,10},{9,11},{10,... | collective-permute-start | bytes 1572872 | tf_op jit(solution)/shard_map/ppermute | solution.py:1614
  402.1 22.3 %collective-permute-start.29 = (bf16[1,1,128,128]{3,2,1,0:T(8,128)(2,1)}, bf16[1,1,128,128]{3,2,1,0:T(8,128)(2,1)S(1)}, u32[]{:S(2)}, u32[]{:S(2)}) collective-permute-start(bf16[1,1,128,128]{3,2,1,0:T(8,128)(2,1)} %bitcast.371), channel_id=1, source_target_pairs={{0,16},{1,17},{2,18},{3,19},{4,12},{5,13},{6,14},{7,15},{8,24},{9,... | collective-permute-start | bytes 98312 | tf_op jit(solution)/shard_map/ppermute | solution.py:1614
  423.4 41.3 %collective-permute-start.31 = (bf16[512,1024]{1,0:T(8,128)(2,1)}, bf16[512,1024]{1,0:T(8,128)(2,1)S(1)}, u32[]{:S(2)}, u32[]{:S(2)}) collective-permute-start(bf16[512,1024]{1,0:T(8,128)(2,1)} %get-tuple-element.203.refs_10_), channel_id=1, source_target_pairs={{4,0},{0,1},{5,2},{1,3},{6,4},{2,5},{7,6},{3,7},{12,8},{8,9},{13,1... | collective-permute-start | bytes 3145736 | tf_op jit(solution)/shard_map/ppermute | solution.py:1643
  436.3 27.2 %collective-permute-start.32 = (bf16[1,2,128,1056]{2,3,1,0:T(8,128)(2,1)}, bf16[1,2,128,1056]{2,3,1,0:T(8,128)(2,1)S(1)}, u32[]{:S(2)}, u32[]{:S(2)}) collective-permute-start(bf16[1,2,128,1056]{2,3,1,0:T(8,128)(2,1)} %get-tuple-element.319), channel_id=1, source_target_pairs={{0,1},{1,0},{2,3},{3,2},{4,5},{5,4},{6,7},{7,6},{8,9},{9,8},{10,11... | collective-permute-start | bytes 1622024 | tf_op jit(solution)/shard_map/ppermute | solution.py:1614
  437.3 27.3 %collective-permute-start.33 = (bf16[1,2,256,256]{3,2,1,0:T(8,128)(2,1)}, bf16[1,2,256,256]{3,2,1,0:T(8,128)(2,1)S(1)}, u32[]{:S(2)}, u32[]{:S(2)}) collective-permute-start(bf16[1,2,256,256]{3,2,1,0:T(8,128)(2,1)} %bitcast.94.refs_18_), channel_id=1, source_target_pairs={{0,1},{1,0},{2,3},{3,2},{4,5},{5,4},{6,7},{7,6},{8,9},{9,8},{10,11... | collective-permute-start | bytes 786440 | tf_op jit(solution)/shard_map/ppermute | solution.py:1614
  438.4 26.4 %collective-permute-start.34 = (bf16[1,2,128,512]{3,2,1,0:T(8,128)(2,1)S(1)}, bf16[1,2,128,512]{3,2,1,0:T(8,128)(2,1)}, u32[]{:S(2)}, u32[]{:S(2)}) collective-permute-start(bf16[1,2,128,512]{3,2,1,0:T(8,128)(2,1)S(1)} %bitcast.370), channel_id=1, source_target_pairs={{0,1},{1,0},{2,3},{3,2},{4,5},{5,4},{6,7},{7,6},{8,9},{9,8},{10,11... | collective-permute-start | bytes 786440 | tf_op jit(solution)/shard_map/ppermute | solution.py:1614
  439.3 23.2 %copy-start.41 = (f32[1,1024]{1,0:T(1,128)S(1)}, f32[1,1024]{1,0:T(1,128)}, u32[]{:S(2)}) copy-start(f32[1,1024]{1,0:T(1,128)} %get-tuple-element.220) | copy-start | bytes 12292
  439.4 23.2 %copy-start.46 = (f32[128]{0:T(128)S(1)}, f32[128]{0:T(128)}, u32[]{:S(2)}) copy-start(f32[128]{0:T(128)} %get-tuple-element.309) | copy-start | bytes 1540
  439.4 23.2 %copy-start.47 = (f32[128]{0:T(128)S(1)}, f32[128]{0:T(128)}, u32[]{:S(2)}) copy-start(f32[128]{0:T(128)} %get-tuple-element.304) | copy-start | bytes 1540
  459.7 49.5 %collective-permute-start.30 = (bf16[512,1024]{1,0:T(8,128)(2,1)}, bf16[512,1024]{1,0:T(8,128)(2,1)S(1)}, u32[]{:S(2)}, u32[]{:S(2)}) collective-permute-start(bf16[512,1024]{1,0:T(8,128)(2,1)} %get-tuple-element.211.refs_6_), channel_id=1, source_target_pairs={{1,0},{5,1},{0,2},{4,3},{3,4},{7,5},{2,6},{6,7},{9,8},{13,9},{8,10... | collective-permute-start | bytes 3145736 | tf_op jit(solution)/shard_map/ppermute | solution.py:1643
  470.9 8.6 %collective-permute-start.35 = (f32[320,128]{1,0:T(8,128)}, f32[320,128]{1,0:T(8,128)S(1)}, u32[]{:S(2)}, u32[]{:S(2)}) collective-permute-start(f32[320,128]{1,0:T(8,128)} %pack.1), channel_id=1, source_target_pairs={{0,4},{1,5},{2,6},{3,7},{4,0},{5,1},{6,2},{7,3},{8,12},{9,13},{10,... | collective-permute-start | bytes 491528 | tf_op jit(solution)/shard_map/ppermute | solution.py:1614
  472.6 36.6 %collective-permute-start.38 = (bf16[1,1,128,1056]{3,2,1,0:T(8,128)(2,1)S(1)}, bf16[1,1,128,1056]{3,2,1,0:T(8,128)(2,1)}, u32[]{:S(2)}, u32[]{:S(2)}) collective-permute-start(bf16[1,1,128,1056]{3,2,1,0:T(8,128)(2,1)S(1)} %bitcast.249), channel_id=1, source_target_pairs={{0,2},{1,3},{2,0},{3,1},{4,6},{5,7},{6,4},{7,5},{8,10},{9,11},{10,... | collective-permute-start | bytes 811016 | tf_op jit(solution)/shard_map/ppermute | solution.py:1614
  479.5 6.6 %collective-permute-start.36 = (f32[320,128]{1,0:T(8,128)S(1)}, f32[320,128]{1,0:T(8,128)S(1)}, u32[]{:S(2)}, u32[]{:S(2)}) collective-permute-start(f32[320,128]{1,0:T(8,128)S(1)} %add.95), channel_id=1, source_target_pairs={{0,8},{1,9},{2,10},{3,11},{4,12},{5,13},{6,14},{7,15},{8,0},{9,1},... | collective-permute-start | bytes 491528 | tf_op jit(solution)/shard_map/ppermute | solution.py:1614
  483.2 23.3 %collective-permute-start.39 = (bf16[1,1,256,256]{3,2,1,0:T(8,128)(2,1)S(1)}, bf16[1,1,256,256]{3,2,1,0:T(8,128)(2,1)}, u32[]{:S(2)}, u32[]{:S(2)}) collective-permute-start(bf16[1,1,256,256]{3,2,1,0:T(8,128)(2,1)S(1)} %bitcast.288), channel_id=1, source_target_pairs={{0,2},{1,3},{2,0},{3,1},{4,6},{5,7},{6,4},{7,5},{8,10},{9,11},{10,... | collective-permute-start | bytes 393224 | tf_op jit(solution)/shard_map/ppermute | solution.py:1614
  483.2 26.0 %collective-permute-start.40 = (bf16[1,1,128,512]{3,2,1,0:T(8,128)(2,1)S(1)}, bf16[1,1,128,512]{3,2,1,0:T(8,128)(2,1)}, u32[]{:S(2)}, u32[]{:S(2)}) collective-permute-start(bf16[1,1,128,512]{3,2,1,0:T(8,128)(2,1)S(1)} %bitcast.291), channel_id=1, source_target_pairs={{0,2},{1,3},{2,0},{3,1},{4,6},{5,7},{6,4},{7,5},{8,10},{9,11},{10,... | collective-permute-start | bytes 393224 | tf_op jit(solution)/shard_map/ppermute | solution.py:1614
  486.2 27.3 %copy-start.21 = (f32[320,128]{1,0:T(8,128)}, f32[320,128]{1,0:T(8,128)S(1)}, u32[]{:S(2)}) copy-start(f32[320,128]{1,0:T(8,128)S(1)} %add.96.refs_0_) | copy-start | bytes 491524
  486.2 27.3 %collective-permute-start.37 = (f32[320,128]{1,0:T(8,128)S(1)}, f32[320,128]{1,0:T(8,128)S(1)}, u32[]{:S(2)}, u32[]{:S(2)}) collective-permute-start(f32[320,128]{1,0:T(8,128)S(1)} %add.96.refs_0_), channel_id=1, source_target_pairs={{0,16},{1,17},{2,18},{3,19},{4,20},{5,21},{6,22},{7,23},{8,24},{9,... | collective-permute-start | bytes 491528 | tf_op jit(solution)/shard_map/ppermute | solution.py:1614
  488.6 28.7 %copy-start.13 = (bf16[512,1024]{1,0:T(8,128)(2,1)S(1)}, bf16[512,1024]{1,0:T(8,128)(2,1)}, u32[]{:S(2)}) copy-start(bf16[512,1024]{1,0:T(8,128)(2,1)} %copy-done.12) | copy-start | bytes 3145732
  516.9 4.5 collective-permute-start.41
  522.1 6.2 %collective-permute-start.42 = (bf16[320,128]{1,0:T(8,128)(2,1)S(1)}, bf16[320,128]{1,0:T(8,128)(2,1)S(1)}, u32[]{:S(2)}, u32[]{:S(2)}) collective-permute-start(bf16[320,128]{1,0:T(8,128)(2,1)S(1)} %get-tuple-element.307), channel_id=1, source_target_pairs={{0,2},{1,3},{2,0},{3,1},{4,6},{5,7},{6,4},{7,5},{8,10},{9,11},{10,... | collective-permute-start | bytes 245768 | tf_op jit(solution)/shard_map/ppermute | solution.py:1614
  (55 other events, 452.1 us)

commit v8 on v7

--- a/solution.py
+++ b/solution.py
@@ -567,8 +567,8 @@
     base = (chunk + 1 - reach) * length
     queries = q_ref[0]
 
-    def first(kt, peak):
-        spot = pl.ds(pl.multiple_of(base + kt * TILE, TILE), TILE)
+    def first(kc, peak):
+        spot = pl.ds(pl.multiple_of(base + kc * length, length), length)
         tile = (
             lax.dot_general(
                 queries, keys[spot, :], (((1,), (1,)), ((), ())), preferred_element_type=f32
@@ -576,21 +576,21 @@
             * scale
         )
         for r in range(tiles):
-            rows = slice(r * TILE, (r + 1) * TILE)
-            gap = (reach - 1) * tiles + r - kt + tiles - 1
-            scores[kt, rows, :] = tile[rows] + bias_ref[gap]
-        return jnp.maximum(peak, jnp.max(scores[kt], axis=1, keepdims=True))
-
-    peak = lax.fori_loop(
-        0, reach * tiles, first, jnp.full((length, 1), 2 * MASKED, f32)
-    )
-
-    def second(kt, sums):
-        terms = jnp.exp(scores[kt] - peak)
-        probs[:, pl.ds(pl.multiple_of(kt * TILE, TILE), TILE)] = terms.astype(bf16)
+            for a in range(tiles):
+                rows = slice(r * TILE, (r + 1) * TILE)
+                cols = slice(a * TILE, (a + 1) * TILE)
+                gap = (reach - 1 - kc) * tiles + r - a + tiles - 1
+                scores[kc, rows, cols] = tile[rows, cols] + bias_ref[gap]
+        return jnp.maximum(peak, jnp.max(scores[kc], axis=1, keepdims=True))
+
+    peak = lax.fori_loop(0, reach, first, jnp.full((length, 1), 2 * MASKED, f32))
+
+    def second(kc, sums):
+        terms = jnp.exp(scores[kc] - peak)
+        probs[:, pl.ds(pl.multiple_of(kc * length, length), length)] = terms.astype(bf16)
         return sums + jnp.sum(terms, axis=1, keepdims=True)
 
-    sums = lax.fori_loop(0, reach * tiles, second, jnp.zeros((length, 1), f32))
+    sums = lax.fori_loop(0, reach, second, jnp.zeros((length, 1), f32))
     lse_ref[0] = jnp.broadcast_to(peak + jnp.log(sums), (length, 128)).T[:1]
     inverse = 1.0 / sums
 
@@ -648,7 +648,7 @@
             scratch_shapes=[
                 pltpu.VMEM((total * length, key_width), bf16),
                 pltpu.VMEM((total * length, value_width), bf16),
-                pltpu.VMEM((total * length // TILE, length, TILE), f32),
+                pltpu.VMEM((total, length, length), f32),
                 pltpu.VMEM((length, total * length), bf16),
                 pltpu.SemaphoreType.DMA((total,)),
                 pltpu.SemaphoreType.DMA((total,)),
@@ -1287,23 +1287,15 @@
         out_ref[...] = total[...] * silu_slope(smooth_ref[...])
 
 
-def smooth_back(main, shared, weight, shared_weight, smoothed, after=(), riders=None):
+def smooth_back(main, shared, weight, shared_weight, smoothed, after=()):
     tokens, width = smoothed.shape
     tile = 1024
 
     def all_of(shape):
         return pl.BlockSpec(shape, lambda i: (0, 0), pipeline_mode=pl.Buffered(1))
 
-    extra = riders or Riders([], 1)
-    taken, given = len(extra.ins), len(extra.out_shapes)
-
-    def body(*refs):
-        first = 5 + taken + len(after)
-        smooth_back_body(*refs[:5], refs[first], *refs[first + 1 + given :])
-        extra.body(refs[5 : 5 + taken], refs[first + 1 : first + 1 + given])
-
-    out = pl.pallas_call(
-        body,
+    return pl.pallas_call(
+        ignoring(smooth_back_body, 5, len(after)),
         grid=(main.shape[1] // tile,),
         in_specs=[
             pl.BlockSpec((tokens, tile), lambda i: (0, i)),
@@ -1312,16 +1304,14 @@
             all_of(shared_weight.shape),
             all_of(smoothed.shape),
         ]
-        + extra.in_specs
         + [pl.BlockSpec(memory_space=pl.ANY)] * len(after),
-        out_specs=[all_of(smoothed.shape)] + extra.out_specs,
-        out_shape=[jax.ShapeDtypeStruct(smoothed.shape, f32)] + extra.out_shapes,
+        out_specs=all_of(smoothed.shape),
+        out_shape=jax.ShapeDtypeStruct(smoothed.shape, f32),
         scratch_shapes=[pltpu.VMEM(smoothed.shape, f32)],
         compiler_params=params(("arbitrary",)),
         name="smooth_back",
         cost_estimate=LONG,
-    )(main, shared, weight, shared_weight, smoothed, *extra.ins, *after)
-    return (out[0], riders.result(out[1:])) if riders else out[0]
+    )(main, shared, weight, shared_weight, smoothed, *after)
 
 
 def by_columns_body(ids_ref, places_ref, left_ref, right_ref, send, keep, plain, turned):
@@ -1400,7 +1390,7 @@
     keep[...] = grad[middle:].reshape(keep.shape)
 
 
-def by_rows(ids, places, left, right, seq=1, after=(), cost=BRIEF, riders=None):
+def by_rows(ids, places, left, right, seq=1, after=(), cost=BRIEF):
     tokens, rows = left.shape
     parts = ids.shape[0]
     half = parts // 2
@@ -1413,16 +1403,8 @@
     split = pl.BlockSpec(
         (half, 1, rows // parts, tile), lambda i, t, u: (0, u[jnp.minimum(i // share, seq - 1)], 0, i % share)
     )
-    extra = riders or Riders([], 1)
-    taken, given = len(extra.ins), len(extra.out_shapes)
-
-    def body(*refs):
-        first = 4 + taken + len(after)
-        by_rows_body(*refs[:4], *refs[first : first + 2], *refs[first + 2 + given :])
-        extra.body(refs[4 : 4 + taken], refs[first + 2 : first + 2 + given])
-
-    out = pl.pallas_call(
-        body,
+    return pl.pallas_call(
+        ignoring(by_rows_body, 4, len(after)),
         grid_spec=pltpu.PrefetchScalarGridSpec(
             num_scalar_prefetch=2,
             grid=(seq * share,),
@@ -1432,20 +1414,18 @@
                 ),
                 pl.BlockSpec((tokens, tile), lambda i, t, u: (0, i)),
             ]
-            + extra.in_specs
             + [pl.BlockSpec(memory_space=pl.ANY)] * len(after),
-            out_specs=[split, split] + extra.out_specs,
+            out_specs=[split, split],
             scratch_shapes=[
                 pltpu.VMEM((rows, tokens), bf16),
                 pltpu.VMEM((rows, tokens), bf16),
             ],
         ),
-        out_shape=[shape, shape] + extra.out_shapes,
+        out_shape=[shape, shape],
         compiler_params=params(("arbitrary",)),
         name="by_rows",
         cost_estimate=cost,
-    )(ids, places, left, right, *extra.ins, *after)
-    return (out[:2], riders.result(out[2:])) if riders else out
+    )(ids, places, left, right, *after)
 
 
 def value_back_body(
@@ -1520,79 +1500,45 @@
     )(ids, places, left, own, others, slope, proj, *after)
 
 
-class Riders:
-    def __init__(self, groups, steps):
-        self.shapes, self.ins, self.whole = [], [], []
-        self.in_specs, self.out_specs, self.out_shapes = [], [], []
-        for pairs, single, kind in groups:
-            halves = 1 if single else 2
-            g, n, rows, columns = pairs[0][0].shape
-            each = n * rows // halves // steps
-            self.shapes.append((len(pairs), halves))
-            for pair in pairs:
-                for v in pair:
-                    self.ins.append(v.reshape(g, halves, n * rows // halves, columns))
-                    self.in_specs.append(
-                        pl.BlockSpec((g, halves, each, columns), lambda i, *_: (0, 0, i, 0))
-                    )
-            for _ in range(halves):
-                self.out_specs.append(
-                    pl.BlockSpec((len(pairs) * g, each, columns), lambda i, *_: (0, i, 0))
+def stage_body(*refs, jobs):
+    ins, outs = list(refs), list(refs[sum(map(sum, jobs)) :])
+    for counts, out in zip(jobs, outs):
+        for g, count in enumerate(counts):
+            total = ins.pop(0)[0].astype(f32)
+            for _ in range(count - 1):
+                total = total + ins.pop(0)[0].astype(f32)
+            out[g] = total.astype(out.dtype)
+
+
+def stage_sums(jobs, after=(), steps=4, cost=BRIEF):
+    for _, rows, _ in jobs:
+        while rows % (16 * steps) and steps > 1:
+            steps //= 2
+    ins, in_specs, out_specs, out_shapes, counts = [], [], [], [], []
+    for terms, rows, kind in jobs:
+        each = rows // steps
+        columns = terms[0][0][0].shape[2]
+        for array, entry, start in (term for group in terms for term in group):
+            ins.append(array)
+            in_specs.append(
+                pl.BlockSpec(
+                    (1, each, columns),
+                    lambda i, entry=entry, first=start // each: (entry, first + i, 0),
                 )
-                self.out_shapes.append(
-                    jax.ShapeDtypeStruct((len(pairs) * g, n * rows // halves, columns), kind)
-                )
-            self.whole.append((halves, (len(pairs) * g, n // halves, rows, columns)))
-
-    @staticmethod
-    def fit(groups, steps):
-        for pairs, single, _ in groups:
-            _, n, rows, _ = pairs[0][0].shape
-            while (n * rows // (1 if single else 2)) % (16 * steps) and steps > 1:
-                steps //= 2
-        return steps
-
-    def body(self, ins, outs):
-        ins, outs = list(ins), list(outs)
-        for pairs, halves in self.shapes:
-            into = [outs.pop(0) for _ in range(halves)]
-            start = 0
-            for _ in range(pairs):
-                kept, arrived = ins.pop(0), ins.pop(0)
-                stop = start + kept.shape[0]
-                for part, out in enumerate(into):
-                    out[start:stop] = (
-                        kept[:, part].astype(f32) + arrived[:, part].astype(f32)
-                    ).astype(out.dtype)
-                start = stop
-
-    def result(self, sums):
-        sums = list(sums)
-        return [
-            tuple(sums.pop(0).reshape(shape) for _ in range(halves))
-            for halves, shape in self.whole
-        ]
-
-
-def stage_sums(groups, after=(), steps=4, cost=BRIEF):
-    steps = Riders.fit(groups, steps)
-    riders = Riders(groups, steps)
-    count = len(riders.ins)
-
-    def body(*refs):
-        riders.body(refs[:count], refs[count + len(after) :])
-
-    sums = pl.pallas_call(
-        body,
+            )
+        out_specs.append(pl.BlockSpec((len(terms), each, columns), lambda i: (0, i, 0)))
+        out_shapes.append(jax.ShapeDtypeStruct((len(terms), rows, columns), kind))
+        counts.append([len(group) for group in terms])
+    return pl.pallas_call(
+        ignoring(functools.partial(stage_body, jobs=counts), len(ins), len(after)),
         grid=(steps,),
-        in_specs=riders.in_specs + [pl.BlockSpec(memory_space=pl.ANY)] * len(after),
-        out_specs=riders.out_specs,
-        out_shape=riders.out_shapes,
+        in_specs=in_specs + [pl.BlockSpec(memory_space=pl.ANY)] * len(after),
+        out_specs=out_specs,
+        out_shape=out_shapes,
         compiler_params=params(("arbitrary",)),
         name="stage_sums",
         cost_estimate=cost,
-    )(*riders.ins, *after)
-    return riders.result(sums)
+    )(*ins, *after)
 
 
 class Layout:
@@ -1704,50 +1650,31 @@
             return lambda d, z: (d ^ (1 << stage if d % 2 == 0 else 1 << (bits - stage)), z)
         return lambda d, z: (d, z ^ (1 << (stage - bits)))
 
-    def turn(self, sums, after, cost=BRIEF, carrier=None, steps=None):
-        sums = [s for s in sums if s.arrived]
+    def turn(self, sums, after, cost=BRIEF):
+        sums = [s for s in sums if s.total is None]
         if not sums:
-            return carrier(None, after) if carrier else after
-        dp_stages = self.dp.bit_length() - 1
-        last = dp_stages + self.seq.bit_length() - 1
-        groups = []
+            return after
+        jobs = []
         for s in sums:
-            pairs = list(zip(s.kept, s.arrived))
-            single = s.stage + 1 == last
-            if s.stage + 1 == dp_stages:
-                single = not s.over_seq
-                if s.over_seq:
-                    pairs = [
-                        tuple(
-                            v.reshape(v.shape[0], self.seq, -1, v.shape[-1]) for v in pair
-                        )
-                        for pair in pairs
-                    ]
-            groups.append((pairs, single, f32 if s.stage + 1 == last else bf16))
-        if carrier:
-            if Riders.fit(groups, steps) == steps:
-                own, out = carrier(Riders(groups, steps), after)
+            s.stage += 1
+            ended = s.stage == s.stages
+            rows = s.rows if ended else s.rows // 2
+            jobs.append((s.terms, rows, f32 if ended and s.over_seq else bf16))
+        out = stage_sums(jobs, after, cost=cost)
+        for s, held, (_, rows, _) in zip(sums, out, jobs):
+            if s.stage == s.stages:
+                s.total = held
             else:
-                out = stage_sums(groups, after, cost=cost)
-                own = carrier(None, [part for held in out for part in held])
-        else:
-            out = stage_sums(groups, after, cost=cost)
-        for s, held, (_, single, _) in zip(sums, out, groups):
-            s.stage += 1
-            s.arrived = ()
-            if single:
-                s.total = held[0]
-            else:
-                s.send([held[0]], [held[1]])
-        if carrier:
-            return own
-        return [part for held in out for part in held]
-
-    def over_seq(self, held):
-        bits = self.seq.bit_length() - 1
-        for bit in range(bits - 1):
-            held = held + self.send(held.astype(bf16), lambda d, z: (d, z ^ (1 << bit))).astype(f32)
-        return held, self.send(held.astype(bf16), lambda d, z: (d, z ^ (1 << (bits - 1))))
+                s.terms = [[(a, e, start + rows) for a, e, start in group] for group in s.terms]
+                s.rows = rows
+                s.send(held)
+        return list(out)
+
+    def from_seq(self, held):
+        return [
+            self.send(held.astype(bf16), lambda d, z: (d, z ^ other))
+            for other in range(1, self.seq)
+        ]
 
 
     def over_dp(self, held):
@@ -1794,11 +1721,13 @@
     )(*ins, *after)
 
 
-def finish_body(
-    mine, other, alpha, damp, beta, eta, alpha_out, damp_out, beta_out, eta_out, *rest
-):
+def finish_body(*refs, terms):
+    alpha, damp, beta, eta, alpha_out, damp_out, beta_out, eta_out, *rest = refs[terms:]
     *rest, rows = rest
-    rows[...] = mine[...] + other[...].astype(f32)
+    total = refs[0][...]
+    for term in refs[1:terms]:
+        total = total + term[...].astype(f32)
+    rows[...] = total
     states = alpha.shape[0]
     groups = alpha.shape[1] // 128
     for c in range(groups):
@@ -1818,36 +1747,48 @@
         start += out.shape[0]
 
 
-def finish(mine, other, alpha, damp, beta, eta, counts):
+def finish(terms, alpha, damp, beta, eta, counts):
     inside = pl.BlockSpec(memory_space=pltpu.VMEM)
-    rows = mine.shape[0]
+    rows = terms[0].shape[0]
     shape = jax.ShapeDtypeStruct(alpha.shape, f32)
     return pl.pallas_call(
-        finish_body,
-        in_specs=[inside] * 6,
+        functools.partial(finish_body, terms=len(terms)),
+        in_specs=[inside] * (len(terms) + 4),
         out_specs=[inside] * (4 + len(counts)),
         out_shape=[shape] * 4 + [jax.ShapeDtypeStruct((n, 128), f32) for n in counts],
         scratch_shapes=[pltpu.VMEM((rows, 128), f32)],
         name="finish",
         cost_estimate=BRIEF,
-    )(mine, other, alpha, damp, beta, eta)
+    )(*terms, alpha, damp, beta, eta)
 
 
 class Sum:
     def __init__(self, layout, *pairs, over_seq=True):
-        self.layout, self.over_seq, self.stage = layout, over_seq, 0
+        self.layout = layout
+        self.stage = 0
+        self.dp_stages = layout.dp.bit_length() - 1
+        self.stages = self.dp_stages + (layout.seq.bit_length() - 1 if over_seq else 0)
+        self.over_seq = over_seq
         self.total = None
-        pairs = [[v.reshape(1, v.shape[0], -1, v.shape[-1]) for v in pair] for pair in pairs]
-        self.send([p[0] for p in pairs], [p[1] for p in pairs])
-
-    def send(self, sent, kept):
-        self.kept = kept
-        self.arrived = [self.layout.send(v, self.layout.partner(self.stage)) for v in sent]
+        pairs = [[v.reshape(1, -1, v.shape[-1]) for v in pair] for pair in pairs]
+        self.rows = pairs[0][1].shape[1]
+        self.terms = [
+            [(kept, 0, 0), (layout.send(sent, layout.partner(0)), 0, 0)] for sent, kept in pairs
+        ]
+
+    def send(self, held):
+        arrived = self.layout.send(held, self.layout.partner(self.stage))
+        for entry, group in enumerate(self.terms):
+            group.append((arrived, entry, 0))
 
     def begin_seq(self, block):
-        self.total = None
-        middle = self.layout.seq // 2
-        self.send([block[None, :middle]], [block[None, middle:]])
+        self.stage = self.dp_stages
+        self.stages = self.stage + self.layout.seq.bit_length() - 1
+        self.over_seq, self.total = True, None
+        block = block.reshape(1, -1, block.shape[-1])
+        self.rows = block.shape[1] // 2
+        self.terms = [[(block, 0, self.rows)]]
+        self.send(block[:, : self.rows])
 
 
 def mm(a, b):
@@ -2077,10 +2018,10 @@
     home_first = layout.homeward(first[0], 0)
     while mix_sum.total is None or shared_sum.total is None:
         after = layout.turn((mix_sum, shared_sum), after)
-    rows = jnp.concatenate([shared_sum.total[0, 0], mix_sum.total[0, 0]], axis=1)
+    rows = jnp.concatenate([shared_sum.total[0], mix_sum.total[0]], axis=1)
     rows = rows.reshape(rows.shape[0], layout.seq, -1).transpose(1, 0, 2)
     mix_sum.begin_seq(rows[blocks])
-    second = scan_back(1, (*after, *mix_sum.kept))
+    second = scan_back(1, (*after, mix_sum.terms[0][0][0]))
     affine_grad = jnp.stack(
         [
             jnp.sum(grad_query * shared_pre * jax.nn.sigmoid(shared_pre), axis=0),
@@ -2105,18 +2046,23 @@
     turned = layout.turn(sums, (second[0], home_first), cost=LONG)
     totals = layout.over_dp(pack(first[1:3], second[1:3], rest, after=turned))
     after = layout.turn(sums, (*turned, home_second))
-    totals = layout.over_seq(later_sum(*totals, after=after))
+    totals = later_sum(*totals, after=after)
     while any(v.total is None for v in sums):
         after = layout.turn(sums, after)
     grad_in = layout.gathered([home_first, home_second]).astype(f32)
-    feed_out_grad, feed_in_grad = feed_sum.total[0, 0].T, feed_sum.total[1, 0]
+    feed_out_grad, feed_in_grad = feed_sum.total[0].T, feed_sum.total[1]
     rows = width // layout.dp
     feed_in_grad = feed_in_grad.reshape(-1, rows, feed_in_grad.shape[-1])
     feed_in_grad = feed_in_grad.transpose(1, 0, 2).reshape(rows, -1)
-    out_grad, value_grad = proj_sum.total[0, 0].T, value_sum.total[0, 0]
-    mix_grad = mix_sum.total[0, 0]
+    out_grad, value_grad = proj_sum.total[0].T, value_sum.total[0]
+    mix_grad = mix_sum.total[0]
     alpha_grad, damp_grad, beta_grad, eta_grad, *parts = finish(
-        *totals, smooth_alpha, smooth_damp, smooth_beta, smooth_eta, [v.shape[0] for v in small]
+        [totals, *layout.from_seq(totals)],
+        smooth_alpha,
+        smooth_damp,
+        smooth_beta,
+        smooth_eta,
+        [v.shape[0] for v in small],
     )
     parts = [v.reshape(-1) for v in parts]
     return (

time: 538 us -> 529 us (0.983)
  Pallas kernels: 377 us -> 351 us
  starting transfers between devices: 43.6 us -> 59.3 us
    ppermute x39 -> x40, starting transfers between devices: 39.1 us -> 51.4 us  [send(): return lax.ppermute(value, AXES, self.pairs(move))]
    pallas_call x1, Pallas kernels: 33.1 us -> 22 us  [attend_back(): pl.pallas_call(ignoring(functools.partial(attend_back_body, total=total),...]
    pallas_call x12, Pallas kernels: 86.3 us -> 78.7 us  [the longest x8 40.2 us: stage_sums(): pl.pallas_call(ignoring(functools.partial(stage_body, jobs=counts), len(i...]
    pallas_call x1, Pallas kernels: 20 us -> 13.3 us  [attend(): pl.pallas_call(functools.partial(attend_body, total=total), grid_spec=plt...]
    ppermute x39 -> x40, waiting for transfers between devices: 49.1 us -> 47.7 us  [send(): return lax.ppermute(value, AXES, self.pairs(move))]
    unnamed x130 -> x139, local copies, waits for them, and re-layouts: 17.7 us -> 18.8 us
  transfers between devices with their start and end apart: 43 -> 44, of which waited for: 10 -> 10; matrix products, arithmetic and copies ran while one was open for 9% -> 9% of each run, Pallas kernels for 55% -> 52%
where the time goes in v8:
time: 529 us; the launch traced here: 522 us
  Pallas kernels  351 us (66%)
  starting transfers between devices  59.3 us (11%)
  waiting for transfers between devices  47.7 us (9%)
  local copies, waits for them, and re-layouts  43.5 us (8%)
  other arithmetic  17.6 us (3%)
    pallas_call x1, Pallas kernels, feed(): pl.pallas_call(ignoring(feed_body, 8, len(after)), grid_spec=pltpu.Prefet...  68.4 us
    ppermute x40, starting transfers between devices, send(): return lax.ppermute(value, AXES, self.pairs(move))  51.4 us
    ppermute x40, waiting for transfers between devices, send(): return lax.ppermute(value, AXES, self.pairs(move))  47.7 us
    pallas_call x2, Pallas kernels, back_scan(): pl.pallas_call(ignoring(back_scan_body, 14, len(after)), grid_spec=pltpu....  40.6 us
    pallas_call x8, Pallas kernels, stage_sums(): pl.pallas_call(ignoring(functools.partial(stage_body, jobs=counts), len(i...  40.2 us
    pallas_call x1, Pallas kernels, attend_back(): pl.pallas_call(ignoring(functools.partial(attend_back_body, total=total),...  22 us
    pallas_call x2, Pallas kernels, front(): pl.pallas_call(ignoring(functools.partial(front_body, fresh=row == 0), 5,...  20.2 us
    pallas_call x1, Pallas kernels, gate(): pl.pallas_call(ignoring(gate_body, 10, len(after)), grid=(tokens // rows,...  19.9 us
  transfers between devices with their start and end apart: 44, of which 10 were waited for; matrix products, arithmetic and copies ran while one was open for 9% of the time, Pallas kernels for 52%

profile of v8, /device:TPU:0, one launch (start us, length us, event | category | flops | bytes accessed | tf_op | source)
XLA Modules:
  0.0 521.6 jit_solution(15017596251880075481)
XLA Ops:
  1.8 3.1 dynamic-slice_bitcast_fusion.2
  4.9 2.5 collective-permute-start.1
  7.6 8.0 %slice.91.refs_7_.right_ref.refs_2_ = bf16[1024,4096]{1,0:T(8,128)(2,1)} slice(bf16[1024,4224]{1,0:T(8,128)(2,1)} %param.30), slice={[0:1024], [128:4224]} | slice | bytes 16777216 | tf_op jit(solution)/shard_map/slice | solution.py:1875
  26.4 6.0 %bias.1 = (f32[9,256,256]{2,1,0:T(8,128)}, f32[9,256,256]{2,1,0:T(8,128)}) custom-call(s32[1]{0:T(128)S(6)} %convert_element_type.34.flag_ref, f32[8,1,512]{2,1,0:T(1,128)} %copy.63.back_row, f32[8,1,512]{2,1,0:T(1,128)} %broadcast_in_dim.42.front_row), custom_call_target="tpu_custom_call" | custom-call | tf_op jit(solution)/shard_map/bias/pallas_call | solution.py:900
  33.1 10.0 %front.2 = (bf16[2,512,1024]{2,1,0:T(8,128)(2,1)}, bf16[2,512,1024]{2,1,0:T(8,128)(2,1)}, bf16[2,512,2048]{2,1,0:T(8,128)(2,1)}, bf16[2,512,2048]{2,1,0:T(8,128)(2,1)}, f32[2,16,8,128]{3,2,1,0:T(8,128)}) custom-call(bf16[512,1024]{1,0:T(8,128)(2,1)} %collective-permute-done.2.refs_0_, f32[1,1024]{1,0:T(1,128)} %bitcast.233, f32[16,8,128]{2,1,0:T(8,128)} %bitcast.206, ...), custom_call_target="tpu_custom_call" | custom-call | flops 1 | bytes 1 | tf_op jit(solution)/shard_map/front/pallas_call | solution.py:130
  43.1 12.6 %collective-permute-done.1.refs_0_ = bf16[512,1024]{1,0:T(8,128)(2,1)S(1)} collective-permute-done((bf16[512,1024]{1,0:T(8,128)(2,1)}, bf16[512,1024]{1,0:T(8,128)(2,1)S(1)}, u32[]{:S(2)}, u32[]{:S(2)}) %collective-permute-start.1) | collective-permute-done | bytes 1048608 | tf_op jit(solution)/shard_map/ppermute | solution.py:1560
  56.7 10.2 %front.3 = (bf16[2,512,1024]{2,1,0:T(8,128)(2,1)}, bf16[2,512,1024]{2,1,0:T(8,128)(2,1)}, bf16[2,512,2048]{2,1,0:T(8,128)(2,1)}, bf16[2,512,2048]{2,1,0:T(8,128)(2,1)}, f32[2,16,8,128]{3,2,1,0:T(8,128)}) custom-call(bf16[512,1024]{1,0:T(8,128)(2,1)} %copy-done.18, ...), custom_call_target="tpu_custom_call", output_to_operand_aliasing={{0}: (5, {}), {1}: (6, {}), {2}: (7, {}), {3}: (8, {}), {4}... | custom-call | flops 1 | bytes 1 | tf_op jit(solution)/shard_map/front/pallas_call | solution.py:130
  68.6 2.4 collective-permute-start.7
  71.0 17.3 %front_scan.1 = (f32[2,512,1024]{2,1,0:T(8,128)}, bf16[2,512,1024]{2,1,0:T(8,128)(2,1)}, f32[2,4,16,8,128]{4,3,2,1,0:T(8,128)}, f32[2,512,128]{2,1,0:T(8,128)}, ...) custom-call(s32[9]{0:T(128)} %concatenate.36.refs_10_.table_ref.refs_0_, ...), custom_call_target="tpu_custom_call" | custom-call | flops 99999997952 | bytes 1 | tf_op jit(solution)/shard_map/front_scan/pallas_call | solution.py:243
  88.9 13.0 %product.1.pre_ref.update_ref.refs_5_.refs_6_ = bf16[1024,4096]{1,0:T(8,128)(2,1)} custom-call(bf16[1024,1024]{1,0:T(8,128)(2,1)} %bitcast.184, bf16[1024,4096]{1,0:T(8,128)(2,1)} %slice.91.refs_7_.right_ref.refs_2_), custom_call_target="tpu_custom_call" | custom-call | flops 1 | bytes 1 | tf_op jit(solution)/shard_map/product/pallas_call | solution.py:1259
  102.6 13.3 %attend.1 = (bf16[2,512,2048]{2,1,0:T(8,128)(2,1)}, bf16[2,512,2048]{2,1,0:T(8,128)(2,1)}, f32[2,1,512]{2,1,0:T(1,128)}) custom-call(s32[9]{0:T(128)} %concatenate.36.refs_10_.table_ref.refs_0_, bf16[2,512,128]{2,1,0:T(8,128)(2,1)} %get-tuple-element.120.q_ref.refs_1_, f32[9,256,256]{2,1,0:T(8,128)} %get-tuple-element.111.refs_6_.bias_ref, ...), custom_call_target="tpu_custom_call" | custom-call | flops 1 | bytes 1 | tf_op jit(solution)/shard_map/attend/pallas_call | solution.py:629
  115.8 12.8 %candidate.1 = (f32[1024,1024]{1,0:T(8,128)}, f32[1024,1024]{1,0:T(8,128)}, bf16[1024,1024]{1,0:T(8,128)(2,1)}) custom-call(bf16[1024,2048]{1,0:T(8,128)(2,1)} %bitcast.176, bf16[2048,1024]{1,0:T(8,128)(2,1)} %refs_9_.1, bf16[1024,4096]{1,0:T(8,128)(2,1)} %product.1.pre_ref.update_ref.refs_5_.refs_6_, ...), custom_call_target="tpu_custom_call" | custom-call | flops 1 | bytes 1 | tf_op jit(solution)/shard_map/candidate/pallas_call | solution.py:950
  129.6 68.4 %feed.1 = (bf16[512,1024]{1,0:T(8,128)(2,1)}, bf16[512,1024]{1,0:T(8,128)(2,1)}, f32[1024,1024]{1,0:T(8,128)}, bf16[4,1024,512]{2,1,0:T(8,128)(2,1)}, bf16[4,102...) custom-call(s32[8]{0:T(128)} %broadcast_select_fusion.1.refs_11_.refs_0_, ...), custom_call_target="tpu_custom_call" | custom-call | flops 1 | bytes 1 | tf_op jit(solution)/shard_map/feed/pallas_call | solution.py:1201
  198.6 6.0 %collective-permute-start.8 = (bf16[512,1024]{1,0:T(8,128)(2,1)}, bf16[512,1024]{1,0:T(8,128)(2,1)}, u32[]{:S(2)}, u32[]{:S(2)}) collective-permute-start(bf16[512,1024]{1,0:T(8,128)(2,1)} %get-tuple-element.129), channel_id=1, source_target_pairs={{1,0},{5,1},{0,2},{4,3},{3,4},{7,5},{2,6},{6,7},{9,8},{13,9},{8,10... | collective-permute-start | bytes 3145736 | tf_op jit(solution)/shard_map/ppermute | solution.py:1589
  204.6 19.9 %gate.1 = (f32[1024,1024]{1,0:T(8,128)}, bf16[1024,4096]{1,0:T(8,128)(2,1)}, bf16[1024,2048]{1,0:T(8,128)(2,1)}, f32[1,1024]{1,0:T(1,128)}) custom-call(f32[1024,1024]{1,0:T(8,128)} %get-tuple-element.131.refs_0_, bf16[512,1024]{1,0:T(8,128)(2,1)} %copy-done.19, bf16[512,1024]{1,0:T(8,128)(2,1)} %collective-permute-done.7.refs_4_.refs_2_, ...), custom_call_target="tpu_custom_call" | custom-call | flops 99999997952 | bytes 1 | tf_op jit(solution)/shard_map/gate/pallas_call | solution.py:1039
  224.5 6.0 %stage_sums.8.refs_4_ = bf16[2,2048,512]{2,1,0:T(8,128)(2,1)} custom-call(bf16[1,4096,512]{2,1,0:T(8,128)(2,1)} %bitcast.156, bf16[1,4096,512]{2,1,0:T(8,128)(2,1)} %collective-permute-done.10.refs_1_, bf16[1,4096,512]{2,1,0:T(8,128)(2,1)} %bitcast.161, bf16[1,4096,512]{2,1,0:T(8,128)(2,1)} %collective-permute-done.11.refs_3_.refs_4_.refs_5_.refs_6_.refs_7_, ...), custom_call_target="tpu_custom_call" | custom-call | flops 1 | bytes 1 | tf_op jit(solution)/shard_map/stage_sums/pallas_call | solution.py:1532
  231.0 15.1 %by_rows.2 = (bf16[4,1,128,4096]{3,2,1,0:T(8,128)(2,1)}, bf16[4,1,128,4096]{3,2,1,0:T(8,128)(2,1)}) custom-call(s32[8]{0:T(128)} %broadcast_select_fusion.1.refs_11_.refs_0_, s32[1]{0:T(128)} %constant.104.clone.1.refs_1_, bf16[1024,1024]{1,0:T(8,128)(2,1)} %bitcast.185, bf16[1024,4096]{1,0:T(8,128)(2,1)} %get-tuple-element.134.refs_3_.refs_2_.refs_0_, ...), custom_call_target="tpu_custom_call" | custom-call | flops 99999997952 | bytes 1 | tf_op jit(solution)/shard_map/by_rows/pallas_call | solution.py:1406
  246.1 11.9 %by_columns.1 = (bf16[4,1024,256]{2,1,0:T(8,128)(2,1)}, bf16[4,1024,256]{2,1,0:T(8,128)(2,1)}) custom-call(s32[8]{0:T(128)} %broadcast_select_fusion.1.refs_11_.refs_0_, s32[4]{0:T(128)} %get-tuple-element.109.refs_12_.refs_1_, bf16[1024,4096]{1,0:T(8,128)(2,1)} %get-tuple-element.134.refs_3_.refs_2_.refs_0_, bf16[1024,2048]{1,0:T(8,128)(2,1)} %bitcast.177, ...), custom_call_target="tpu_custom_call" | custom-call | flops 1 | bytes 1 | tf_op jit(solution)/shard_map/by_columns/pallas_call | solution.py:1350
  259.5 22.0 %attend_back.1 = (f32[2,512,128]{2,1,0:T(8,128)}, bf16[2,512,128]{2,1,0:T(8,128)(2,1)}, bf16[2,512,2048]{2,1,0:T(8,128)(2,1)}, bf16[2,512,2176]{2,1,0:T(8,128)(2,1)}, f32[8,1,512]{2,1,0:T(1,128)}) custom-call(s32[9]{0:T(128)} %concatenate.36.refs_10_.table_ref.refs_0_, bf16[2,512,128]{2,1,0:T(8,128)(2,1)} %get-tuple-element.120.q_ref.refs_1_, ...), custom_call_target="tpu_custom_call" | custom-call | flops 99999997952 | bytes 1 | tf_op jit(solution)/shard_map/attend_back/pallas_call | solution.py:812
  283.4 5.7 %stage_sums.9 = (bf16[2,1024,512]{2,1,0:T(8,128)(2,1)}, bf16[1,2048,256]{2,1,0:T(8,128)(2,1)}) custom-call(bf16[1,4096,512]{2,1,0:T(8,128)(2,1)} %bitcast.157, bf16[1,4096,512]{2,1,0:T(8,128)(2,1)} %collective-permute-done.10.refs_1_, bf16[2,2048,512]{2,1,0:T(8,128)(2,1)} %collective-permute-done.14.refs_2_.refs_5_.refs_6_.refs_7_.refs_8_, ...), custom_call_target="tpu_custom_call" | custom-call | flops 99999997952 | bytes 1 | tf_op jit(solution)/shard_map/stage_sums/pallas_call | solution.py:1532
  289.1 11.7 %collective-permute-start.16 = (bf16[2,1024,512]{2,1,0:T(8,128)(2,1)}, bf16[2,1024,512]{2,1,0:T(8,128)(2,1)}, u32[]{:S(2)}, u32[]{:S(2)}) collective-permute-start(bf16[2,1024,512]{2,1,0:T(8,128)(2,1)} %get-tuple-element.153.refs_7_), channel_id=1, source_target_pairs={{0,16},{1,17},{2,18},{3,19},{4,12},{5,13},{6,14},{7,15},{8,24},{9,... | collective-permute-start | bytes 6291464 | tf_op jit(solution)/shard_map/ppermute | solution.py:1560
  300.9 15.9 %value_back.1 = (f32[1024,1024]{1,0:T(8,128)}, bf16[4,4,128,512]{3,2,1,0:T(8,128)(2,1)}, bf16[4,4,128,512]{3,2,1,0:T(8,128)(2,1)}) custom-call(s32[8]{0:T(128)} %broadcast_select_fusion.1.refs_11_.refs_0_, s32[4]{0:T(128)} %get-tuple-element.109.refs_12_.refs_1_, bf16[1024,1024]{1,0:T(8,128)(2,1)} %bitcast.201, bf16[1024,2048]{1,0:T(8,128)(2,1)} %bitcast.268, ...), custom_call_target="tpu_custom_call" | custom-call | flops 99999997952 | bytes 1 | tf_op jit(solution)/shard_map/value_back/pallas_call | solution.py:1477
  317.0 2.5 fusion.8
  319.5 4.4 by_rows.3
  324.3 4.5 stage_sums.10.refs_5_
  328.7 2.1 collective-permute-start.22
  330.8 17.1 %smooth_back.1 = f32[1024,1024]{1,0:T(8,128)} custom-call(bf16[1024,4096]{1,0:T(8,128)(2,1)} %get-tuple-element.134.refs_3_.refs_2_.refs_0_, bf16[1024,128]{1,0:T(8,128)(2,1)} %get-tuple-element.270.refs_3_.refs_1_, bf16[1024,4096]{1,0:T(8,128)(2,1)} %slice.91.refs_7_.right_ref.refs_2_, bf16[1024,128]{1,0:T(8,128)(2,1)} %slice.92.refs_8_.proj_ref.refs_3_, ...), custom_call_target="tpu_custom_call" | custom-call | flops 99999997952 | bytes 1 | tf_op jit(solution)/shard_map/smooth_back/pallas_call | solution.py:1297
  349.2 5.6 %stage_sums.11 = (bf16[2,512,512]{2,1,0:T(8,128)(2,1)}, bf16[1,1024,512]{2,1,0:T(8,128)(2,1)}, bf16[1,1024,256]{2,1,0:T(8,128)(2,1)}, bf16[1,256,128]{2,1,0:T(8,128)(2,1)}) custom-call(bf16[1,4096,512]{2,1,0:T(8,128)(2,1)} %bitcast.158, bf16[1,4096,512]{2,1,0:T(8,128)(2,1)} %collective-permute-done.10.refs_1_, ...), custom_call_target="tpu_custom_call" | custom-call | flops 1 | bytes 1 | tf_op jit(solution)/shard_map/stage_sums/pallas_call | solution.py:1532
  354.8 2.5 collective-permute-start.21
  357.3 2.0 collective-permute-start.23
  361.3 8.1 %back_ends.1.refs_19_.refs_12_ = f32[2,16,8,128]{3,2,1,0:T(8,128)} custom-call(f32[2,512,1024]{2,1,0:T(8,128)} %bitcast.179, f32[16,8,128]{2,1,0:T(8,128)} %bitcast.209, bf16[2,512,512]{2,1,0:T(8,128)(2,1)} %get-tuple-element.162.refs_2_, bf16[1,1024,512]{2,1,0:T(8,128)(2,1)} %get-tuple-element.163.refs_3_, ...), custom_call_target="tpu_custom_call" | custom-call | flops 1 | bytes 1 | tf_op jit(solution)/shard_map/back_ends/pallas_call | solution.py:322
  371.1 2.0 collective-permute-done.24.refs_18_.refs_26_
  373.0 7.8 %collective-permute-done.21.refs_4_.refs_9_.refs_10_ = bf16[2,512,512]{2,1,0:T(8,128)(2,1)S(1)} collective-permute-done((bf16[2,512,512]{2,1,0:T(8,128)(2,1)}, bf16[2,512,512]{2,1,0:T(8,128)(2,1)S(1)}, u32[]{:S(2)}, u32[]{:S(2)}) %collective-permute-start.21) | collective-permute-done | bytes 1048608 | tf_op jit(solution)/shard_map/ppermute | solution.py:1560
  382.9 5.3 %stage_sums.12 = (bf16[2,256,512]{2,1,0:T(8,128)(2,1)}, bf16[1,128,4096]{2,1,0:T(8,128)(2,1)}, bf16[1,512,512]{2,1,0:T(8,128)(2,1)}, bf16[1,128,128]{2,1,0:T(8,128)(2,1)}) custom-call(bf16[1,4096,512]{2,1,0:T(8,128)(2,1)} %bitcast.159, bf16[1,4096,512]{2,1,0:T(8,128)(2,1)} %collective-permute-done.10.refs_1_, ...), custom_call_target="tpu_custom_call" | custom-call | flops 1 | bytes 1 | tf_op jit(solution)/shard_map/stage_sums/pallas_call | solution.py:1532
  391.7 20.2 %back_scan.2 = (bf16[512,1024]{1,0:T(8,128)(2,1)}, f32[16,8,128]{2,1,0:T(8,128)}, f32[16,8,128]{2,1,0:T(8,128)}, f32[1,1024]{1,0:T(1,128)}, f32[1,1024]{1,0:T(1,128)}) custom-call(s32[9]{0:T(128)} %concatenate.36.refs_10_.table_ref.refs_0_, s32[1]{0:T(128)} %constant.104.clone.1.refs_1_, bf16[2,512,1024]{2,1,0:T(8,128)(2,1)} %get-tuple-element.117.x_ref.refs_2_, ...), custom_call_target="tpu_custom_call" | custom-call | flops 99999997952 | bytes 1 | tf_op jit(solution)/shard_map/back_scan/pallas_call | solution.py:468
  416.0 6.0 %stage_sums.13 = (f32[2,256,512]{2,1,0:T(8,128)}, bf16[1,128,4096]{2,1,0:T(8,128)(2,1)}, bf16[1,256,512]{2,1,0:T(8,128)(2,1)}, bf16[1,512,256]{2,1,0:T(8,128)(2,1)}, bf16[1,128,128]{2,1,0:T(8,128)(2,1)}) custom-call(bf16[1,4096,512]{2,1,0:T(8,128)(2,1)} %bitcast.160, bf16[1,4096,512]{2,1,0:T(8,128)(2,1)} %collective-permute-done.10.refs_1_, ...), custom_call_target="tpu_custom_call" | custom-call | flops 1 | bytes 1 | tf_op jit(solution)/shard_map/stage_sums/pallas_call | solution.py:1532
  426.0 2.1 collective-permute-start.32
  428.2 1.9 collective-permute-start.34
  430.2 20.4 %back_scan.3 = (bf16[512,1024]{1,0:T(8,128)(2,1)}, f32[16,8,128]{2,1,0:T(8,128)}, f32[16,8,128]{2,1,0:T(8,128)}, f32[1,1024]{1,0:T(1,128)}, f32[1,1024]{1,0:T(1,128)}) custom-call(s32[9]{0:T(128)} %concatenate.36.refs_10_.table_ref.refs_0_, s32[1]{0:T(128)} %constant.103.clone.1.refs_1_, bf16[2,512,1024]{2,1,0:T(8,128)(2,1)} %get-tuple-element.117.x_ref.refs_2_, ...), custom_call_target="tpu_custom_call" | custom-call | flops 99999997952 | bytes 1 | tf_op jit(solution)/shard_map/back_scan/pallas_call | solution.py:468
  454.8 3.2 collective-permute-done.34.refs_11_.refs_13_
  458.7 3.5 stage_sums.14
  465.6 5.0 collective-permute-start.38
  473.2 2.9 collective-permute-start.40
  480.2 15.3 %collective-permute-done.39.refs_8_ = bf16[1,256,256]{2,1,0:T(8,128)(2,1)S(1)} collective-permute-done((bf16[1,256,256]{2,1,0:T(8,128)(2,1)S(1)}, bf16[1,256,256]{2,1,0:T(8,128)(2,1)S(1)}, u32[]{:S(2)}, u32[]{:S(2)}) %collective-permute-start.39) | collective-permute-done | bytes 131104 | tf_op jit(solution)/shard_map/ppermute | solution.py:1560
  495.5 2.8 collective-permute-done.40.refs_14_
  500.1 3.7 stage_sums.15
  508.2 3.4 collective-permute-start.42
  513.0 2.3 maximum_convert_fusion
  (265 shorter events, 69.3 us)
Async XLA Ops:
  1.3 23.2 %collective-permute-start = (f32[2]{0:T(128)S(1)}, f32[2]{0:T(128)S(1)}, u32[]{:S(2)}, u32[]{:S(2)}) collective-permute-start(f32[2]{0:T(128)S(1)} %convert_element_type.33), channel_id=1, source_target_pairs={{0,4},{1,5},{2,6},{3,7},{4,0},{5,1},{6,2},{7,3},{8,12},{9,13},{10,... | collective-permute-start | bytes 32 | tf_op jit(solution)/shard_map/ppermute | solution.py:1560
  4.9 27.6 %collective-permute-start.2 = (bf16[512,1024]{1,0:T(8,128)(2,1)}, bf16[512,1024]{1,0:T(8,128)(2,1)}, u32[]{:S(2)}, u32[]{:S(2)}) collective-permute-start(bf16[512,1024]{1,0:T(8,128)(2,1)} %get-tuple-element.277), channel_id=1, source_target_pairs={{0,4},{1,0},{2,5},{3,1},{4,6},{5,2},{6,7},{7,3},{8,12},{9,8},{10,1... | collective-permute-start | bytes 3145736 | tf_op jit(solution)/shard_map/ppermute | solution.py:1560
  4.9 50.8 %collective-permute-start.1 = (bf16[512,1024]{1,0:T(8,128)(2,1)}, bf16[512,1024]{1,0:T(8,128)(2,1)S(1)}, u32[]{:S(2)}, u32[]{:S(2)}) collective-permute-start(bf16[512,1024]{1,0:T(8,128)(2,1)} %get-tuple-element.278), channel_id=1, source_target_pairs={{0,1},{1,5},{2,0},{3,4},{4,3},{5,7},{6,2},{7,6},{8,9},{9,13},{10,8... | collective-permute-start | bytes 3145736 | tf_op jit(solution)/shard_map/ppermute | solution.py:1560
  66.9 1.6 collective-permute-start.3
  66.9 35.0 %collective-permute-start.5 = (bf16[2,512,2048]{2,1,0:T(8,128)(2,1)}, bf16[2,512,2048]{2,1,0:T(8,128)(2,1)}, u32[]{:S(2)}, u32[]{:S(2)}) collective-permute-start(bf16[2,512,2048]{2,1,0:T(8,128)(2,1)} %get-tuple-element.123.v_own.refs_7_), channel_id=1, source_target_pairs={{0,4},{1,5},{2,6},{3,7},{4,0},{5,1},{6,2},{7,3},{8,12},{9,13},{10,... | collective-permute-start | bytes 12582920 | tf_op jit(solution)/shard_map/ppermute | solution.py:1560
  68.5 60.2 %collective-permute-start.6 = (bf16[512,1024]{1,0:T(8,128)(2,1)S(1)}, bf16[512,1024]{1,0:T(8,128)(2,1)S(1)}, u32[]{:S(2)}, u32[]{:S(2)}) collective-permute-start(bf16[512,1024]{1,0:T(8,128)(2,1)S(1)} %copy-done.6), channel_id=1, source_target_pairs={{0,4},{1,0},{2,5},{3,1},{4,6},{5,2},{6,7},{7,3},{8,12},{9,8},{10,1... | collective-permute-start | bytes 3145736 | tf_op jit(solution)/shard_map/ppermute | solution.py:1560
  68.6 60.0 %collective-permute-start.7 = (bf16[512,1024]{1,0:T(8,128)(2,1)S(1)}, bf16[512,1024]{1,0:T(8,128)(2,1)}, u32[]{:S(2)}, u32[]{:S(2)}) collective-permute-start(bf16[512,1024]{1,0:T(8,128)(2,1)S(1)} %copy-done.5), channel_id=1, source_target_pairs={{0,1},{1,5},{2,0},{3,4},{4,3},{5,7},{6,2},{7,6},{8,9},{9,13},{10,8... | collective-permute-start | bytes 3145736 | tf_op jit(solution)/shard_map/ppermute | solution.py:1560
  88.3 13.6 %collective-permute-start.4 = (bf16[2,512,128]{2,1,0:T(8,128)(2,1)}, bf16[2,512,128]{2,1,0:T(8,128)(2,1)S(1)}, u32[]{:S(2)}, u32[]{:S(2)}) collective-permute-start(bf16[2,512,128]{2,1,0:T(8,128)(2,1)} %get-tuple-element.122.k_own.refs_5_), channel_id=1, source_target_pairs={{0,4},{1,5},{2,6},{3,7},{4,0},{5,1},{6,2},{7,3},{8,12},{9,13},{10,... | collective-permute-start | bytes 786440 | tf_op jit(solution)/shard_map/ppermute | solution.py:1560
  198.0 26.5 %collective-permute-start.10 = (bf16[1,4096,512]{2,1,0:T(8,128)(2,1)}, bf16[1,4096,512]{2,1,0:T(8,128)(2,1)}, u32[]{:S(2)}, u32[]{:S(2)}) collective-permute-start(bf16[1,4096,512]{2,1,0:T(8,128)(2,1)} %bitcast.255), channel_id=1, source_target_pairs={{0,4},{1,5},{2,6},{3,7},{4,0},{5,1},{6,2},{7,3},{8,12},{9,13},{10,... | collective-permute-start | bytes 12582920 | tf_op jit(solution)/shard_map/ppermute | solution.py:1560
  198.5 26.0 %collective-permute-start.11 = (bf16[1,4096,512]{2,1,0:T(8,128)(2,1)}, bf16[1,4096,512]{2,1,0:T(8,128)(2,1)}, u32[]{:S(2)}, u32[]{:S(2)}) collective-permute-start(bf16[1,4096,512]{2,1,0:T(8,128)(2,1)} %bitcast.254), channel_id=1, source_target_pairs={{0,4},{1,5},{2,6},{3,7},{4,0},{5,1},{6,2},{7,3},{8,12},{9,13},{10,... | collective-permute-start | bytes 12582920 | tf_op jit(solution)/shard_map/ppermute | solution.py:1560
  198.6 60.9 %collective-permute-start.8 = (bf16[512,1024]{1,0:T(8,128)(2,1)}, bf16[512,1024]{1,0:T(8,128)(2,1)}, u32[]{:S(2)}, u32[]{:S(2)}) collective-permute-start(bf16[512,1024]{1,0:T(8,128)(2,1)} %get-tuple-element.129), channel_id=1, source_target_pairs={{1,0},{5,1},{0,2},{4,3},{3,4},{7,5},{2,6},{6,7},{9,8},{13,9},{8,10... | collective-permute-start | bytes 3145736 | tf_op jit(solution)/shard_map/ppermute | solution.py:1589
  204.6 54.9 %collective-permute-start.9 = (bf16[512,1024]{1,0:T(8,128)(2,1)}, bf16[512,1024]{1,0:T(8,128)(2,1)}, u32[]{:S(2)}, u32[]{:S(2)}) collective-permute-start(bf16[512,1024]{1,0:T(8,128)(2,1)} %get-tuple-element.130), channel_id=1, source_target_pairs={{4,0},{0,1},{5,2},{1,3},{6,4},{2,5},{7,6},{3,7},{12,8},{8,9},{13,1... | collective-permute-start | bytes 3145736 | tf_op jit(solution)/shard_map/ppermute | solution.py:1589
  230.5 51.5 %collective-permute-start.14 = (bf16[2,2048,512]{2,1,0:T(8,128)(2,1)}, bf16[2,2048,512]{2,1,0:T(8,128)(2,1)}, u32[]{:S(2)}, u32[]{:S(2)}) collective-permute-start(bf16[2,2048,512]{2,1,0:T(8,128)(2,1)} %stage_sums.8.refs_4_), channel_id=1, source_target_pairs={{0,8},{1,9},{2,10},{3,11},{4,20},{5,21},{6,22},{7,23},{8,0},{9,1},... | collective-permute-start | bytes 12582920 | tf_op jit(solution)/shard_map/ppermute | solution.py:1560
  258.0 24.1 %collective-permute-start.15 = (bf16[1,4096,256]{2,1,0:T(8,128)(2,1)}, bf16[1,4096,256]{2,1,0:T(8,128)(2,1)S(1)}, u32[]{:S(2)}, u32[]{:S(2)}) collective-permute-start(bf16[1,4096,256]{2,1,0:T(8,128)(2,1)} %bitcast.257), channel_id=1, source_target_pairs={{0,4},{1,5},{2,6},{3,7},{4,0},{5,1},{6,2},{7,3},{8,12},{9,13},{10,... | collective-permute-start | bytes 6291464 | tf_op jit(solution)/shard_map/ppermute | solution.py:1560
  281.5 19.4 %collective-permute-start.12 = (bf16[2,512,2176]{2,1,0:T(8,128)(2,1)}, bf16[2,512,2176]{2,1,0:T(8,128)(2,1)}, u32[]{:S(2)}, u32[]{:S(2)}) collective-permute-start(bf16[2,512,2176]{2,1,0:T(8,128)(2,1)} %get-tuple-element.146), channel_id=1, source_target_pairs={{0,4},{1,5},{2,6},{3,7},{4,0},{5,1},{6,2},{7,3},{8,12},{9,13},{10,... | collective-permute-start | bytes 13369352 | tf_op jit(solution)/shard_map/ppermute | solution.py:1560
  281.6 42.7 %collective-permute-start.13 = (bf16[1,512,4096]{2,1,0:T(8,128)(2,1)}, bf16[1,512,4096]{2,1,0:T(8,128)(2,1)}, u32[]{:S(2)}, u32[]{:S(2)}) collective-permute-start(bf16[1,512,4096]{2,1,0:T(8,128)(2,1)} %bitcast.194), channel_id=1, source_target_pairs={{0,4},{1,5},{2,6},{3,7},{4,0},{5,1},{6,2},{7,3},{8,12},{9,13},{10,... | collective-permute-start | bytes 12582920 | tf_op jit(solution)/shard_map/ppermute | solution.py:1560
  289.1 58.8 %collective-permute-start.16 = (bf16[2,1024,512]{2,1,0:T(8,128)(2,1)}, bf16[2,1024,512]{2,1,0:T(8,128)(2,1)}, u32[]{:S(2)}, u32[]{:S(2)}) collective-permute-start(bf16[2,1024,512]{2,1,0:T(8,128)(2,1)} %get-tuple-element.153.refs_7_), channel_id=1, source_target_pairs={{0,16},{1,17},{2,18},{3,19},{4,12},{5,13},{6,14},{7,15},{8,24},{9,... | collective-permute-start | bytes 6291464 | tf_op jit(solution)/shard_map/ppermute | solution.py:1560
  300.8 47.0 %collective-permute-start.18 = (bf16[1,2048,256]{2,1,0:T(8,128)(2,1)}, bf16[1,2048,256]{2,1,0:T(8,128)(2,1)}, u32[]{:S(2)}, u32[]{:S(2)}) collective-permute-start(bf16[1,2048,256]{2,1,0:T(8,128)(2,1)} %get-tuple-element.154.refs_8_), channel_id=1, source_target_pairs={{0,8},{1,9},{2,10},{3,11},{4,20},{5,21},{6,22},{7,23},{8,0},{9,1},... | collective-permute-start | bytes 3145736 | tf_op jit(solution)/shard_map/ppermute | solution.py:1560
  316.8 31.1 %collective-permute-start.17 = (bf16[1,2048,512]{2,1,0:T(8,128)(2,1)}, bf16[1,2048,512]{2,1,0:T(8,128)(2,1)S(1)}, u32[]{:S(2)}, u32[]{:S(2)}) collective-permute-start(bf16[1,2048,512]{2,1,0:T(8,128)(2,1)} %bitcast.256), channel_id=1, source_target_pairs={{0,4},{1,5},{2,6},{3,7},{4,0},{5,1},{6,2},{7,3},{8,12},{9,13},{10,... | collective-permute-start | bytes 6291464 | tf_op jit(solution)/shard_map/ppermute | solution.py:1560
  324.0 23.9 %collective-permute-start.19 = (bf16[1,512,128]{2,1,0:T(8,128)(2,1)}, bf16[1,512,128]{2,1,0:T(8,128)(2,1)S(1)}, u32[]{:S(2)}, u32[]{:S(2)}) collective-permute-start(bf16[1,512,128]{2,1,0:T(8,128)(2,1)} %bitcast.222), channel_id=1, source_target_pairs={{0,4},{1,5},{2,6},{3,7},{4,0},{5,1},{6,2},{7,3},{8,12},{9,13},{10,... | collective-permute-start | bytes 393224 | tf_op jit(solution)/shard_map/ppermute | solution.py:1560
  328.7 41.4 %collective-permute-start.22 = (bf16[1,256,4096]{2,1,0:T(8,128)(2,1)}, bf16[1,256,4096]{2,1,0:T(8,128)(2,1)}, u32[]{:S(2)}, u32[]{:S(2)}) collective-permute-start(bf16[1,256,4096]{2,1,0:T(8,128)(2,1)} %stage_sums.10.refs_5_), channel_id=1, source_target_pairs={{0,8},{1,9},{2,10},{3,11},{4,20},{5,21},{6,22},{7,23},{8,0},{9,1},... | collective-permute-start | bytes 6291464 | tf_op jit(solution)/shard_map/ppermute | solution.py:1560
  354.8 26.1 %collective-permute-start.21 = (bf16[2,512,512]{2,1,0:T(8,128)(2,1)}, bf16[2,512,512]{2,1,0:T(8,128)(2,1)S(1)}, u32[]{:S(2)}, u32[]{:S(2)}) collective-permute-start(bf16[2,512,512]{2,1,0:T(8,128)(2,1)} %get-tuple-element.162.refs_2_), channel_id=1, source_target_pairs={{0,1},{1,0},{2,3},{3,2},{4,5},{5,4},{6,7},{7,6},{8,9},{9,8},{10,11... | collective-permute-start | bytes 3145736 | tf_op jit(solution)/shard_map/ppermute | solution.py:1560
  357.3 23.6 %collective-permute-start.23 = (bf16[1,1024,512]{2,1,0:T(8,128)(2,1)}, bf16[1,1024,512]{2,1,0:T(8,128)(2,1)S(1)}, u32[]{:S(2)}, u32[]{:S(2)}) collective-permute-start(bf16[1,1024,512]{2,1,0:T(8,128)(2,1)} %get-tuple-element.163.refs_3_), channel_id=1, source_target_pairs={{0,8},{1,9},{2,10},{3,11},{4,20},{5,21},{6,22},{7,23},{8,0},{9,1},... | collective-permute-start | bytes 3145736 | tf_op jit(solution)/shard_map/ppermute | solution.py:1560
  361.1 11.9 %collective-permute-start.24 = (bf16[1,256,128]{2,1,0:T(8,128)(2,1)}, bf16[1,256,128]{2,1,0:T(8,128)(2,1)S(1)}, u32[]{:S(2)}, u32[]{:S(2)}) collective-permute-start(bf16[1,256,128]{2,1,0:T(8,128)(2,1)} %get-tuple-element.165.refs_5_), channel_id=1, source_target_pairs={{0,8},{1,9},{2,10},{3,11},{4,20},{5,21},{6,22},{7,23},{8,0},{9,1},... | collective-permute-start | bytes 196616 | tf_op jit(solution)/shard_map/ppermute | solution.py:1560
  369.4 21.9 %collective-permute-start.20 = (f32[2,16,8,128]{3,2,1,0:T(8,128)}, f32[2,16,8,128]{3,2,1,0:T(8,128)}, u32[]{:S(2)}, u32[]{:S(2)}) collective-permute-start(f32[2,16,8,128]{3,2,1,0:T(8,128)} %back_ends.1.refs_19_.refs_12_), channel_id=1, source_target_pairs={{0,4},{1,5},{2,6},{3,7},{4,0},{5,1},{6,2},{7,3},{8,12},{9,13},{10,... | collective-permute-start | bytes 393224 | tf_op jit(solution)/shard_map/ppermute | solution.py:1560
  370.2 41.7 %collective-permute-start.28 = (bf16[1,1024,256]{2,1,0:T(8,128)(2,1)}, bf16[1,1024,256]{2,1,0:T(8,128)(2,1)S(1)}, u32[]{:S(2)}, u32[]{:S(2)}) collective-permute-start(bf16[1,1024,256]{2,1,0:T(8,128)(2,1)} %get-tuple-element.164.refs_4_), channel_id=1, source_target_pairs={{0,16},{1,17},{2,18},{3,19},{4,12},{5,13},{6,14},{7,15},{8,24},{9,... | collective-permute-start | bytes 1572872 | tf_op jit(solution)/shard_map/ppermute | solution.py:1560
  388.1 25.8 %collective-permute-start.26 = (bf16[1,128,4096]{2,1,0:T(8,128)(2,1)}, bf16[1,128,4096]{2,1,0:T(8,128)(2,1)S(1)}, u32[]{:S(2)}, u32[]{:S(2)}) collective-permute-start(bf16[1,128,4096]{2,1,0:T(8,128)(2,1)} %get-tuple-element.167.refs_15_), channel_id=1, source_target_pairs={{0,16},{1,17},{2,18},{3,19},{4,12},{5,13},{6,14},{7,15},{8,24},{9,... | collective-permute-start | bytes 3145736 | tf_op jit(solution)/shard_map/ppermute | solution.py:1560
  388.4 25.5 %collective-permute-start.25 = (bf16[2,256,512]{2,1,0:T(8,128)(2,1)}, bf16[2,256,512]{2,1,0:T(8,128)(2,1)S(1)}, u32[]{:S(2)}, u32[]{:S(2)}) collective-permute-start(bf16[2,256,512]{2,1,0:T(8,128)(2,1)} %get-tuple-element.166.refs_14_), channel_id=1, source_target_pairs={{0,2},{1,3},{2,0},{3,1},{4,6},{5,7},{6,4},{7,5},{8,10},{9,11},{10,... | collective-permute-start | bytes 1572872 | tf_op jit(solution)/shard_map/ppermute | solution.py:1560
  389.6 24.3 %collective-permute-start.27 = (bf16[1,512,512]{2,1,0:T(8,128)(2,1)}, bf16[1,512,512]{2,1,0:T(8,128)(2,1)S(1)}, u32[]{:S(2)}, u32[]{:S(2)}) collective-permute-start(bf16[1,512,512]{2,1,0:T(8,128)(2,1)} %get-tuple-element.168.refs_16_), channel_id=1, source_target_pairs={{0,16},{1,17},{2,18},{3,19},{4,12},{5,13},{6,14},{7,15},{8,24},{9,... | collective-permute-start | bytes 1572872 | tf_op jit(solution)/shard_map/ppermute | solution.py:1560
  391.3 21.8 %collective-permute-start.29 = (bf16[1,128,128]{2,1,0:T(8,128)(2,1)}, bf16[1,128,128]{2,1,0:T(8,128)(2,1)S(1)}, u32[]{:S(2)}, u32[]{:S(2)}) collective-permute-start(bf16[1,128,128]{2,1,0:T(8,128)(2,1)} %get-tuple-element.169.refs_17_), channel_id=1, source_target_pairs={{0,16},{1,17},{2,18},{3,19},{4,12},{5,13},{6,14},{7,15},{8,24},{9,... | collective-permute-start | bytes 98312 | tf_op jit(solution)/shard_map/ppermute | solution.py:1560
  411.9 42.9 %collective-permute-start.31 = (bf16[512,1024]{1,0:T(8,128)(2,1)}, bf16[512,1024]{1,0:T(8,128)(2,1)}, u32[]{:S(2)}, u32[]{:S(2)}) collective-permute-start(bf16[512,1024]{1,0:T(8,128)(2,1)} %get-tuple-element.170.refs_28_), channel_id=1, source_target_pairs={{4,0},{0,1},{5,2},{1,3},{6,4},{2,5},{7,6},{3,7},{12,8},{8,9},{13,1... | collective-permute-start | bytes 3145736 | tf_op jit(solution)/shard_map/ppermute | solution.py:1589
  426.0 27.7 %collective-permute-start.32 = (bf16[1,256,1056]{1,2,0:T(8,128)(2,1)S(1)}, bf16[1,256,1056]{1,2,0:T(8,128)(2,1)S(1)}, u32[]{:S(2)}, u32[]{:S(2)}) collective-permute-start(bf16[1,256,1056]{1,2,0:T(8,128)(2,1)S(1)} %copy.66), channel_id=1, source_target_pairs={{0,1},{1,0},{2,3},{3,2},{4,5},{5,4},{6,7},{7,6},{8,9},{9,8},{10,11... | collective-permute-start | bytes 1622024 | tf_op jit(solution)/shard_map/ppermute | solution.py:1560
  428.1 26.7 %collective-permute-start.33 = (bf16[1,512,256]{2,1,0:T(8,128)(2,1)}, bf16[1,512,256]{2,1,0:T(8,128)(2,1)S(1)}, u32[]{:S(2)}, u32[]{:S(2)}) collective-permute-start(bf16[1,512,256]{2,1,0:T(8,128)(2,1)} %get-tuple-element.174.refs_17_), channel_id=1, source_target_pairs={{0,1},{1,0},{2,3},{3,2},{4,5},{5,4},{6,7},{7,6},{8,9},{9,8},{10,11... | collective-permute-start | bytes 786440 | tf_op jit(solution)/shard_map/ppermute | solution.py:1560
  428.2 29.8 %collective-permute-start.34 = (bf16[1,256,512]{2,1,0:T(8,128)(2,1)S(1)}, bf16[1,256,512]{2,1,0:T(8,128)(2,1)S(1)}, u32[]{:S(2)}, u32[]{:S(2)}) collective-permute-start(bf16[1,256,512]{2,1,0:T(8,128)(2,1)S(1)} %copy-done.63), channel_id=1, source_target_pairs={{0,1},{1,0},{2,3},{3,2},{4,5},{5,4},{6,7},{7,6},{8,9},{9,8},{10,11... | collective-permute-start | bytes 786440 | tf_op jit(solution)/shard_map/ppermute | solution.py:1560
  430.1 22.5 %copy-start.44 = (f32[32,128]{1,0:T(8,128)S(1)}, f32[32,128]{1,0:T(8,128)}, u32[]{:S(2)}) copy-start(f32[32,128]{1,0:T(8,128)} %pad_bitcast_fusion) | copy-start | bytes 49156
  430.2 22.5 %copy-start.48 = (f32[1,1024]{1,0:T(1,128)S(1)}, f32[1,1024]{1,0:T(1,128)}, u32[]{:S(2)}) copy-start(f32[1,1024]{1,0:T(1,128)} %get-tuple-element.185) | copy-start | bytes 12292
  430.2 22.5 %copy-start.53 = (f32[128]{0:T(128)S(1)}, f32[128]{0:T(128)}, u32[]{:S(2)}) copy-start(f32[128]{0:T(128)} %get-tuple-element.269) | copy-start | bytes 1540
  450.6 47.8 %collective-permute-start.30 = (bf16[512,1024]{1,0:T(8,128)(2,1)}, bf16[512,1024]{1,0:T(8,128)(2,1)S(1)}, u32[]{:S(2)}, u32[]{:S(2)}) collective-permute-start(bf16[512,1024]{1,0:T(8,128)(2,1)} %get-tuple-element.176.refs_12_), channel_id=1, source_target_pairs={{1,0},{5,1},{0,2},{4,3},{3,4},{7,5},{2,6},{6,7},{9,8},{13,9},{8,10... | collective-permute-start | bytes 3145736 | tf_op jit(solution)/shard_map/ppermute | solution.py:1589
  463.9 6.8 %collective-permute-start.35 = (f32[320,128]{1,0:T(8,128)}, f32[320,128]{1,0:T(8,128)S(1)}, u32[]{:S(2)}, u32[]{:S(2)}) collective-permute-start(f32[320,128]{1,0:T(8,128)} %pack.1), channel_id=1, source_target_pairs={{0,4},{1,5},{2,6},{3,7},{4,0},{5,1},{6,2},{7,3},{8,12},{9,13},{10,... | collective-permute-start | bytes 491528 | tf_op jit(solution)/shard_map/ppermute | solution.py:1560
  465.6 32.7 %collective-permute-start.38 = (bf16[1,128,1056]{2,1,0:T(8,128)(2,1)S(1)}, bf16[1,128,1056]{2,1,0:T(8,128)(2,1)S(1)}, u32[]{:S(2)}, u32[]{:S(2)}) collective-permute-start(bf16[1,128,1056]{2,1,0:T(8,128)(2,1)S(1)} %copy-done.17), channel_id=1, source_target_pairs={{0,2},{1,3},{2,0},{3,1},{4,6},{5,7},{6,4},{7,5},{8,10},{9,11},{10,... | collective-permute-start | bytes 811016 | tf_op jit(solution)/shard_map/ppermute | solution.py:1560
  470.7 6.4 %collective-permute-start.36 = (f32[320,128]{1,0:T(8,128)S(1)}, f32[320,128]{1,0:T(8,128)S(1)}, u32[]{:S(2)}, u32[]{:S(2)}) collective-permute-start(f32[320,128]{1,0:T(8,128)S(1)} %add.92), channel_id=1, source_target_pairs={{0,8},{1,9},{2,10},{3,11},{4,12},{5,13},{6,14},{7,15},{8,0},{9,1},... | collective-permute-start | bytes 491528 | tf_op jit(solution)/shard_map/ppermute | solution.py:1560
  473.1 22.4 %collective-permute-start.39 = (bf16[1,256,256]{2,1,0:T(8,128)(2,1)S(1)}, bf16[1,256,256]{2,1,0:T(8,128)(2,1)S(1)}, u32[]{:S(2)}, u32[]{:S(2)}) collective-permute-start(bf16[1,256,256]{2,1,0:T(8,128)(2,1)S(1)} %copy-done.27), channel_id=1, source_target_pairs={{0,2},{1,3},{2,0},{3,1},{4,6},{5,7},{6,4},{7,5},{8,10},{9,11},{10,... | collective-permute-start | bytes 393224 | tf_op jit(solution)/shard_map/ppermute | solution.py:1560
  473.2 25.1 %collective-permute-start.40 = (bf16[1,128,512]{2,1,0:T(8,128)(2,1)S(1)}, bf16[1,128,512]{2,1,0:T(8,128)(2,1)S(1)}, u32[]{:S(2)}, u32[]{:S(2)}) collective-permute-start(bf16[1,128,512]{2,1,0:T(8,128)(2,1)S(1)} %copy-done.28), channel_id=1, source_target_pairs={{0,2},{1,3},{2,0},{3,1},{4,6},{5,7},{6,4},{7,5},{8,10},{9,11},{10,... | collective-permute-start | bytes 393224 | tf_op jit(solution)/shard_map/ppermute | solution.py:1560
  477.0 26.8 %copy-start.25 = (f32[320,128]{1,0:T(8,128)}, f32[320,128]{1,0:T(8,128)S(1)}, u32[]{:S(2)}) copy-start(f32[320,128]{1,0:T(8,128)S(1)} %add.93.refs_0_) | copy-start | bytes 491524
  477.1 26.8 %collective-permute-start.37 = (f32[320,128]{1,0:T(8,128)S(1)}, f32[320,128]{1,0:T(8,128)S(1)}, u32[]{:S(2)}, u32[]{:S(2)}) collective-permute-start(f32[320,128]{1,0:T(8,128)S(1)} %add.93.refs_0_), channel_id=1, source_target_pairs={{0,16},{1,17},{2,18},{3,19},{4,20},{5,21},{6,22},{7,23},{8,24},{9,... | collective-permute-start | bytes 491528 | tf_op jit(solution)/shard_map/ppermute | solution.py:1560
  507.1 10.0 %collective-permute-start.41 = (bf16[320,128]{1,0:T(8,128)(2,1)S(1)}, bf16[320,128]{1,0:T(8,128)(2,1)S(1)}, u32[]{:S(2)}, u32[]{:S(2)}) collective-permute-start(bf16[320,128]{1,0:T(8,128)(2,1)S(1)} %convert_element_type.41), channel_id=1, source_target_pairs={{0,1},{1,0},{2,3},{3,2},{4,5},{5,4},{6,7},{7,6},{8,9},{9,8},{10,11... | collective-permute-start | bytes 245768 | tf_op jit(solution)/shard_map/ppermute | solution.py:1560
  508.2 10.0 %collective-permute-start.42 = (bf16[320,128]{1,0:T(8,128)(2,1)S(1)}, bf16[320,128]{1,0:T(8,128)(2,1)S(1)}, u32[]{:S(2)}, u32[]{:S(2)}) collective-permute-start(bf16[320,128]{1,0:T(8,128)(2,1)S(1)} %convert_element_type.41), channel_id=1, source_target_pairs={{0,2},{1,3},{2,0},{3,1},{4,6},{5,7},{6,4},{7,5},{8,10},{9,11},{10,... | collective-permute-start | bytes 245768 | tf_op jit(solution)/shard_map/ppermute | solution.py:1560
  511.6 6.6 %collective-permute-start.43 = (bf16[320,128]{1,0:T(8,128)(2,1)S(1)}, bf16[320,128]{1,0:T(8,128)(2,1)S(1)}, u32[]{:S(2)}, u32[]{:S(2)}) collective-permute-start(bf16[320,128]{1,0:T(8,128)(2,1)S(1)} %convert_element_type.41), channel_id=1, source_target_pairs={{0,3},{1,2},{2,1},{3,0},{4,7},{5,6},{6,5},{7,4},{8,11},{9,10},{10,... | collective-permute-start | bytes 245768 | tf_op jit(solution)/shard_map/ppermute | solution.py:1560
  (61 other events, 461.8 us)

commit v9 on v8

--- a/solution.py
+++ b/solution.py
@@ -1510,7 +1510,7 @@
             out[g] = total.astype(out.dtype)
 
 
-def stage_sums(jobs, after=(), steps=4, cost=BRIEF):
+def stage_sums(jobs, after=(), steps=2, cost=BRIEF):
     for _, rows, _ in jobs:
         while rows % (16 * steps) and steps > 1:
             steps //= 2

time: 529 us -> 523 us (0.989)
  starting transfers between devices: 59.3 us -> 46.8 us
  Pallas kernels: 351 us -> 361 us
    pallas_call x1, Pallas kernels: 22 us -> 32.9 us  [attend_back(): pl.pallas_call(ignoring(functools.partial(attend_back_body, total=total),...]
    ppermute x40, starting transfers between devices: 51.4 us -> 42.8 us  [send(): return lax.ppermute(value, AXES, self.pairs(move))]
    pallas_call x8, Pallas kernels: 40.2 us -> 33.7 us  [stage_sums(): pl.pallas_call(ignoring(functools.partial(stage_body, jobs=counts), len(i...]
  transfers between devices with their start and end apart: 44 -> 44, of which waited for: 10 -> 9; matrix products, arithmetic and copies ran while one was open for 9% -> 9% of each run, Pallas kernels for 52% -> 54%
where the time goes in v9:
time: 523 us; the launch traced here: 517 us
  Pallas kernels  361 us (69%)
  starting transfers between devices  46.8 us (9%)
  waiting for transfers between devices  45.1 us (9%)
  local copies, waits for them, and re-layouts  43.9 us (8%)
  other arithmetic  17.6 us (3%)
    pallas_call x1, Pallas kernels, feed(): pl.pallas_call(ignoring(feed_body, 8, len(after)), grid_spec=pltpu.Prefet...  68.3 us
    ppermute x40, waiting for transfers between devices, send(): return lax.ppermute(value, AXES, self.pairs(move))  45.1 us
    ppermute x40, starting transfers between devices, send(): return lax.ppermute(value, AXES, self.pairs(move))  42.8 us
    pallas_call x2, Pallas kernels, back_scan(): pl.pallas_call(ignoring(back_scan_body, 14, len(after)), grid_spec=pltpu....  40.6 us
    pallas_call x8, Pallas kernels, stage_sums(): pl.pallas_call(ignoring(functools.partial(stage_body, jobs=counts), len(i...  33.7 us
    pallas_call x1, Pallas kernels, attend_back(): pl.pallas_call(ignoring(functools.partial(attend_back_body, total=total),...  32.9 us
    pallas_call x2, Pallas kernels, front(): pl.pallas_call(ignoring(functools.partial(front_body, fresh=row == 0), 5,...  20.2 us
    pallas_call x2, Pallas kernels, by_rows(): pl.pallas_call(ignoring(by_rows_body, 4, len(after)), grid_spec=pltpu.Pre...  19.9 us
  transfers between devices with their start and end apart: 44, of which 9 were waited for; matrix products, arithmetic and copies ran while one was open for 9% of the time, Pallas kernels for 54%

profile of v9, /device:TPU:0, one launch (start us, length us, event | category | flops | bytes accessed | tf_op | source)
XLA Modules:
  0.0 516.9 jit_solution(6151634509788582259)
XLA Ops:
  1.8 3.1 dynamic-slice_bitcast_fusion.2
  4.9 2.5 collective-permute-start.1
  7.6 8.0 %slice.91.refs_7_.right_ref.refs_2_ = bf16[1024,4096]{1,0:T(8,128)(2,1)} slice(bf16[1024,4224]{1,0:T(8,128)(2,1)} %param.30), slice={[0:1024], [128:4224]} | slice | bytes 16777216 | tf_op jit(solution)/shard_map/slice | solution.py:1875
  26.4 6.0 %bias.1 = (f32[9,256,256]{2,1,0:T(8,128)}, f32[9,256,256]{2,1,0:T(8,128)}) custom-call(s32[1]{0:T(128)S(6)} %convert_element_type.34.flag_ref, f32[8,1,512]{2,1,0:T(1,128)} %copy.63.back_row, f32[8,1,512]{2,1,0:T(1,128)} %broadcast_in_dim.42.front_row), custom_call_target="tpu_custom_call" | custom-call | tf_op jit(solution)/shard_map/bias/pallas_call | solution.py:900
  33.1 10.0 %front.2 = (bf16[2,512,1024]{2,1,0:T(8,128)(2,1)}, bf16[2,512,1024]{2,1,0:T(8,128)(2,1)}, bf16[2,512,2048]{2,1,0:T(8,128)(2,1)}, bf16[2,512,2048]{2,1,0:T(8,128)(2,1)}, f32[2,16,8,128]{3,2,1,0:T(8,128)}) custom-call(bf16[512,1024]{1,0:T(8,128)(2,1)} %collective-permute-done.2.refs_0_, f32[1,1024]{1,0:T(1,128)} %bitcast.233, f32[16,8,128]{2,1,0:T(8,128)} %bitcast.206, ...), custom_call_target="tpu_custom_call" | custom-call | flops 1 | bytes 1 | tf_op jit(solution)/shard_map/front/pallas_call | solution.py:130
  43.1 12.6 %collective-permute-done.1.refs_0_ = bf16[512,1024]{1,0:T(8,128)(2,1)S(1)} collective-permute-done((bf16[512,1024]{1,0:T(8,128)(2,1)}, bf16[512,1024]{1,0:T(8,128)(2,1)S(1)}, u32[]{:S(2)}, u32[]{:S(2)}) %collective-permute-start.1) | collective-permute-done | bytes 1048608 | tf_op jit(solution)/shard_map/ppermute | solution.py:1560
  56.7 10.2 %front.3 = (bf16[2,512,1024]{2,1,0:T(8,128)(2,1)}, bf16[2,512,1024]{2,1,0:T(8,128)(2,1)}, bf16[2,512,2048]{2,1,0:T(8,128)(2,1)}, bf16[2,512,2048]{2,1,0:T(8,128)(2,1)}, f32[2,16,8,128]{3,2,1,0:T(8,128)}) custom-call(bf16[512,1024]{1,0:T(8,128)(2,1)} %copy-done.18, ...), custom_call_target="tpu_custom_call", output_to_operand_aliasing={{0}: (5, {}), {1}: (6, {}), {2}: (7, {}), {3}: (8, {}), {4}... | custom-call | flops 1 | bytes 1 | tf_op jit(solution)/shard_map/front/pallas_call | solution.py:130
  68.6 2.4 collective-permute-start.7
  71.0 17.3 %front_scan.1 = (f32[2,512,1024]{2,1,0:T(8,128)}, bf16[2,512,1024]{2,1,0:T(8,128)(2,1)}, f32[2,4,16,8,128]{4,3,2,1,0:T(8,128)}, f32[2,512,128]{2,1,0:T(8,128)}, ...) custom-call(s32[9]{0:T(128)} %concatenate.36.refs_10_.table_ref.refs_0_, ...), custom_call_target="tpu_custom_call" | custom-call | flops 99999997952 | bytes 1 | tf_op jit(solution)/shard_map/front_scan/pallas_call | solution.py:243
  88.9 13.0 %product.1.pre_ref.update_ref.refs_5_.refs_6_ = bf16[1024,4096]{1,0:T(8,128)(2,1)} custom-call(bf16[1024,1024]{1,0:T(8,128)(2,1)} %bitcast.184, bf16[1024,4096]{1,0:T(8,128)(2,1)} %slice.91.refs_7_.right_ref.refs_2_), custom_call_target="tpu_custom_call" | custom-call | flops 1 | bytes 1 | tf_op jit(solution)/shard_map/product/pallas_call | solution.py:1259
  102.6 18.3 %attend.1 = (bf16[2,512,2048]{2,1,0:T(8,128)(2,1)}, bf16[2,512,2048]{2,1,0:T(8,128)(2,1)}, f32[2,1,512]{2,1,0:T(1,128)}) custom-call(s32[9]{0:T(128)} %concatenate.36.refs_10_.table_ref.refs_0_, bf16[2,512,128]{2,1,0:T(8,128)(2,1)} %get-tuple-element.120.q_ref.refs_1_, f32[9,256,256]{2,1,0:T(8,128)} %get-tuple-element.111.refs_6_.bias_ref, ...), custom_call_target="tpu_custom_call" | custom-call | flops 1 | bytes 1 | tf_op jit(solution)/shard_map/attend/pallas_call | solution.py:629
  120.9 12.8 %candidate.1 = (f32[1024,1024]{1,0:T(8,128)}, f32[1024,1024]{1,0:T(8,128)}, bf16[1024,1024]{1,0:T(8,128)(2,1)}) custom-call(bf16[1024,2048]{1,0:T(8,128)(2,1)} %bitcast.176, bf16[2048,1024]{1,0:T(8,128)(2,1)} %refs_9_.1, bf16[1024,4096]{1,0:T(8,128)(2,1)} %product.1.pre_ref.update_ref.refs_5_.refs_6_, ...), custom_call_target="tpu_custom_call" | custom-call | flops 1 | bytes 1 | tf_op jit(solution)/shard_map/candidate/pallas_call | solution.py:950
  134.7 68.3 %feed.1 = (bf16[512,1024]{1,0:T(8,128)(2,1)}, bf16[512,1024]{1,0:T(8,128)(2,1)}, f32[1024,1024]{1,0:T(8,128)}, bf16[4,1024,512]{2,1,0:T(8,128)(2,1)}, bf16[4,102...) custom-call(s32[8]{0:T(128)} %broadcast_select_fusion.1.refs_11_.refs_0_, ...), custom_call_target="tpu_custom_call" | custom-call | flops 1 | bytes 1 | tf_op jit(solution)/shard_map/feed/pallas_call | solution.py:1201
  203.6 2.0 collective-permute-start.9
  205.7 19.8 %gate.1 = (f32[1024,1024]{1,0:T(8,128)}, bf16[1024,4096]{1,0:T(8,128)(2,1)}, bf16[1024,2048]{1,0:T(8,128)(2,1)}, f32[1,1024]{1,0:T(1,128)}) custom-call(f32[1024,1024]{1,0:T(8,128)} %get-tuple-element.131.refs_0_, bf16[512,1024]{1,0:T(8,128)(2,1)} %copy-done.19, bf16[512,1024]{1,0:T(8,128)(2,1)} %collective-permute-done.7.refs_4_.refs_2_, ...), custom_call_target="tpu_custom_call" | custom-call | flops 99999997952 | bytes 1 | tf_op jit(solution)/shard_map/gate/pallas_call | solution.py:1039
  225.5 5.2 %stage_sums.8.refs_4_ = bf16[2,2048,512]{2,1,0:T(8,128)(2,1)} custom-call(bf16[1,4096,512]{2,1,0:T(8,128)(2,1)} %bitcast.156, bf16[1,4096,512]{2,1,0:T(8,128)(2,1)} %collective-permute-done.10.refs_1_, bf16[1,4096,512]{2,1,0:T(8,128)(2,1)} %bitcast.161, bf16[1,4096,512]{2,1,0:T(8,128)(2,1)} %collective-permute-done.11.refs_3_.refs_4_.refs_5_.refs_6_.refs_7_, ...), custom_call_target="tpu_custom_call" | custom-call | flops 1 | bytes 1 | tf_op jit(solution)/shard_map/stage_sums/pallas_call | solution.py:1532
  231.2 15.1 %by_rows.2 = (bf16[4,1,128,4096]{3,2,1,0:T(8,128)(2,1)}, bf16[4,1,128,4096]{3,2,1,0:T(8,128)(2,1)}) custom-call(s32[8]{0:T(128)} %broadcast_select_fusion.1.refs_11_.refs_0_, s32[1]{0:T(128)} %constant.104.clone.1.refs_1_, bf16[1024,1024]{1,0:T(8,128)(2,1)} %bitcast.185, bf16[1024,4096]{1,0:T(8,128)(2,1)} %get-tuple-element.134.refs_3_.refs_2_.refs_0_, ...), custom_call_target="tpu_custom_call" | custom-call | flops 99999997952 | bytes 1 | tf_op jit(solution)/shard_map/by_rows/pallas_call | solution.py:1406
  246.3 11.9 %by_columns.1 = (bf16[4,1024,256]{2,1,0:T(8,128)(2,1)}, bf16[4,1024,256]{2,1,0:T(8,128)(2,1)}) custom-call(s32[8]{0:T(128)} %broadcast_select_fusion.1.refs_11_.refs_0_, s32[4]{0:T(128)} %get-tuple-element.109.refs_12_.refs_1_, bf16[1024,4096]{1,0:T(8,128)(2,1)} %get-tuple-element.134.refs_3_.refs_2_.refs_0_, bf16[1024,2048]{1,0:T(8,128)(2,1)} %bitcast.177, ...), custom_call_target="tpu_custom_call" | custom-call | flops 1 | bytes 1 | tf_op jit(solution)/shard_map/by_columns/pallas_call | solution.py:1350
  258.2 32.9 %attend_back.1 = (f32[2,512,128]{2,1,0:T(8,128)}, bf16[2,512,128]{2,1,0:T(8,128)(2,1)}, bf16[2,512,2048]{2,1,0:T(8,128)(2,1)}, bf16[2,512,2176]{2,1,0:T(8,128)(2,1)}, f32[8,1,512]{2,1,0:T(1,128)}) custom-call(s32[9]{0:T(128)} %concatenate.36.refs_10_.table_ref.refs_0_, bf16[2,512,128]{2,1,0:T(8,128)(2,1)} %get-tuple-element.120.q_ref.refs_1_, ...), custom_call_target="tpu_custom_call" | custom-call | flops 99999997952 | bytes 1 | tf_op jit(solution)/shard_map/attend_back/pallas_call | solution.py:812
  293.1 5.0 stage_sums.9
  298.1 2.5 collective-permute-start.16
  301.2 15.9 %value_back.1 = (f32[1024,1024]{1,0:T(8,128)}, bf16[4,4,128,512]{3,2,1,0:T(8,128)(2,1)}, bf16[4,4,128,512]{3,2,1,0:T(8,128)(2,1)}) custom-call(s32[8]{0:T(128)} %broadcast_select_fusion.1.refs_11_.refs_0_, s32[4]{0:T(128)} %get-tuple-element.109.refs_12_.refs_1_, bf16[1024,1024]{1,0:T(8,128)(2,1)} %bitcast.201, bf16[1024,2048]{1,0:T(8,128)(2,1)} %bitcast.268, ...), custom_call_target="tpu_custom_call" | custom-call | flops 99999997952 | bytes 1 | tf_op jit(solution)/shard_map/value_back/pallas_call | solution.py:1477
  317.2 2.5 fusion.8
  319.6 4.8 by_rows.3
  325.0 3.4 stage_sums.10.refs_5_
  329.8 17.1 %smooth_back.1 = f32[1024,1024]{1,0:T(8,128)} custom-call(bf16[1024,4096]{1,0:T(8,128)(2,1)} %get-tuple-element.134.refs_3_.refs_2_.refs_0_, bf16[1024,128]{1,0:T(8,128)(2,1)} %get-tuple-element.270.refs_3_.refs_1_, bf16[1024,4096]{1,0:T(8,128)(2,1)} %slice.91.refs_7_.right_ref.refs_2_, bf16[1024,128]{1,0:T(8,128)(2,1)} %slice.92.refs_8_.proj_ref.refs_3_, ...), custom_call_target="tpu_custom_call" | custom-call | flops 99999997952 | bytes 1 | tf_op jit(solution)/shard_map/smooth_back/pallas_call | solution.py:1297
  348.3 4.8 stage_sums.11
  353.1 2.4 collective-permute-start.21
  359.5 8.1 %back_ends.1.refs_19_.refs_12_ = f32[2,16,8,128]{3,2,1,0:T(8,128)} custom-call(f32[2,512,1024]{2,1,0:T(8,128)} %bitcast.179, f32[16,8,128]{2,1,0:T(8,128)} %bitcast.209, bf16[2,512,512]{2,1,0:T(8,128)(2,1)} %get-tuple-element.162.refs_2_, bf16[1,1024,512]{2,1,0:T(8,128)(2,1)} %get-tuple-element.163.refs_3_, ...), custom_call_target="tpu_custom_call" | custom-call | flops 1 | bytes 1 | tf_op jit(solution)/shard_map/back_ends/pallas_call | solution.py:322
  368.5 2.8 collective-permute-done.24.refs_18_.refs_26_
  371.3 6.9 %collective-permute-done.21.refs_4_.refs_9_.refs_10_ = bf16[2,512,512]{2,1,0:T(8,128)(2,1)S(1)} collective-permute-done((bf16[2,512,512]{2,1,0:T(8,128)(2,1)}, bf16[2,512,512]{2,1,0:T(8,128)(2,1)S(1)}, u32[]{:S(2)}, u32[]{:S(2)}) %collective-permute-start.21) | collective-permute-done | bytes 1048608 | tf_op jit(solution)/shard_map/ppermute | solution.py:1560
  380.2 4.7 stage_sums.12
  388.1 20.2 %back_scan.2 = (bf16[512,1024]{1,0:T(8,128)(2,1)}, f32[16,8,128]{2,1,0:T(8,128)}, f32[16,8,128]{2,1,0:T(8,128)}, f32[1,1024]{1,0:T(1,128)}, f32[1,1024]{1,0:T(1,128)}) custom-call(s32[9]{0:T(128)} %concatenate.36.refs_10_.table_ref.refs_0_, s32[1]{0:T(128)} %constant.104.clone.1.refs_1_, bf16[2,512,1024]{2,1,0:T(8,128)(2,1)} %get-tuple-element.117.x_ref.refs_2_, ...), custom_call_target="tpu_custom_call" | custom-call | flops 99999997952 | bytes 1 | tf_op jit(solution)/shard_map/back_scan/pallas_call | solution.py:468
  408.4 1.8 collective-permute-start.31
  412.7 5.7 %stage_sums.13 = (f32[2,256,512]{2,1,0:T(8,128)}, bf16[1,128,4096]{2,1,0:T(8,128)(2,1)}, bf16[1,256,512]{2,1,0:T(8,128)(2,1)}, bf16[1,512,256]{2,1,0:T(8,128)(2,1)}, bf16[1,128,128]{2,1,0:T(8,128)(2,1)}) custom-call(bf16[1,4096,512]{2,1,0:T(8,128)(2,1)} %bitcast.160, bf16[1,4096,512]{2,1,0:T(8,128)(2,1)} %collective-permute-done.10.refs_1_, ...), custom_call_target="tpu_custom_call" | custom-call | flops 1 | bytes 1 | tf_op jit(solution)/shard_map/stage_sums/pallas_call | solution.py:1532
  422.4 2.5 collective-permute-start.32
  425.0 1.9 collective-permute-start.34
  427.0 20.4 %back_scan.3 = (bf16[512,1024]{1,0:T(8,128)(2,1)}, f32[16,8,128]{2,1,0:T(8,128)}, f32[16,8,128]{2,1,0:T(8,128)}, f32[1,1024]{1,0:T(1,128)}, f32[1,1024]{1,0:T(1,128)}) custom-call(s32[9]{0:T(128)} %concatenate.36.refs_10_.table_ref.refs_0_, s32[1]{0:T(128)} %constant.103.clone.1.refs_1_, bf16[2,512,1024]{2,1,0:T(8,128)(2,1)} %get-tuple-element.117.x_ref.refs_2_, ...), custom_call_target="tpu_custom_call" | custom-call | flops 99999997952 | bytes 1 | tf_op jit(solution)/shard_map/back_scan/pallas_call | solution.py:468
  452.2 2.3 stage_sums.14
  458.0 8.1 %collective-permute-start.38 = (bf16[1,128,1056]{2,1,0:T(8,128)(2,1)S(1)}, bf16[1,128,1056]{2,1,0:T(8,128)(2,1)S(1)}, u32[]{:S(2)}, u32[]{:S(2)}) collective-permute-start(bf16[1,128,1056]{2,1,0:T(8,128)(2,1)S(1)} %copy-done.17), channel_id=1, source_target_pairs={{0,2},{1,3},{2,0},{3,1},{4,6},{5,7},{6,4},{7,5},{8,10},{9,11},{10,... | collective-permute-start | bytes 811016 | tf_op jit(solution)/shard_map/ppermute | solution.py:1560
  466.2 1.8 collective-permute-start.36
  469.5 2.9 collective-permute-start.40
  474.8 17.8 %collective-permute-done.39.refs_8_ = bf16[1,256,256]{2,1,0:T(8,128)(2,1)S(1)} collective-permute-done((bf16[1,256,256]{2,1,0:T(8,128)(2,1)S(1)}, bf16[1,256,256]{2,1,0:T(8,128)(2,1)S(1)}, u32[]{:S(2)}, u32[]{:S(2)}) %collective-permute-start.39) | collective-permute-done | bytes 131104 | tf_op jit(solution)/shard_map/ppermute | solution.py:1560
  492.6 2.8 collective-permute-done.40.refs_14_
  497.1 2.6 stage_sums.15
  503.6 3.4 collective-permute-start.42
  508.9 2.3 maximum_convert_fusion
  514.8 1.9 finish.1
  (265 shorter events, 64.0 us)
Async XLA Ops:
  1.3 23.2 %collective-permute-start = (f32[2]{0:T(128)S(1)}, f32[2]{0:T(128)S(1)}, u32[]{:S(2)}, u32[]{:S(2)}) collective-permute-start(f32[2]{0:T(128)S(1)} %convert_element_type.33), channel_id=1, source_target_pairs={{0,4},{1,5},{2,6},{3,7},{4,0},{5,1},{6,2},{7,3},{8,12},{9,13},{10,... | collective-permute-start | bytes 32 | tf_op jit(solution)/shard_map/ppermute | solution.py:1560
  4.9 27.6 %collective-permute-start.2 = (bf16[512,1024]{1,0:T(8,128)(2,1)}, bf16[512,1024]{1,0:T(8,128)(2,1)}, u32[]{:S(2)}, u32[]{:S(2)}) collective-permute-start(bf16[512,1024]{1,0:T(8,128)(2,1)} %get-tuple-element.277), channel_id=1, source_target_pairs={{0,4},{1,0},{2,5},{3,1},{4,6},{5,2},{6,7},{7,3},{8,12},{9,8},{10,1... | collective-permute-start | bytes 3145736 | tf_op jit(solution)/shard_map/ppermute | solution.py:1560
  4.9 50.8 %collective-permute-start.1 = (bf16[512,1024]{1,0:T(8,128)(2,1)}, bf16[512,1024]{1,0:T(8,128)(2,1)S(1)}, u32[]{:S(2)}, u32[]{:S(2)}) collective-permute-start(bf16[512,1024]{1,0:T(8,128)(2,1)} %get-tuple-element.278), channel_id=1, source_target_pairs={{0,1},{1,5},{2,0},{3,4},{4,3},{5,7},{6,2},{7,6},{8,9},{9,13},{10,8... | collective-permute-start | bytes 3145736 | tf_op jit(solution)/shard_map/ppermute | solution.py:1560
  66.9 1.6 collective-permute-start.3
  66.9 35.0 %collective-permute-start.5 = (bf16[2,512,2048]{2,1,0:T(8,128)(2,1)}, bf16[2,512,2048]{2,1,0:T(8,128)(2,1)}, u32[]{:S(2)}, u32[]{:S(2)}) collective-permute-start(bf16[2,512,2048]{2,1,0:T(8,128)(2,1)} %get-tuple-element.123.v_own.refs_7_), channel_id=1, source_target_pairs={{0,4},{1,5},{2,6},{3,7},{4,0},{5,1},{6,2},{7,3},{8,12},{9,13},{10,... | collective-permute-start | bytes 12582920 | tf_op jit(solution)/shard_map/ppermute | solution.py:1560
  68.5 65.2 %collective-permute-start.6 = (bf16[512,1024]{1,0:T(8,128)(2,1)S(1)}, bf16[512,1024]{1,0:T(8,128)(2,1)S(1)}, u32[]{:S(2)}, u32[]{:S(2)}) collective-permute-start(bf16[512,1024]{1,0:T(8,128)(2,1)S(1)} %copy-done.6), channel_id=1, source_target_pairs={{0,4},{1,0},{2,5},{3,1},{4,6},{5,2},{6,7},{7,3},{8,12},{9,8},{10,1... | collective-permute-start | bytes 3145736 | tf_op jit(solution)/shard_map/ppermute | solution.py:1560
  68.6 65.1 %collective-permute-start.7 = (bf16[512,1024]{1,0:T(8,128)(2,1)S(1)}, bf16[512,1024]{1,0:T(8,128)(2,1)}, u32[]{:S(2)}, u32[]{:S(2)}) collective-permute-start(bf16[512,1024]{1,0:T(8,128)(2,1)S(1)} %copy-done.5), channel_id=1, source_target_pairs={{0,1},{1,5},{2,0},{3,4},{4,3},{5,7},{6,2},{7,6},{8,9},{9,13},{10,8... | collective-permute-start | bytes 3145736 | tf_op jit(solution)/shard_map/ppermute | solution.py:1560
  88.3 13.6 %collective-permute-start.4 = (bf16[2,512,128]{2,1,0:T(8,128)(2,1)}, bf16[2,512,128]{2,1,0:T(8,128)(2,1)S(1)}, u32[]{:S(2)}, u32[]{:S(2)}) collective-permute-start(bf16[2,512,128]{2,1,0:T(8,128)(2,1)} %get-tuple-element.122.k_own.refs_5_), channel_id=1, source_target_pairs={{0,4},{1,5},{2,6},{3,7},{4,0},{5,1},{6,2},{7,3},{8,12},{9,13},{10,... | collective-permute-start | bytes 786440 | tf_op jit(solution)/shard_map/ppermute | solution.py:1560
  203.0 22.5 %collective-permute-start.10 = (bf16[1,4096,512]{2,1,0:T(8,128)(2,1)}, bf16[1,4096,512]{2,1,0:T(8,128)(2,1)}, u32[]{:S(2)}, u32[]{:S(2)}) collective-permute-start(bf16[1,4096,512]{2,1,0:T(8,128)(2,1)} %bitcast.255), channel_id=1, source_target_pairs={{0,4},{1,5},{2,6},{3,7},{4,0},{5,1},{6,2},{7,3},{8,12},{9,13},{10,... | collective-permute-start | bytes 12582920 | tf_op jit(solution)/shard_map/ppermute | solution.py:1560
  203.5 22.0 %collective-permute-start.11 = (bf16[1,4096,512]{2,1,0:T(8,128)(2,1)}, bf16[1,4096,512]{2,1,0:T(8,128)(2,1)}, u32[]{:S(2)}, u32[]{:S(2)}) collective-permute-start(bf16[1,4096,512]{2,1,0:T(8,128)(2,1)} %bitcast.254), channel_id=1, source_target_pairs={{0,4},{1,5},{2,6},{3,7},{4,0},{5,1},{6,2},{7,3},{8,12},{9,13},{10,... | collective-permute-start | bytes 12582920 | tf_op jit(solution)/shard_map/ppermute | solution.py:1560
  203.6 54.6 %collective-permute-start.8 = (bf16[512,1024]{1,0:T(8,128)(2,1)}, bf16[512,1024]{1,0:T(8,128)(2,1)}, u32[]{:S(2)}, u32[]{:S(2)}) collective-permute-start(bf16[512,1024]{1,0:T(8,128)(2,1)} %get-tuple-element.129), channel_id=1, source_target_pairs={{1,0},{5,1},{0,2},{4,3},{3,4},{7,5},{2,6},{6,7},{9,8},{13,9},{8,10... | collective-permute-start | bytes 3145736 | tf_op jit(solution)/shard_map/ppermute | solution.py:1589
  203.6 54.6 %collective-permute-start.9 = (bf16[512,1024]{1,0:T(8,128)(2,1)}, bf16[512,1024]{1,0:T(8,128)(2,1)}, u32[]{:S(2)}, u32[]{:S(2)}) collective-permute-start(bf16[512,1024]{1,0:T(8,128)(2,1)} %get-tuple-element.130), channel_id=1, source_target_pairs={{4,0},{0,1},{5,2},{1,3},{6,4},{2,5},{7,6},{3,7},{12,8},{8,9},{13,1... | collective-permute-start | bytes 3145736 | tf_op jit(solution)/shard_map/ppermute | solution.py:1589
  230.7 61.0 %collective-permute-start.14 = (bf16[2,2048,512]{2,1,0:T(8,128)(2,1)}, bf16[2,2048,512]{2,1,0:T(8,128)(2,1)}, u32[]{:S(2)}, u32[]{:S(2)}) collective-permute-start(bf16[2,2048,512]{2,1,0:T(8,128)(2,1)} %stage_sums.8.refs_4_), channel_id=1, source_target_pairs={{0,8},{1,9},{2,10},{3,11},{4,20},{5,21},{6,22},{7,23},{8,0},{9,1},... | collective-permute-start | bytes 12582920 | tf_op jit(solution)/shard_map/ppermute | solution.py:1560
  258.2 33.6 %collective-permute-start.15 = (bf16[1,4096,256]{2,1,0:T(8,128)(2,1)}, bf16[1,4096,256]{2,1,0:T(8,128)(2,1)S(1)}, u32[]{:S(2)}, u32[]{:S(2)}) collective-permute-start(bf16[1,4096,256]{2,1,0:T(8,128)(2,1)} %bitcast.257), channel_id=1, source_target_pairs={{0,4},{1,5},{2,6},{3,7},{4,0},{5,1},{6,2},{7,3},{8,12},{9,13},{10,... | collective-permute-start | bytes 6291464 | tf_op jit(solution)/shard_map/ppermute | solution.py:1560
  291.1 10.0 %collective-permute-start.12 = (bf16[2,512,2176]{2,1,0:T(8,128)(2,1)}, bf16[2,512,2176]{2,1,0:T(8,128)(2,1)}, u32[]{:S(2)}, u32[]{:S(2)}) collective-permute-start(bf16[2,512,2176]{2,1,0:T(8,128)(2,1)} %get-tuple-element.146), channel_id=1, source_target_pairs={{0,4},{1,5},{2,6},{3,7},{4,0},{5,1},{6,2},{7,3},{8,12},{9,13},{10,... | collective-permute-start | bytes 13369352 | tf_op jit(solution)/shard_map/ppermute | solution.py:1560
  291.7 33.3 %collective-permute-start.13 = (bf16[1,512,4096]{2,1,0:T(8,128)(2,1)}, bf16[1,512,4096]{2,1,0:T(8,128)(2,1)}, u32[]{:S(2)}, u32[]{:S(2)}) collective-permute-start(bf16[1,512,4096]{2,1,0:T(8,128)(2,1)} %bitcast.194), channel_id=1, source_target_pairs={{0,4},{1,5},{2,6},{3,7},{4,0},{5,1},{6,2},{7,3},{8,12},{9,13},{10,... | collective-permute-start | bytes 12582920 | tf_op jit(solution)/shard_map/ppermute | solution.py:1560
  298.1 48.8 %collective-permute-start.16 = (bf16[2,1024,512]{2,1,0:T(8,128)(2,1)}, bf16[2,1024,512]{2,1,0:T(8,128)(2,1)}, u32[]{:S(2)}, u32[]{:S(2)}) collective-permute-start(bf16[2,1024,512]{2,1,0:T(8,128)(2,1)} %get-tuple-element.153.refs_7_), channel_id=1, source_target_pairs={{0,16},{1,17},{2,18},{3,19},{4,12},{5,13},{6,14},{7,15},{8,24},{9,... | collective-permute-start | bytes 6291464 | tf_op jit(solution)/shard_map/ppermute | solution.py:1560
  300.6 46.3 %collective-permute-start.18 = (bf16[1,2048,256]{2,1,0:T(8,128)(2,1)}, bf16[1,2048,256]{2,1,0:T(8,128)(2,1)}, u32[]{:S(2)}, u32[]{:S(2)}) collective-permute-start(bf16[1,2048,256]{2,1,0:T(8,128)(2,1)} %get-tuple-element.154.refs_8_), channel_id=1, source_target_pairs={{0,8},{1,9},{2,10},{3,11},{4,20},{5,21},{6,22},{7,23},{8,0},{9,1},... | collective-permute-start | bytes 3145736 | tf_op jit(solution)/shard_map/ppermute | solution.py:1560
  317.1 29.8 %collective-permute-start.17 = (bf16[1,2048,512]{2,1,0:T(8,128)(2,1)}, bf16[1,2048,512]{2,1,0:T(8,128)(2,1)S(1)}, u32[]{:S(2)}, u32[]{:S(2)}) collective-permute-start(bf16[1,2048,512]{2,1,0:T(8,128)(2,1)} %bitcast.256), channel_id=1, source_target_pairs={{0,4},{1,5},{2,6},{3,7},{4,0},{5,1},{6,2},{7,3},{8,12},{9,13},{10,... | collective-permute-start | bytes 6291464 | tf_op jit(solution)/shard_map/ppermute | solution.py:1560
  324.5 22.4 %collective-permute-start.19 = (bf16[1,512,128]{2,1,0:T(8,128)(2,1)}, bf16[1,512,128]{2,1,0:T(8,128)(2,1)S(1)}, u32[]{:S(2)}, u32[]{:S(2)}) collective-permute-start(bf16[1,512,128]{2,1,0:T(8,128)(2,1)} %bitcast.222), channel_id=1, source_target_pairs={{0,4},{1,5},{2,6},{3,7},{4,0},{5,1},{6,2},{7,3},{8,12},{9,13},{10,... | collective-permute-start | bytes 393224 | tf_op jit(solution)/shard_map/ppermute | solution.py:1560
  328.3 40.0 %collective-permute-start.22 = (bf16[1,256,4096]{2,1,0:T(8,128)(2,1)}, bf16[1,256,4096]{2,1,0:T(8,128)(2,1)}, u32[]{:S(2)}, u32[]{:S(2)}) collective-permute-start(bf16[1,256,4096]{2,1,0:T(8,128)(2,1)} %stage_sums.10.refs_5_), channel_id=1, source_target_pairs={{0,8},{1,9},{2,10},{3,11},{4,20},{5,21},{6,22},{7,23},{8,0},{9,1},... | collective-permute-start | bytes 6291464 | tf_op jit(solution)/shard_map/ppermute | solution.py:1560
  353.1 25.1 %collective-permute-start.21 = (bf16[2,512,512]{2,1,0:T(8,128)(2,1)}, bf16[2,512,512]{2,1,0:T(8,128)(2,1)S(1)}, u32[]{:S(2)}, u32[]{:S(2)}) collective-permute-start(bf16[2,512,512]{2,1,0:T(8,128)(2,1)} %get-tuple-element.162.refs_2_), channel_id=1, source_target_pairs={{0,1},{1,0},{2,3},{3,2},{4,5},{5,4},{6,7},{7,6},{8,9},{9,8},{10,11... | collective-permute-start | bytes 3145736 | tf_op jit(solution)/shard_map/ppermute | solution.py:1560
  355.5 22.7 %collective-permute-start.23 = (bf16[1,1024,512]{2,1,0:T(8,128)(2,1)}, bf16[1,1024,512]{2,1,0:T(8,128)(2,1)S(1)}, u32[]{:S(2)}, u32[]{:S(2)}) collective-permute-start(bf16[1,1024,512]{2,1,0:T(8,128)(2,1)} %get-tuple-element.163.refs_3_), channel_id=1, source_target_pairs={{0,8},{1,9},{2,10},{3,11},{4,20},{5,21},{6,22},{7,23},{8,0},{9,1},... | collective-permute-start | bytes 3145736 | tf_op jit(solution)/shard_map/ppermute | solution.py:1560
  357.9 13.3 %collective-permute-start.24 = (bf16[1,256,128]{2,1,0:T(8,128)(2,1)}, bf16[1,256,128]{2,1,0:T(8,128)(2,1)S(1)}, u32[]{:S(2)}, u32[]{:S(2)}) collective-permute-start(bf16[1,256,128]{2,1,0:T(8,128)(2,1)} %get-tuple-element.165.refs_5_), channel_id=1, source_target_pairs={{0,8},{1,9},{2,10},{3,11},{4,20},{5,21},{6,22},{7,23},{8,0},{9,1},... | collective-permute-start | bytes 196616 | tf_op jit(solution)/shard_map/ppermute | solution.py:1560
  367.6 20.0 %collective-permute-start.20 = (f32[2,16,8,128]{3,2,1,0:T(8,128)}, f32[2,16,8,128]{3,2,1,0:T(8,128)}, u32[]{:S(2)}, u32[]{:S(2)}) collective-permute-start(f32[2,16,8,128]{3,2,1,0:T(8,128)} %back_ends.1.refs_19_.refs_12_), channel_id=1, source_target_pairs={{0,4},{1,5},{2,6},{3,7},{4,0},{5,1},{6,2},{7,3},{8,12},{9,13},{10,... | collective-permute-start | bytes 393224 | tf_op jit(solution)/shard_map/ppermute | solution.py:1560
  368.4 40.0 %collective-permute-start.28 = (bf16[1,1024,256]{2,1,0:T(8,128)(2,1)}, bf16[1,1024,256]{2,1,0:T(8,128)(2,1)S(1)}, u32[]{:S(2)}, u32[]{:S(2)}) collective-permute-start(bf16[1,1024,256]{2,1,0:T(8,128)(2,1)} %get-tuple-element.164.refs_4_), channel_id=1, source_target_pairs={{0,16},{1,17},{2,18},{3,19},{4,12},{5,13},{6,14},{7,15},{8,24},{9,... | collective-permute-start | bytes 1572872 | tf_op jit(solution)/shard_map/ppermute | solution.py:1560
  384.8 25.8 %collective-permute-start.26 = (bf16[1,128,4096]{2,1,0:T(8,128)(2,1)}, bf16[1,128,4096]{2,1,0:T(8,128)(2,1)S(1)}, u32[]{:S(2)}, u32[]{:S(2)}) collective-permute-start(bf16[1,128,4096]{2,1,0:T(8,128)(2,1)} %get-tuple-element.167.refs_15_), channel_id=1, source_target_pairs={{0,16},{1,17},{2,18},{3,19},{4,12},{5,13},{6,14},{7,15},{8,24},{9,... | collective-permute-start | bytes 3145736 | tf_op jit(solution)/shard_map/ppermute | solution.py:1560
  386.1 24.5 %collective-permute-start.25 = (bf16[2,256,512]{2,1,0:T(8,128)(2,1)}, bf16[2,256,512]{2,1,0:T(8,128)(2,1)S(1)}, u32[]{:S(2)}, u32[]{:S(2)}) collective-permute-start(bf16[2,256,512]{2,1,0:T(8,128)(2,1)} %get-tuple-element.166.refs_14_), channel_id=1, source_target_pairs={{0,2},{1,3},{2,0},{3,1},{4,6},{5,7},{6,4},{7,5},{8,10},{9,11},{10,... | collective-permute-start | bytes 1572872 | tf_op jit(solution)/shard_map/ppermute | solution.py:1560
  386.1 24.6 %collective-permute-start.27 = (bf16[1,512,512]{2,1,0:T(8,128)(2,1)}, bf16[1,512,512]{2,1,0:T(8,128)(2,1)S(1)}, u32[]{:S(2)}, u32[]{:S(2)}) collective-permute-start(bf16[1,512,512]{2,1,0:T(8,128)(2,1)} %get-tuple-element.168.refs_16_), channel_id=1, source_target_pairs={{0,16},{1,17},{2,18},{3,19},{4,12},{5,13},{6,14},{7,15},{8,24},{9,... | collective-permute-start | bytes 1572872 | tf_op jit(solution)/shard_map/ppermute | solution.py:1560
  387.6 22.5 %collective-permute-start.29 = (bf16[1,128,128]{2,1,0:T(8,128)(2,1)}, bf16[1,128,128]{2,1,0:T(8,128)(2,1)S(1)}, u32[]{:S(2)}, u32[]{:S(2)}) collective-permute-start(bf16[1,128,128]{2,1,0:T(8,128)(2,1)} %get-tuple-element.169.refs_17_), channel_id=1, source_target_pairs={{0,16},{1,17},{2,18},{3,19},{4,12},{5,13},{6,14},{7,15},{8,24},{9,... | collective-permute-start | bytes 98312 | tf_op jit(solution)/shard_map/ppermute | solution.py:1560
  408.4 42.4 %collective-permute-start.31 = (bf16[512,1024]{1,0:T(8,128)(2,1)}, bf16[512,1024]{1,0:T(8,128)(2,1)}, u32[]{:S(2)}, u32[]{:S(2)}) collective-permute-start(bf16[512,1024]{1,0:T(8,128)(2,1)} %get-tuple-element.170.refs_28_), channel_id=1, source_target_pairs={{4,0},{0,1},{5,2},{1,3},{6,4},{2,5},{7,6},{3,7},{12,8},{8,9},{13,1... | collective-permute-start | bytes 3145736 | tf_op jit(solution)/shard_map/ppermute | solution.py:1589
  422.4 27.4 %collective-permute-start.32 = (bf16[1,256,1056]{1,2,0:T(8,128)(2,1)S(1)}, bf16[1,256,1056]{1,2,0:T(8,128)(2,1)S(1)}, u32[]{:S(2)}, u32[]{:S(2)}) collective-permute-start(bf16[1,256,1056]{1,2,0:T(8,128)(2,1)S(1)} %copy.66), channel_id=1, source_target_pairs={{0,1},{1,0},{2,3},{3,2},{4,5},{5,4},{6,7},{7,6},{8,9},{9,8},{10,11... | collective-permute-start | bytes 1622024 | tf_op jit(solution)/shard_map/ppermute | solution.py:1560
  424.9 25.9 %collective-permute-start.33 = (bf16[1,512,256]{2,1,0:T(8,128)(2,1)}, bf16[1,512,256]{2,1,0:T(8,128)(2,1)S(1)}, u32[]{:S(2)}, u32[]{:S(2)}) collective-permute-start(bf16[1,512,256]{2,1,0:T(8,128)(2,1)} %get-tuple-element.174.refs_17_), channel_id=1, source_target_pairs={{0,1},{1,0},{2,3},{3,2},{4,5},{5,4},{6,7},{7,6},{8,9},{9,8},{10,11... | collective-permute-start | bytes 786440 | tf_op jit(solution)/shard_map/ppermute | solution.py:1560
  425.0 25.9 %collective-permute-start.34 = (bf16[1,256,512]{2,1,0:T(8,128)(2,1)S(1)}, bf16[1,256,512]{2,1,0:T(8,128)(2,1)S(1)}, u32[]{:S(2)}, u32[]{:S(2)}) collective-permute-start(bf16[1,256,512]{2,1,0:T(8,128)(2,1)S(1)} %copy-done.63), channel_id=1, source_target_pairs={{0,1},{1,0},{2,3},{3,2},{4,5},{5,4},{6,7},{7,6},{8,9},{9,8},{10,11... | collective-permute-start | bytes 786440 | tf_op jit(solution)/shard_map/ppermute | solution.py:1560
  426.9 22.0 %copy-start.44 = (f32[32,128]{1,0:T(8,128)S(1)}, f32[32,128]{1,0:T(8,128)}, u32[]{:S(2)}) copy-start(f32[32,128]{1,0:T(8,128)} %pad_bitcast_fusion) | copy-start | bytes 49156
  426.9 22.0 %copy-start.48 = (f32[1,1024]{1,0:T(1,128)S(1)}, f32[1,1024]{1,0:T(1,128)}, u32[]{:S(2)}) copy-start(f32[1,1024]{1,0:T(1,128)} %get-tuple-element.185) | copy-start | bytes 12292
  427.0 21.9 %copy-start.53 = (f32[128]{0:T(128)S(1)}, f32[128]{0:T(128)}, u32[]{:S(2)}) copy-start(f32[128]{0:T(128)} %get-tuple-element.269) | copy-start | bytes 1540
  447.3 48.0 %collective-permute-start.30 = (bf16[512,1024]{1,0:T(8,128)(2,1)}, bf16[512,1024]{1,0:T(8,128)(2,1)S(1)}, u32[]{:S(2)}, u32[]{:S(2)}) collective-permute-start(bf16[512,1024]{1,0:T(8,128)(2,1)} %get-tuple-element.176.refs_12_), channel_id=1, source_target_pairs={{1,0},{5,1},{0,2},{4,3},{3,4},{7,5},{2,6},{6,7},{9,8},{13,9},{8,10... | collective-permute-start | bytes 3145736 | tf_op jit(solution)/shard_map/ppermute | solution.py:1589
  456.2 9.9 %collective-permute-start.35 = (f32[320,128]{1,0:T(8,128)}, f32[320,128]{1,0:T(8,128)S(1)}, u32[]{:S(2)}, u32[]{:S(2)}) collective-permute-start(f32[320,128]{1,0:T(8,128)} %pack.1), channel_id=1, source_target_pairs={{0,4},{1,5},{2,6},{3,7},{4,0},{5,1},{6,2},{7,3},{8,12},{9,13},{10,... | collective-permute-start | bytes 491528 | tf_op jit(solution)/shard_map/ppermute | solution.py:1560
  458.0 37.4 %collective-permute-start.38 = (bf16[1,128,1056]{2,1,0:T(8,128)(2,1)S(1)}, bf16[1,128,1056]{2,1,0:T(8,128)(2,1)S(1)}, u32[]{:S(2)}, u32[]{:S(2)}) collective-permute-start(bf16[1,128,1056]{2,1,0:T(8,128)(2,1)S(1)} %copy-done.17), channel_id=1, source_target_pairs={{0,2},{1,3},{2,0},{3,1},{4,6},{5,7},{6,4},{7,5},{8,10},{9,11},{10,... | collective-permute-start | bytes 811016 | tf_op jit(solution)/shard_map/ppermute | solution.py:1560
  466.2 6.4 %collective-permute-start.36 = (f32[320,128]{1,0:T(8,128)S(1)}, f32[320,128]{1,0:T(8,128)S(1)}, u32[]{:S(2)}, u32[]{:S(2)}) collective-permute-start(f32[320,128]{1,0:T(8,128)S(1)} %add.92), channel_id=1, source_target_pairs={{0,8},{1,9},{2,10},{3,11},{4,12},{5,13},{6,14},{7,15},{8,0},{9,1},... | collective-permute-start | bytes 491528 | tf_op jit(solution)/shard_map/ppermute | solution.py:1560
  469.4 23.2 %collective-permute-start.39 = (bf16[1,256,256]{2,1,0:T(8,128)(2,1)S(1)}, bf16[1,256,256]{2,1,0:T(8,128)(2,1)S(1)}, u32[]{:S(2)}, u32[]{:S(2)}) collective-permute-start(bf16[1,256,256]{2,1,0:T(8,128)(2,1)S(1)} %copy-done.27), channel_id=1, source_target_pairs={{0,2},{1,3},{2,0},{3,1},{4,6},{5,7},{6,4},{7,5},{8,10},{9,11},{10,... | collective-permute-start | bytes 393224 | tf_op jit(solution)/shard_map/ppermute | solution.py:1560
  469.5 25.9 %collective-permute-start.40 = (bf16[1,128,512]{2,1,0:T(8,128)(2,1)S(1)}, bf16[1,128,512]{2,1,0:T(8,128)(2,1)S(1)}, u32[]{:S(2)}, u32[]{:S(2)}) collective-permute-start(bf16[1,128,512]{2,1,0:T(8,128)(2,1)S(1)} %copy-done.28), channel_id=1, source_target_pairs={{0,2},{1,3},{2,0},{3,1},{4,6},{5,7},{6,4},{7,5},{8,10},{9,11},{10,... | collective-permute-start | bytes 393224 | tf_op jit(solution)/shard_map/ppermute | solution.py:1560
  472.5 27.2 %copy-start.25 = (f32[320,128]{1,0:T(8,128)}, f32[320,128]{1,0:T(8,128)S(1)}, u32[]{:S(2)}) copy-start(f32[320,128]{1,0:T(8,128)S(1)} %add.93.refs_0_) | copy-start | bytes 491524
  472.5 27.2 %collective-permute-start.37 = (f32[320,128]{1,0:T(8,128)S(1)}, f32[320,128]{1,0:T(8,128)S(1)}, u32[]{:S(2)}, u32[]{:S(2)}) collective-permute-start(f32[320,128]{1,0:T(8,128)S(1)} %add.93.refs_0_), channel_id=1, source_target_pairs={{0,16},{1,17},{2,18},{3,19},{4,20},{5,21},{6,22},{7,23},{8,24},{9,... | collective-permute-start | bytes 491528 | tf_op jit(solution)/shard_map/ppermute | solution.py:1560
  503.1 10.0 %collective-permute-start.41 = (bf16[320,128]{1,0:T(8,128)(2,1)S(1)}, bf16[320,128]{1,0:T(8,128)(2,1)S(1)}, u32[]{:S(2)}, u32[]{:S(2)}) collective-permute-start(bf16[320,128]{1,0:T(8,128)(2,1)S(1)} %convert_element_type.41), channel_id=1, source_target_pairs={{0,1},{1,0},{2,3},{3,2},{4,5},{5,4},{6,7},{7,6},{8,9},{9,8},{10,11... | collective-permute-start | bytes 245768 | tf_op jit(solution)/shard_map/ppermute | solution.py:1560
  503.6 10.0 %collective-permute-start.42 = (bf16[320,128]{1,0:T(8,128)(2,1)S(1)}, bf16[320,128]{1,0:T(8,128)(2,1)S(1)}, u32[]{:S(2)}, u32[]{:S(2)}) collective-permute-start(bf16[320,128]{1,0:T(8,128)(2,1)S(1)} %convert_element_type.41), channel_id=1, source_target_pairs={{0,2},{1,3},{2,0},{3,1},{4,6},{5,7},{6,4},{7,5},{8,10},{9,11},{10,... | collective-permute-start | bytes 245768 | tf_op jit(solution)/shard_map/ppermute | solution.py:1560
  506.9 6.6 %collective-permute-start.43 = (bf16[320,128]{1,0:T(8,128)(2,1)S(1)}, bf16[320,128]{1,0:T(8,128)(2,1)S(1)}, u32[]{:S(2)}, u32[]{:S(2)}) collective-permute-start(bf16[320,128]{1,0:T(8,128)(2,1)S(1)} %convert_element_type.41), channel_id=1, source_target_pairs={{0,3},{1,2},{2,1},{3,0},{4,7},{5,6},{6,5},{7,4},{8,11},{9,10},{10,... | collective-permute-start | bytes 245768 | tf_op jit(solution)/shard_map/ppermute | solution.py:1560
  (61 other events, 460.4 us)

commit v10 on v9

--- a/solution.py
+++ b/solution.py
@@ -1085,20 +1085,14 @@
 
 
 def placed_transpose(places_ref, sources, plain, ordered):
-    start = 0
-    for source in sources:
-        plain[:, start : start + source.shape[0]] = source[...].T
-        start += source.shape[0]
-    count = places_ref.shape[0]
-    rows = plain.shape[0] // count
-
-    def place(q, _):
-        ordered[pl.ds(pl.multiple_of(places_ref[q] * rows, rows), rows), :] = plain[
-            pl.ds(pl.multiple_of(q * rows, rows), rows), :
-        ]
-        return 0
-
-    lax.fori_loop(0, count, place, 0)
+    rows = ordered.shape[0] // places_ref.shape[0]
+    for q in range(places_ref.shape[0]):
+        place = pl.ds(pl.multiple_of(places_ref[q] * rows, rows), rows)
+        start = 0
+        for source in sources:
+            stop = start + source.shape[0]
+            ordered[place, start:stop] = source[:, q * rows : (q + 1) * rows].T
+            start = stop
 
 
 def feed_body(

time: 523 us -> 523 us (level)
  Pallas kernels: 361 us -> 345 us
  starting transfers between devices: 46.8 us -> 58.7 us
  waiting for transfers between devices: 45.1 us -> 50.9 us
    pallas_call x1, Pallas kernels: 32.9 us -> 21.8 us  [attend_back(): pl.pallas_call(ignoring(functools.partial(attend_back_body, total=total),...]
    ppermute x40, starting transfers between devices: 42.8 us -> 50.7 us  [send(): return lax.ppermute(value, AXES, self.pairs(move))]
    ppermute x40, waiting for transfers between devices: 45.1 us -> 50.9 us  [send(): return lax.ppermute(value, AXES, self.pairs(move))]
  transfers between devices with their start and end apart: 44 -> 44, of which waited for: 9 -> 10; matrix products, arithmetic and copies ran while one was open for 9% -> 9% of each run, Pallas kernels for 54% -> 51%
where the time goes in v10:
time: 523 us; the launch traced here: 517 us
  Pallas kernels  345 us (66%)
  starting transfers between devices  58.7 us (11%)
  waiting for transfers between devices  50.9 us (10%)
  local copies, waits for them, and re-layouts  43.2 us (8%)
  other arithmetic  17.6 us (3%)
    pallas_call x1, Pallas kernels, feed(): pl.pallas_call(ignoring(feed_body, 8, len(after)), grid_spec=pltpu.Prefet...  68.1 us
    ppermute x40, waiting for transfers between devices, send(): return lax.ppermute(value, AXES, self.pairs(move))  50.9 us
    ppermute x40, starting transfers between devices, send(): return lax.ppermute(value, AXES, self.pairs(move))  50.7 us
    pallas_call x2, Pallas kernels, back_scan(): pl.pallas_call(ignoring(back_scan_body, 14, len(after)), grid_spec=pltpu....  40.6 us
    pallas_call x8, Pallas kernels, stage_sums(): pl.pallas_call(ignoring(functools.partial(stage_body, jobs=counts), len(i...  33.7 us
    pallas_call x1, Pallas kernels, attend_back(): pl.pallas_call(ignoring(functools.partial(attend_back_body, total=total),...  21.8 us
    pallas_call x2, Pallas kernels, front(): pl.pallas_call(ignoring(functools.partial(front_body, fresh=row == 0), 5,...  20.2 us
    pallas_call x2, Pallas kernels, by_rows(): pl.pallas_call(ignoring(by_rows_body, 4, len(after)), grid_spec=pltpu.Pre...  19.9 us
  transfers between devices with their start and end apart: 44, of which 10 were waited for; matrix products, arithmetic and copies ran while one was open for 9% of the time, Pallas kernels for 51%

profile of v10, /device:TPU:0, one launch (start us, length us, event | category | flops | bytes accessed | tf_op | source)
XLA Modules:
  0.0 517.3 jit_solution(11886922202320791906)
XLA Ops:
  1.8 3.1 dynamic-slice_bitcast_fusion.2
  4.9 2.5 collective-permute-start.1
  7.6 8.0 %slice.91.refs_7_.right_ref.refs_2_ = bf16[1024,4096]{1,0:T(8,128)(2,1)} slice(bf16[1024,4224]{1,0:T(8,128)(2,1)} %param.30), slice={[0:1024], [128:4224]} | slice | bytes 16777216 | tf_op jit(solution)/shard_map/slice | solution.py:1869
  26.4 6.0 %bias.1 = (f32[9,256,256]{2,1,0:T(8,128)}, f32[9,256,256]{2,1,0:T(8,128)}) custom-call(s32[1]{0:T(128)S(6)} %convert_element_type.34.flag_ref, f32[8,1,512]{2,1,0:T(1,128)} %copy.63.back_row, f32[8,1,512]{2,1,0:T(1,128)} %broadcast_in_dim.42.front_row), custom_call_target="tpu_custom_call" | custom-call | tf_op jit(solution)/shard_map/bias/pallas_call | solution.py:900
  33.1 10.0 %front.2 = (bf16[2,512,1024]{2,1,0:T(8,128)(2,1)}, bf16[2,512,1024]{2,1,0:T(8,128)(2,1)}, bf16[2,512,2048]{2,1,0:T(8,128)(2,1)}, bf16[2,512,2048]{2,1,0:T(8,128)(2,1)}, f32[2,16,8,128]{3,2,1,0:T(8,128)}) custom-call(bf16[512,1024]{1,0:T(8,128)(2,1)} %collective-permute-done.2.refs_0_, f32[1,1024]{1,0:T(1,128)} %bitcast.233, f32[16,8,128]{2,1,0:T(8,128)} %bitcast.206, ...), custom_call_target="tpu_custom_call" | custom-call | flops 1 | bytes 1 | tf_op jit(solution)/shard_map/front/pallas_call | solution.py:130
  43.1 12.6 %collective-permute-done.1.refs_0_ = bf16[512,1024]{1,0:T(8,128)(2,1)S(1)} collective-permute-done((bf16[512,1024]{1,0:T(8,128)(2,1)}, bf16[512,1024]{1,0:T(8,128)(2,1)S(1)}, u32[]{:S(2)}, u32[]{:S(2)}) %collective-permute-start.1) | collective-permute-done | bytes 1048608 | tf_op jit(solution)/shard_map/ppermute | solution.py:1554
  56.7 10.2 %front.3 = (bf16[2,512,1024]{2,1,0:T(8,128)(2,1)}, bf16[2,512,1024]{2,1,0:T(8,128)(2,1)}, bf16[2,512,2048]{2,1,0:T(8,128)(2,1)}, bf16[2,512,2048]{2,1,0:T(8,128)(2,1)}, f32[2,16,8,128]{3,2,1,0:T(8,128)}) custom-call(bf16[512,1024]{1,0:T(8,128)(2,1)} %copy-done.18, ...), custom_call_target="tpu_custom_call", output_to_operand_aliasing={{0}: (5, {}), {1}: (6, {}), {2}: (7, {}), {3}: (8, {}), {4}... | custom-call | flops 1 | bytes 1 | tf_op jit(solution)/shard_map/front/pallas_call | solution.py:130
  68.6 2.4 collective-permute-start.7
  71.0 17.3 %front_scan.1 = (f32[2,512,1024]{2,1,0:T(8,128)}, bf16[2,512,1024]{2,1,0:T(8,128)(2,1)}, f32[2,4,16,8,128]{4,3,2,1,0:T(8,128)}, f32[2,512,128]{2,1,0:T(8,128)}, ...) custom-call(s32[9]{0:T(128)} %concatenate.36.refs_10_.table_ref.refs_0_, ...), custom_call_target="tpu_custom_call" | custom-call | flops 99999997952 | bytes 1 | tf_op jit(solution)/shard_map/front_scan/pallas_call | solution.py:243
  88.9 13.0 %product.1.pre_ref.update_ref.refs_5_.refs_6_ = bf16[1024,4096]{1,0:T(8,128)(2,1)} custom-call(bf16[1024,1024]{1,0:T(8,128)(2,1)} %bitcast.184, bf16[1024,4096]{1,0:T(8,128)(2,1)} %slice.91.refs_7_.right_ref.refs_2_), custom_call_target="tpu_custom_call" | custom-call | flops 1 | bytes 1 | tf_op jit(solution)/shard_map/product/pallas_call | solution.py:1253
  102.6 13.3 %attend.1 = (bf16[2,512,2048]{2,1,0:T(8,128)(2,1)}, bf16[2,512,2048]{2,1,0:T(8,128)(2,1)}, f32[2,1,512]{2,1,0:T(1,128)}) custom-call(s32[9]{0:T(128)} %concatenate.36.refs_10_.table_ref.refs_0_, bf16[2,512,128]{2,1,0:T(8,128)(2,1)} %get-tuple-element.120.q_ref.refs_1_, f32[9,256,256]{2,1,0:T(8,128)} %get-tuple-element.111.refs_6_.bias_ref, ...), custom_call_target="tpu_custom_call" | custom-call | flops 1 | bytes 1 | tf_op jit(solution)/shard_map/attend/pallas_call | solution.py:629
  115.8 12.8 %candidate.1 = (f32[1024,1024]{1,0:T(8,128)}, f32[1024,1024]{1,0:T(8,128)}, bf16[1024,1024]{1,0:T(8,128)(2,1)}) custom-call(bf16[1024,2048]{1,0:T(8,128)(2,1)} %bitcast.176, bf16[2048,1024]{1,0:T(8,128)(2,1)} %refs_9_.1, bf16[1024,4096]{1,0:T(8,128)(2,1)} %product.1.pre_ref.update_ref.refs_5_.refs_6_, ...), custom_call_target="tpu_custom_call" | custom-call | flops 1 | bytes 1 | tf_op jit(solution)/shard_map/candidate/pallas_call | solution.py:950
  129.6 68.1 %feed.1 = (bf16[512,1024]{1,0:T(8,128)(2,1)}, bf16[512,1024]{1,0:T(8,128)(2,1)}, f32[1024,1024]{1,0:T(8,128)}, bf16[4,1024,512]{2,1,0:T(8,128)(2,1)}, bf16[4,102...) custom-call(s32[8]{0:T(128)} %broadcast_select_fusion.1.refs_11_.refs_0_, ...), custom_call_target="tpu_custom_call" | custom-call | flops 1 | bytes 1 | tf_op jit(solution)/shard_map/feed/pallas_call | solution.py:1195
  199.3 4.0 collective-permute-start.9
  203.3 19.9 %gate.1 = (f32[1024,1024]{1,0:T(8,128)}, bf16[1024,4096]{1,0:T(8,128)(2,1)}, bf16[1024,2048]{1,0:T(8,128)(2,1)}, f32[1,1024]{1,0:T(1,128)}) custom-call(f32[1024,1024]{1,0:T(8,128)} %get-tuple-element.131.refs_0_, bf16[512,1024]{1,0:T(8,128)(2,1)} %copy-done.19, bf16[512,1024]{1,0:T(8,128)(2,1)} %collective-permute-done.7.refs_4_.refs_2_, ...), custom_call_target="tpu_custom_call" | custom-call | flops 99999997952 | bytes 1 | tf_op jit(solution)/shard_map/gate/pallas_call | solution.py:1039
  223.2 5.2 %stage_sums.8.refs_4_ = bf16[2,2048,512]{2,1,0:T(8,128)(2,1)} custom-call(bf16[1,4096,512]{2,1,0:T(8,128)(2,1)} %bitcast.156, bf16[1,4096,512]{2,1,0:T(8,128)(2,1)} %collective-permute-done.10.refs_1_, bf16[1,4096,512]{2,1,0:T(8,128)(2,1)} %bitcast.161, bf16[1,4096,512]{2,1,0:T(8,128)(2,1)} %collective-permute-done.11.refs_3_.refs_4_.refs_5_.refs_6_.refs_7_, ...), custom_call_target="tpu_custom_call" | custom-call | flops 1 | bytes 1 | tf_op jit(solution)/shard_map/stage_sums/pallas_call | solution.py:1526
  228.4 3.6 collective-permute-start.14
  232.0 15.1 %by_rows.2 = (bf16[4,1,128,4096]{3,2,1,0:T(8,128)(2,1)}, bf16[4,1,128,4096]{3,2,1,0:T(8,128)(2,1)}) custom-call(s32[8]{0:T(128)} %broadcast_select_fusion.1.refs_11_.refs_0_, s32[1]{0:T(128)} %constant.104.clone.1.refs_1_, bf16[1024,1024]{1,0:T(8,128)(2,1)} %bitcast.185, bf16[1024,4096]{1,0:T(8,128)(2,1)} %get-tuple-element.134.refs_3_.refs_2_.refs_0_, ...), custom_call_target="tpu_custom_call" | custom-call | flops 99999997952 | bytes 1 | tf_op jit(solution)/shard_map/by_rows/pallas_call | solution.py:1400
  247.1 11.7 %by_columns.1 = (bf16[4,1024,256]{2,1,0:T(8,128)(2,1)}, bf16[4,1024,256]{2,1,0:T(8,128)(2,1)}) custom-call(s32[8]{0:T(128)} %broadcast_select_fusion.1.refs_11_.refs_0_, s32[4]{0:T(128)} %get-tuple-element.109.refs_12_.refs_1_, bf16[1024,4096]{1,0:T(8,128)(2,1)} %get-tuple-element.134.refs_3_.refs_2_.refs_0_, bf16[1024,2048]{1,0:T(8,128)(2,1)} %bitcast.177, ...), custom_call_target="tpu_custom_call" | custom-call | flops 1 | bytes 1 | tf_op jit(solution)/shard_map/by_columns/pallas_call | solution.py:1344
  258.9 21.8 %attend_back.1 = (f32[2,512,128]{2,1,0:T(8,128)}, bf16[2,512,128]{2,1,0:T(8,128)(2,1)}, bf16[2,512,2048]{2,1,0:T(8,128)(2,1)}, bf16[2,512,2176]{2,1,0:T(8,128)(2,1)}, f32[8,1,512]{2,1,0:T(1,128)}) custom-call(s32[9]{0:T(128)} %concatenate.36.refs_10_.table_ref.refs_0_, bf16[2,512,128]{2,1,0:T(8,128)(2,1)} %get-tuple-element.120.q_ref.refs_1_, ...), custom_call_target="tpu_custom_call" | custom-call | flops 99999997952 | bytes 1 | tf_op jit(solution)/shard_map/attend_back/pallas_call | solution.py:812
  282.6 5.0 stage_sums.9
  287.7 11.1 %collective-permute-start.16 = (bf16[2,1024,512]{2,1,0:T(8,128)(2,1)}, bf16[2,1024,512]{2,1,0:T(8,128)(2,1)}, u32[]{:S(2)}, u32[]{:S(2)}) collective-permute-start(bf16[2,1024,512]{2,1,0:T(8,128)(2,1)} %get-tuple-element.153.refs_7_), channel_id=1, source_target_pairs={{0,16},{1,17},{2,18},{3,19},{4,12},{5,13},{6,14},{7,15},{8,24},{9,... | collective-permute-start | bytes 6291464 | tf_op jit(solution)/shard_map/ppermute | solution.py:1554
  299.8 15.9 %value_back.1 = (f32[1024,1024]{1,0:T(8,128)}, bf16[4,4,128,512]{3,2,1,0:T(8,128)(2,1)}, bf16[4,4,128,512]{3,2,1,0:T(8,128)(2,1)}) custom-call(s32[8]{0:T(128)} %broadcast_select_fusion.1.refs_11_.refs_0_, s32[4]{0:T(128)} %get-tuple-element.109.refs_12_.refs_1_, bf16[1024,1024]{1,0:T(8,128)(2,1)} %bitcast.201, bf16[1024,2048]{1,0:T(8,128)(2,1)} %bitcast.268, ...), custom_call_target="tpu_custom_call" | custom-call | flops 99999997952 | bytes 1 | tf_op jit(solution)/shard_map/value_back/pallas_call | solution.py:1471
  315.8 2.5 fusion.8
  318.3 4.8 by_rows.3
  323.6 3.4 stage_sums.10.refs_5_
  328.0 17.1 %smooth_back.1 = f32[1024,1024]{1,0:T(8,128)} custom-call(bf16[1024,4096]{1,0:T(8,128)(2,1)} %get-tuple-element.134.refs_3_.refs_2_.refs_0_, bf16[1024,128]{1,0:T(8,128)(2,1)} %get-tuple-element.270.refs_3_.refs_1_, bf16[1024,4096]{1,0:T(8,128)(2,1)} %slice.91.refs_7_.right_ref.refs_2_, bf16[1024,128]{1,0:T(8,128)(2,1)} %slice.92.refs_8_.proj_ref.refs_3_, ...), custom_call_target="tpu_custom_call" | custom-call | flops 99999997952 | bytes 1 | tf_op jit(solution)/shard_map/smooth_back/pallas_call | solution.py:1291
  346.4 4.8 stage_sums.11
  351.3 2.5 collective-permute-start.21
  357.7 8.1 %back_ends.1.refs_19_.refs_12_ = f32[2,16,8,128]{3,2,1,0:T(8,128)} custom-call(f32[2,512,1024]{2,1,0:T(8,128)} %bitcast.179, f32[16,8,128]{2,1,0:T(8,128)} %bitcast.209, bf16[2,512,512]{2,1,0:T(8,128)(2,1)} %get-tuple-element.162.refs_2_, bf16[1,1024,512]{2,1,0:T(8,128)(2,1)} %get-tuple-element.163.refs_3_, ...), custom_call_target="tpu_custom_call" | custom-call | flops 1 | bytes 1 | tf_op jit(solution)/shard_map/back_ends/pallas_call | solution.py:322
  366.6 1.9 collective-permute-start.28
  369.5 7.8 %collective-permute-done.21.refs_4_.refs_9_.refs_10_ = bf16[2,512,512]{2,1,0:T(8,128)(2,1)S(1)} collective-permute-done((bf16[2,512,512]{2,1,0:T(8,128)(2,1)}, bf16[2,512,512]{2,1,0:T(8,128)(2,1)S(1)}, u32[]{:S(2)}, u32[]{:S(2)}) %collective-permute-start.21) | collective-permute-done | bytes 1048608 | tf_op jit(solution)/shard_map/ppermute | solution.py:1554
  379.3 4.7 stage_sums.12
  387.7 20.2 %back_scan.2 = (bf16[512,1024]{1,0:T(8,128)(2,1)}, f32[16,8,128]{2,1,0:T(8,128)}, f32[16,8,128]{2,1,0:T(8,128)}, f32[1,1024]{1,0:T(1,128)}, f32[1,1024]{1,0:T(1,128)}) custom-call(s32[9]{0:T(128)} %concatenate.36.refs_10_.table_ref.refs_0_, s32[1]{0:T(128)} %constant.104.clone.1.refs_1_, bf16[2,512,1024]{2,1,0:T(8,128)(2,1)} %get-tuple-element.117.x_ref.refs_2_, ...), custom_call_target="tpu_custom_call" | custom-call | flops 99999997952 | bytes 1 | tf_op jit(solution)/shard_map/back_scan/pallas_call | solution.py:468
  407.9 1.9 collective-permute-start.31
  409.8 2.4 collective-permute-done.25.refs_5_.refs_11_
  414.2 5.7 %stage_sums.13 = (f32[2,256,512]{2,1,0:T(8,128)}, bf16[1,128,4096]{2,1,0:T(8,128)(2,1)}, bf16[1,256,512]{2,1,0:T(8,128)(2,1)}, bf16[1,512,256]{2,1,0:T(8,128)(2,1)}, bf16[1,128,128]{2,1,0:T(8,128)(2,1)}) custom-call(bf16[1,4096,512]{2,1,0:T(8,128)(2,1)} %bitcast.160, bf16[1,4096,512]{2,1,0:T(8,128)(2,1)} %collective-permute-done.10.refs_1_, ...), custom_call_target="tpu_custom_call" | custom-call | flops 1 | bytes 1 | tf_op jit(solution)/shard_map/stage_sums/pallas_call | solution.py:1526
  424.0 2.0 collective-permute-start.33
  426.2 20.4 %back_scan.3 = (bf16[512,1024]{1,0:T(8,128)(2,1)}, f32[16,8,128]{2,1,0:T(8,128)}, f32[16,8,128]{2,1,0:T(8,128)}, f32[1,1024]{1,0:T(1,128)}, f32[1,1024]{1,0:T(1,128)}) custom-call(s32[9]{0:T(128)} %concatenate.36.refs_10_.table_ref.refs_0_, s32[1]{0:T(128)} %constant.103.clone.1.refs_1_, bf16[2,512,1024]{2,1,0:T(8,128)(2,1)} %get-tuple-element.117.x_ref.refs_2_, ...), custom_call_target="tpu_custom_call" | custom-call | flops 99999997952 | bytes 1 | tf_op jit(solution)/shard_map/back_scan/pallas_call | solution.py:468
  451.0 3.7 collective-permute-done.34.refs_11_.refs_13_
  455.4 2.3 stage_sums.14
  461.1 3.4 collective-permute-start.38
  467.2 2.9 collective-permute-start.40
  474.7 18.7 %collective-permute-done.39.refs_8_ = bf16[1,256,256]{2,1,0:T(8,128)(2,1)S(1)} collective-permute-done((bf16[1,256,256]{2,1,0:T(8,128)(2,1)S(1)}, bf16[1,256,256]{2,1,0:T(8,128)(2,1)S(1)}, u32[]{:S(2)}, u32[]{:S(2)}) %collective-permute-start.39) | collective-permute-done | bytes 131104 | tf_op jit(solution)/shard_map/ppermute | solution.py:1554
  493.4 2.8 collective-permute-done.40.refs_14_
  497.9 2.6 stage_sums.15
  503.9 3.4 collective-permute-start.42
  509.7 2.3 maximum_convert_fusion
  (265 shorter events, 70.4 us)
Async XLA Ops:
  1.3 23.2 %collective-permute-start = (f32[2]{0:T(128)S(1)}, f32[2]{0:T(128)S(1)}, u32[]{:S(2)}, u32[]{:S(2)}) collective-permute-start(f32[2]{0:T(128)S(1)} %convert_element_type.33), channel_id=1, source_target_pairs={{0,4},{1,5},{2,6},{3,7},{4,0},{5,1},{6,2},{7,3},{8,12},{9,13},{10,... | collective-permute-start | bytes 32 | tf_op jit(solution)/shard_map/ppermute | solution.py:1554
  4.9 27.6 %collective-permute-start.2 = (bf16[512,1024]{1,0:T(8,128)(2,1)}, bf16[512,1024]{1,0:T(8,128)(2,1)}, u32[]{:S(2)}, u32[]{:S(2)}) collective-permute-start(bf16[512,1024]{1,0:T(8,128)(2,1)} %get-tuple-element.277), channel_id=1, source_target_pairs={{0,4},{1,0},{2,5},{3,1},{4,6},{5,2},{6,7},{7,3},{8,12},{9,8},{10,1... | collective-permute-start | bytes 3145736 | tf_op jit(solution)/shard_map/ppermute | solution.py:1554
  4.9 50.8 %collective-permute-start.1 = (bf16[512,1024]{1,0:T(8,128)(2,1)}, bf16[512,1024]{1,0:T(8,128)(2,1)S(1)}, u32[]{:S(2)}, u32[]{:S(2)}) collective-permute-start(bf16[512,1024]{1,0:T(8,128)(2,1)} %get-tuple-element.278), channel_id=1, source_target_pairs={{0,1},{1,5},{2,0},{3,4},{4,3},{5,7},{6,2},{7,6},{8,9},{9,13},{10,8... | collective-permute-start | bytes 3145736 | tf_op jit(solution)/shard_map/ppermute | solution.py:1554
  66.9 1.6 collective-permute-start.3
  66.9 35.0 %collective-permute-start.5 = (bf16[2,512,2048]{2,1,0:T(8,128)(2,1)}, bf16[2,512,2048]{2,1,0:T(8,128)(2,1)}, u32[]{:S(2)}, u32[]{:S(2)}) collective-permute-start(bf16[2,512,2048]{2,1,0:T(8,128)(2,1)} %get-tuple-element.123.v_own.refs_7_), channel_id=1, source_target_pairs={{0,4},{1,5},{2,6},{3,7},{4,0},{5,1},{6,2},{7,3},{8,12},{9,13},{10,... | collective-permute-start | bytes 12582920 | tf_op jit(solution)/shard_map/ppermute | solution.py:1554
  68.5 60.2 %collective-permute-start.6 = (bf16[512,1024]{1,0:T(8,128)(2,1)S(1)}, bf16[512,1024]{1,0:T(8,128)(2,1)S(1)}, u32[]{:S(2)}, u32[]{:S(2)}) collective-permute-start(bf16[512,1024]{1,0:T(8,128)(2,1)S(1)} %copy-done.6), channel_id=1, source_target_pairs={{0,4},{1,0},{2,5},{3,1},{4,6},{5,2},{6,7},{7,3},{8,12},{9,8},{10,1... | collective-permute-start | bytes 3145736 | tf_op jit(solution)/shard_map/ppermute | solution.py:1554
  68.6 60.0 %collective-permute-start.7 = (bf16[512,1024]{1,0:T(8,128)(2,1)S(1)}, bf16[512,1024]{1,0:T(8,128)(2,1)}, u32[]{:S(2)}, u32[]{:S(2)}) collective-permute-start(bf16[512,1024]{1,0:T(8,128)(2,1)S(1)} %copy-done.5), channel_id=1, source_target_pairs={{0,1},{1,5},{2,0},{3,4},{4,3},{5,7},{6,2},{7,6},{8,9},{9,13},{10,8... | collective-permute-start | bytes 3145736 | tf_op jit(solution)/shard_map/ppermute | solution.py:1554
  88.3 13.6 %collective-permute-start.4 = (bf16[2,512,128]{2,1,0:T(8,128)(2,1)}, bf16[2,512,128]{2,1,0:T(8,128)(2,1)S(1)}, u32[]{:S(2)}, u32[]{:S(2)}) collective-permute-start(bf16[2,512,128]{2,1,0:T(8,128)(2,1)} %get-tuple-element.122.k_own.refs_5_), channel_id=1, source_target_pairs={{0,4},{1,5},{2,6},{3,7},{4,0},{5,1},{6,2},{7,3},{8,12},{9,13},{10,... | collective-permute-start | bytes 786440 | tf_op jit(solution)/shard_map/ppermute | solution.py:1554
  197.7 25.5 %collective-permute-start.10 = (bf16[1,4096,512]{2,1,0:T(8,128)(2,1)}, bf16[1,4096,512]{2,1,0:T(8,128)(2,1)}, u32[]{:S(2)}, u32[]{:S(2)}) collective-permute-start(bf16[1,4096,512]{2,1,0:T(8,128)(2,1)} %bitcast.255), channel_id=1, source_target_pairs={{0,4},{1,5},{2,6},{3,7},{4,0},{5,1},{6,2},{7,3},{8,12},{9,13},{10,... | collective-permute-start | bytes 12582920 | tf_op jit(solution)/shard_map/ppermute | solution.py:1554
  198.3 24.9 %collective-permute-start.11 = (bf16[1,4096,512]{2,1,0:T(8,128)(2,1)}, bf16[1,4096,512]{2,1,0:T(8,128)(2,1)}, u32[]{:S(2)}, u32[]{:S(2)}) collective-permute-start(bf16[1,4096,512]{2,1,0:T(8,128)(2,1)} %bitcast.254), channel_id=1, source_target_pairs={{0,4},{1,5},{2,6},{3,7},{4,0},{5,1},{6,2},{7,3},{8,12},{9,13},{10,... | collective-permute-start | bytes 12582920 | tf_op jit(solution)/shard_map/ppermute | solution.py:1554
  198.4 60.5 %collective-permute-start.8 = (bf16[512,1024]{1,0:T(8,128)(2,1)}, bf16[512,1024]{1,0:T(8,128)(2,1)}, u32[]{:S(2)}, u32[]{:S(2)}) collective-permute-start(bf16[512,1024]{1,0:T(8,128)(2,1)} %get-tuple-element.129), channel_id=1, source_target_pairs={{1,0},{5,1},{0,2},{4,3},{3,4},{7,5},{2,6},{6,7},{9,8},{13,9},{8,10... | collective-permute-start | bytes 3145736 | tf_op jit(solution)/shard_map/ppermute | solution.py:1583
  199.3 59.5 %collective-permute-start.9 = (bf16[512,1024]{1,0:T(8,128)(2,1)}, bf16[512,1024]{1,0:T(8,128)(2,1)}, u32[]{:S(2)}, u32[]{:S(2)}) collective-permute-start(bf16[512,1024]{1,0:T(8,128)(2,1)} %get-tuple-element.130), channel_id=1, source_target_pairs={{4,0},{0,1},{5,2},{1,3},{6,4},{2,5},{7,6},{3,7},{12,8},{8,9},{13,1... | collective-permute-start | bytes 3145736 | tf_op jit(solution)/shard_map/ppermute | solution.py:1583
  228.4 52.9 %collective-permute-start.14 = (bf16[2,2048,512]{2,1,0:T(8,128)(2,1)}, bf16[2,2048,512]{2,1,0:T(8,128)(2,1)}, u32[]{:S(2)}, u32[]{:S(2)}) collective-permute-start(bf16[2,2048,512]{2,1,0:T(8,128)(2,1)} %stage_sums.8.refs_4_), channel_id=1, source_target_pairs={{0,8},{1,9},{2,10},{3,11},{4,20},{5,21},{6,22},{7,23},{8,0},{9,1},... | collective-permute-start | bytes 12582920 | tf_op jit(solution)/shard_map/ppermute | solution.py:1554
  258.8 22.5 %collective-permute-start.15 = (bf16[1,4096,256]{2,1,0:T(8,128)(2,1)}, bf16[1,4096,256]{2,1,0:T(8,128)(2,1)S(1)}, u32[]{:S(2)}, u32[]{:S(2)}) collective-permute-start(bf16[1,4096,256]{2,1,0:T(8,128)(2,1)} %bitcast.257), channel_id=1, source_target_pairs={{0,4},{1,5},{2,6},{3,7},{4,0},{5,1},{6,2},{7,3},{8,12},{9,13},{10,... | collective-permute-start | bytes 6291464 | tf_op jit(solution)/shard_map/ppermute | solution.py:1554
  280.7 19.1 %collective-permute-start.12 = (bf16[2,512,2176]{2,1,0:T(8,128)(2,1)}, bf16[2,512,2176]{2,1,0:T(8,128)(2,1)}, u32[]{:S(2)}, u32[]{:S(2)}) collective-permute-start(bf16[2,512,2176]{2,1,0:T(8,128)(2,1)} %get-tuple-element.146), channel_id=1, source_target_pairs={{0,4},{1,5},{2,6},{3,7},{4,0},{5,1},{6,2},{7,3},{8,12},{9,13},{10,... | collective-permute-start | bytes 13369352 | tf_op jit(solution)/shard_map/ppermute | solution.py:1554
  281.2 42.4 %collective-permute-start.13 = (bf16[1,512,4096]{2,1,0:T(8,128)(2,1)}, bf16[1,512,4096]{2,1,0:T(8,128)(2,1)}, u32[]{:S(2)}, u32[]{:S(2)}) collective-permute-start(bf16[1,512,4096]{2,1,0:T(8,128)(2,1)} %bitcast.194), channel_id=1, source_target_pairs={{0,4},{1,5},{2,6},{3,7},{4,0},{5,1},{6,2},{7,3},{8,12},{9,13},{10,... | collective-permute-start | bytes 12582920 | tf_op jit(solution)/shard_map/ppermute | solution.py:1554
  287.7 57.4 %collective-permute-start.16 = (bf16[2,1024,512]{2,1,0:T(8,128)(2,1)}, bf16[2,1024,512]{2,1,0:T(8,128)(2,1)}, u32[]{:S(2)}, u32[]{:S(2)}) collective-permute-start(bf16[2,1024,512]{2,1,0:T(8,128)(2,1)} %get-tuple-element.153.refs_7_), channel_id=1, source_target_pairs={{0,16},{1,17},{2,18},{3,19},{4,12},{5,13},{6,14},{7,15},{8,24},{9,... | collective-permute-start | bytes 6291464 | tf_op jit(solution)/shard_map/ppermute | solution.py:1554
  298.8 46.3 %collective-permute-start.18 = (bf16[1,2048,256]{2,1,0:T(8,128)(2,1)}, bf16[1,2048,256]{2,1,0:T(8,128)(2,1)}, u32[]{:S(2)}, u32[]{:S(2)}) collective-permute-start(bf16[1,2048,256]{2,1,0:T(8,128)(2,1)} %get-tuple-element.154.refs_8_), channel_id=1, source_target_pairs={{0,8},{1,9},{2,10},{3,11},{4,20},{5,21},{6,22},{7,23},{8,0},{9,1},... | collective-permute-start | bytes 3145736 | tf_op jit(solution)/shard_map/ppermute | solution.py:1554
  315.7 29.4 %collective-permute-start.17 = (bf16[1,2048,512]{2,1,0:T(8,128)(2,1)}, bf16[1,2048,512]{2,1,0:T(8,128)(2,1)S(1)}, u32[]{:S(2)}, u32[]{:S(2)}) collective-permute-start(bf16[1,2048,512]{2,1,0:T(8,128)(2,1)} %bitcast.256), channel_id=1, source_target_pairs={{0,4},{1,5},{2,6},{3,7},{4,0},{5,1},{6,2},{7,3},{8,12},{9,13},{10,... | collective-permute-start | bytes 6291464 | tf_op jit(solution)/shard_map/ppermute | solution.py:1554
  323.1 22.0 %collective-permute-start.19 = (bf16[1,512,128]{2,1,0:T(8,128)(2,1)}, bf16[1,512,128]{2,1,0:T(8,128)(2,1)S(1)}, u32[]{:S(2)}, u32[]{:S(2)}) collective-permute-start(bf16[1,512,128]{2,1,0:T(8,128)(2,1)} %bitcast.222), channel_id=1, source_target_pairs={{0,4},{1,5},{2,6},{3,7},{4,0},{5,1},{6,2},{7,3},{8,12},{9,13},{10,... | collective-permute-start | bytes 393224 | tf_op jit(solution)/shard_map/ppermute | solution.py:1554
  327.0 39.7 %collective-permute-start.22 = (bf16[1,256,4096]{2,1,0:T(8,128)(2,1)}, bf16[1,256,4096]{2,1,0:T(8,128)(2,1)}, u32[]{:S(2)}, u32[]{:S(2)}) collective-permute-start(bf16[1,256,4096]{2,1,0:T(8,128)(2,1)} %stage_sums.10.refs_5_), channel_id=1, source_target_pairs={{0,8},{1,9},{2,10},{3,11},{4,20},{5,21},{6,22},{7,23},{8,0},{9,1},... | collective-permute-start | bytes 6291464 | tf_op jit(solution)/shard_map/ppermute | solution.py:1554
  351.3 26.0 %collective-permute-start.21 = (bf16[2,512,512]{2,1,0:T(8,128)(2,1)}, bf16[2,512,512]{2,1,0:T(8,128)(2,1)S(1)}, u32[]{:S(2)}, u32[]{:S(2)}) collective-permute-start(bf16[2,512,512]{2,1,0:T(8,128)(2,1)} %get-tuple-element.162.refs_2_), channel_id=1, source_target_pairs={{0,1},{1,0},{2,3},{3,2},{4,5},{5,4},{6,7},{7,6},{8,9},{9,8},{10,11... | collective-permute-start | bytes 3145736 | tf_op jit(solution)/shard_map/ppermute | solution.py:1554
  353.8 23.5 %collective-permute-start.23 = (bf16[1,1024,512]{2,1,0:T(8,128)(2,1)}, bf16[1,1024,512]{2,1,0:T(8,128)(2,1)S(1)}, u32[]{:S(2)}, u32[]{:S(2)}) collective-permute-start(bf16[1,1024,512]{2,1,0:T(8,128)(2,1)} %get-tuple-element.163.refs_3_), channel_id=1, source_target_pairs={{0,8},{1,9},{2,10},{3,11},{4,20},{5,21},{6,22},{7,23},{8,0},{9,1},... | collective-permute-start | bytes 3145736 | tf_op jit(solution)/shard_map/ppermute | solution.py:1554
  356.6 12.9 %collective-permute-start.24 = (bf16[1,256,128]{2,1,0:T(8,128)(2,1)}, bf16[1,256,128]{2,1,0:T(8,128)(2,1)S(1)}, u32[]{:S(2)}, u32[]{:S(2)}) collective-permute-start(bf16[1,256,128]{2,1,0:T(8,128)(2,1)} %get-tuple-element.165.refs_5_), channel_id=1, source_target_pairs={{0,8},{1,9},{2,10},{3,11},{4,20},{5,21},{6,22},{7,23},{8,0},{9,1},... | collective-permute-start | bytes 196616 | tf_op jit(solution)/shard_map/ppermute | solution.py:1554
  365.8 20.2 %collective-permute-start.20 = (f32[2,16,8,128]{3,2,1,0:T(8,128)}, f32[2,16,8,128]{3,2,1,0:T(8,128)}, u32[]{:S(2)}, u32[]{:S(2)}) collective-permute-start(f32[2,16,8,128]{3,2,1,0:T(8,128)} %back_ends.1.refs_19_.refs_12_), channel_id=1, source_target_pairs={{0,4},{1,5},{2,6},{3,7},{4,0},{5,1},{6,2},{7,3},{8,12},{9,13},{10,... | collective-permute-start | bytes 393224 | tf_op jit(solution)/shard_map/ppermute | solution.py:1554
  366.6 41.3 %collective-permute-start.28 = (bf16[1,1024,256]{2,1,0:T(8,128)(2,1)}, bf16[1,1024,256]{2,1,0:T(8,128)(2,1)S(1)}, u32[]{:S(2)}, u32[]{:S(2)}) collective-permute-start(bf16[1,1024,256]{2,1,0:T(8,128)(2,1)} %get-tuple-element.164.refs_4_), channel_id=1, source_target_pairs={{0,16},{1,17},{2,18},{3,19},{4,12},{5,13},{6,14},{7,15},{8,24},{9,... | collective-permute-start | bytes 1572872 | tf_op jit(solution)/shard_map/ppermute | solution.py:1554
  383.9 28.3 %collective-permute-start.26 = (bf16[1,128,4096]{2,1,0:T(8,128)(2,1)}, bf16[1,128,4096]{2,1,0:T(8,128)(2,1)S(1)}, u32[]{:S(2)}, u32[]{:S(2)}) collective-permute-start(bf16[1,128,4096]{2,1,0:T(8,128)(2,1)} %get-tuple-element.167.refs_15_), channel_id=1, source_target_pairs={{0,16},{1,17},{2,18},{3,19},{4,12},{5,13},{6,14},{7,15},{8,24},{9,... | collective-permute-start | bytes 3145736 | tf_op jit(solution)/shard_map/ppermute | solution.py:1554
  385.1 27.1 %collective-permute-start.25 = (bf16[2,256,512]{2,1,0:T(8,128)(2,1)}, bf16[2,256,512]{2,1,0:T(8,128)(2,1)S(1)}, u32[]{:S(2)}, u32[]{:S(2)}) collective-permute-start(bf16[2,256,512]{2,1,0:T(8,128)(2,1)} %get-tuple-element.166.refs_14_), channel_id=1, source_target_pairs={{0,2},{1,3},{2,0},{3,1},{4,6},{5,7},{6,4},{7,5},{8,10},{9,11},{10,... | collective-permute-start | bytes 1572872 | tf_op jit(solution)/shard_map/ppermute | solution.py:1554
  385.6 26.5 %collective-permute-start.27 = (bf16[1,512,512]{2,1,0:T(8,128)(2,1)}, bf16[1,512,512]{2,1,0:T(8,128)(2,1)S(1)}, u32[]{:S(2)}, u32[]{:S(2)}) collective-permute-start(bf16[1,512,512]{2,1,0:T(8,128)(2,1)} %get-tuple-element.168.refs_16_), channel_id=1, source_target_pairs={{0,16},{1,17},{2,18},{3,19},{4,12},{5,13},{6,14},{7,15},{8,24},{9,... | collective-permute-start | bytes 1572872 | tf_op jit(solution)/shard_map/ppermute | solution.py:1554
  386.1 23.7 %collective-permute-start.29 = (bf16[1,128,128]{2,1,0:T(8,128)(2,1)}, bf16[1,128,128]{2,1,0:T(8,128)(2,1)S(1)}, u32[]{:S(2)}, u32[]{:S(2)}) collective-permute-start(bf16[1,128,128]{2,1,0:T(8,128)(2,1)} %get-tuple-element.169.refs_17_), channel_id=1, source_target_pairs={{0,16},{1,17},{2,18},{3,19},{4,12},{5,13},{6,14},{7,15},{8,24},{9,... | collective-permute-start | bytes 98312 | tf_op jit(solution)/shard_map/ppermute | solution.py:1554
  407.9 43.1 %collective-permute-start.31 = (bf16[512,1024]{1,0:T(8,128)(2,1)}, bf16[512,1024]{1,0:T(8,128)(2,1)}, u32[]{:S(2)}, u32[]{:S(2)}) collective-permute-start(bf16[512,1024]{1,0:T(8,128)(2,1)} %get-tuple-element.170.refs_28_), channel_id=1, source_target_pairs={{4,0},{0,1},{5,2},{1,3},{6,4},{2,5},{7,6},{3,7},{12,8},{8,9},{13,1... | collective-permute-start | bytes 3145736 | tf_op jit(solution)/shard_map/ppermute | solution.py:1583
  423.9 26.0 %collective-permute-start.32 = (bf16[1,256,1056]{1,2,0:T(8,128)(2,1)S(1)}, bf16[1,256,1056]{1,2,0:T(8,128)(2,1)S(1)}, u32[]{:S(2)}, u32[]{:S(2)}) collective-permute-start(bf16[1,256,1056]{1,2,0:T(8,128)(2,1)S(1)} %copy.66), channel_id=1, source_target_pairs={{0,1},{1,0},{2,3},{3,2},{4,5},{5,4},{6,7},{7,6},{8,9},{9,8},{10,11... | collective-permute-start | bytes 1622024 | tf_op jit(solution)/shard_map/ppermute | solution.py:1554
  424.0 27.0 %collective-permute-start.33 = (bf16[1,512,256]{2,1,0:T(8,128)(2,1)}, bf16[1,512,256]{2,1,0:T(8,128)(2,1)S(1)}, u32[]{:S(2)}, u32[]{:S(2)}) collective-permute-start(bf16[1,512,256]{2,1,0:T(8,128)(2,1)} %get-tuple-element.174.refs_17_), channel_id=1, source_target_pairs={{0,1},{1,0},{2,3},{3,2},{4,5},{5,4},{6,7},{7,6},{8,9},{9,8},{10,11... | collective-permute-start | bytes 786440 | tf_op jit(solution)/shard_map/ppermute | solution.py:1554
  426.0 28.6 %collective-permute-start.34 = (bf16[1,256,512]{2,1,0:T(8,128)(2,1)S(1)}, bf16[1,256,512]{2,1,0:T(8,128)(2,1)S(1)}, u32[]{:S(2)}, u32[]{:S(2)}) collective-permute-start(bf16[1,256,512]{2,1,0:T(8,128)(2,1)S(1)} %copy-done.63), channel_id=1, source_target_pairs={{0,1},{1,0},{2,3},{3,2},{4,5},{5,4},{6,7},{7,6},{8,9},{9,8},{10,11... | collective-permute-start | bytes 786440 | tf_op jit(solution)/shard_map/ppermute | solution.py:1554
  426.1 22.9 %copy-start.44 = (f32[32,128]{1,0:T(8,128)S(1)}, f32[32,128]{1,0:T(8,128)}, u32[]{:S(2)}) copy-start(f32[32,128]{1,0:T(8,128)} %pad_bitcast_fusion) | copy-start | bytes 49156
  426.1 22.9 %copy-start.48 = (f32[1,1024]{1,0:T(1,128)S(1)}, f32[1,1024]{1,0:T(1,128)}, u32[]{:S(2)}) copy-start(f32[1,1024]{1,0:T(1,128)} %get-tuple-element.185) | copy-start | bytes 12292
  426.2 22.9 %copy-start.53 = (f32[128]{0:T(128)S(1)}, f32[128]{0:T(128)}, u32[]{:S(2)}) copy-start(f32[128]{0:T(128)} %get-tuple-element.269) | copy-start | bytes 1540
  446.6 49.6 %collective-permute-start.30 = (bf16[512,1024]{1,0:T(8,128)(2,1)}, bf16[512,1024]{1,0:T(8,128)(2,1)S(1)}, u32[]{:S(2)}, u32[]{:S(2)}) collective-permute-start(bf16[512,1024]{1,0:T(8,128)(2,1)} %get-tuple-element.176.refs_12_), channel_id=1, source_target_pairs={{1,0},{5,1},{0,2},{4,3},{3,4},{7,5},{2,6},{6,7},{9,8},{13,9},{8,10... | collective-permute-start | bytes 3145736 | tf_op jit(solution)/shard_map/ppermute | solution.py:1583
  459.4 5.2 collective-permute-start.35
  461.1 35.0 %collective-permute-start.38 = (bf16[1,128,1056]{2,1,0:T(8,128)(2,1)S(1)}, bf16[1,128,1056]{2,1,0:T(8,128)(2,1)S(1)}, u32[]{:S(2)}, u32[]{:S(2)}) collective-permute-start(bf16[1,128,1056]{2,1,0:T(8,128)(2,1)S(1)} %copy-done.17), channel_id=1, source_target_pairs={{0,2},{1,3},{2,0},{3,1},{4,6},{5,7},{6,4},{7,5},{8,10},{9,11},{10,... | collective-permute-start | bytes 811016 | tf_op jit(solution)/shard_map/ppermute | solution.py:1554
  464.6 6.4 %collective-permute-start.36 = (f32[320,128]{1,0:T(8,128)S(1)}, f32[320,128]{1,0:T(8,128)S(1)}, u32[]{:S(2)}, u32[]{:S(2)}) collective-permute-start(f32[320,128]{1,0:T(8,128)S(1)} %add.92), channel_id=1, source_target_pairs={{0,8},{1,9},{2,10},{3,11},{4,12},{5,13},{6,14},{7,15},{8,0},{9,1},... | collective-permute-start | bytes 491528 | tf_op jit(solution)/shard_map/ppermute | solution.py:1554
  467.1 26.2 %collective-permute-start.39 = (bf16[1,256,256]{2,1,0:T(8,128)(2,1)S(1)}, bf16[1,256,256]{2,1,0:T(8,128)(2,1)S(1)}, u32[]{:S(2)}, u32[]{:S(2)}) collective-permute-start(bf16[1,256,256]{2,1,0:T(8,128)(2,1)S(1)} %copy-done.27), channel_id=1, source_target_pairs={{0,2},{1,3},{2,0},{3,1},{4,6},{5,7},{6,4},{7,5},{8,10},{9,11},{10,... | collective-permute-start | bytes 393224 | tf_op jit(solution)/shard_map/ppermute | solution.py:1554
  467.2 29.0 %collective-permute-start.40 = (bf16[1,128,512]{2,1,0:T(8,128)(2,1)S(1)}, bf16[1,128,512]{2,1,0:T(8,128)(2,1)S(1)}, u32[]{:S(2)}, u32[]{:S(2)}) collective-permute-start(bf16[1,128,512]{2,1,0:T(8,128)(2,1)S(1)} %copy-done.28), channel_id=1, source_target_pairs={{0,2},{1,3},{2,0},{3,1},{4,6},{5,7},{6,4},{7,5},{8,10},{9,11},{10,... | collective-permute-start | bytes 393224 | tf_op jit(solution)/shard_map/ppermute | solution.py:1554
  471.0 29.6 %copy-start.25 = (f32[320,128]{1,0:T(8,128)}, f32[320,128]{1,0:T(8,128)S(1)}, u32[]{:S(2)}) copy-start(f32[320,128]{1,0:T(8,128)S(1)} %add.93.refs_0_) | copy-start | bytes 491524
  471.0 29.6 %collective-permute-start.37 = (f32[320,128]{1,0:T(8,128)S(1)}, f32[320,128]{1,0:T(8,128)S(1)}, u32[]{:S(2)}, u32[]{:S(2)}) collective-permute-start(f32[320,128]{1,0:T(8,128)S(1)} %add.93.refs_0_), channel_id=1, source_target_pairs={{0,16},{1,17},{2,18},{3,19},{4,20},{5,21},{6,22},{7,23},{8,24},{9,... | collective-permute-start | bytes 491528 | tf_op jit(solution)/shard_map/ppermute | solution.py:1554
  503.9 10.0 %collective-permute-start.41 = (bf16[320,128]{1,0:T(8,128)(2,1)S(1)}, bf16[320,128]{1,0:T(8,128)(2,1)S(1)}, u32[]{:S(2)}, u32[]{:S(2)}) collective-permute-start(bf16[320,128]{1,0:T(8,128)(2,1)S(1)} %convert_element_type.41), channel_id=1, source_target_pairs={{0,1},{1,0},{2,3},{3,2},{4,5},{5,4},{6,7},{7,6},{8,9},{9,8},{10,11... | collective-permute-start | bytes 245768 | tf_op jit(solution)/shard_map/ppermute | solution.py:1554
  503.9 10.0 %collective-permute-start.42 = (bf16[320,128]{1,0:T(8,128)(2,1)S(1)}, bf16[320,128]{1,0:T(8,128)(2,1)S(1)}, u32[]{:S(2)}, u32[]{:S(2)}) collective-permute-start(bf16[320,128]{1,0:T(8,128)(2,1)S(1)} %convert_element_type.41), channel_id=1, source_target_pairs={{0,2},{1,3},{2,0},{3,1},{4,6},{5,7},{6,4},{7,5},{8,10},{9,11},{10,... | collective-permute-start | bytes 245768 | tf_op jit(solution)/shard_map/ppermute | solution.py:1554
  507.3 6.6 %collective-permute-start.43 = (bf16[320,128]{1,0:T(8,128)(2,1)S(1)}, bf16[320,128]{1,0:T(8,128)(2,1)S(1)}, u32[]{:S(2)}, u32[]{:S(2)}) collective-permute-start(bf16[320,128]{1,0:T(8,128)(2,1)S(1)} %convert_element_type.41), channel_id=1, source_target_pairs={{0,3},{1,2},{2,1},{3,0},{4,7},{5,6},{6,5},{7,4},{8,11},{9,10},{10,... | collective-permute-start | bytes 245768 | tf_op jit(solution)/shard_map/ppermute | solution.py:1554
  (61 other events, 457.0 us)
